TPU v7x, 32 devices: a whole 2x2x4 slice. The times are simulated.
32 devices in a mesh: groups: 2 (over y), dp: 4 (over x, core), fsdp: 4 (over z).
Axes of the slice: x: 2, y: 2, z: 4, core: 2. Of those that a mesh axis runs over, the one named last changes fastest.
Arguments:
- facies: int32 [128, 64, 2048], P(('groups', 'dp', 'fsdp')), parts along dimension 0, may hold values from 0 to 3
- prior_draws: bfloat16 [128, 512], P(('groups', 'dp', 'fsdp')), parts along dimension 0, may hold values from -6 to 6
- recon_grad: bfloat16 [128, 512], P(('groups', 'dp', 'fsdp')), parts along dimension 0, may hold values from -0.796875 to 0.796875
- w_embed: bfloat16 [256, 128], replicated, may hold values from -0.75 to 0.75
- w_conv: bfloat16 [1024, 256], replicated, may hold values from -0.1875 to 0.1875
- w_head: bfloat16 [256, 512], replicated, may hold values from -1 to 1
Outputs:
- grad_embed: float32 [512, 128], P(('groups', 'fsdp')), parts along dimension 0
- grad_conv: float32 [2048, 256], P(('groups', 'fsdp')), parts along dimension 0
- grad_head: float32 [512, 512], P(('groups', 'fsdp')), parts along dimension 0
There are 2 independent parts, one for each index of `groups`. A program takes and returns all parts, laid end to end along the dimension named above; an argument that names none is the same for every part. Nothing has to cross between parts.
All inputs are finite; a program needn't handle non-finite values.
Results may differ from a plain program's by a relative error of at most 0.0012.
Values may be sent and summed in bfloat16 or wider, within the bound.
No kernel may reach another device: no remote copies, remote signals or barrier semaphores. Data moves between devices by JAX's collectives and lax.ppermute only.
A program may use at most 256 MiB of HBM per device.

v0:
```python
import jax
import jax.numpy as jnp
from jax import lax
from jax.sharding import PartitionSpec as P

PATCH_X = 64
PATCH_Y = 64
PATCH_Z = 32


def silu_slope(pre_act):
    sigmoid_val = jax.nn.sigmoid(pre_act)
    return sigmoid_val * (1.0 + pre_act * (1.0 - sigmoid_val))


def embed_rows(facies, levels_count):
    samples = facies.shape[0]
    voxels = facies.reshape(samples, PATCH_X // 4, 4, PATCH_Y // 4, 4, PATCH_Z // 4, 4)
    voxels = voxels.transpose(0, 1, 3, 5, 2, 4, 6).reshape(-1, 64)
    levels = jnp.arange(levels_count, dtype=jnp.int32)
    one_hot = (voxels[:, :, None] == levels[None, None, :]).astype(jnp.bfloat16)
    return one_hot.reshape(voxels.shape[0], 64 * levels_count)


def group_cells(rows_in, samples, grid_x, grid_y, grid_z):
    channels = rows_in.shape[1]
    blocks = rows_in.reshape(samples, grid_x // 2, 2, grid_y // 2, 2, grid_z // 2, 2, channels)
    blocks = blocks.transpose(0, 1, 3, 5, 2, 4, 6, 7)
    return blocks.reshape(-1, 8 * channels)


def spread_cells(rows_in, samples, grid_x, grid_y, grid_z):
    channels = rows_in.shape[1] // 8
    blocks = rows_in.reshape(samples, grid_x // 2, grid_y // 2, grid_z // 2, 2, 2, 2, channels)
    blocks = blocks.transpose(0, 1, 4, 2, 5, 3, 6, 7)
    return blocks.reshape(-1, channels)


def encode(facies, w_embed, w_conv, w_head):
    samples = facies.shape[0]
    grid_x, grid_y, grid_z = (PATCH_X // 4, PATCH_Y // 4, PATCH_Z // 4)
    one_hot = embed_rows(facies, w_embed.shape[0] // 64)
    pre_embed = jnp.dot(one_hot, w_embed, preferred_element_type=jnp.float32)
    hidden = jax.nn.silu(pre_embed).astype(jnp.bfloat16)
    conv_in = group_cells(hidden, samples, grid_x, grid_y, grid_z)
    pre_conv = jnp.dot(conv_in, w_conv, preferred_element_type=jnp.float32)
    pooled = jnp.mean(jax.nn.silu(pre_conv).reshape(samples, -1, pre_conv.shape[1]), axis=1).astype(
        jnp.bfloat16
    )
    latent = jnp.dot(pooled, w_head, preferred_element_type=jnp.float32).astype(jnp.bfloat16)
    return (one_hot, pre_embed, conv_in, pre_conv, pooled, latent)


def kernel_block(queries, query_square, key_rows, latent_width):
    inner_prod = lax.dot_general(
        queries, key_rows, (((1,), (1,)), ((), ())), preferred_element_type=jnp.float32
    )
    key_float = key_rows.astype(jnp.float32)
    key_square = jnp.sum(key_float * key_float, axis=1)
    square_dist = query_square[:, None] + key_square[None, :] - 2.0 * inner_prod
    kernel = jnp.exp(-square_dist / latent_width)
    mixed = jnp.dot(kernel.astype(jnp.bfloat16), key_rows, preferred_element_type=jnp.float32)
    return (jnp.sum(kernel, axis=1), mixed)


def key_adder(queries):
    query_float = queries.astype(jnp.float32)
    query_square = jnp.sum(query_float * query_float, axis=1)
    latent_width = queries.shape[1]

    def add_block(totals, pieces, offset):
        self_sum, self_mix = kernel_block(queries, query_square, pieces[0], latent_width)
        cross_sum, cross_mix = kernel_block(queries, query_square, pieces[1], latent_width)
        return (self_sum, cross_sum, self_mix, cross_mix)

    return add_block


def back_signals(grid_dims, cotangent, pre_embed, pre_conv, w_conv, w_head):
    samples = cotangent.shape[0]
    cell_count = pre_conv.shape[0] // samples
    back_pool = lax.dot_general(
        cotangent, w_head, (((1,), (1,)), ((), ())), preferred_element_type=jnp.float32
    )
    slope = silu_slope(pre_conv).reshape(samples, cell_count, pre_conv.shape[1])
    conv_grad = (
        (back_pool[:, None, :] / cell_count * slope).reshape(pre_conv.shape).astype(jnp.bfloat16)
    )
    back_rows = lax.dot_general(
        conv_grad, w_conv, (((1,), (1,)), ((), ())), preferred_element_type=jnp.float32
    )
    spread = spread_cells(back_rows, samples, grid_dims[0], grid_dims[1], grid_dims[2])
    embed_grad = (spread * silu_slope(pre_embed)).astype(jnp.bfloat16)
    return (conv_grad, embed_grad)


def column_term(left_rows, right_rows):

    def term_rows(offset, number):
        return lax.dot_general(
            left_rows, right_rows, (((0,), (0,)), ((), ())), preferred_element_type=jnp.float32
        )

    return term_rows


def reduce_share(term_rows, shard_rows):
    return lax.psum_scatter(
        term_rows(jnp.int32(0), shard_rows * lax.axis_size("fsdp")),
        "fsdp",
        scatter_dimension=0,
        tiled=True,
    )


def shards(facies, prior_draws, recon_grad, w_embed, w_conv, w_head):
    one_hot, pre_embed, conv_in, pre_conv, pooled, latent = encode(facies, w_embed, w_conv, w_head)
    add_keys = key_adder(latent)
    rows_here = latent.shape[0]
    latent_width = latent.shape[1]
    zero_sums = (
        jnp.zeros((rows_here,), jnp.float32),
        jnp.zeros((rows_here,), jnp.float32),
        jnp.zeros((rows_here, latent_width), jnp.float32),
        jnp.zeros((rows_here, latent_width), jnp.float32),
    )
    totals = add_keys(
        zero_sums,
        (
            lax.all_gather(latent, ("dp", "fsdp"), axis=0, tiled=True),
            lax.all_gather(prior_draws, ("dp", "fsdp"), axis=0, tiled=True),
        ),
        jnp.int32(0),
    )
    total_count = rows_here * lax.axis_size("dp") * lax.axis_size("fsdp")
    latent_float = latent.astype(jnp.float32)
    pull = (
        -32.0
        / total_count
        * ((totals[0] - totals[1])[:, None] * latent_float - totals[2] + totals[3])
    )
    cotangent = (recon_grad.astype(jnp.float32) + pull).astype(jnp.bfloat16)
    grid_dims = (PATCH_X // 4, PATCH_Y // 4, PATCH_Z // 4)
    conv_grad, embed_grad = back_signals(grid_dims, cotangent, pre_embed, pre_conv, w_conv, w_head)
    term_embed = column_term(one_hot, embed_grad)
    term_conv = column_term(conv_in, conv_grad)
    term_head = column_term(pooled, cotangent)
    group_size = lax.axis_size("fsdp")
    embed_share = w_embed.shape[0] // group_size
    conv_share = w_conv.shape[0] // group_size
    head_share = w_head.shape[0] // group_size
    share_embed = reduce_share(term_embed, embed_share)
    share_conv = reduce_share(term_conv, conv_share)
    share_head = reduce_share(term_head, head_share)
    summed = lax.psum((share_embed, share_conv, share_head), "dp")
    return (summed[0], summed[1], summed[2])


def solution(mesh):
    return jax.shard_map(
        shards,
        mesh=mesh,
        in_specs=(
            P(("groups", "dp", "fsdp"), None, None),
            P(("groups", "dp", "fsdp"), None),
            P(("groups", "dp", "fsdp"), None),
            P(),
            P(),
            P(),
        ),
        out_specs=(
            P(("groups", "fsdp"), None),
            P(("groups", "fsdp"), None),
            P(("groups", "fsdp"), None),
        ),
        check_vma=False,
    )
```

profile of v0, /device:TPU:0, one launch (start us, length us, event | category | flops | bytes accessed | tf_op | source)
XLA Modules:
  0.0 436.1 jit_solution(8016983887424328869)
XLA Ops:
  7.2 0.0 copy-start
  7.2 0.0 reduce-scatter.8.cloned.1.call-start
  7.2 71.5 %reshape.41 = s32[4,16,4,16,4,8,4]{6,5,4,3,2,1,0:T(8,128)} reshape(s32[4,64,2048]{2,1,0:T(8,128)} %param.6) | data formatting | bytes 4194304 | tf_op jit(solution)/shard_map/reshape | solution.py:18
  78.7 119.2 %copy.15 = s32[4,16,16,8,4,4,4]{3,2,1,0,6,5,4:T(8,128)} copy(s32[4,16,16,8,4,4,4]{6,3,5,2,4,1,0:T(8,128)} %bitcast) | data formatting | bytes 4194304 | tf_op jit(solution)/shard_map/transpose | solution.py:19
  197.9 27.5 %eq.22 = s32[8192,64]{0,1:T(8,128)S(1)} reshape(s32[4,16,16,8,4,4,4]{3,2,1,0,6,5,4:T(8,128)} %copy.15) | data formatting | bytes 4194304 | tf_op jit(solution)/shard_map/eq | solution.py:21
  225.4 5.6 %eq.23 = s32[8192,64,4]{0,2,1:T(4,128)} broadcast(s32[8192,64]{0,1:T(8,128)S(1)} %eq.22), dimensions={0,1} | broadcast | bytes 10485760 | tf_op jit(solution)/shard_map/eq | solution.py:21
  231.0 10.0 %eq.24 = s32[8192,256]{0,1:T(8,128)} reshape(s32[8192,64,4]{0,2,1:T(4,128)} %eq.23) | data formatting | bytes 16777216 | tf_op jit(solution)/shard_map/eq | solution.py:21
  241.0 0.1 eq.26
  241.2 0.0 copy-start.7
  241.2 4.3 broadcast_compare_fusion
  245.5 0.0 copy-done.7
  245.5 4.5 %multiply_convert_fusion.1 = (bf16[8192,128]{1,0:T(8,128)(2,1)S(1)}, f32[8192,128]{1,0:T(8,128)}) fusion(pred[8192,256]{0,1:T(32,128)(4,1)S(1)} %broadcast_compare_fusion, bf16[256,128]{1,0:T(8,128)(2,1)S(1)} %copy-done.7), kind=kOutput, calls=%fused_computation.1 | convolution fusion | flops 542113792 | bytes 8454144 | tf_op jit(solution)/shard_map/dot_general | solution.py:43
  250.0 1.7 copy.26
  251.8 2.7 reshape.43
  254.6 3.5 bitcast_reduce_fusion
  258.1 0.3 fusion.15
  258.4 34.4 %all-gather = bf16[16,4,512]{2,1,0:T(4,128)(2,1)S(1)} all-gather(bf16[1,4,512]{2,1,0:T(4,128)(2,1)S(1)} %bitcast.53), channel_id=1, replica_groups=mesh['groups'=2,'dp'=4,'fsdp'=4] {'dp','fsdp'}, dimensions={0}, use_global_device_ids=true | all-gather | bytes 69632 | tf_op jit(solution)/shard_map/all_gather | solution.py:130
  292.7 0.1 multiply_reduce_fusion.1
  292.9 0.0 copy-done.5
  292.9 28.9 %all-gather.1 = bf16[16,4,512]{2,1,0:T(4,128)(2,1)S(1)} all-gather(bf16[1,4,512]{2,1,0:T(4,128)(2,1)S(1)} %bitcast.54), channel_id=1, replica_groups=mesh['groups'=2,'dp'=4,'fsdp'=4] {'dp','fsdp'}, dimensions={0}, use_global_device_ids=true | all-gather | bytes 69632 | tf_op jit(solution)/shard_map/all_gather | solution.py:131
  321.8 0.1 multiply_reduce_fusion
  321.9 0.2 fusion.22
  322.2 0.3 fusion.23
  322.4 0.1 convolution_subtract_fusion
  322.6 0.1 fusion.3
  322.7 1.1 fusion.18
  323.8 0.0 reduce-scatter.8.cloned.1.call-update
  323.8 0.0 reduce-scatter.6.cloned.1.call-start
  323.9 0.1 convolution_multiply_fusion
  324.0 1.6 fusion.12
  325.6 1.7 fusion.24
  327.4 0.0 reduce-scatter.6.cloned.1.call-update
  327.4 0.3 reduce-scatter.4.cloned.1.call-start
  327.7 0.1 dot_general.48
  327.8 0.7 convolution_bitcast_fusion
  328.6 2.3 copy.18
  330.8 0.5 copy-done.8
  331.4 3.0 fusion
  334.4 0.0 reduce-scatter.4.cloned.1.call-update
  334.5 0.0 all-reduce.3.cloned.1.call-start
  334.5 10.0 %reduce-scatter.8.cloned.1.call-done = f32[64,512]{1,0:T(8,128)} async-done(((f32[256,512]{1,0:T(8,128)}), f32[64,512]{1,0:T(8,128)}) %reduce-scatter.8.cloned.1.call-update) | async-done | bytes 131088 | tf_op jit(solution)/shard_map/reduce_scatter | solution.py:108
  344.5 27.8 %reduce-scatter.6.cloned.1.call-done = f32[256,256]{1,0:T(8,128)} async-done(((f32[1024,256]{1,0:T(8,128)}), f32[256,256]{1,0:T(8,128)}) %reduce-scatter.6.cloned.1.call-update) | async-done | bytes 262160 | tf_op jit(solution)/shard_map/reduce_scatter | solution.py:108
  372.3 0.0 all-reduce.3.cloned.1.call-update
  372.3 20.8 %reduce-scatter.4.cloned.1.call-done = f32[64,128]{1,0:T(8,128)} async-done(((f32[256,128]{1,0:T(8,128)}), f32[64,128]{1,0:T(8,128)}) %reduce-scatter.4.cloned.1.call-update) | async-done | bytes 32784 | tf_op jit(solution)/shard_map/reduce_scatter | solution.py:108
  393.1 11.4 %psum.21 = f32[64,128]{1,0:T(8,128)} all-reduce(f32[64,128]{1,0:T(8,128)} %reduce-scatter.4.cloned.1.call-done), channel_id=1, replica_groups=mesh['groups'=2,'dp'=4,'fsdp'=4] {'dp'}, use_global_device_ids=true, to_apply=%region_7.8 | all-reduce | flops 8192 | bytes 65536 | tf_op jit(solution)/shard_map/psum | solution.py:155
  404.5 21.8 %all-reduce.3.cloned.1.call-done = (f32[256,256]{1,0:T(8,128)}, f32[64,512]{1,0:T(8,128)}) async-done(((f32[256,256]{1,0:T(8,128)}, f32[64,512]{1,0:T(8,128)}), (f32[256,256]{1,0:T(8,128)}, f32[64,512]{1,0:T(8,128)})) %all-reduce.3.cloned.1.call-update) | async-done | bytes 393232 | tf_op jit(solution)/shard_map/psum | solution.py:155
  426.3 1.7 copy.32
  428.0 1.6 copy.33
  (17 shorter events, 0.1 us)
Async XLA Ops:
  7.2 247.4 %copy-start = (bf16[1024,256]{1,0:T(8,128)(2,1)S(1)}, bf16[1024,256]{1,0:T(8,128)(2,1)}, u32[]{:S(2)}) copy-start(bf16[1024,256]{1,0:T(8,128)(2,1)} %param.10) | copy-start | bytes 1572868
  7.2 337.4 %reduce-scatter.8.cloned.1.call-start = ((), (), s32[]{:S(2)}) async-start(), calls=%async_computation.5 | async-start | bytes 655360 | tf_op jit(solution)/shard_map/reduce_scatter | solution.py:108
  241.2 4.3 copy-start.7
  245.5 4.5 %copy-start.2 = (pred[8192,256]{0,1:T(32,128)(4,1)}, pred[8192,256]{0,1:T(32,128)(4,1)S(1)}, u32[]{:S(2)}) copy-start(pred[8192,256]{0,1:T(32,128)(4,1)S(1)} %broadcast_compare_fusion) | copy-start | bytes 6291460
  254.5 3.6 copy-start.4
  254.5 38.3 %copy-start.5 = (bf16[4,512]{1,0:T(4,128)(2,1)S(1)}, bf16[4,512]{1,0:T(4,128)(2,1)}, u32[]{:S(2)}) copy-start(bf16[4,512]{1,0:T(4,128)(2,1)} %param.7) | copy-start | bytes 12292
  254.5 68.0 %copy-start.6 = (bf16[4,512]{1,0:T(4,128)(2,1)S(1)}, bf16[4,512]{1,0:T(4,128)(2,1)}, u32[]{:S(2)}) copy-start(bf16[4,512]{1,0:T(4,128)(2,1)} %param.8) | copy-start | bytes 12292
  254.5 71.1 %copy-start.1 = (bf16[1024,1024]{1,0:T(8,128)(2,1)S(1)}, bf16[1024,1024]{1,0:T(8,128)(2,1)}, u32[]{:S(2)}) copy-start(bf16[1024,1024]{1,0:T(8,128)(2,1)} %reshape.43) | copy-start | bytes 6291460
  323.8 48.5 %reduce-scatter.6.cloned.1.call-start = ((), (), s32[]{:S(2)}) async-start(), calls=%async_computation.4 | async-start | bytes 1310720 | tf_op jit(solution)/shard_map/reduce_scatter | solution.py:108
  327.4 65.7 %reduce-scatter.4.cloned.1.call-start = ((), (), s32[]{:S(2)}) async-start(), calls=%async_computation.3 | async-start | bytes 163840 | tf_op jit(solution)/shard_map/reduce_scatter | solution.py:108
  328.5 2.3 copy-start.3
  328.6 2.8 copy-start.8
  334.5 91.9 %all-reduce.3.cloned.1.call-start = ((), (), s32[]{:S(2)}) async-start(), calls=%async_computation.6 | async-start | bytes 786432 | tf_op jit(solution)/shard_map/psum | solution.py:155
Sparse Core Ops, SparseCore 0:
  323.9 20.5 reduce-scatter.7
  346.8 25.4 reduce-scatter.5
  375.2 17.8 reduce-scatter.3
  395.4 30.8 all-reduce.2
where the time goes:
time: 437 us; the launch traced here: 436 us
  local copies, waits for them, and re-layouts  245 us (56%)
  waiting for transfers between devices  80.5 us (18%)
  blocking collectives  74.7 us (17%)
  matrix products  15.8 us (4%)
  between operations  13.9 us (3%)
  other arithmetic  6.15 us (1%)
    transpose x1, local copies, waits for them, and re-layouts, embed_rows(): voxels = voxels.transpose(0, 1, 3, 5, 2, 4, 6).reshape(-1, 64)  119 us
    reshape x1, local copies, waits for them, and re-layouts, embed_rows(): facies.reshape(samples, PATCH_X // 4, 4, PATCH_Y // 4, 4, PATCH_Z // 4, 4)  71.5 us
    reduce_scatter x3, waiting for transfers between devices, reduce_share(): lax.psum_scatter(term_rows(jnp.int32(0), shard_rows * lax.axis_size('fsdp...  58.6 us
    eq x5, local copies, waits for them, and re-layouts, embed_rows(): one_hot = (voxels[:, :, None] == levels[None, None, :]).astype(jnp.bfloat16)  43.2 us
    all_gather x1, blocking collectives, shards(): lax.all_gather(latent, ('dp', 'fsdp'), axis=0, tiled=True)  34.4 us
    all_gather x1, blocking collectives, shards(): lax.all_gather(prior_draws, ('dp', 'fsdp'), axis=0, tiled=True)  28.9 us
    psum x1, waiting for transfers between devices, shards(): summed = lax.psum((share_embed, share_conv, share_head), 'dp')  21.8 us
    psum x1, blocking collectives, shards(): summed = lax.psum((share_embed, share_conv, share_head), 'dp')  11.4 us
  transfers between devices with their start and end apart: 4, of which 4 were waited for; matrix products, arithmetic and copies ran while one was open for 2% of the time, Pallas kernels for 0%

commit v1 on v0

v1 whole, which is shorter than its diff:
```python
import jax
import jax.numpy as jnp
from jax import lax
from jax.experimental import pallas as pl
from jax.experimental.pallas import tpu as pltpu
from jax.sharding import PartitionSpec as P

PATCH_X = 64
PATCH_Y = 64
PATCH_Z = 32
LEVELS = 4
GROUP = ("dp", "fsdp")
NT = (((1,), (1,)), ((), ()))
F32 = jnp.float32
BF16 = jnp.bfloat16


def iota(shape, dim):
    return lax.broadcasted_iota(jnp.int32, shape, dim)


def mm(left, right):
    return jnp.dot(left, right, preferred_element_type=F32)


def mm_nt(left, right):
    return lax.dot_general(left, right, NT, preferred_element_type=F32)


def spread_matrix():
    out_row = iota((512, 128), 0)
    lane = iota((512, 128), 1)
    pair, half = out_row // 128, out_row // 64 % 2
    row_dy, row_dz = out_row // 16 % 4, out_row // 4 % 4
    lane_dy, lane_c, lane_dz = lane // 32, lane // 4 % 8, lane % 4
    hit = (row_dy == lane_dy) & (row_dz == lane_dz) & (lane_c == 2 * pair + half)
    return jnp.where(hit, 1.0, 0.0).astype(BF16)


def pair_weights(w_embed):
    turned = jnp.transpose(w_embed.astype(F32)).astype(BF16)
    halves = []
    for half in range(2):
        row = iota((256, 512), 0)
        lane = iota((256, 512), 1)
        hit = (row // 64 == lane // 128) & (row % 64 == lane % 64) & (lane // 64 % 2 == half)
        halves.append(mm(turned, jnp.where(hit, 1.0, 0.0).astype(BF16)))
    return jnp.concatenate(halves, axis=0).astype(BF16)


def sigmoid(value):
    return 1.0 / (1.0 + jnp.exp(-value))


def forward_kernel(facies, w_embed, w_conv, pooled, one_hot, pre_embed, hidden, pre_conv, packed, sorted_rows):
    row, lane = iota((256, 256), 0), iota((256, 256), 1)
    order = jnp.where((row // 32 == lane % 8) & (row % 32 == lane // 8), 1.0, 0.0).astype(BF16)
    for at in range(0, facies.shape[1], 512):
        part = facies[:, pl.ds(at, 512)].astype(F32).astype(BF16)
        sorted_rows[:, pl.ds(at, 512)] = mm(order, part).astype(BF16)
    spread = spread_matrix()
    level = iota((512, 256), 0) % 4
    for t in range(8):
        for dy2 in range(2):
            j, dx = 2 * (t // 4) + dy2, t % 4
            rows = [
                sorted_rows[pl.ds(t * 32, 32), pl.ds((2 * b2 + dy2) * 128, 128)] for b2 in range(8)
            ]
            voxels = jnp.concatenate(rows, axis=0)
            copied = mm_nt(spread, voxels)
            hot = jnp.where(copied == level.astype(F32), 1.0, 0.0).astype(BF16)
            for cp in range(4):
                one_hot[cp, j, pl.ds(dx * 128, 128), :] = hot[cp * 128 : (cp + 1) * 128]
    packed[...] = pair_weights(w_embed[...])
    conv_turned = jnp.transpose(w_conv[...].astype(F32)).astype(BF16)
    sums = jnp.zeros((256, 128), F32)
    for cp in range(4):
        for j in range(4):
            pre = mm(packed[...], one_hot[cp, j])
            pre_embed[cp, j] = pre
            hidden[cp, j] = (pre * sigmoid(pre)).astype(BF16)
        pre = mm(conv_turned, hidden[cp].reshape(1024, 256))
        pre_conv[cp] = pre
        act = pre * sigmoid(pre)
        sums = sums + act[:, :128] + act[:, 128:]
    pick = jnp.where(iota((8, 128), 1) // 8 % 4 == iota((8, 128), 0), 1.0, 0.0)
    total = lax.dot_general(pick, sums, NT, precision=lax.Precision.HIGHEST, preferred_element_type=F32)
    pooled[...] = (total[:4] / 256.0).astype(BF16)


def pair_kernel(queries, query_square, keys):
    inner = mm_nt(queries, keys)
    key_float = keys.astype(F32)
    count = keys.shape[0]
    key_square = jnp.sum(key_float * key_float, axis=1, keepdims=True)
    key_row = jnp.transpose(jnp.broadcast_to(key_square, (count, 128)))[:1]
    kern = jnp.exp(-(query_square + key_row - 2.0 * inner) / keys.shape[1])
    return jnp.sum(kern, axis=1, keepdims=True), mm(kern.astype(BF16), keys)


def backward_kernel(
    sizes, pooled_rel, side_rel, w_head, w_conv, one_hot, pre_embed, hidden, pre_conv,
    grad_embed, grad_conv, grad_head, pooled_abs, side_abs, head_full
):
    devices, fsdp = sizes
    here = lax.axis_index("dp") * fsdp + lax.axis_index("fsdp")
    for step in range(devices):
        owner = lax.rem(here + (devices - step), devices)
        pooled_abs[owner] = pooled_rel[step].astype(F32)
        side_abs[owner] = side_rel[step].astype(F32)
    samples = pooled_abs.shape[1]
    count = devices * samples
    pooled = pooled_abs[...].reshape(count, pooled_abs.shape[2]).astype(BF16)
    prior = side_abs[:, :samples].reshape(count, side_abs.shape[2]).astype(BF16)
    recon = side_abs[:, samples:].reshape(count, side_abs.shape[2])
    latent = mm(pooled, w_head[...]).astype(BF16)
    latent_float = latent.astype(F32)
    square = jnp.sum(latent_float * latent_float, axis=1, keepdims=True)
    self_sum, self_mix = pair_kernel(latent, square, latent)
    cross_sum, cross_mix = pair_kernel(latent, square, prior)
    pull = -32.0 / count * ((self_sum - cross_sum) * latent_float - self_mix + cross_mix)
    cotangent = (recon + pull).astype(BF16)
    turned = jnp.transpose(pooled.astype(F32)).astype(BF16)
    head_full[...] = mm(turned, cotangent)
    share = grad_head.shape[0]
    start = pl.multiple_of(lax.axis_index("fsdp") * share, share)
    grad_head[...] = head_full[pl.ds(start, share), :]

    lane_sample = iota((128, count), 0) // 8 % 4 + samples * here
    pick = jnp.where(lane_sample == iota((128, count), 1), 1.0, 0.0).astype(BF16)
    lanes = mm(pick, cotangent).astype(BF16)
    back_pool = mm_nt(w_head[...], lanes) / 256.0
    back_pool = jnp.concatenate([back_pool, back_pool], axis=1)
    grads = []
    conv_total = None
    for cp in range(4):
        pre = pre_conv[cp]
        gate = sigmoid(pre)
        grads.append((back_pool * (gate * (1.0 + pre * (1.0 - gate)))).astype(BF16))
        term = mm_nt(hidden[cp].reshape(1024, 256), grads[cp])
        conv_total = term if cp == 0 else conv_total + term
    grad_conv[...] = conv_total
    embed_total = None
    for cp in range(4):
        for j in range(4):
            rows = mm(w_conv[pl.ds(j * 256, 256), :], grads[cp])
            pre = pre_embed[cp, j]
            gate = sigmoid(pre)
            signal = (rows * (gate * (1.0 + pre * (1.0 - gate)))).astype(BF16)
            term = mm_nt(one_hot[cp, j], signal)
            embed_total = term if embed_total is None else embed_total + term
    for dx in range(4):
        grad_embed[pl.ds(dx * 64, 64), :] = (
            embed_total[dx * 128 : dx * 128 + 64, :128] + embed_total[dx * 128 + 64 : dx * 128 + 128, 128:]
        )


VMEM = pl.BlockSpec(memory_space=pltpu.VMEM)


def forward(facies, w_embed, w_conv):
    samples = facies.shape[0]
    return pl.pallas_call(
        forward_kernel,
        out_shape=(
            jax.ShapeDtypeStruct((samples, 256), BF16),
            jax.ShapeDtypeStruct((4, 4, 512, 256), BF16),
            jax.ShapeDtypeStruct((4, 4, 256, 256), F32),
            jax.ShapeDtypeStruct((4, 4, 256, 256), BF16),
            jax.ShapeDtypeStruct((4, 256, 256), F32),
        ),
        in_specs=[VMEM] * 3,
        out_specs=(VMEM,) * 5,
        scratch_shapes=[pltpu.VMEM((256, 512), BF16), pltpu.VMEM((256, 2048), BF16)],
        compiler_params=pltpu.CompilerParams(vmem_limit_bytes=30 * 2**20),
        name="forward",
    )(facies.reshape(samples * PATCH_X, PATCH_Y * PATCH_Z), w_embed, w_conv)


def backward(sizes, pooled_rel, side_rel, w_head, w_conv, saved):
    devices, fsdp = sizes
    samples = pooled_rel.shape[1]
    return pl.pallas_call(
        lambda *refs: backward_kernel(sizes, *refs),
        out_shape=(
            jax.ShapeDtypeStruct((256, 128), F32),
            jax.ShapeDtypeStruct((1024, 256), F32),
            jax.ShapeDtypeStruct((256 // fsdp, 512), F32),
        ),
        in_specs=[VMEM] * 8,
        out_specs=(VMEM,) * 3,
        scratch_shapes=[
            pltpu.VMEM((devices, samples, 256), F32),
            pltpu.VMEM((devices, 2 * samples, 512), F32),
            pltpu.VMEM((256, 512), F32),
        ],
        compiler_params=pltpu.CompilerParams(vmem_limit_bytes=30 * 2**20),
        name="backward",
    )(pooled_rel, side_rel, w_head, w_conv, *saved)


def gather_relative(block, devices):
    if devices > 16:
        full = lax.all_gather(block, GROUP, axis=0)
        here = lax.axis_index(GROUP)
        return jnp.take(full, lax.rem(here + devices - jnp.arange(devices), devices), axis=0)
    blocks = [block]
    for step in range(1, devices):
        blocks.append(lax.ppermute(block, GROUP, [(i, (i + step) % devices) for i in range(devices)]))
    return jnp.stack(blocks)


def reduce_to_owner(grad, dp, fsdp):
    width = grad.shape[1]
    xs = dp // 2
    piece = grad.shape[0] // (fsdp * dp)
    blocks = grad.reshape(fsdp, xs, 2, piece, width)
    core = lax.axis_index("dp") % 2
    x_here, f_here = lax.axis_index("dp") // 2, lax.axis_index("fsdp")
    keep = lax.dynamic_index_in_dim(blocks, core, 2, keepdims=False)
    send = lax.dynamic_index_in_dim(blocks, 1 - core, 2, keepdims=False)
    held = keep + lax.ppermute(send, "dp", [(i, i ^ 1) for i in range(dp)])

    def block_at(dx, df):
        return lax.dynamic_slice(
            held, ((f_here + df) % fsdp, (x_here + dx) % xs, 0, 0), (1, 1, piece, width)
        )[0, 0]

    total = block_at(0, 0)
    for dx in range(xs):
        for df in range(fsdp):
            if dx == 0 and df == 0:
                continue
            pairs = []
            for d in range(dp):
                for f in range(fsdp):
                    to = ((d // 2 + dx) % xs * 2 + d % 2) * fsdp + (f + df) % fsdp
                    pairs.append((d * fsdp + f, to))
            total = total + lax.ppermute(block_at(dx, df), GROUP, pairs)
    parts = [total]
    for step in range(1, dp):
        parts.append(lax.ppermute(total, "dp", [(i, (i + step) % dp) for i in range(dp)]))
    stacked = jnp.stack(parts)
    order = (lax.axis_index("dp") + dp - jnp.arange(dp)) % dp
    return jnp.take(stacked, order, axis=0).reshape(dp * piece, width)


def shards(facies, prior_draws, recon_grad, w_embed, w_conv, w_head):
    dp, fsdp = lax.axis_size("dp"), lax.axis_size("fsdp")
    devices = dp * fsdp
    side_rel = gather_relative(jnp.concatenate([prior_draws, recon_grad], axis=0), devices)
    pooled, *saved = forward(facies, w_embed, w_conv)
    pooled_rel = gather_relative(pooled, devices)
    grad_embed, grad_conv, grad_head = backward((devices, fsdp), pooled_rel, side_rel, w_head, w_conv, saved)
    return (
        reduce_to_owner(grad_embed, dp, fsdp),
        reduce_to_owner(grad_conv, dp, fsdp),
        grad_head,
    )


def solution(mesh):
    return jax.shard_map(
        shards,
        mesh=mesh,
        in_specs=(
            P(("groups", "dp", "fsdp"), None, None),
            P(("groups", "dp", "fsdp"), None),
            P(("groups", "dp", "fsdp"), None),
            P(),
            P(),
            P(),
        ),
        out_specs=(
            P(("groups", "fsdp"), None),
            P(("groups", "fsdp"), None),
            P(("groups", "fsdp"), None),
        ),
        check_vma=False,
    )
```

time: 437 us -> 111 us (0.25)
  local copies, waits for them, and re-layouts: 245 us -> 15.6 us
  blocking collectives: 74.7 us -> 0 us
  starting transfers between devices: 0.39 us -> 74.4 us
  waiting for transfers between devices: 80.5 us -> 8.2 us
  matrix products: 15.8 us -> 0 us
  between operations: 13.9 us -> 0.9 us
  Pallas kernels: 0 us -> 8.24 us
    transpose x2 -> x0, local copies, waits for them, and re-layouts: 122 us -> none  [the longest x1 119 us: embed_rows(): voxels = voxels.transpose(0, 1, 3, 5, 2, 4, 6).reshape(-1, 64)]
    reshape x3 -> x0, local copies, waits for them, and re-layouts: 76 us -> none  [the longest x1 71.5 us: embed_rows(): facies.reshape(samples, PATCH_X // 4, 4, PATCH_Y // 4, 4, PATCH_Z // 4, 4)]
    ppermute x0 -> x52, starting transfers between devices: none -> 74.4 us  [the longest x30 44.2 us: gather_relative(): lax.ppermute(block, GROUP, [(i, (i + step) % devices) for i in range(devi...]
    all_gather x2 -> x0, blocking collectives: 63.3 us -> none  [the longest x1 34.4 us: shards(): lax.all_gather(latent, ('dp', 'fsdp'), axis=0, tiled=True)]
    reduce_scatter x3 -> x0, waiting for transfers between devices: 58.6 us -> none  [reduce_share(): lax.psum_scatter(term_rows(jnp.int32(0), shard_rows * lax.axis_size('fsdp...]
    eq x5 -> x0, local copies, waits for them, and re-layouts: 43.2 us -> none  [embed_rows(): one_hot = (voxels[:, :, None] == levels[None, None, :]).astype(jnp.bfloat16)]
    psum x1 -> x0, waiting for transfers between devices: 21.8 us -> none  [shards(): summed = lax.psum((share_embed, share_conv, share_head), 'dp')]
    dot_general x12 -> x0, matrix products: 15.8 us -> none  [the longest x3 5.86 us: term_rows(): lax.dot_general(left_rows, right_rows, (((0,), (0,)), ((), ())), preferre...]
  transfers between devices with their start and end apart: 4 -> 52, of which waited for: 4 -> 11; matrix products, arithmetic and copies ran while one was open for 2% -> 3% of each run, Pallas kernels for 0% -> 0%
where the time goes in v1:
time: 111 us; the launch traced here: 110 us
  starting transfers between devices  74.4 us (67%)
  local copies, waits for them, and re-layouts  15.6 us (14%)
  Pallas kernels  8.24 us (7%)
  waiting for transfers between devices  8.2 us (7%)
  other arithmetic  3.11 us (3%)
    ppermute x30, starting transfers between devices, gather_relative(): lax.ppermute(block, GROUP, [(i, (i + step) % devices) for i in range(devi...  44.2 us
    ppermute x14, starting transfers between devices, reduce_to_owner(): total = total + lax.ppermute(block_at(dx, df), GROUP, pairs)  24.2 us
    unnamed x47, local copies, waits for them, and re-layouts  14 us
    ppermute x6, starting transfers between devices, reduce_to_owner(): lax.ppermute(total, 'dp', [(i, (i + step) % dp) for i in range(dp)])  5.39 us
    pallas_call x1, Pallas kernels, backward(): pl.pallas_call(lambda *refs: backward_kernel(sizes, *refs), out_shape=(ja...  4.16 us
    pallas_call x1, Pallas kernels, forward(): pl.pallas_call(forward_kernel, out_shape=(jax.ShapeDtypeStruct((samples,...  4.08 us
    ppermute x14, waiting for transfers between devices, reduce_to_owner(): total = total + lax.ppermute(block_at(dx, df), GROUP, pairs)  4.03 us
    ppermute x30, waiting for transfers between devices, gather_relative(): lax.ppermute(block, GROUP, [(i, (i + step) % devices) for i in range(devi...  2.23 us
  transfers between devices with their start and end apart: 52, of which 11 were waited for; matrix products, arithmetic and copies ran while one was open for 3% of the time, Pallas kernels for 0%

profile of v1, /device:TPU:0, one launch (start us, length us, event | category | flops | bytes accessed | tf_op | source)
XLA Modules:
  0.0 110.5 jit_solution(912709305526545006)
XLA Ops:
  0.6 1.6 %copy-done.4 = s32[4,64,2048]{2,1,0:T(8,128)S(1)} copy-done((s32[4,64,2048]{2,1,0:T(8,128)S(1)}, s32[4,64,2048]{2,1,0:T(8,128)}, u32[]{:S(2)}) %copy-start.4) | copy-done | bytes 2097176
  2.2 1.0 copy-done.5
  4.1 4.1 %forward.1 = (bf16[4,256]{1,0:T(4,128)(2,1)S(1)}, bf16[4,4,512,256]{3,2,1,0:T(8,128)(2,1)S(1)}, f32[4,4,256,256]{3,2,1,0:T(8,128)S(1)}, bf16[4,4,256,256]{3,2,1,0:T(8,128)(2,1)S(1)}, f32[4,256,256]{2,1,0:T(8,128)S(1)}) custom-call(s32[256,2048]{1,0:T(8,128)S(1)} %bitcast.145, bf16[256,128]{1,0:T(8,128)(2,1)S(1)} %copy-done.8, bf16[1024,256]{1,0:T(8,128)(2,1)S(1)} %copy-done.5), custom_call_target="tpu_custom_call" | custom-call | tf_op jit(solution)/shard_map/forward/pallas_call | solution.py:163
  8.2 2.0 %copy-done = bf16[4,4,512,256]{3,2,1,0:T(8,128)(2,1)} copy-done((bf16[4,4,512,256]{3,2,1,0:T(8,128)(2,1)}, bf16[4,4,512,256]{3,2,1,0:T(8,128)(2,1)S(1)}, u32[]{:S(2)}) %copy-start) | copy-done | bytes 4194328
  10.2 2.0 %copy-done.2 = f32[4,4,256,256]{3,2,1,0:T(8,128)} copy-done((f32[4,4,256,256]{3,2,1,0:T(8,128)}, f32[4,4,256,256]{3,2,1,0:T(8,128)S(1)}, u32[]{:S(2)}) %copy-start.2) | copy-done | bytes 4194328
  12.2 3.0 %collective-permute-start = (bf16[4,256]{1,0:T(4,128)(2,1)S(1)}, bf16[4,256]{1,0:T(4,128)(2,1)S(1)}, u32[]{:S(2)}, u32[]{:S(2)}) collective-permute-start(bf16[4,256]{1,0:T(4,128)(2,1)S(1)} %get-tuple-element.11), channel_id=1, source_target_pairs={{0,1},{1,2},{2,3},{3,4},{4,5},{5,6},{6,7},{7,8},{8,9},{9,10},{10,1... | collective-permute-start | bytes 6152 | tf_op jit(solution)/shard_map/ppermute | solution.py:209
  15.2 2.6 %collective-permute-start.1 = (bf16[4,256]{1,0:T(4,128)(2,1)S(1)}, bf16[4,256]{1,0:T(4,128)(2,1)S(1)}, u32[]{:S(2)}, u32[]{:S(2)}) collective-permute-start(bf16[4,256]{1,0:T(4,128)(2,1)S(1)} %get-tuple-element.11), channel_id=1, source_target_pairs={{0,2},{1,3},{2,4},{3,5},{4,6},{5,7},{6,8},{7,9},{8,10},{9,11},{10,... | collective-permute-start | bytes 6152 | tf_op jit(solution)/shard_map/ppermute | solution.py:209
  18.3 1.6 %collective-permute-start.3 = (bf16[4,256]{1,0:T(4,128)(2,1)S(1)}, bf16[4,256]{1,0:T(4,128)(2,1)S(1)}, u32[]{:S(2)}, u32[]{:S(2)}) collective-permute-start(bf16[4,256]{1,0:T(4,128)(2,1)S(1)} %get-tuple-element.11), channel_id=1, source_target_pairs={{0,4},{1,5},{2,6},{3,7},{4,8},{5,9},{6,10},{7,11},{8,12},{9,13},{1... | collective-permute-start | bytes 6152 | tf_op jit(solution)/shard_map/ppermute | solution.py:209
  22.1 3.1 %collective-permute-start.6 = (bf16[4,256]{1,0:T(4,128)(2,1)S(1)}, bf16[4,256]{1,0:T(4,128)(2,1)S(1)}, u32[]{:S(2)}, u32[]{:S(2)}) collective-permute-start(bf16[4,256]{1,0:T(4,128)(2,1)S(1)} %get-tuple-element.11), channel_id=1, source_target_pairs={{0,7},{1,8},{2,9},{3,10},{4,11},{5,12},{6,13},{7,14},{8,15},{9,0},... | collective-permute-start | bytes 6152 | tf_op jit(solution)/shard_map/ppermute | solution.py:209
  25.2 1.0 collective-permute-start.7
  26.8 2.7 %collective-permute-start.9 = (bf16[4,256]{1,0:T(4,128)(2,1)S(1)}, bf16[4,256]{1,0:T(4,128)(2,1)S(1)}, u32[]{:S(2)}, u32[]{:S(2)}) collective-permute-start(bf16[4,256]{1,0:T(4,128)(2,1)S(1)} %get-tuple-element.11), channel_id=1, source_target_pairs={{0,10},{1,11},{2,12},{3,13},{4,14},{5,15},{6,0},{7,1},{8,2},{9,3},... | collective-permute-start | bytes 6152 | tf_op jit(solution)/shard_map/ppermute | solution.py:209
  29.6 3.1 %collective-permute-start.10 = (bf16[4,256]{1,0:T(4,128)(2,1)S(1)}, bf16[4,256]{1,0:T(4,128)(2,1)S(1)}, u32[]{:S(2)}, u32[]{:S(2)}) collective-permute-start(bf16[4,256]{1,0:T(4,128)(2,1)S(1)} %get-tuple-element.11), channel_id=1, source_target_pairs={{0,11},{1,12},{2,13},{3,14},{4,15},{5,0},{6,1},{7,2},{8,3},{9,4},{... | collective-permute-start | bytes 6152 | tf_op jit(solution)/shard_map/ppermute | solution.py:209
  34.1 3.4 %collective-permute-start.14 = (bf16[4,256]{1,0:T(4,128)(2,1)S(1)}, bf16[4,256]{1,0:T(4,128)(2,1)S(1)}, u32[]{:S(2)}, u32[]{:S(2)}) collective-permute-start(bf16[4,256]{1,0:T(4,128)(2,1)S(1)} %get-tuple-element.11), channel_id=1, source_target_pairs={{0,15},{1,0},{2,1},{3,2},{4,3},{5,4},{6,5},{7,6},{8,7},{9,8},{10,9... | collective-permute-start | bytes 6152 | tf_op jit(solution)/shard_map/ppermute | solution.py:209
  38.1 1.5 %collective-permute-start.16 = (bf16[8,512]{1,0:T(8,128)(2,1)S(1)}, bf16[8,512]{1,0:T(8,128)(2,1)S(1)}, u32[]{:S(2)}, u32[]{:S(2)}) collective-permute-start(bf16[8,512]{1,0:T(8,128)(2,1)S(1)} %pad_maximum_fusion.2), channel_id=1, source_target_pairs={{0,2},{1,3},{2,4},{3,5},{4,6},{5,7},{6,8},{7,9},{8,10},{9,11},{10,... | collective-permute-start | bytes 24584 | tf_op jit(solution)/shard_map/ppermute | solution.py:209
  39.7 1.8 %collective-permute-start.17 = (bf16[8,512]{1,0:T(8,128)(2,1)S(1)}, bf16[8,512]{1,0:T(8,128)(2,1)S(1)}, u32[]{:S(2)}, u32[]{:S(2)}) collective-permute-start(bf16[8,512]{1,0:T(8,128)(2,1)S(1)} %pad_maximum_fusion.2), channel_id=1, source_target_pairs={{0,3},{1,4},{2,5},{3,6},{4,7},{5,8},{6,9},{7,10},{8,11},{9,12},{10... | collective-permute-start | bytes 24584 | tf_op jit(solution)/shard_map/ppermute | solution.py:209
  41.5 1.0 collective-permute-start.18
  43.3 1.0 collective-permute-start.20
  44.4 2.6 %collective-permute-start.21 = (bf16[8,512]{1,0:T(8,128)(2,1)S(1)}, bf16[8,512]{1,0:T(8,128)(2,1)S(1)}, u32[]{:S(2)}, u32[]{:S(2)}) collective-permute-start(bf16[8,512]{1,0:T(8,128)(2,1)S(1)} %pad_maximum_fusion.2), channel_id=1, source_target_pairs={{0,7},{1,8},{2,9},{3,10},{4,11},{5,12},{6,13},{7,14},{8,15},{9,0},... | collective-permute-start | bytes 24584 | tf_op jit(solution)/shard_map/ppermute | solution.py:209
  47.0 1.0 collective-permute-start.22
  48.9 2.2 %collective-permute-start.24 = (bf16[8,512]{1,0:T(8,128)(2,1)S(1)}, bf16[8,512]{1,0:T(8,128)(2,1)S(1)}, u32[]{:S(2)}, u32[]{:S(2)}) collective-permute-start(bf16[8,512]{1,0:T(8,128)(2,1)S(1)} %pad_maximum_fusion.2), channel_id=1, source_target_pairs={{0,10},{1,11},{2,12},{3,13},{4,14},{5,15},{6,0},{7,1},{8,2},{9,3},... | collective-permute-start | bytes 24584 | tf_op jit(solution)/shard_map/ppermute | solution.py:209
  51.1 3.3 %collective-permute-start.25 = (bf16[8,512]{1,0:T(8,128)(2,1)S(1)}, bf16[8,512]{1,0:T(8,128)(2,1)S(1)}, u32[]{:S(2)}, u32[]{:S(2)}) collective-permute-start(bf16[8,512]{1,0:T(8,128)(2,1)S(1)} %pad_maximum_fusion.2), channel_id=1, source_target_pairs={{0,11},{1,12},{2,13},{3,14},{4,15},{5,0},{6,1},{7,2},{8,3},{9,4},{... | collective-permute-start | bytes 24584 | tf_op jit(solution)/shard_map/ppermute | solution.py:209
  54.6 1.2 %collective-permute-start.28 = (bf16[8,512]{1,0:T(8,128)(2,1)S(1)}, bf16[8,512]{1,0:T(8,128)(2,1)S(1)}, u32[]{:S(2)}, u32[]{:S(2)}) collective-permute-start(bf16[8,512]{1,0:T(8,128)(2,1)S(1)} %pad_maximum_fusion.2), channel_id=1, source_target_pairs={{0,14},{1,15},{2,0},{3,1},{4,2},{5,3},{6,4},{7,5},{8,6},{9,7},{10,... | collective-permute-start | bytes 24584 | tf_op jit(solution)/shard_map/ppermute | solution.py:209
  55.8 3.2 %collective-permute-start.29 = (bf16[8,512]{1,0:T(8,128)(2,1)S(1)}, bf16[8,512]{1,0:T(8,128)(2,1)S(1)}, u32[]{:S(2)}, u32[]{:S(2)}) collective-permute-start(bf16[8,512]{1,0:T(8,128)(2,1)S(1)} %pad_maximum_fusion.2), channel_id=1, source_target_pairs={{0,15},{1,0},{2,1},{3,2},{4,3},{5,4},{6,5},{7,6},{8,7},{9,8},{10,9... | collective-permute-start | bytes 24584 | tf_op jit(solution)/shard_map/ppermute | solution.py:209
  59.0 1.1 collective-permute-done.27
  60.3 2.2 %copy-done.1 = bf16[4,4,512,256]{3,2,1,0:T(8,128)(2,1)S(1)} copy-done((bf16[4,4,512,256]{3,2,1,0:T(8,128)(2,1)S(1)}, bf16[4,4,512,256]{3,2,1,0:T(8,128)(2,1)}, u32[]{:S(2)}) %copy-start.1) | copy-done | bytes 4194328
  62.5 2.2 %copy-done.3 = f32[4,4,256,256]{3,2,1,0:T(8,128)S(1)} copy-done((f32[4,4,256,256]{3,2,1,0:T(8,128)S(1)}, f32[4,4,256,256]{3,2,1,0:T(8,128)}, u32[]{:S(2)}) %copy-start.3) | copy-done | bytes 4194328
  64.7 1.0 copy-done.6
  66.7 4.2 %backward.1 = (f32[256,128]{1,0:T(8,128)S(1)}, f32[1024,256]{1,0:T(8,128)S(1)}, f32[64,512]{1,0:T(8,128)}) custom-call(bf16[16,4,256]{2,1,0:T(4,128)(2,1)S(1)} %constant_dynamic-update-slice_fusion.refs_0_, bf16[16,8,512]{2,1,0:T(8,128)(2,1)S(1)} %constant_dynamic-update-slice_fusion.16.refs_1_, bf16[256,512]{1,0:T(8,128)(2,1)S(1)} %copy-done.7, ...), custom_call_target="tpu_custom_call" | custom-call | tf_op jit(solution)/shard_map/backward/pallas_call | solution.py:183
  72.3 2.1 %collective-permute-start.31 = (f32[16,128]{1,0:T(8,128)S(1)}, f32[16,128]{1,0:T(8,128)S(1)}, u32[]{:S(2)}, u32[]{:S(2)}) collective-permute-start(f32[16,128]{1,0:T(8,128)S(1)} %get-tuple-element.26), channel_id=1, source_target_pairs={{0,1},{1,2},{2,3},{3,0},{4,5},{5,6},{6,7},{7,4},{8,9},{9,10},{10,1... | collective-permute-start | bytes 24584 | tf_op jit(solution)/shard_map/ppermute | solution.py:239
  74.3 2.5 %collective-permute-start.32 = (f32[16,128]{1,0:T(8,128)S(1)}, f32[16,128]{1,0:T(8,128)S(1)}, u32[]{:S(2)}, u32[]{:S(2)}) collective-permute-start(f32[16,128]{1,0:T(8,128)S(1)} %get-tuple-element.32), channel_id=1, source_target_pairs={{0,2},{1,3},{2,0},{3,1},{4,6},{5,7},{6,4},{7,5},{8,10},{9,11},{10,... | collective-permute-start | bytes 24584 | tf_op jit(solution)/shard_map/ppermute | solution.py:239
  76.9 1.4 %collective-permute-start.34 = (f32[16,128]{1,0:T(8,128)S(1)}, f32[16,128]{1,0:T(8,128)S(1)}, u32[]{:S(2)}, u32[]{:S(2)}) collective-permute-start(f32[16,128]{1,0:T(8,128)S(1)} %get-tuple-element.30), channel_id=1, source_target_pairs={{0,8},{1,9},{2,10},{3,11},{4,12},{5,13},{6,14},{7,15},{8,0},{9,1},... | collective-permute-start | bytes 24584 | tf_op jit(solution)/shard_map/ppermute | solution.py:239
  78.3 2.1 %collective-permute-start.35 = (f32[16,128]{1,0:T(8,128)S(1)}, f32[16,128]{1,0:T(8,128)S(1)}, u32[]{:S(2)}, u32[]{:S(2)}) collective-permute-start(f32[16,128]{1,0:T(8,128)S(1)} %get-tuple-element.29), channel_id=1, source_target_pairs={{0,9},{1,10},{2,11},{3,8},{4,13},{5,14},{6,15},{7,12},{8,1},{9,2},... | collective-permute-start | bytes 24584 | tf_op jit(solution)/shard_map/ppermute | solution.py:239
  80.5 1.4 %collective-permute-start.36 = (f32[16,128]{1,0:T(8,128)S(1)}, f32[16,128]{1,0:T(8,128)S(1)}, u32[]{:S(2)}, u32[]{:S(2)}) collective-permute-start(f32[16,128]{1,0:T(8,128)S(1)} %get-tuple-element.28), channel_id=1, source_target_pairs={{0,10},{1,11},{2,8},{3,9},{4,14},{5,15},{6,12},{7,13},{8,2},{9,3},... | collective-permute-start | bytes 24584 | tf_op jit(solution)/shard_map/ppermute | solution.py:239
  81.9 1.9 %collective-permute-start.37 = (f32[16,128]{1,0:T(8,128)S(1)}, f32[16,128]{1,0:T(8,128)S(1)}, u32[]{:S(2)}, u32[]{:S(2)}) collective-permute-start(f32[16,128]{1,0:T(8,128)S(1)} %get-tuple-element.27), channel_id=1, source_target_pairs={{0,11},{1,8},{2,9},{3,10},{4,15},{5,12},{6,13},{7,14},{8,3},{9,0},... | collective-permute-start | bytes 24584 | tf_op jit(solution)/shard_map/ppermute | solution.py:239
  84.7 1.2 %collective-permute-done.36 = f32[16,128]{1,0:T(8,128)S(1)} collective-permute-done((f32[16,128]{1,0:T(8,128)S(1)}, f32[16,128]{1,0:T(8,128)S(1)}, u32[]{:S(2)}, u32[]{:S(2)}) %collective-permute-start.36) | collective-permute-done | bytes 8224 | tf_op jit(solution)/shard_map/ppermute | solution.py:239
  86.5 1.1 collective-permute-start.39
  87.6 1.4 %collective-permute-start.40 = (f32[16,128]{1,0:T(8,128)S(1)}, f32[16,128]{1,0:T(8,128)S(1)}, u32[]{:S(2)}, u32[]{:S(2)}) collective-permute-start(f32[16,128]{1,0:T(8,128)S(1)} %fusion.11), channel_id=1, source_target_pairs={{0,12},{4,0},{8,4},{12,8},{1,13},{5,1},{9,5},{13,9},{2,14},{6,2},{... | collective-permute-start | bytes 24584 | tf_op jit(solution)/shard_map/ppermute | solution.py:242
  89.1 1.7 %collective-permute-start.42 = (f32[64,256]{1,0:T(8,128)S(1)}, f32[64,256]{1,0:T(8,128)S(1)}, u32[]{:S(2)}, u32[]{:S(2)}) collective-permute-start(f32[64,256]{1,0:T(8,128)S(1)} %get-tuple-element.19), channel_id=1, source_target_pairs={{0,1},{1,2},{2,3},{3,0},{4,5},{5,6},{6,7},{7,4},{8,9},{9,10},{10,1... | collective-permute-start | bytes 196616 | tf_op jit(solution)/shard_map/ppermute | solution.py:239
  90.8 2.2 %collective-permute-start.43 = (f32[64,256]{1,0:T(8,128)S(1)}, f32[64,256]{1,0:T(8,128)S(1)}, u32[]{:S(2)}, u32[]{:S(2)}) collective-permute-start(f32[64,256]{1,0:T(8,128)S(1)} %get-tuple-element.25), channel_id=1, source_target_pairs={{0,2},{1,3},{2,0},{3,1},{4,6},{5,7},{6,4},{7,5},{8,10},{9,11},{10,... | collective-permute-start | bytes 196616 | tf_op jit(solution)/shard_map/ppermute | solution.py:239
  93.4 1.1 collective-permute-start.44
  94.4 1.0 collective-permute-start.45
  95.4 1.4 %collective-permute-start.46 = (f32[64,256]{1,0:T(8,128)S(1)}, f32[64,256]{1,0:T(8,128)S(1)}, u32[]{:S(2)}, u32[]{:S(2)}) collective-permute-start(f32[64,256]{1,0:T(8,128)S(1)} %get-tuple-element.22), channel_id=1, source_target_pairs={{0,9},{1,10},{2,11},{3,8},{4,13},{5,14},{6,15},{7,12},{8,1},{9,2},... | collective-permute-start | bytes 196616 | tf_op jit(solution)/shard_map/ppermute | solution.py:239
  96.9 1.3 %collective-permute-start.47 = (f32[64,256]{1,0:T(8,128)S(1)}, f32[64,256]{1,0:T(8,128)S(1)}, u32[]{:S(2)}, u32[]{:S(2)}) collective-permute-start(f32[64,256]{1,0:T(8,128)S(1)} %get-tuple-element.21), channel_id=1, source_target_pairs={{0,10},{1,11},{2,8},{3,9},{4,14},{5,15},{6,12},{7,13},{8,2},{9,3},... | collective-permute-start | bytes 196616 | tf_op jit(solution)/shard_map/ppermute | solution.py:239
  98.2 4.0 %collective-permute-start.48 = (f32[64,256]{1,0:T(8,128)S(1)}, f32[64,256]{1,0:T(8,128)S(1)}, u32[]{:S(2)}, u32[]{:S(2)}) collective-permute-start(f32[64,256]{1,0:T(8,128)S(1)} %get-tuple-element.20), channel_id=1, source_target_pairs={{0,11},{1,8},{2,9},{3,10},{4,15},{5,12},{6,13},{7,14},{8,3},{9,0},... | collective-permute-start | bytes 196616 | tf_op jit(solution)/shard_map/ppermute | solution.py:239
  102.8 1.4 %collective-permute-done.47 = f32[64,256]{1,0:T(8,128)S(1)} collective-permute-done((f32[64,256]{1,0:T(8,128)S(1)}, f32[64,256]{1,0:T(8,128)S(1)}, u32[]{:S(2)}, u32[]{:S(2)}) %collective-permute-start.47) | collective-permute-done | bytes 65568 | tf_op jit(solution)/shard_map/ppermute | solution.py:239
  104.3 1.4 %collective-permute-start.50 = (f32[64,256]{1,0:T(8,128)S(1)}, f32[64,256]{1,0:T(8,128)S(1)}, u32[]{:S(2)}, u32[]{:S(2)}) collective-permute-start(f32[64,256]{1,0:T(8,128)S(1)} %fusion.5), channel_id=1, source_target_pairs={{0,8},{4,12},{8,0},{12,4},{1,9},{5,13},{9,1},{13,5},{2,10},{6,14},... | collective-permute-start | bytes 196616 | tf_op jit(solution)/shard_map/ppermute | solution.py:242
  105.7 1.4 %collective-permute-start.51 = (f32[64,256]{1,0:T(8,128)S(1)}, f32[64,256]{1,0:T(8,128)S(1)}, u32[]{:S(2)}, u32[]{:S(2)}) collective-permute-start(f32[64,256]{1,0:T(8,128)S(1)} %fusion.5), channel_id=1, source_target_pairs={{0,12},{4,0},{8,4},{12,8},{1,13},{5,1},{9,5},{13,9},{2,14},{6,2},{... | collective-permute-start | bytes 196616 | tf_op jit(solution)/shard_map/ppermute | solution.py:242
  108.0 1.0 collective-permute-done.50
  (130 shorter events, 15.7 us)
Async XLA Ops:
  12.2 9.7 %collective-permute-start = (bf16[4,256]{1,0:T(4,128)(2,1)S(1)}, bf16[4,256]{1,0:T(4,128)(2,1)S(1)}, u32[]{:S(2)}, u32[]{:S(2)}) collective-permute-start(bf16[4,256]{1,0:T(4,128)(2,1)S(1)} %get-tuple-element.11), channel_id=1, source_target_pairs={{0,1},{1,2},{2,3},{3,4},{4,5},{5,6},{6,7},{7,8},{8,9},{9,10},{10,1... | collective-permute-start | bytes 6152 | tf_op jit(solution)/shard_map/ppermute | solution.py:209
  15.2 6.9 %collective-permute-start.1 = (bf16[4,256]{1,0:T(4,128)(2,1)S(1)}, bf16[4,256]{1,0:T(4,128)(2,1)S(1)}, u32[]{:S(2)}, u32[]{:S(2)}) collective-permute-start(bf16[4,256]{1,0:T(4,128)(2,1)S(1)} %get-tuple-element.11), channel_id=1, source_target_pairs={{0,2},{1,3},{2,4},{3,5},{4,6},{5,7},{6,8},{7,9},{8,10},{9,11},{10,... | collective-permute-start | bytes 6152 | tf_op jit(solution)/shard_map/ppermute | solution.py:209
  17.8 7.3 %collective-permute-start.2 = (bf16[4,256]{1,0:T(4,128)(2,1)S(1)}, bf16[4,256]{1,0:T(4,128)(2,1)S(1)}, u32[]{:S(2)}, u32[]{:S(2)}) collective-permute-start(bf16[4,256]{1,0:T(4,128)(2,1)S(1)} %get-tuple-element.11), channel_id=1, source_target_pairs={{0,3},{1,4},{2,5},{3,6},{4,7},{5,8},{6,9},{7,10},{8,11},{9,12},{10... | collective-permute-start | bytes 6152 | tf_op jit(solution)/shard_map/ppermute | solution.py:209
  18.3 7.9 %collective-permute-start.3 = (bf16[4,256]{1,0:T(4,128)(2,1)S(1)}, bf16[4,256]{1,0:T(4,128)(2,1)S(1)}, u32[]{:S(2)}, u32[]{:S(2)}) collective-permute-start(bf16[4,256]{1,0:T(4,128)(2,1)S(1)} %get-tuple-element.11), channel_id=1, source_target_pairs={{0,4},{1,5},{2,6},{3,7},{4,8},{5,9},{6,10},{7,11},{8,12},{9,13},{1... | collective-permute-start | bytes 6152 | tf_op jit(solution)/shard_map/ppermute | solution.py:209
  19.9 6.9 %collective-permute-start.4 = (bf16[4,256]{1,0:T(4,128)(2,1)S(1)}, bf16[4,256]{1,0:T(4,128)(2,1)S(1)}, u32[]{:S(2)}, u32[]{:S(2)}) collective-permute-start(bf16[4,256]{1,0:T(4,128)(2,1)S(1)} %get-tuple-element.11), channel_id=1, source_target_pairs={{0,5},{1,6},{2,7},{3,8},{4,9},{5,10},{6,11},{7,12},{8,13},{9,14},{... | collective-permute-start | bytes 6152 | tf_op jit(solution)/shard_map/ppermute | solution.py:209
  21.9 7.6 %collective-permute-start.5 = (bf16[4,256]{1,0:T(4,128)(2,1)S(1)}, bf16[4,256]{1,0:T(4,128)(2,1)S(1)}, u32[]{:S(2)}, u32[]{:S(2)}) collective-permute-start(bf16[4,256]{1,0:T(4,128)(2,1)S(1)} %get-tuple-element.11), channel_id=1, source_target_pairs={{0,6},{1,7},{2,8},{3,9},{4,10},{5,11},{6,12},{7,13},{8,14},{9,15},... | collective-permute-start | bytes 6152 | tf_op jit(solution)/shard_map/ppermute | solution.py:209
  22.1 10.6 %collective-permute-start.6 = (bf16[4,256]{1,0:T(4,128)(2,1)S(1)}, bf16[4,256]{1,0:T(4,128)(2,1)S(1)}, u32[]{:S(2)}, u32[]{:S(2)}) collective-permute-start(bf16[4,256]{1,0:T(4,128)(2,1)S(1)} %get-tuple-element.11), channel_id=1, source_target_pairs={{0,7},{1,8},{2,9},{3,10},{4,11},{5,12},{6,13},{7,14},{8,15},{9,0},... | collective-permute-start | bytes 6152 | tf_op jit(solution)/shard_map/ppermute | solution.py:209
  25.2 8.0 %collective-permute-start.7 = (bf16[4,256]{1,0:T(4,128)(2,1)S(1)}, bf16[4,256]{1,0:T(4,128)(2,1)S(1)}, u32[]{:S(2)}, u32[]{:S(2)}) collective-permute-start(bf16[4,256]{1,0:T(4,128)(2,1)S(1)} %get-tuple-element.11), channel_id=1, source_target_pairs={{0,8},{1,9},{2,10},{3,11},{4,12},{5,13},{6,14},{7,15},{8,0},{9,1},... | collective-permute-start | bytes 6152 | tf_op jit(solution)/shard_map/ppermute | solution.py:209
  26.2 7.0 %collective-permute-start.8 = (bf16[4,256]{1,0:T(4,128)(2,1)S(1)}, bf16[4,256]{1,0:T(4,128)(2,1)S(1)}, u32[]{:S(2)}, u32[]{:S(2)}) collective-permute-start(bf16[4,256]{1,0:T(4,128)(2,1)S(1)} %get-tuple-element.11), channel_id=1, source_target_pairs={{0,9},{1,10},{2,11},{3,12},{4,13},{5,14},{6,15},{7,0},{8,1},{9,2},... | collective-permute-start | bytes 6152 | tf_op jit(solution)/shard_map/ppermute | solution.py:209
  26.8 7.3 %collective-permute-start.9 = (bf16[4,256]{1,0:T(4,128)(2,1)S(1)}, bf16[4,256]{1,0:T(4,128)(2,1)S(1)}, u32[]{:S(2)}, u32[]{:S(2)}) collective-permute-start(bf16[4,256]{1,0:T(4,128)(2,1)S(1)} %get-tuple-element.11), channel_id=1, source_target_pairs={{0,10},{1,11},{2,12},{3,13},{4,14},{5,15},{6,0},{7,1},{8,2},{9,3},... | collective-permute-start | bytes 6152 | tf_op jit(solution)/shard_map/ppermute | solution.py:209
  29.6 8.0 %collective-permute-start.10 = (bf16[4,256]{1,0:T(4,128)(2,1)S(1)}, bf16[4,256]{1,0:T(4,128)(2,1)S(1)}, u32[]{:S(2)}, u32[]{:S(2)}) collective-permute-start(bf16[4,256]{1,0:T(4,128)(2,1)S(1)} %get-tuple-element.11), channel_id=1, source_target_pairs={{0,11},{1,12},{2,13},{3,14},{4,15},{5,0},{6,1},{7,2},{8,3},{9,4},{... | collective-permute-start | bytes 6152 | tf_op jit(solution)/shard_map/ppermute | solution.py:209
  32.7 5.5 %collective-permute-start.11 = (bf16[4,256]{1,0:T(4,128)(2,1)S(1)}, bf16[4,256]{1,0:T(4,128)(2,1)S(1)}, u32[]{:S(2)}, u32[]{:S(2)}) collective-permute-start(bf16[4,256]{1,0:T(4,128)(2,1)S(1)} %get-tuple-element.11), channel_id=1, source_target_pairs={{0,12},{1,13},{2,14},{3,15},{4,0},{5,1},{6,2},{7,3},{8,4},{9,5},{1... | collective-permute-start | bytes 6152 | tf_op jit(solution)/shard_map/ppermute | solution.py:209
  33.2 6.5 %collective-permute-start.12 = (bf16[4,256]{1,0:T(4,128)(2,1)S(1)}, bf16[4,256]{1,0:T(4,128)(2,1)S(1)}, u32[]{:S(2)}, u32[]{:S(2)}) collective-permute-start(bf16[4,256]{1,0:T(4,128)(2,1)S(1)} %get-tuple-element.11), channel_id=1, source_target_pairs={{0,13},{1,14},{2,15},{3,0},{4,1},{5,2},{6,3},{7,4},{8,5},{9,6},{10... | collective-permute-start | bytes 6152 | tf_op jit(solution)/shard_map/ppermute | solution.py:209
  33.3 8.2 %collective-permute-start.13 = (bf16[4,256]{1,0:T(4,128)(2,1)S(1)}, bf16[4,256]{1,0:T(4,128)(2,1)S(1)}, u32[]{:S(2)}, u32[]{:S(2)}) collective-permute-start(bf16[4,256]{1,0:T(4,128)(2,1)S(1)} %get-tuple-element.11), channel_id=1, source_target_pairs={{0,14},{1,15},{2,0},{3,1},{4,2},{5,3},{6,4},{7,5},{8,6},{9,7},{10,... | collective-permute-start | bytes 6152 | tf_op jit(solution)/shard_map/ppermute | solution.py:209
  34.1 8.3 %collective-permute-start.14 = (bf16[4,256]{1,0:T(4,128)(2,1)S(1)}, bf16[4,256]{1,0:T(4,128)(2,1)S(1)}, u32[]{:S(2)}, u32[]{:S(2)}) collective-permute-start(bf16[4,256]{1,0:T(4,128)(2,1)S(1)} %get-tuple-element.11), channel_id=1, source_target_pairs={{0,15},{1,0},{2,1},{3,2},{4,3},{5,4},{6,5},{7,6},{8,7},{9,8},{10,9... | collective-permute-start | bytes 6152 | tf_op jit(solution)/shard_map/ppermute | solution.py:209
  37.5 5.8 %collective-permute-start.15 = (bf16[8,512]{1,0:T(8,128)(2,1)S(1)}, bf16[8,512]{1,0:T(8,128)(2,1)S(1)}, u32[]{:S(2)}, u32[]{:S(2)}) collective-permute-start(bf16[8,512]{1,0:T(8,128)(2,1)S(1)} %pad_maximum_fusion.2), channel_id=1, source_target_pairs={{0,1},{1,2},{2,3},{3,4},{4,5},{5,6},{6,7},{7,8},{8,9},{9,10},{10,1... | collective-permute-start | bytes 24584 | tf_op jit(solution)/shard_map/ppermute | solution.py:209
  38.1 6.2 %collective-permute-start.16 = (bf16[8,512]{1,0:T(8,128)(2,1)S(1)}, bf16[8,512]{1,0:T(8,128)(2,1)S(1)}, u32[]{:S(2)}, u32[]{:S(2)}) collective-permute-start(bf16[8,512]{1,0:T(8,128)(2,1)S(1)} %pad_maximum_fusion.2), channel_id=1, source_target_pairs={{0,2},{1,3},{2,4},{3,5},{4,6},{5,7},{6,8},{7,9},{8,10},{9,11},{10,... | collective-permute-start | bytes 24584 | tf_op jit(solution)/shard_map/ppermute | solution.py:209
  39.7 7.4 %collective-permute-start.17 = (bf16[8,512]{1,0:T(8,128)(2,1)S(1)}, bf16[8,512]{1,0:T(8,128)(2,1)S(1)}, u32[]{:S(2)}, u32[]{:S(2)}) collective-permute-start(bf16[8,512]{1,0:T(8,128)(2,1)S(1)} %pad_maximum_fusion.2), channel_id=1, source_target_pairs={{0,3},{1,4},{2,5},{3,6},{4,7},{5,8},{6,9},{7,10},{8,11},{9,12},{10... | collective-permute-start | bytes 24584 | tf_op jit(solution)/shard_map/ppermute | solution.py:209
  41.5 6.5 %collective-permute-start.18 = (bf16[8,512]{1,0:T(8,128)(2,1)S(1)}, bf16[8,512]{1,0:T(8,128)(2,1)S(1)}, u32[]{:S(2)}, u32[]{:S(2)}) collective-permute-start(bf16[8,512]{1,0:T(8,128)(2,1)S(1)} %pad_maximum_fusion.2), channel_id=1, source_target_pairs={{0,4},{1,5},{2,6},{3,7},{4,8},{5,9},{6,10},{7,11},{8,12},{9,13},{1... | collective-permute-start | bytes 24584 | tf_op jit(solution)/shard_map/ppermute | solution.py:209
  42.5 6.4 %collective-permute-start.19 = (bf16[8,512]{1,0:T(8,128)(2,1)S(1)}, bf16[8,512]{1,0:T(8,128)(2,1)S(1)}, u32[]{:S(2)}, u32[]{:S(2)}) collective-permute-start(bf16[8,512]{1,0:T(8,128)(2,1)S(1)} %pad_maximum_fusion.2), channel_id=1, source_target_pairs={{0,5},{1,6},{2,7},{3,8},{4,9},{5,10},{6,11},{7,12},{8,13},{9,14},{... | collective-permute-start | bytes 24584 | tf_op jit(solution)/shard_map/ppermute | solution.py:209
  43.3 7.8 %collective-permute-start.20 = (bf16[8,512]{1,0:T(8,128)(2,1)S(1)}, bf16[8,512]{1,0:T(8,128)(2,1)S(1)}, u32[]{:S(2)}, u32[]{:S(2)}) collective-permute-start(bf16[8,512]{1,0:T(8,128)(2,1)S(1)} %pad_maximum_fusion.2), channel_id=1, source_target_pairs={{0,6},{1,7},{2,8},{3,9},{4,10},{5,11},{6,12},{7,13},{8,14},{9,15},... | collective-permute-start | bytes 24584 | tf_op jit(solution)/shard_map/ppermute | solution.py:209
  44.4 10.1 %collective-permute-start.21 = (bf16[8,512]{1,0:T(8,128)(2,1)S(1)}, bf16[8,512]{1,0:T(8,128)(2,1)S(1)}, u32[]{:S(2)}, u32[]{:S(2)}) collective-permute-start(bf16[8,512]{1,0:T(8,128)(2,1)S(1)} %pad_maximum_fusion.2), channel_id=1, source_target_pairs={{0,7},{1,8},{2,9},{3,10},{4,11},{5,12},{6,13},{7,14},{8,15},{9,0},... | collective-permute-start | bytes 24584 | tf_op jit(solution)/shard_map/ppermute | solution.py:209
  47.0 7.5 %collective-permute-start.22 = (bf16[8,512]{1,0:T(8,128)(2,1)S(1)}, bf16[8,512]{1,0:T(8,128)(2,1)S(1)}, u32[]{:S(2)}, u32[]{:S(2)}) collective-permute-start(bf16[8,512]{1,0:T(8,128)(2,1)S(1)} %pad_maximum_fusion.2), channel_id=1, source_target_pairs={{0,8},{1,9},{2,10},{3,11},{4,12},{5,13},{6,14},{7,15},{8,0},{9,1},... | collective-permute-start | bytes 24584 | tf_op jit(solution)/shard_map/ppermute | solution.py:209
  48.0 6.6 %collective-permute-start.23 = (bf16[8,512]{1,0:T(8,128)(2,1)S(1)}, bf16[8,512]{1,0:T(8,128)(2,1)S(1)}, u32[]{:S(2)}, u32[]{:S(2)}) collective-permute-start(bf16[8,512]{1,0:T(8,128)(2,1)S(1)} %pad_maximum_fusion.2), channel_id=1, source_target_pairs={{0,9},{1,10},{2,11},{3,12},{4,13},{5,14},{6,15},{7,0},{8,1},{9,2},... | collective-permute-start | bytes 24584 | tf_op jit(solution)/shard_map/ppermute | solution.py:209
  48.9 6.9 %collective-permute-start.24 = (bf16[8,512]{1,0:T(8,128)(2,1)S(1)}, bf16[8,512]{1,0:T(8,128)(2,1)S(1)}, u32[]{:S(2)}, u32[]{:S(2)}) collective-permute-start(bf16[8,512]{1,0:T(8,128)(2,1)S(1)} %pad_maximum_fusion.2), channel_id=1, source_target_pairs={{0,10},{1,11},{2,12},{3,13},{4,14},{5,15},{6,0},{7,1},{8,2},{9,3},... | collective-permute-start | bytes 24584 | tf_op jit(solution)/shard_map/ppermute | solution.py:209
  51.1 7.8 %collective-permute-start.25 = (bf16[8,512]{1,0:T(8,128)(2,1)S(1)}, bf16[8,512]{1,0:T(8,128)(2,1)S(1)}, u32[]{:S(2)}, u32[]{:S(2)}) collective-permute-start(bf16[8,512]{1,0:T(8,128)(2,1)S(1)} %pad_maximum_fusion.2), channel_id=1, source_target_pairs={{0,11},{1,12},{2,13},{3,14},{4,15},{5,0},{6,1},{7,2},{8,3},{9,4},{... | collective-permute-start | bytes 24584 | tf_op jit(solution)/shard_map/ppermute | solution.py:209
  54.5 5.6 %collective-permute-start.27 = (bf16[8,512]{1,0:T(8,128)(2,1)S(1)}, bf16[8,512]{1,0:T(8,128)(2,1)S(1)}, u32[]{:S(2)}, u32[]{:S(2)}) collective-permute-start(bf16[8,512]{1,0:T(8,128)(2,1)S(1)} %pad_maximum_fusion.2), channel_id=1, source_target_pairs={{0,13},{1,14},{2,15},{3,0},{4,1},{5,2},{6,3},{7,4},{8,5},{9,6},{10... | collective-permute-start | bytes 24584 | tf_op jit(solution)/shard_map/ppermute | solution.py:209
  54.6 5.5 %collective-permute-start.28 = (bf16[8,512]{1,0:T(8,128)(2,1)S(1)}, bf16[8,512]{1,0:T(8,128)(2,1)S(1)}, u32[]{:S(2)}, u32[]{:S(2)}) collective-permute-start(bf16[8,512]{1,0:T(8,128)(2,1)S(1)} %pad_maximum_fusion.2), channel_id=1, source_target_pairs={{0,14},{1,15},{2,0},{3,1},{4,2},{5,3},{6,4},{7,5},{8,6},{9,7},{10,... | collective-permute-start | bytes 24584 | tf_op jit(solution)/shard_map/ppermute | solution.py:209
  55.8 4.6 %collective-permute-start.29 = (bf16[8,512]{1,0:T(8,128)(2,1)S(1)}, bf16[8,512]{1,0:T(8,128)(2,1)S(1)}, u32[]{:S(2)}, u32[]{:S(2)}) collective-permute-start(bf16[8,512]{1,0:T(8,128)(2,1)S(1)} %pad_maximum_fusion.2), channel_id=1, source_target_pairs={{0,15},{1,0},{2,1},{3,2},{4,3},{5,4},{6,5},{7,6},{8,7},{9,8},{10,9... | collective-permute-start | bytes 24584 | tf_op jit(solution)/shard_map/ppermute | solution.py:209
  71.0 18.0 %collective-permute-start.41 = (f32[4,2,64,256]{3,2,1,0:T(8,128)S(1)}, f32[4,2,64,256]{3,2,1,0:T(8,128)S(1)}, u32[]{:S(2)}, u32[]{:S(2)}) collective-permute-start(f32[4,2,64,256]{3,2,1,0:T(8,128)S(1)} %dynamic-slice_bitcast_fusion), channel_id=1, source_target_pairs={{0,4},{4,0},{8,12},{12,8},{1,5},{5,1},{9,13},{13,9},{2,6},{6,2},{1... | collective-permute-start | bytes 1572872 | tf_op jit(solution)/shard_map/ppermute | solution.py:222
  72.3 6.1 %collective-permute-start.31 = (f32[16,128]{1,0:T(8,128)S(1)}, f32[16,128]{1,0:T(8,128)S(1)}, u32[]{:S(2)}, u32[]{:S(2)}) collective-permute-start(f32[16,128]{1,0:T(8,128)S(1)} %get-tuple-element.26), channel_id=1, source_target_pairs={{0,1},{1,2},{2,3},{3,0},{4,5},{5,6},{6,7},{7,4},{8,9},{9,10},{10,1... | collective-permute-start | bytes 24584 | tf_op jit(solution)/shard_map/ppermute | solution.py:239
  74.3 6.1 %collective-permute-start.32 = (f32[16,128]{1,0:T(8,128)S(1)}, f32[16,128]{1,0:T(8,128)S(1)}, u32[]{:S(2)}, u32[]{:S(2)}) collective-permute-start(f32[16,128]{1,0:T(8,128)S(1)} %get-tuple-element.32), channel_id=1, source_target_pairs={{0,2},{1,3},{2,0},{3,1},{4,6},{5,7},{6,4},{7,5},{8,10},{9,11},{10,... | collective-permute-start | bytes 24584 | tf_op jit(solution)/shard_map/ppermute | solution.py:239
  76.9 5.0 %collective-permute-start.33 = (f32[16,128]{1,0:T(8,128)S(1)}, f32[16,128]{1,0:T(8,128)S(1)}, u32[]{:S(2)}, u32[]{:S(2)}) collective-permute-start(f32[16,128]{1,0:T(8,128)S(1)} %get-tuple-element.31), channel_id=1, source_target_pairs={{0,3},{1,0},{2,1},{3,2},{4,7},{5,4},{6,5},{7,6},{8,11},{9,8},{10,9... | collective-permute-start | bytes 24584 | tf_op jit(solution)/shard_map/ppermute | solution.py:239
  76.9 6.9 %collective-permute-start.34 = (f32[16,128]{1,0:T(8,128)S(1)}, f32[16,128]{1,0:T(8,128)S(1)}, u32[]{:S(2)}, u32[]{:S(2)}) collective-permute-start(f32[16,128]{1,0:T(8,128)S(1)} %get-tuple-element.30), channel_id=1, source_target_pairs={{0,8},{1,9},{2,10},{3,11},{4,12},{5,13},{6,14},{7,15},{8,0},{9,1},... | collective-permute-start | bytes 24584 | tf_op jit(solution)/shard_map/ppermute | solution.py:239
  78.3 6.3 %collective-permute-start.35 = (f32[16,128]{1,0:T(8,128)S(1)}, f32[16,128]{1,0:T(8,128)S(1)}, u32[]{:S(2)}, u32[]{:S(2)}) collective-permute-start(f32[16,128]{1,0:T(8,128)S(1)} %get-tuple-element.29), channel_id=1, source_target_pairs={{0,9},{1,10},{2,11},{3,8},{4,13},{5,14},{6,15},{7,12},{8,1},{9,2},... | collective-permute-start | bytes 24584 | tf_op jit(solution)/shard_map/ppermute | solution.py:239
  80.5 5.4 %collective-permute-start.36 = (f32[16,128]{1,0:T(8,128)S(1)}, f32[16,128]{1,0:T(8,128)S(1)}, u32[]{:S(2)}, u32[]{:S(2)}) collective-permute-start(f32[16,128]{1,0:T(8,128)S(1)} %get-tuple-element.28), channel_id=1, source_target_pairs={{0,10},{1,11},{2,8},{3,9},{4,14},{5,15},{6,12},{7,13},{8,2},{9,3},... | collective-permute-start | bytes 24584 | tf_op jit(solution)/shard_map/ppermute | solution.py:239
  81.9 4.6 %collective-permute-start.37 = (f32[16,128]{1,0:T(8,128)S(1)}, f32[16,128]{1,0:T(8,128)S(1)}, u32[]{:S(2)}, u32[]{:S(2)}) collective-permute-start(f32[16,128]{1,0:T(8,128)S(1)} %get-tuple-element.27), channel_id=1, source_target_pairs={{0,11},{1,8},{2,9},{3,10},{4,15},{5,12},{6,13},{7,14},{8,3},{9,0},... | collective-permute-start | bytes 24584 | tf_op jit(solution)/shard_map/ppermute | solution.py:239
  86.5 6.9 %collective-permute-start.38 = (f32[16,128]{1,0:T(8,128)S(1)}, f32[16,128]{1,0:T(8,128)S(1)}, u32[]{:S(2)}, u32[]{:S(2)}) collective-permute-start(f32[16,128]{1,0:T(8,128)S(1)} %fusion.11), channel_id=1, source_target_pairs={{0,4},{4,8},{8,12},{12,0},{1,5},{5,9},{9,13},{13,1},{2,6},{6,10},{... | collective-permute-start | bytes 24584 | tf_op jit(solution)/shard_map/ppermute | solution.py:242
  86.5 7.9 %collective-permute-start.39 = (f32[16,128]{1,0:T(8,128)S(1)}, f32[16,128]{1,0:T(8,128)S(1)}, u32[]{:S(2)}, u32[]{:S(2)}) collective-permute-start(f32[16,128]{1,0:T(8,128)S(1)} %fusion.11), channel_id=1, source_target_pairs={{0,8},{4,12},{8,0},{12,4},{1,9},{5,13},{9,1},{13,5},{2,10},{6,14},... | collective-permute-start | bytes 24584 | tf_op jit(solution)/shard_map/ppermute | solution.py:242
  87.6 7.8 %collective-permute-start.40 = (f32[16,128]{1,0:T(8,128)S(1)}, f32[16,128]{1,0:T(8,128)S(1)}, u32[]{:S(2)}, u32[]{:S(2)}) collective-permute-start(f32[16,128]{1,0:T(8,128)S(1)} %fusion.11), channel_id=1, source_target_pairs={{0,12},{4,0},{8,4},{12,8},{1,13},{5,1},{9,5},{13,9},{2,14},{6,2},{... | collective-permute-start | bytes 24584 | tf_op jit(solution)/shard_map/ppermute | solution.py:242
  89.1 7.7 %collective-permute-start.42 = (f32[64,256]{1,0:T(8,128)S(1)}, f32[64,256]{1,0:T(8,128)S(1)}, u32[]{:S(2)}, u32[]{:S(2)}) collective-permute-start(f32[64,256]{1,0:T(8,128)S(1)} %get-tuple-element.19), channel_id=1, source_target_pairs={{0,1},{1,2},{2,3},{3,0},{4,5},{5,6},{6,7},{7,4},{8,9},{9,10},{10,1... | collective-permute-start | bytes 196616 | tf_op jit(solution)/shard_map/ppermute | solution.py:239
  90.8 7.3 %collective-permute-start.43 = (f32[64,256]{1,0:T(8,128)S(1)}, f32[64,256]{1,0:T(8,128)S(1)}, u32[]{:S(2)}, u32[]{:S(2)}) collective-permute-start(f32[64,256]{1,0:T(8,128)S(1)} %get-tuple-element.25), channel_id=1, source_target_pairs={{0,2},{1,3},{2,0},{3,1},{4,6},{5,7},{6,4},{7,5},{8,10},{9,11},{10,... | collective-permute-start | bytes 196616 | tf_op jit(solution)/shard_map/ppermute | solution.py:239
  93.4 9.4 %collective-permute-start.44 = (f32[64,256]{1,0:T(8,128)S(1)}, f32[64,256]{1,0:T(8,128)S(1)}, u32[]{:S(2)}, u32[]{:S(2)}) collective-permute-start(f32[64,256]{1,0:T(8,128)S(1)} %get-tuple-element.24), channel_id=1, source_target_pairs={{0,3},{1,0},{2,1},{3,2},{4,7},{5,4},{6,5},{7,6},{8,11},{9,8},{10,9... | collective-permute-start | bytes 196616 | tf_op jit(solution)/shard_map/ppermute | solution.py:239
  94.4 8.4 %collective-permute-start.45 = (f32[64,256]{1,0:T(8,128)S(1)}, f32[64,256]{1,0:T(8,128)S(1)}, u32[]{:S(2)}, u32[]{:S(2)}) collective-permute-start(f32[64,256]{1,0:T(8,128)S(1)} %get-tuple-element.23), channel_id=1, source_target_pairs={{0,8},{1,9},{2,10},{3,11},{4,12},{5,13},{6,14},{7,15},{8,0},{9,1},... | collective-permute-start | bytes 196616 | tf_op jit(solution)/shard_map/ppermute | solution.py:239
  95.4 7.3 %collective-permute-start.46 = (f32[64,256]{1,0:T(8,128)S(1)}, f32[64,256]{1,0:T(8,128)S(1)}, u32[]{:S(2)}, u32[]{:S(2)}) collective-permute-start(f32[64,256]{1,0:T(8,128)S(1)} %get-tuple-element.22), channel_id=1, source_target_pairs={{0,9},{1,10},{2,11},{3,8},{4,13},{5,14},{6,15},{7,12},{8,1},{9,2},... | collective-permute-start | bytes 196616 | tf_op jit(solution)/shard_map/ppermute | solution.py:239
  96.9 7.3 %collective-permute-start.47 = (f32[64,256]{1,0:T(8,128)S(1)}, f32[64,256]{1,0:T(8,128)S(1)}, u32[]{:S(2)}, u32[]{:S(2)}) collective-permute-start(f32[64,256]{1,0:T(8,128)S(1)} %get-tuple-element.21), channel_id=1, source_target_pairs={{0,10},{1,11},{2,8},{3,9},{4,14},{5,15},{6,12},{7,13},{8,2},{9,3},... | collective-permute-start | bytes 196616 | tf_op jit(solution)/shard_map/ppermute | solution.py:239
  98.2 6.0 %collective-permute-start.48 = (f32[64,256]{1,0:T(8,128)S(1)}, f32[64,256]{1,0:T(8,128)S(1)}, u32[]{:S(2)}, u32[]{:S(2)}) collective-permute-start(f32[64,256]{1,0:T(8,128)S(1)} %get-tuple-element.20), channel_id=1, source_target_pairs={{0,11},{1,8},{2,9},{3,10},{4,15},{5,12},{6,13},{7,14},{8,3},{9,0},... | collective-permute-start | bytes 196616 | tf_op jit(solution)/shard_map/ppermute | solution.py:239
  104.3 4.8 %collective-permute-start.50 = (f32[64,256]{1,0:T(8,128)S(1)}, f32[64,256]{1,0:T(8,128)S(1)}, u32[]{:S(2)}, u32[]{:S(2)}) collective-permute-start(f32[64,256]{1,0:T(8,128)S(1)} %fusion.5), channel_id=1, source_target_pairs={{0,8},{4,12},{8,0},{12,4},{1,9},{5,13},{9,1},{13,5},{2,10},{6,14},... | collective-permute-start | bytes 196616 | tf_op jit(solution)/shard_map/ppermute | solution.py:242
  (13 other events, 26.9 us)

commit v2 on v1

v2 whole, which is shorter than its diff:
```python
import jax
import jax.numpy as jnp
from jax import lax
from jax.experimental import pallas as pl
from jax.experimental.pallas import tpu as pltpu
from jax.sharding import PartitionSpec as P

PATCH_X = 64
PATCH_Y = 64
PATCH_Z = 32
LEVELS = 4
GROUP = ("dp", "fsdp")
NT = (((1,), (1,)), ((), ()))
F32 = jnp.float32
BF16 = jnp.bfloat16


def iota(shape, dim):
    return lax.broadcasted_iota(jnp.int32, shape, dim)


def mm(left, right):
    return jnp.dot(left, right, preferred_element_type=F32)


def mm_nt(left, right):
    return lax.dot_general(left, right, NT, preferred_element_type=F32)


def spread_matrix():
    out_row = iota((512, 128), 0)
    lane = iota((512, 128), 1)
    pair, half = out_row // 128, out_row // 64 % 2
    row_dy, row_dz = out_row // 16 % 4, out_row // 4 % 4
    lane_dy, lane_c, lane_dz = lane // 32, lane // 4 % 8, lane % 4
    hit = (row_dy == lane_dy) & (row_dz == lane_dz) & (lane_c == 2 * pair + half)
    return jnp.where(hit, 1.0, 0.0).astype(BF16)


def pair_weights(w_embed):
    turned = jnp.transpose(w_embed.astype(F32)).astype(BF16)
    halves = []
    for half in range(2):
        row = iota((256, 512), 0)
        lane = iota((256, 512), 1)
        hit = (row // 64 == lane // 128) & (row % 64 == lane % 64) & (lane // 64 % 2 == half)
        halves.append(mm(turned, jnp.where(hit, 1.0, 0.0).astype(BF16)))
    return jnp.concatenate(halves, axis=0).astype(BF16)


def sigmoid(value):
    return 1.0 / (1.0 + jnp.exp(-value))


def forward_kernel(
    facies_hbm, prior_hbm, recon_hbm, w_embed_hbm, w_conv_hbm,
    block, one_hot_hbm, pre_embed_hbm, hidden_hbm, pre_conv_hbm,
    facies, prior, recon, w_embed, w_conv, one_hot, pre_embed, hidden, pre_conv, packed, sorted_rows, in_sem, out_sem
):
    parts = 4
    width = facies.shape[1] // parts
    loads = [
        pltpu.make_async_copy(
            facies_hbm.at[:, pl.ds(i * width, width)], facies.at[:, pl.ds(i * width, width)], in_sem.at[i]
        )
        for i in range(parts)
    ]
    for source, target in ((w_embed_hbm, w_embed), (w_conv_hbm, w_conv), (prior_hbm, prior), (recon_hbm, recon)):
        loads.append(pltpu.make_async_copy(source, target, in_sem.at[len(loads)]))
    for load in loads:
        load.start()
    row, lane = iota((256, 256), 0), iota((256, 256), 1)
    order = jnp.where((row // 32 == lane % 8) & (row % 32 == lane // 8), 1.0, 0.0).astype(BF16)
    spread = spread_matrix()
    level = (iota((512, 256), 0) % 4).astype(F32)
    for i in range(parts):
        loads[i].wait()
        part = facies[:, pl.ds(i * width, width)].astype(F32).astype(BF16)
        sorted_rows[:, pl.ds(i * width, width)] = mm(order, part).astype(BF16)
    for t in range(8):
        for dy2 in range(2):
            j, dx = 2 * (t // 4) + dy2, t % 4
            rows = [sorted_rows[pl.ds(t * 32, 32), pl.ds((2 * b2 + dy2) * 128, 128)] for b2 in range(8)]
            copied = mm_nt(spread, jnp.concatenate(rows, axis=0))
            hot = jnp.where(copied == level, 1.0, 0.0).astype(BF16)
            for cp in range(4):
                one_hot[cp, j, pl.ds(dx * 128, 128), :] = hot[cp * 128 : (cp + 1) * 128]
    stores = []

    def save(source, target):
        stores.append(pltpu.make_async_copy(source, target, out_sem.at[len(stores)]))
        stores[-1].start()

    for cp in range(4):
        save(one_hot.at[cp], one_hot_hbm.at[cp])
    loads[4].wait()
    packed[...] = pair_weights(w_embed[...])
    loads[5].wait()
    conv_turned = jnp.transpose(w_conv[...].astype(F32)).astype(BF16)
    sums = jnp.zeros((256, 128), F32)
    for cp in range(4):
        for j in range(4):
            pre = mm(packed[...], one_hot[cp, j])
            pre_embed[cp, j] = pre
            save(pre_embed.at[cp, j], pre_embed_hbm.at[cp, j])
            hidden[cp, j] = (pre * sigmoid(pre)).astype(BF16)
        save(hidden.at[cp], hidden_hbm.at[cp])
        pre = mm(conv_turned, hidden[cp].reshape(1024, 256))
        pre_conv[cp] = pre
        save(pre_conv.at[cp], pre_conv_hbm.at[cp])
        act = pre * sigmoid(pre)
        sums = sums + act[:, :128] + act[:, 128:]
    pick = jnp.where(iota((8, 128), 1) // 8 % 4 == iota((8, 128), 0), 1.0, 0.0)
    total = lax.dot_general(pick, sums, NT, precision=lax.Precision.HIGHEST, preferred_element_type=F32)
    loads[6].wait()
    loads[7].wait()
    block[:, pl.ds(0, 512)] = prior[...]
    block[:, pl.ds(512, 512)] = recon[...]
    block[:, pl.ds(1024, 256)] = (total[:4] / 256.0).astype(BF16)
    for store in stores:
        store.wait()


def pair_kernel(queries, query_square, keys):
    inner = mm_nt(queries, keys)
    key_float = keys.astype(F32)
    count = keys.shape[0]
    key_square = jnp.sum(key_float * key_float, axis=1, keepdims=True)
    key_row = jnp.transpose(jnp.broadcast_to(key_square, (count, 128)))[:1]
    kern = jnp.exp(-(query_square + key_row - 2.0 * inner) / keys.shape[1])
    return jnp.sum(kern, axis=1, keepdims=True), mm(kern.astype(BF16), keys)


def backward_kernel(
    sizes, gathered, w_head_hbm, w_conv_hbm, one_hot_hbm, pre_embed_hbm, hidden_hbm, pre_conv_hbm,
    keep, send, grad_head,
    w_head, w_conv, one_hot, pre_embed, hidden, pre_conv, ordered, head_full, sem
):
    dp, fsdp = sizes
    devices = dp * fsdp
    loads = []

    def load(source, target):
        loads.append(pltpu.make_async_copy(source, target, sem.at[len(loads)]))
        loads[-1].start()
        return loads[-1]

    head_load = load(w_head_hbm, w_head)
    pre_conv_load = load(pre_conv_hbm, pre_conv)
    hidden_loads = [load(hidden_hbm.at[cp], hidden.at[cp]) for cp in range(4)]
    conv_load = load(w_conv_hbm, w_conv)
    embed_loads = [
        (load(pre_embed_hbm.at[cp], pre_embed.at[cp]), load(one_hot_hbm.at[cp], one_hot.at[cp])) for cp in range(4)
    ]
    dp_here, fsdp_here = lax.axis_index("dp"), lax.axis_index("fsdp")
    here = dp_here * fsdp + fsdp_here
    for place in range(devices):
        if devices == 16:
            x = (dp_here // 2) ^ (place & 1)
            z = fsdp_here ^ (place >> 1 & 3)
            owner = (2 * x + (lax.rem(dp_here, 2) ^ (place >> 3))) * fsdp + z
        else:
            owner = place
        ordered[owner] = gathered[place].astype(F32)
    samples = ordered.shape[1]
    count = devices * samples
    full = ordered[...].reshape(count, ordered.shape[2])
    prior = full[:, :512].astype(BF16)
    recon = full[:, 512:1024]
    pooled = full[:, 1024:].astype(BF16)
    head_load.wait()
    latent = mm(pooled, w_head[...]).astype(BF16)
    latent_float = latent.astype(F32)
    square = jnp.sum(latent_float * latent_float, axis=1, keepdims=True)
    self_sum, self_mix = pair_kernel(latent, square, latent)
    cross_sum, cross_mix = pair_kernel(latent, square, prior)
    pull = -32.0 / count * ((self_sum - cross_sum) * latent_float - self_mix + cross_mix)
    cotangent = (recon + pull).astype(BF16)
    turned = jnp.transpose(full[:, 1024:]).astype(BF16)
    head_full[...] = mm(turned, cotangent)
    share = grad_head.shape[0]
    start = pl.multiple_of(fsdp_here * share, share)
    grad_head[...] = head_full[pl.ds(start, share), :]

    lane_sample = iota((128, count), 0) // 8 % 4 + samples * here
    pick = jnp.where(lane_sample == iota((128, count), 1), 1.0, 0.0).astype(BF16)
    lanes = mm(pick, cotangent).astype(BF16)
    back_pool = mm_nt(w_head[...], lanes) / 256.0
    back_pool = jnp.concatenate([back_pool, back_pool], axis=1)
    grads = []
    conv_total = None
    pre_conv_load.wait()
    for cp in range(4):
        pre = pre_conv[cp]
        gate = sigmoid(pre)
        grads.append((back_pool * (gate * (1.0 + pre * (1.0 - gate)))).astype(BF16))
        hidden_loads[cp].wait()
        term = mm_nt(hidden[cp].reshape(1024, 256), grads[cp])
        conv_total = term if cp == 0 else conv_total + term
    core_zero = lax.rem(dp_here, 2) == 0
    xs, conv_rows, embed_rows = dp // 2, 1024 // devices, 256 // devices
    for x in range(xs):
        for f in range(fsdp):
            at = (f * dp + 2 * x) * conv_rows
            first, second = conv_total[at : at + conv_rows], conv_total[at + conv_rows : at + 2 * conv_rows]
            keep[x, f, pl.ds(0, conv_rows), :] = jnp.where(core_zero, first, second)
            send[x, f, pl.ds(0, conv_rows), :] = jnp.where(core_zero, second, first)
    embed_total = None
    conv_load.wait()
    for cp in range(4):
        embed_loads[cp][0].wait()
        embed_loads[cp][1].wait()
        for j in range(4):
            rows = mm(w_conv[pl.ds(j * 256, 256), :], grads[cp])
            pre = pre_embed[cp, j]
            gate = sigmoid(pre)
            signal = (rows * (gate * (1.0 + pre * (1.0 - gate)))).astype(BF16)
            term = mm_nt(one_hot[cp, j], signal)
            embed_total = term if embed_total is None else embed_total + term
    embed = jnp.concatenate(
        [
            embed_total[dx * 128 : dx * 128 + 64, :128] + embed_total[dx * 128 + 64 : dx * 128 + 128, 128:]
            for dx in range(4)
        ],
        axis=0,
    )
    half = embed_rows // 2
    for x in range(xs):
        for f in range(fsdp):
            for side in range(2):
                at = (f * dp + 2 * x) * embed_rows + side * half
                first, second = embed[at : at + half], embed[at + embed_rows : at + embed_rows + half]
                place = (x, f, pl.ds(conv_rows, half), pl.ds(side * 128, 128))
                keep[place] = jnp.where(core_zero, first, second)
                send[place] = jnp.where(core_zero, second, first)


VMEM = pl.BlockSpec(memory_space=pltpu.VMEM)
HBM = pl.BlockSpec(memory_space=pltpu.HBM)
SAVED = (
    ((4, 4, 512, 256), BF16),
    ((4, 4, 256, 256), F32),
    ((4, 4, 256, 256), BF16),
    ((4, 256, 256), F32),
)


def forward(facies, prior_draws, recon_grad, w_embed, w_conv):
    samples = facies.shape[0]
    latent_width = prior_draws.shape[1]
    rows, lanes = samples * PATCH_X, PATCH_Y * PATCH_Z
    return pl.pallas_call(
        forward_kernel,
        out_shape=(jax.ShapeDtypeStruct((samples, 2 * latent_width + 256), BF16),)
        + tuple(jax.ShapeDtypeStruct(shape, kind) for shape, kind in SAVED),
        in_specs=[HBM] * 5,
        out_specs=(VMEM,) + (HBM,) * 4,
        scratch_shapes=[
            pltpu.VMEM((rows, lanes), jnp.int32),
            pltpu.VMEM(prior_draws.shape, BF16),
            pltpu.VMEM(recon_grad.shape, BF16),
            pltpu.VMEM(w_embed.shape, BF16),
            pltpu.VMEM(w_conv.shape, BF16),
            *[pltpu.VMEM(shape, kind) for shape, kind in SAVED],
            pltpu.VMEM((256, 512), BF16),
            pltpu.VMEM((rows, lanes), BF16),
            pltpu.SemaphoreType.DMA((8,)),
            pltpu.SemaphoreType.DMA((28,)),
        ],
        compiler_params=pltpu.CompilerParams(vmem_limit_bytes=30 * 2**20),
        name="forward",
    )(facies.reshape(rows, lanes), prior_draws, recon_grad, w_embed, w_conv)


def backward(sizes, gathered, w_head, w_conv, saved):
    dp, fsdp = sizes
    devices, samples, width = gathered.shape
    payload = jax.ShapeDtypeStruct((dp // 2, fsdp, (1024 + 128) // devices, 256), F32)
    return pl.pallas_call(
        lambda *refs: backward_kernel(sizes, *refs),
        out_shape=(payload, payload, jax.ShapeDtypeStruct((256 // fsdp, 512), F32)),
        in_specs=[VMEM] + [HBM] * 6,
        out_specs=(VMEM,) * 3,
        scratch_shapes=[
            pltpu.VMEM(w_head.shape, BF16),
            pltpu.VMEM(w_conv.shape, BF16),
            *[pltpu.VMEM(shape, kind) for shape, kind in SAVED],
            pltpu.VMEM((devices, samples, width), F32),
            pltpu.VMEM((256, 512), F32),
            pltpu.SemaphoreType.DMA((15,)),
        ],
        compiler_params=pltpu.CompilerParams(vmem_limit_bytes=32 * 2**20),
        name="backward",
    )(gathered, w_head, w_conv, *saved)


def place_of(x, core, z, fsdp):
    return (2 * x + core) * fsdp + z


def exchange(block, dp, fsdp, flip_x, flip_core, flip_z):
    pairs = []
    for x in range(dp // 2):
        for core in range(2):
            for z in range(fsdp):
                pairs.append((place_of(x, core, z, fsdp), place_of(x ^ flip_x, core ^ flip_core, z ^ flip_z, fsdp)))
    return lax.ppermute(block, GROUP, pairs)


def gather_blocks(block, dp, fsdp):
    if (dp, fsdp) != (4, 4):
        return lax.all_gather(block, GROUP, axis=0)
    stacked = block[None]
    for flips in ((1, 0, 0), (0, 0, 1), (0, 0, 2), (0, 1, 0)):
        stacked = jnp.concatenate([stacked, exchange(stacked, dp, fsdp, *flips)], axis=0)
    return stacked


def exponent_of(part):
    top = jnp.max(jnp.abs(part))
    return jnp.clip(jnp.floor(jnp.log2(jnp.maximum(top, 1e-37))) - 14.0, -124.0, 114.0)


def reduce_to_owner(keep, send, dp, fsdp):
    xs, _, rows, width = keep.shape
    conv_rows = rows * 8 // 9
    held = keep + exchange(send, dp, fsdp, 0, 1, 0)
    conv, embed = held[:, :, :conv_rows], held[:, :, conv_rows:]
    conv_step, embed_step = exponent_of(conv), exponent_of(embed)
    spare = 16 * (rows // 16 + 1) - rows
    tail = jnp.where(jnp.arange(spare)[:, None] == 0, conv_step, embed_step)
    tail = jnp.broadcast_to(tail, (xs, fsdp, spare, width))
    coded = jnp.concatenate([conv * jnp.exp2(-conv_step), embed * jnp.exp2(-embed_step), tail], axis=2)
    coded = coded.astype(jnp.float16).reshape(xs * fsdp, rows + spare, width)
    groups = [[place_of(x, core, z, fsdp) for x in range(xs) for z in range(fsdp)] for core in range(2)]
    got = lax.all_to_all(coded, GROUP, 0, 0, axis_index_groups=groups, tiled=True).astype(F32)
    conv_scale = jnp.exp2(got[:, rows : rows + 1, :1])
    embed_scale = jnp.exp2(got[:, rows + 1 : rows + 2, :1])
    is_conv = jnp.arange(rows)[None, :, None] < conv_rows
    total = jnp.sum(got[:, :rows] * jnp.where(is_conv, conv_scale, embed_scale), axis=0)
    if dp != 4:
        return lax.all_gather(total, "dp", axis=0).reshape(xs, 2, rows, width)
    x, core = lax.axis_index("dp") // 2, lax.axis_index("dp") % 2
    other = exchange(total, dp, fsdp, 1, 0, 0)
    column = jnp.stack([jnp.where(x == 0, total, other), jnp.where(x == 0, other, total)])
    sibling = exchange(column, dp, fsdp, 0, 1, 0)
    return jnp.stack([jnp.where(core == 0, column, sibling), jnp.where(core == 0, sibling, column)], axis=1)


def shards(facies, prior_draws, recon_grad, w_embed, w_conv, w_head):
    dp, fsdp = lax.axis_size("dp"), lax.axis_size("fsdp")
    block, *saved = forward(facies, prior_draws, recon_grad, w_embed, w_conv)
    gathered = gather_blocks(block, dp, fsdp)
    keep, send, grad_head = backward((dp, fsdp), gathered, w_head, w_conv, saved)
    summed = reduce_to_owner(keep, send, dp, fsdp)
    conv_rows = summed.shape[2] * 8 // 9
    embed = summed[:, :, conv_rows:].reshape(dp, -1, 2, 128).transpose(0, 2, 1, 3)
    return (
        embed.reshape(256 // fsdp, 128),
        summed[:, :, :conv_rows].reshape(1024 // fsdp, 256),
        grad_head,
    )


def solution(mesh):
    return jax.shard_map(
        shards,
        mesh=mesh,
        in_specs=(
            P(("groups", "dp", "fsdp"), None, None),
            P(("groups", "dp", "fsdp"), None),
            P(("groups", "dp", "fsdp"), None),
            P(),
            P(),
            P(),
        ),
        out_specs=(
            P(("groups", "fsdp"), None),
            P(("groups", "fsdp"), None),
            P(("groups", "fsdp"), None),
        ),
        check_vma=False,
    )
```

time: 111 us -> 71.9 us (0.65)
  starting transfers between devices: 74.4 us -> 15.7 us
  waiting for transfers between devices: 8.2 us -> 25.1 us
  Pallas kernels: 8.24 us -> 18.2 us
  local copies, waits for them, and re-layouts: 15.6 us -> 5.96 us
  between operations: 0.9 us -> 2.25 us
    ppermute x52 -> x7, starting transfers between devices: 74.4 us -> 9.27 us  [exchange(): return lax.ppermute(block, GROUP, pairs)]
    all_to_all x0 -> x1, waiting for transfers between devices: none -> 11.5 us  [reduce_to_owner(): lax.all_to_all(coded, GROUP, 0, 0, axis_index_groups=groups, tiled=True)]
    unnamed x47 -> x16, local copies, waits for them, and re-layouts: 14 us -> 5.84 us
    pallas_call x1, Pallas kernels: 4.08 us -> 11.1 us  [forward(): pl.pallas_call(forward_kernel, out_shape=(jax.ShapeDtypeStruct((samples,...]
    all_to_all x0 -> x1, starting transfers between devices: none -> 6.46 us  [reduce_to_owner(): lax.all_to_all(coded, GROUP, 0, 0, axis_index_groups=groups, tiled=True)]
    ppermute x52 -> x7, waiting for transfers between devices: 8.2 us -> 13.6 us  [exchange(): return lax.ppermute(block, GROUP, pairs)]
    pallas_call x1, Pallas kernels: 4.16 us -> 7.07 us  [backward(): pl.pallas_call(lambda *refs: backward_kernel(sizes, *refs), out_shape=(pa...]
    select_n x3 -> x1, other arithmetic: 1.51 us -> 0.07 us  [reduce_to_owner(): jnp.where(is_conv, conv_scale, embed_scale)]
  transfers between devices with their start and end apart: 52 -> 8, of which waited for: 11 -> 8; matrix products, arithmetic and copies ran while one was open for 3% -> 0% of each run, Pallas kernels for 0% -> 0%
where the time goes in v2:
time: 71.9 us; the launch traced here: 71.4 us
  waiting for transfers between devices  25.1 us (35%)
  Pallas kernels  18.2 us (25%)
  starting transfers between devices  15.7 us (22%)
  local copies, waits for them, and re-layouts  5.96 us (8%)
  other arithmetic  4.17 us (6%)
  between operations  2.25 us (3%)
    ppermute x7, waiting for transfers between devices, exchange(): return lax.ppermute(block, GROUP, pairs)  13.6 us
    all_to_all x1, waiting for transfers between devices, reduce_to_owner(): lax.all_to_all(coded, GROUP, 0, 0, axis_index_groups=groups, tiled=True)  11.5 us
    pallas_call x1, Pallas kernels, forward(): pl.pallas_call(forward_kernel, out_shape=(jax.ShapeDtypeStruct((samples,...  11.1 us
    ppermute x7, starting transfers between devices, exchange(): return lax.ppermute(block, GROUP, pairs)  9.27 us
    pallas_call x1, Pallas kernels, backward(): pl.pallas_call(lambda *refs: backward_kernel(sizes, *refs), out_shape=(pa...  7.07 us
    all_to_all x1, starting transfers between devices, reduce_to_owner(): lax.all_to_all(coded, GROUP, 0, 0, axis_index_groups=groups, tiled=True)  6.46 us
    unnamed x16, local copies, waits for them, and re-layouts  5.84 us
  transfers between devices with their start and end apart: 8, of which 8 were waited for; matrix products, arithmetic and copies ran while one was open for 0% of the time, Pallas kernels for 0%

profile of v2, /device:TPU:0, one launch (start us, length us, event | category | flops | bytes accessed | tf_op | source)
XLA Modules:
  0.0 71.4 jit_solution(13278661329573134006)
XLA Ops:
  0.6 0.0 copy-start
  0.6 1.6 %copy-done = s32[4,64,2048]{2,1,0:T(8,128)S(1)} copy-done((s32[4,64,2048]{2,1,0:T(8,128)S(1)}, s32[4,64,2048]{2,1,0:T(8,128)}, u32[]{:S(2)}) %copy-start) | copy-done | bytes 2097176
  2.2 0.0 copy-start.1
  2.2 1.0 %copy-done.1 = bf16[1024,256]{1,0:T(8,128)(2,1)S(1)} copy-done((bf16[1024,256]{1,0:T(8,128)(2,1)S(1)}, bf16[1024,256]{1,0:T(8,128)(2,1)}, u32[]{:S(2)}) %copy-start.1) | copy-done | bytes 524312
  3.3 0.0 copy-start.3
  3.3 0.8 %copy-done.3 = bf16[256,128]{1,0:T(8,128)(2,1)S(1)} copy-done((bf16[256,128]{1,0:T(8,128)(2,1)S(1)}, bf16[256,128]{1,0:T(8,128)(2,1)}, u32[]{:S(2)}) %copy-start.3) | copy-done | bytes 65560
  4.1 0.0 copy-start.4
  4.1 0.7 copy-done.4
  4.8 0.0 copy-start.5
  4.8 0.7 copy-done.5
  5.5 11.1 %forward.1 = (bf16[4,1280]{1,0:T(4,128)(2,1)S(1)}, bf16[4,4,512,256]{3,2,1,0:T(8,128)(2,1)S(1)}, f32[4,4,256,256]{3,2,1,0:T(8,128)S(1)}, bf16[4,4,256,256]{3,2,1,0:T(8,128)(2,1)S(1)}, f32[4,256,256]{2,1,0:T(8,128)S(1)}) custom-call(s32[256,2048]{1,0:T(8,128)S(1)} %bitcast.21, bf16[4,512]{1,0:T(4,128)(2,1)S(1)} %copy-done.4, bf16[4,512]{1,0:T(4,128)(2,1)S(1)} %copy-done.5, ...), custom_call_target="tpu_custom_call" | custom-call | tf_op jit(solution)/shard_map/forward/pallas_call | solution.py:252
  16.6 3.0 %collective-permute-start = (bf16[1,4,1280]{2,1,0:T(4,128)(2,1)S(1)}, bf16[1,4,1280]{2,1,0:T(4,128)(2,1)S(1)}, u32[]{:S(2)}, u32[]{:S(2)}) collective-permute-start(bf16[1,4,1280]{2,1,0:T(4,128)(2,1)S(1)} %bitcast.22), channel_id=1, source_target_pairs={{0,8},{1,9},{2,10},{3,11},{4,12},{5,13},{6,14},{7,15},{8,0},{9,1},... | collective-permute-start | bytes 30728 | tf_op jit(solution)/shard_map/ppermute | solution.py:307
  19.6 1.6 %collective-permute-done = bf16[1,4,1280]{2,1,0:T(4,128)(2,1)S(1)} collective-permute-done((bf16[1,4,1280]{2,1,0:T(4,128)(2,1)S(1)}, bf16[1,4,1280]{2,1,0:T(4,128)(2,1)S(1)}, u32[]{:S(2)}, u32[]{:S(2)}) %collective-permute-start) | collective-permute-done | bytes 10272 | tf_op jit(solution)/shard_map/ppermute | solution.py:307
  21.3 2.2 %collective-permute-start.1 = (bf16[2,4,1280]{2,1,0:T(4,128)(2,1)S(1)}, bf16[2,4,1280]{2,1,0:T(4,128)(2,1)S(1)}, u32[]{:S(2)}, u32[]{:S(2)}) collective-permute-start(bf16[2,4,1280]{2,1,0:T(4,128)(2,1)S(1)} %pad_maximum_fusion.5), channel_id=1, source_target_pairs={{0,1},{1,0},{2,3},{3,2},{4,5},{5,4},{6,7},{7,6},{8,9},{9,8},{10,11... | collective-permute-start | bytes 61448 | tf_op jit(solution)/shard_map/ppermute | solution.py:307
  23.5 1.7 %collective-permute-done.1 = bf16[2,4,1280]{2,1,0:T(4,128)(2,1)S(1)} collective-permute-done((bf16[2,4,1280]{2,1,0:T(4,128)(2,1)S(1)}, bf16[2,4,1280]{2,1,0:T(4,128)(2,1)S(1)}, u32[]{:S(2)}, u32[]{:S(2)}) %collective-permute-start.1) | collective-permute-done | bytes 20512 | tf_op jit(solution)/shard_map/ppermute | solution.py:307
  25.3 3.1 %collective-permute-start.2 = (bf16[4,4,1280]{2,1,0:T(4,128)(2,1)S(1)}, bf16[4,4,1280]{2,1,0:T(4,128)(2,1)S(1)}, u32[]{:S(2)}, u32[]{:S(2)}) collective-permute-start(bf16[4,4,1280]{2,1,0:T(4,128)(2,1)S(1)} %pad_maximum_fusion.3), channel_id=1, source_target_pairs={{0,2},{1,3},{2,0},{3,1},{4,6},{5,7},{6,4},{7,5},{8,10},{9,11},{10,... | collective-permute-start | bytes 122888 | tf_op jit(solution)/shard_map/ppermute | solution.py:307
  28.4 2.0 %collective-permute-done.2 = bf16[4,4,1280]{2,1,0:T(4,128)(2,1)S(1)} collective-permute-done((bf16[4,4,1280]{2,1,0:T(4,128)(2,1)S(1)}, bf16[4,4,1280]{2,1,0:T(4,128)(2,1)S(1)}, u32[]{:S(2)}, u32[]{:S(2)}) %collective-permute-start.2) | collective-permute-done | bytes 40992 | tf_op jit(solution)/shard_map/ppermute | solution.py:307
  30.4 0.1 pad_maximum_fusion.2
  30.4 0.1 collective-permute-start.3
  30.5 1.2 %collective-permute-done.3 = bf16[8,4,1280]{2,1,0:T(4,128)(2,1)S(1)} collective-permute-done((bf16[8,4,1280]{2,1,0:T(4,128)(2,1)S(1)}, bf16[8,4,1280]{2,1,0:T(4,128)(2,1)S(1)}, u32[]{:S(2)}, u32[]{:S(2)}) %collective-permute-start.3) | collective-permute-done | bytes 81952 | tf_op jit(solution)/shard_map/ppermute | solution.py:307
  31.8 0.0 copy-start.2
  31.8 0.9 %copy-done.2 = bf16[256,512]{1,0:T(8,128)(2,1)S(1)} copy-done((bf16[256,512]{1,0:T(8,128)(2,1)S(1)}, bf16[256,512]{1,0:T(8,128)(2,1)}, u32[]{:S(2)}) %copy-start.2) | copy-done | bytes 262168
  32.8 7.1 %backward.1 = (f32[2,4,72,256]{3,2,1,0:T(8,128)S(1)}, f32[2,4,72,256]{3,2,1,0:T(8,128)S(1)}, f32[64,512]{1,0:T(8,128)}) custom-call(bf16[16,4,1280]{2,1,0:T(4,128)(2,1)S(1)} %constant_dynamic-update-slice_fusion.refs_0_, bf16[256,512]{1,0:T(8,128)(2,1)S(1)} %copy-done.2, bf16[1024,256]{1,0:T(8,128)(2,1)S(1)} %copy-done.1, ...), custom_call_target="tpu_custom_call" | custom-call | tf_op jit(solution)/shard_map/backward/pallas_call | solution.py:279
  39.9 0.2 collective-permute-start.4
  40.1 1.8 %collective-permute-done.4 = f32[2,4,72,256]{3,2,1,0:T(8,128)S(1)} collective-permute-done((f32[2,4,72,256]{3,2,1,0:T(8,128)S(1)}, f32[2,4,72,256]{3,2,1,0:T(8,128)S(1)}, u32[]{:S(2)}, u32[]{:S(2)}) %collective-permute-start.4) | collective-permute-done | bytes 589856 | tf_op jit(solution)/shard_map/ppermute | solution.py:307
  41.9 0.1 add.11
  42.0 0.6 abs_reduce_fusion
  42.6 0.6 abs_reduce_fusion.1
  44.8 0.1 pad.6.clone
  44.9 0.8 %maximum_maximum_fusion = f16[8,80,256]{2,1,0:T(8,128)(2,1)} fusion(f16[8,8,256]{2,1,0:T(8,128)(2,1)S(1)} %bitcast.28, f16[8,64,256]{2,1,0:T(8,128)(2,1)S(1)} %bitcast.26, f16[80]{0:T(256)(128)(2,1)S(1)} %pad.6.clone), kind=kLoop, calls=%fused_computation.4 | loop fusion | flops 327680 | bytes 622752 | tf_op jit(solution)/shard_map/concatenate | solution.py:333
  45.7 6.5 %all-to-all-start = ((f16[8,80,256]{2,1,0:T(8,128)(2,1)}), f16[8,80,256]{2,1,0:T(8,128)(2,1)S(1)}, u32[]{:S(2)}, u32[]{:S(2)}) async-start(f16[8,80,256]{2,1,0:T(8,128)(2,1)} %maximum_maximum_fusion), calls=%async_computation | async-start | bytes 655360 | tf_op jit(solution)/shard_map/all_to_all | solution.py:336
  52.2 11.5 %all-to-all-done = f16[8,80,256]{2,1,0:T(8,128)(2,1)S(1)} async-done(((f16[8,80,256]{2,1,0:T(8,128)(2,1)}), f16[8,80,256]{2,1,0:T(8,128)(2,1)S(1)}, u32[]{:S(2)}, u32[]{:S(2)}) %all-to-all-start) | async-done | bytes 327712 | tf_op jit(solution)/shard_map/all_to_all | solution.py:336
  63.7 0.1 convert_element_type.5
  63.8 0.2 fusion.3
  63.9 0.1 broadcast_select_fusion
  64.0 0.1 fusion
  64.1 0.6 collective-permute-start.5
  64.8 3.8 %collective-permute-done.5 = f32[72,256]{1,0:T(8,128)S(1)} collective-permute-done((f32[72,256]{1,0:T(8,128)S(1)}, f32[72,256]{1,0:T(8,128)S(1)}, u32[]{:S(2)}, u32[]{:S(2)}) %collective-permute-start.5) | collective-permute-done | bytes 73760 | tf_op jit(solution)/shard_map/ppermute | solution.py:307
  68.6 0.1 collective-permute-start.6
  68.7 1.3 %collective-permute-done.6 = f32[2,72,256]{2,1,0:T(8,128)S(1)} collective-permute-done((f32[2,72,256]{2,1,0:T(8,128)S(1)}, f32[2,72,256]{2,1,0:T(8,128)S(1)}, u32[]{:S(2)}, u32[]{:S(2)}) %collective-permute-start.6) | collective-permute-done | bytes 147488 | tf_op jit(solution)/shard_map/ppermute | solution.py:307
  70.1 0.7 %pad_maximum_fusion = f32[2,2,64,256]{3,2,1,0:T(8,128)} fusion(f32[2,1,72,256]{3,2,1,0:T(8,128)S(1)} %get-tuple-element.22, f32[2,1,72,256]{3,2,1,0:T(8,128)S(1)} %get-tuple-element.21), kind=kLoop, calls=%fused_computation.5 | loop fusion | flops 65536 | bytes 557056 | tf_op jit(solution)/shard_map/stack | solution.py:347
  70.8 0.6 pad_maximum_fusion.4
  (14 shorter events, 0.3 us)
Async XLA Ops:
  0.6 1.6 %copy-start = (s32[4,64,2048]{2,1,0:T(8,128)S(1)}, s32[4,64,2048]{2,1,0:T(8,128)}, u32[]{:S(2)}) copy-start(s32[4,64,2048]{2,1,0:T(8,128)} %param.6) | copy-start | bytes 6291460
  2.2 1.0 %copy-start.1 = (bf16[1024,256]{1,0:T(8,128)(2,1)S(1)}, bf16[1024,256]{1,0:T(8,128)(2,1)}, u32[]{:S(2)}) copy-start(bf16[1024,256]{1,0:T(8,128)(2,1)} %refs_2_.1) | copy-start | bytes 1572868
  3.3 0.8 %copy-start.3 = (bf16[256,128]{1,0:T(8,128)(2,1)S(1)}, bf16[256,128]{1,0:T(8,128)(2,1)}, u32[]{:S(2)}) copy-start(bf16[256,128]{1,0:T(8,128)(2,1)} %w_embed_hbm.1) | copy-start | bytes 196612
  4.1 0.7 copy-start.4
  4.8 0.7 copy-start.5
  16.6 4.7 %collective-permute-start = (bf16[1,4,1280]{2,1,0:T(4,128)(2,1)S(1)}, bf16[1,4,1280]{2,1,0:T(4,128)(2,1)S(1)}, u32[]{:S(2)}, u32[]{:S(2)}) collective-permute-start(bf16[1,4,1280]{2,1,0:T(4,128)(2,1)S(1)} %bitcast.22), channel_id=1, source_target_pairs={{0,8},{1,9},{2,10},{3,11},{4,12},{5,13},{6,14},{7,15},{8,0},{9,1},... | collective-permute-start | bytes 30728 | tf_op jit(solution)/shard_map/ppermute | solution.py:307
  21.3 3.9 %collective-permute-start.1 = (bf16[2,4,1280]{2,1,0:T(4,128)(2,1)S(1)}, bf16[2,4,1280]{2,1,0:T(4,128)(2,1)S(1)}, u32[]{:S(2)}, u32[]{:S(2)}) collective-permute-start(bf16[2,4,1280]{2,1,0:T(4,128)(2,1)S(1)} %pad_maximum_fusion.5), channel_id=1, source_target_pairs={{0,1},{1,0},{2,3},{3,2},{4,5},{5,4},{6,7},{7,6},{8,9},{9,8},{10,11... | collective-permute-start | bytes 61448 | tf_op jit(solution)/shard_map/ppermute | solution.py:307
  25.3 5.1 %collective-permute-start.2 = (bf16[4,4,1280]{2,1,0:T(4,128)(2,1)S(1)}, bf16[4,4,1280]{2,1,0:T(4,128)(2,1)S(1)}, u32[]{:S(2)}, u32[]{:S(2)}) collective-permute-start(bf16[4,4,1280]{2,1,0:T(4,128)(2,1)S(1)} %pad_maximum_fusion.3), channel_id=1, source_target_pairs={{0,2},{1,3},{2,0},{3,1},{4,6},{5,7},{6,4},{7,5},{8,10},{9,11},{10,... | collective-permute-start | bytes 122888 | tf_op jit(solution)/shard_map/ppermute | solution.py:307
  30.4 1.3 %collective-permute-start.3 = (bf16[8,4,1280]{2,1,0:T(4,128)(2,1)S(1)}, bf16[8,4,1280]{2,1,0:T(4,128)(2,1)S(1)}, u32[]{:S(2)}, u32[]{:S(2)}) collective-permute-start(bf16[8,4,1280]{2,1,0:T(4,128)(2,1)S(1)} %pad_maximum_fusion.2), channel_id=1, source_target_pairs={{0,4},{1,5},{2,6},{3,7},{4,0},{5,1},{6,2},{7,3},{8,12},{9,13},{10,... | collective-permute-start | bytes 245768 | tf_op jit(solution)/shard_map/ppermute | solution.py:307
  31.8 1.0 %copy-start.2 = (bf16[256,512]{1,0:T(8,128)(2,1)S(1)}, bf16[256,512]{1,0:T(8,128)(2,1)}, u32[]{:S(2)}) copy-start(bf16[256,512]{1,0:T(8,128)(2,1)} %refs_1_.1) | copy-start | bytes 786436
  39.9 2.1 %collective-permute-start.4 = (f32[2,4,72,256]{3,2,1,0:T(8,128)S(1)}, f32[2,4,72,256]{3,2,1,0:T(8,128)S(1)}, u32[]{:S(2)}, u32[]{:S(2)}) collective-permute-start(f32[2,4,72,256]{3,2,1,0:T(8,128)S(1)} %get-tuple-element.17), channel_id=1, source_target_pairs={{0,4},{1,5},{2,6},{3,7},{4,0},{5,1},{6,2},{7,3},{8,12},{9,13},{10,... | collective-permute-start | bytes 1769480 | tf_op jit(solution)/shard_map/ppermute | solution.py:307
  45.7 18.0 %all-to-all-start = ((f16[8,80,256]{2,1,0:T(8,128)(2,1)}), f16[8,80,256]{2,1,0:T(8,128)(2,1)S(1)}, u32[]{:S(2)}, u32[]{:S(2)}) async-start(f16[8,80,256]{2,1,0:T(8,128)(2,1)} %maximum_maximum_fusion), calls=%async_computation | async-start | bytes 655360 | tf_op jit(solution)/shard_map/all_to_all | solution.py:336
  64.1 4.4 %collective-permute-start.5 = (f32[72,256]{1,0:T(8,128)S(1)}, f32[72,256]{1,0:T(8,128)S(1)}, u32[]{:S(2)}, u32[]{:S(2)}) collective-permute-start(f32[72,256]{1,0:T(8,128)S(1)} %fusion), channel_id=1, source_target_pairs={{0,8},{1,9},{2,10},{3,11},{4,12},{5,13},{6,14},{7,15},{8,0},{9,1},... | collective-permute-start | bytes 221192 | tf_op jit(solution)/shard_map/ppermute | solution.py:307
  68.6 1.4 %collective-permute-start.6 = (f32[2,72,256]{2,1,0:T(8,128)S(1)}, f32[2,72,256]{2,1,0:T(8,128)S(1)}, u32[]{:S(2)}, u32[]{:S(2)}) collective-permute-start(f32[2,72,256]{2,1,0:T(8,128)S(1)} %pad_maximum_fusion.1), channel_id=1, source_target_pairs={{0,4},{1,5},{2,6},{3,7},{4,0},{5,1},{6,2},{7,3},{8,12},{9,13},{10,... | collective-permute-start | bytes 442376 | tf_op jit(solution)/shard_map/ppermute | solution.py:307

commit v3 on v2

v3 whole, which is shorter than its diff:
```python
import jax
import jax.numpy as jnp
from jax import lax
from jax.experimental import pallas as pl
from jax.experimental.pallas import tpu as pltpu
from jax.sharding import PartitionSpec as P

PATCH_X = 64
PATCH_Y = 64
PATCH_Z = 32
LEVELS = 4
GROUP = ("dp", "fsdp")
NT = (((1,), (1,)), ((), ()))
F32 = jnp.float32
BF16 = jnp.bfloat16


def iota(shape, dim):
    return lax.broadcasted_iota(jnp.int32, shape, dim)


def mm(left, right):
    return jnp.dot(left, right, preferred_element_type=F32)


def mm_nt(left, right):
    return lax.dot_general(left, right, NT, preferred_element_type=F32)


def spread_matrix():
    out_row = iota((512, 128), 0)
    lane = iota((512, 128), 1)
    pair, half = out_row // 128, out_row // 64 % 2
    row_dy, row_dz = out_row // 16 % 4, out_row // 4 % 4
    lane_dy, lane_c, lane_dz = lane // 32, lane // 4 % 8, lane % 4
    hit = (row_dy == lane_dy) & (row_dz == lane_dz) & (lane_c == 2 * pair + half)
    return jnp.where(hit, 1.0, 0.0).astype(BF16)


def pair_weights(w_embed):
    turned = jnp.transpose(w_embed.astype(F32)).astype(BF16)
    halves = []
    for half in range(2):
        row = iota((256, 512), 0)
        lane = iota((256, 512), 1)
        hit = (row // 64 == lane // 128) & (row % 64 == lane % 64) & (lane // 64 % 2 == half)
        halves.append(mm(turned, jnp.where(hit, 1.0, 0.0).astype(BF16)))
    return jnp.concatenate(halves, axis=0).astype(BF16)


def sigmoid(value):
    return 1.0 / (1.0 + jnp.exp(-value))


def forward_kernel(
    facies_hbm, prior_hbm, recon_hbm, w_embed_hbm, w_conv_hbm, w_head_hbm,
    block, one_hot, pre_embed, hidden, pre_conv, w_conv, w_head,
    facies, prior, recon, w_embed, packed, sorted_rows, sem
):
    parts = 4
    width = facies.shape[1] // parts
    loads = [
        pltpu.make_async_copy(
            facies_hbm.at[:, pl.ds(i * width, width)], facies.at[:, pl.ds(i * width, width)], sem.at[i]
        )
        for i in range(parts)
    ]
    for source, target in (
        (w_embed_hbm, w_embed), (w_conv_hbm, w_conv), (prior_hbm, prior), (recon_hbm, recon), (w_head_hbm, w_head)
    ):
        loads.append(pltpu.make_async_copy(source, target, sem.at[len(loads)]))
    for load in loads:
        load.start()
    row, lane = iota((256, 256), 0), iota((256, 256), 1)
    order = jnp.where((row // 32 == lane % 8) & (row % 32 == lane // 8), 1.0, 0.0).astype(BF16)
    spread = spread_matrix()
    level = (iota((512, 256), 0) % 4).astype(F32)
    for i in range(parts):
        loads[i].wait()
        part = facies[:, pl.ds(i * width, width)].astype(F32).astype(BF16)
        sorted_rows[:, pl.ds(i * width, width)] = mm(order, part).astype(BF16)
    for t in range(8):
        for dy2 in range(2):
            j, dx = 2 * (t // 4) + dy2, t % 4
            rows = [sorted_rows[pl.ds(t * 32, 32), pl.ds((2 * b2 + dy2) * 128, 128)] for b2 in range(8)]
            copied = mm_nt(spread, jnp.concatenate(rows, axis=0))
            hot = jnp.where(copied == level, 1.0, 0.0).astype(BF16)
            for cp in range(4):
                one_hot[cp, j, pl.ds(dx * 128, 128), :] = hot[cp * 128 : (cp + 1) * 128]
    loads[4].wait()
    packed[...] = pair_weights(w_embed[...])
    loads[5].wait()
    conv_turned = jnp.transpose(w_conv[...].astype(F32)).astype(BF16)
    sums = jnp.zeros((256, 128), F32)
    for cp in range(4):
        for j in range(4):
            pre = mm(packed[...], one_hot[cp, j])
            pre_embed[cp, j] = pre
            hidden[cp, j] = (pre * sigmoid(pre)).astype(BF16)
        pre = mm(conv_turned, hidden[cp].reshape(1024, 256))
        pre_conv[cp] = pre
        act = pre * sigmoid(pre)
        sums = sums + act[:, :128] + act[:, 128:]
    pick = jnp.where(iota((8, 128), 1) // 8 % 4 == iota((8, 128), 0), 1.0, 0.0)
    total = lax.dot_general(pick, sums, NT, precision=lax.Precision.HIGHEST, preferred_element_type=F32)
    for load in loads[6:]:
        load.wait()
    block[:, pl.ds(0, 512)] = prior[...]
    block[:, pl.ds(512, 512)] = recon[...]
    block[:, pl.ds(1024, 256)] = (total[:4] / 256.0).astype(BF16)


def pair_kernel(queries, query_square, keys):
    inner = mm_nt(queries, keys)
    key_float = keys.astype(F32)
    count = keys.shape[0]
    key_square = jnp.sum(key_float * key_float, axis=1, keepdims=True)
    key_row = jnp.transpose(jnp.broadcast_to(key_square, (count, 128)))[:1]
    kern = jnp.exp(-(query_square + key_row - 2.0 * inner) / keys.shape[1])
    return jnp.sum(kern, axis=1, keepdims=True), mm(kern.astype(BF16), keys)


def backward_kernel(
    sizes, gathered, one_hot, pre_embed, hidden, pre_conv, w_conv, w_head,
    keep, send, grad_head,
    ordered, head_full
):
    dp, fsdp = sizes
    devices = dp * fsdp
    dp_here, fsdp_here = lax.axis_index("dp"), lax.axis_index("fsdp")
    here = dp_here * fsdp + fsdp_here
    for owner in range(devices):
        ordered[owner] = gathered[owner].astype(F32)
    samples = ordered.shape[1]
    count = devices * samples
    full = ordered[...].reshape(count, ordered.shape[2])
    prior = full[:, :512].astype(BF16)
    recon = full[:, 512:1024]
    pooled = full[:, 1024:].astype(BF16)
    latent = mm(pooled, w_head[...]).astype(BF16)
    latent_float = latent.astype(F32)
    square = jnp.sum(latent_float * latent_float, axis=1, keepdims=True)
    self_sum, self_mix = pair_kernel(latent, square, latent)
    cross_sum, cross_mix = pair_kernel(latent, square, prior)
    pull = -32.0 / count * ((self_sum - cross_sum) * latent_float - self_mix + cross_mix)
    cotangent = (recon + pull).astype(BF16)
    turned = jnp.transpose(full[:, 1024:]).astype(BF16)
    head_full[...] = mm(turned, cotangent)
    share = grad_head.shape[0]
    start = pl.multiple_of(fsdp_here * share, share)
    grad_head[...] = head_full[pl.ds(start, share), :]

    lane_sample = iota((128, count), 0) // 8 % 4 + samples * here
    pick = jnp.where(lane_sample == iota((128, count), 1), 1.0, 0.0).astype(BF16)
    lanes = mm(pick, cotangent).astype(BF16)
    back_pool = mm_nt(w_head[...], lanes) / 256.0
    back_pool = jnp.concatenate([back_pool, back_pool], axis=1)
    grads = []
    conv_total = None
    for cp in range(4):
        pre = pre_conv[cp]
        gate = sigmoid(pre)
        grads.append((back_pool * (gate * (1.0 + pre * (1.0 - gate)))).astype(BF16))
        term = mm_nt(hidden[cp].reshape(1024, 256), grads[cp])
        conv_total = term if cp == 0 else conv_total + term
    core_zero = lax.rem(dp_here, 2) == 0
    rows = 1024 // fsdp // 2
    for f in range(fsdp):
        at = 2 * f * rows
        first, second = conv_total[at : at + rows], conv_total[at + rows : at + 2 * rows]
        keep[f, pl.ds(0, rows), :] = jnp.where(core_zero, first, second)
        send[f, pl.ds(0, rows), :] = jnp.where(core_zero, second, first)
    embed_total = None
    for cp in range(4):
        for j in range(4):
            back_rows = mm(w_conv[pl.ds(j * 256, 256), :], grads[cp])
            pre = pre_embed[cp, j]
            gate = sigmoid(pre)
            signal = (back_rows * (gate * (1.0 + pre * (1.0 - gate)))).astype(BF16)
            term = mm_nt(one_hot[cp, j], signal)
            embed_total = term if embed_total is None else embed_total + term
    embed = jnp.concatenate(
        [
            embed_total[dx * 128 : dx * 128 + 64, :128] + embed_total[dx * 128 + 64 : dx * 128 + 128, 128:]
            for dx in range(4)
        ],
        axis=0,
    )
    half = 256 // fsdp // 4
    for f in range(fsdp):
        for side in range(2):
            at = (4 * f + side) * half
            first, second = embed[at : at + half], embed[at + 2 * half : at + 3 * half]
            place = (f, pl.ds(rows, half), pl.ds(side * 128, 128))
            keep[place] = jnp.where(core_zero, first, second)
            send[place] = jnp.where(core_zero, second, first)


def exponent_of(part):
    top = jnp.max(jnp.max(jnp.max(jnp.abs(part), axis=0), axis=0, keepdims=True), axis=1, keepdims=True)
    return jnp.clip(jnp.floor(jnp.log2(jnp.maximum(top, 1e-37))) - 14.0, -124.0, 114.0)


def scale_kernel(keep, other, coded):
    rows = keep.shape[1]
    conv_rows = rows * 8 // 9
    held = keep[...] + other[...]
    conv, embed = held[:, :conv_rows], held[:, conv_rows:]
    conv_step, embed_step = exponent_of(conv), exponent_of(embed)
    coded[:, pl.ds(0, conv_rows), :] = conv * jnp.exp2(-conv_step)[None]
    coded[:, pl.ds(conv_rows, rows - conv_rows), :] = embed * jnp.exp2(-embed_step)[None]
    spare = coded.shape[1] - rows
    tail = jnp.where(iota((spare, coded.shape[2]), 0) == 0, conv_step, embed_step)
    coded[:, pl.ds(rows, spare), :] = jnp.broadcast_to(tail[None], (coded.shape[0], spare, coded.shape[2]))


def output_kernel(own, other, grad_embed, grad_conv):
    rows = own.shape[0]
    conv_rows, half = rows * 8 // 9, rows // 9
    core_zero = lax.rem(lax.axis_index("dp"), 2) == 0
    first = jnp.where(core_zero, own[...], other[...])
    second = jnp.where(core_zero, other[...], own[...])
    for at, part in ((0, first), (1, second)):
        grad_conv[pl.ds(at * conv_rows, conv_rows), :] = part[:conv_rows]
        grad_embed[pl.ds(at * 2 * half, half), :] = part[conv_rows:, :128]
        grad_embed[pl.ds((at * 2 + 1) * half, half), :] = part[conv_rows:, 128:]


VMEM = pl.BlockSpec(memory_space=pltpu.VMEM)
HBM = pl.BlockSpec(memory_space=pltpu.HBM)
SAVED = (
    ((4, 4, 512, 256), BF16),
    ((4, 4, 256, 256), F32),
    ((4, 4, 256, 256), BF16),
    ((4, 256, 256), F32),
)


def forward(facies, prior_draws, recon_grad, w_embed, w_conv, w_head):
    samples = facies.shape[0]
    latent_width = prior_draws.shape[1]
    rows, lanes = samples * PATCH_X, PATCH_Y * PATCH_Z
    operands = (facies.reshape(rows, lanes), prior_draws, recon_grad, w_embed, w_conv, w_head)
    return pl.pallas_call(
        forward_kernel,
        out_shape=(pltpu.VMEM((samples, 2 * latent_width + 256), BF16),)
        + tuple(pltpu.VMEM(shape, kind) for shape, kind in SAVED)
        + (pltpu.VMEM(w_conv.shape, BF16), pltpu.VMEM(w_head.shape, BF16)),
        in_specs=[HBM] * 6,
        out_specs=(VMEM,) * 7,
        scratch_shapes=[
            pltpu.VMEM((rows, lanes), jnp.int32),
            pltpu.VMEM(prior_draws.shape, BF16),
            pltpu.VMEM(recon_grad.shape, BF16),
            pltpu.VMEM(w_embed.shape, BF16),
            pltpu.VMEM((256, 512), BF16),
            pltpu.VMEM((rows, lanes), BF16),
            pltpu.SemaphoreType.DMA((9,)),
        ],
        compiler_params=pltpu.CompilerParams(vmem_limit_bytes=30 * 2**20),
        name="forward",
    )(*(pltpu.with_memory_space_constraint(operand, pltpu.HBM) for operand in operands))


def backward(sizes, gathered, saved):
    dp, fsdp = sizes
    devices, samples, width = gathered.shape
    payload = jax.ShapeDtypeStruct((fsdp, (1024 + 128) // fsdp // 2, 256), F32)
    return pl.pallas_call(
        lambda *refs: backward_kernel(sizes, *refs),
        out_shape=(payload, payload, jax.ShapeDtypeStruct((256 // fsdp, 512), F32)),
        in_specs=[VMEM] * 7,
        out_specs=(VMEM,) * 3,
        scratch_shapes=[pltpu.VMEM((devices, samples, width), F32), pltpu.VMEM((256, 512), F32)],
        compiler_params=pltpu.CompilerParams(vmem_limit_bytes=30 * 2**20),
        name="backward",
    )(gathered, *saved)


def place_of(x, core, z, fsdp):
    return (2 * x + core) * fsdp + z


def exchange(block, dp, fsdp, flip_x, flip_core):
    pairs = []
    for x in range(dp // 2):
        for core in range(2):
            for z in range(fsdp):
                pairs.append((place_of(x, core, z, fsdp), place_of(x ^ flip_x, core ^ flip_core, z, fsdp)))
    return lax.ppermute(block, GROUP, pairs)


def gather_blocks(block, devices):
    copies = jnp.broadcast_to(block[None], (devices,) + block.shape)
    return lax.all_to_all(copies, GROUP, 0, 0, tiled=True)


def reduce_to_owner(keep, send, dp, fsdp):
    _, rows, width = keep.shape
    conv_rows = rows * 8 // 9
    spare = 16 * (rows // 16 + 1) - rows
    coded = pl.pallas_call(
        scale_kernel,
        out_shape=jax.ShapeDtypeStruct((fsdp, rows + spare, width), F32),
        in_specs=[VMEM] * 2,
        out_specs=VMEM,
        compiler_params=pltpu.CompilerParams(vmem_limit_bytes=16 * 2**20),
        name="scale",
    )(keep, exchange(send, dp, fsdp, 0, 1)).astype(jnp.float16)
    got = lax.all_to_all(coded, "fsdp", 0, 0, tiled=True).astype(F32)
    conv_scale = jnp.exp2(got[:, rows : rows + 1, :1])
    embed_scale = jnp.exp2(got[:, rows + 1 : rows + 2, :1])
    is_conv = jnp.arange(rows)[None, :, None] < conv_rows
    total = jnp.sum(got[:, :rows] * jnp.where(is_conv, conv_scale, embed_scale), axis=0)
    flip = 1
    while flip < dp // 2:
        total = total + exchange(total, dp, fsdp, flip, 0)
        flip *= 2
    return total, exchange(total, dp, fsdp, 0, 1)


def shards(facies, prior_draws, recon_grad, w_embed, w_conv, w_head):
    dp, fsdp = lax.axis_size("dp"), lax.axis_size("fsdp")
    block, *saved = forward(facies, prior_draws, recon_grad, w_embed, w_conv, w_head)
    gathered = gather_blocks(block, dp * fsdp)
    keep, send, grad_head = backward((dp, fsdp), gathered, saved)
    own, other = reduce_to_owner(keep, send, dp, fsdp)
    grad_embed, grad_conv = pl.pallas_call(
        output_kernel,
        out_shape=(
            jax.ShapeDtypeStruct((256 // fsdp, 128), F32),
            jax.ShapeDtypeStruct((1024 // fsdp, 256), F32),
        ),
        in_specs=[VMEM] * 2,
        out_specs=(VMEM,) * 2,
        compiler_params=pltpu.CompilerParams(vmem_limit_bytes=16 * 2**20),
        name="outputs",
    )(own, other)
    return (grad_embed, grad_conv, grad_head)


def solution(mesh):
    return jax.shard_map(
        shards,
        mesh=mesh,
        in_specs=(
            P(("groups", "dp", "fsdp"), None, None),
            P(("groups", "dp", "fsdp"), None),
            P(("groups", "dp", "fsdp"), None),
            P(),
            P(),
            P(),
        ),
        out_specs=(
            P(("groups", "fsdp"), None),
            P(("groups", "fsdp"), None),
            P(("groups", "fsdp"), None),
        ),
        check_vma=False,
    )
```

time: 71.9 us -> 51.3 us (0.71)
  blocking collectives: 0 us -> 14.8 us
  starting transfers between devices: 15.7 us -> 4.98 us
  Pallas kernels: 18.2 us -> 11.2 us
  waiting for transfers between devices: 25.1 us -> 18.1 us
  local copies, waits for them, and re-layouts: 5.96 us -> 0.05 us
  other arithmetic: 4.17 us -> 1.18 us
  between operations: 2.25 us -> 0.71 us
    all_to_all x0 -> x1, blocking collectives: none -> 14.8 us  [gather_blocks(): return lax.all_to_all(copies, GROUP, 0, 0, tiled=True)]
    ppermute x7 -> x3, starting transfers between devices: 9.27 us -> 1.52 us  [exchange(): return lax.ppermute(block, GROUP, pairs)]
    ppermute x7 -> x3, waiting for transfers between devices: 13.6 us -> 7.22 us  [exchange(): return lax.ppermute(block, GROUP, pairs)]
    unnamed x16 -> x0, local copies, waits for them, and re-layouts: 5.84 us -> none
    pallas_call x1 -> x3, Pallas kernels: 11.1 us -> 6.97 us  [the longest x1 6.04 us: forward(): pl.pallas_call(forward_kernel, out_shape=(pltpu.VMEM((samples, 2 * latent...]
    all_to_all x1, starting transfers between devices: 6.46 us -> 3.45 us  [reduce_to_owner(): got = lax.all_to_all(coded, 'fsdp', 0, 0, tiled=True).astype(F32)]
    pallas_call x1, Pallas kernels: 7.07 us -> 4.26 us  [backward(): pl.pallas_call(lambda *refs: backward_kernel(sizes, *refs), out_shape=(pa...]
    reduce_max x2 -> x0, other arithmetic: 1.24 us -> none  [exponent_of(): top = jnp.max(jnp.abs(part))]
  transfers between devices with their start and end apart: 8 -> 4, of which waited for: 8 -> 4; matrix products, arithmetic and copies ran while one was open for 0% -> 0% of each run, Pallas kernels for 0% -> 0%
where the time goes in v3:
time: 51.3 us; the launch traced here: 51 us
  waiting for transfers between devices  18.1 us (35%)
  blocking collectives  14.8 us (29%)
  Pallas kernels  11.2 us (22%)
  starting transfers between devices  4.98 us (10%)
  other arithmetic  1.18 us (2%)
  between operations  0.71 us (1%)
    all_to_all x1, blocking collectives, gather_blocks(): return lax.all_to_all(copies, GROUP, 0, 0, tiled=True)  14.8 us
    all_to_all x1, waiting for transfers between devices, reduce_to_owner(): got = lax.all_to_all(coded, 'fsdp', 0, 0, tiled=True).astype(F32)  10.9 us
    ppermute x3, waiting for transfers between devices, exchange(): return lax.ppermute(block, GROUP, pairs)  7.22 us
    pallas_call x1, Pallas kernels, forward(): pl.pallas_call(forward_kernel, out_shape=(pltpu.VMEM((samples, 2 * latent...  6.04 us
    pallas_call x1, Pallas kernels, backward(): pl.pallas_call(lambda *refs: backward_kernel(sizes, *refs), out_shape=(pa...  4.26 us
    all_to_all x1, starting transfers between devices, reduce_to_owner(): got = lax.all_to_all(coded, 'fsdp', 0, 0, tiled=True).astype(F32)  3.45 us
    ppermute x3, starting transfers between devices, exchange(): return lax.ppermute(block, GROUP, pairs)  1.52 us
  transfers between devices with their start and end apart: 4, of which 4 were waited for; matrix products, arithmetic and copies ran while one was open for 0% of the time, Pallas kernels for 0%

profile of v3, /device:TPU:0, one launch (start us, length us, event | category | flops | bytes accessed | tf_op | source)
XLA Modules:
  0.0 51.0 jit_solution(6329818042104537016)
XLA Ops:
  0.6 6.0 %forward.1 = (bf16[4,1280]{1,0:T(4,128)(2,1)S(1)}, bf16[4,4,512,256]{3,2,1,0:T(8,128)(2,1)S(1)}, f32[4,4,256,256]{3,2,1,0:T(8,128)S(1)}, bf16[4,4,256,256]{3,2,1...) custom-call(s32[256,2048]{1,0:T(8,128)} %bitcast.1, ...), custom_call_target="tpu_custom_call" | custom-call | tf_op jit(solution)/shard_map/forward/pallas_call | solution.py:244
  6.7 14.8 %all_to_all.10.refs_0_ = bf16[16,4,1280]{2,1,0:T(4,128)(2,1)S(1)} all-to-all(bf16[16,4,1280]{2,1,0:T(4,128)(2,1)S(1)} %broadcast_in_dim.35), channel_id=1, replica_groups=mesh['groups'=2,'dp'=4,'fsdp'=4] {'dp','fsdp'}, dimensions={0} | all-to-all | bytes 327680 | tf_op jit(solution)/shard_map/all_to_all | solution.py:295
  21.5 4.3 %backward.1 = (f32[4,144,256]{2,1,0:T(8,128)S(1)}, f32[4,144,256]{2,1,0:T(8,128)S(1)}, f32[64,512]{1,0:T(8,128)}) custom-call(bf16[16,4,1280]{2,1,0:T(4,128)(2,1)S(1)} %all_to_all.10.refs_0_, bf16[4,4,512,256]{3,2,1,0:T(8,128)(2,1)S(1)} %get-tuple-element.16.refs_1_, f32[4,4,256,256]{3,2,1,0:T(8,128)S(1)} %get-tuple-element.17.refs_2_, ...), custom_call_target="tpu_custom_call" | custom-call | tf_op jit(solution)/shard_map/backward/pallas_call | solution.py:269
  25.8 0.3 collective-permute-start
  26.1 1.8 %collective-permute-done.other = f32[4,144,256]{2,1,0:T(8,128)S(1)} collective-permute-done((f32[4,144,256]{2,1,0:T(8,128)S(1)}, f32[4,144,256]{2,1,0:T(8,128)S(1)}, u32[]{:S(2)}, u32[]{:S(2)}) %collective-permute-start) | collective-permute-done | bytes 589856 | tf_op jit(solution)/shard_map/ppermute | solution.py:290
  27.8 0.2 scale.1
  28.0 0.8 %convert_element_type.6 = f16[4,160,256]{2,1,0:T(8,128)(2,1)} convert(f32[4,160,256]{2,1,0:T(8,128)S(1)} %scale.1) | non-fusion elementwise | flops 163840 | bytes 983040 | tf_op jit(solution)/shard_map/convert_element_type | solution.py:309
  28.8 3.5 %all-to-all-start.1 = ((f16[4,160,256]{2,1,0:T(8,128)(2,1)}), f16[4,160,256]{2,1,0:T(8,128)(2,1)S(1)}, u32[]{:S(2)}, u32[]{:S(2)}) async-start(f16[4,160,256]{2,1,0:T(8,128)(2,1)} %convert_element_type.6), calls=%async_computation.1 | async-start | bytes 655360 | tf_op jit(solution)/shard_map/all_to_all | solution.py:310
  32.3 10.9 %all-to-all-done.1 = f16[4,160,256]{2,1,0:T(8,128)(2,1)S(1)} async-done(((f16[4,160,256]{2,1,0:T(8,128)(2,1)}), f16[4,160,256]{2,1,0:T(8,128)(2,1)S(1)}, u32[]{:S(2)}, u32[]{:S(2)}) %all-to-all-start.1) | async-done | bytes 327712 | tf_op jit(solution)/shard_map/all_to_all | solution.py:310
  43.2 0.1 convert_element_type.7
  43.3 0.1 fusion.3
  43.4 0.1 broadcast_select_fusion
  43.5 0.1 fusion
  43.6 1.1 %collective-permute-start.1 = (f32[144,256]{1,0:T(8,128)S(1)}, f32[144,256]{1,0:T(8,128)S(1)}, u32[]{:S(2)}, u32[]{:S(2)}) collective-permute-start(f32[144,256]{1,0:T(8,128)S(1)} %fusion), channel_id=1, source_target_pairs={{0,8},{1,9},{2,10},{3,11},{4,12},{5,13},{6,14},{7,15},{8,0},{9,1},... | collective-permute-start | bytes 442376 | tf_op jit(solution)/shard_map/ppermute | solution.py:290
  44.8 4.1 %collective-permute-done.1 = f32[144,256]{1,0:T(8,128)S(1)} collective-permute-done((f32[144,256]{1,0:T(8,128)S(1)}, f32[144,256]{1,0:T(8,128)S(1)}, u32[]{:S(2)}, u32[]{:S(2)}) %collective-permute-start.1) | collective-permute-done | bytes 147488 | tf_op jit(solution)/shard_map/ppermute | solution.py:290
  48.9 0.1 collective-permute-start.2
  49.0 1.4 %collective-permute-done.2.other = f32[144,256]{1,0:T(8,128)S(1)} collective-permute-done((f32[144,256]{1,0:T(8,128)S(1)}, f32[144,256]{1,0:T(8,128)S(1)}, u32[]{:S(2)}, u32[]{:S(2)}) %collective-permute-start.2) | collective-permute-done | bytes 147488 | tf_op jit(solution)/shard_map/ppermute | solution.py:290
  50.3 0.7 %outputs.1 = (f32[64,128]{1,0:T(8,128)}, f32[256,256]{1,0:T(8,128)}) custom-call(f32[144,256]{1,0:T(8,128)S(1)} %add.3.own, f32[144,256]{1,0:T(8,128)S(1)} %collective-permute-done.2.other), custom_call_target="tpu_custom_call" | custom-call | tf_op jit(solution)/shard_map/outputs/pallas_call | solution.py:328
  (3 shorter events, 0.1 us)
Async XLA Ops:
  25.8 2.1 %collective-permute-start = (f32[4,144,256]{2,1,0:T(8,128)S(1)}, f32[4,144,256]{2,1,0:T(8,128)S(1)}, u32[]{:S(2)}, u32[]{:S(2)}) collective-permute-start(f32[4,144,256]{2,1,0:T(8,128)S(1)} %get-tuple-element.23), channel_id=1, source_target_pairs={{0,4},{1,5},{2,6},{3,7},{4,0},{5,1},{6,2},{7,3},{8,12},{9,13},{10,... | collective-permute-start | bytes 1769480 | tf_op jit(solution)/shard_map/ppermute | solution.py:290
  28.8 14.4 %all-to-all-start.1 = ((f16[4,160,256]{2,1,0:T(8,128)(2,1)}), f16[4,160,256]{2,1,0:T(8,128)(2,1)S(1)}, u32[]{:S(2)}, u32[]{:S(2)}) async-start(f16[4,160,256]{2,1,0:T(8,128)(2,1)} %convert_element_type.6), calls=%async_computation.1 | async-start | bytes 655360 | tf_op jit(solution)/shard_map/all_to_all | solution.py:310
  43.6 5.2 %collective-permute-start.1 = (f32[144,256]{1,0:T(8,128)S(1)}, f32[144,256]{1,0:T(8,128)S(1)}, u32[]{:S(2)}, u32[]{:S(2)}) collective-permute-start(f32[144,256]{1,0:T(8,128)S(1)} %fusion), channel_id=1, source_target_pairs={{0,8},{1,9},{2,10},{3,11},{4,12},{5,13},{6,14},{7,15},{8,0},{9,1},... | collective-permute-start | bytes 442376 | tf_op jit(solution)/shard_map/ppermute | solution.py:290
  48.9 1.4 %collective-permute-start.2 = (f32[144,256]{1,0:T(8,128)S(1)}, f32[144,256]{1,0:T(8,128)S(1)}, u32[]{:S(2)}, u32[]{:S(2)}) collective-permute-start(f32[144,256]{1,0:T(8,128)S(1)} %add.3.own), channel_id=1, source_target_pairs={{0,4},{1,5},{2,6},{3,7},{4,0},{5,1},{6,2},{7,3},{8,12},{9,13},{10,... | collective-permute-start | bytes 442376 | tf_op jit(solution)/shard_map/ppermute | solution.py:290

commit v4 on v3

--- a/solution.py
+++ b/solution.py
@@ -197,21 +197,64 @@
 
 
 def exponent_of(part):
-    top = jnp.max(jnp.max(jnp.max(jnp.abs(part), axis=0), axis=0, keepdims=True), axis=1, keepdims=True)
+    top = jnp.abs(part)
+    while top.ndim > 2:
+        top = jnp.max(top, axis=0)
+    top = jnp.max(jnp.max(top, axis=0, keepdims=True), axis=1, keepdims=True)
     return jnp.clip(jnp.floor(jnp.log2(jnp.maximum(top, 1e-37))) - 14.0, -124.0, 114.0)
 
 
-def scale_kernel(keep, other, coded):
+def store_coded(coded, part):
+    rows = part.shape[0]
+    conv_rows = rows * 8 // 9
+    conv, embed = part[:conv_rows], part[conv_rows:]
+    steps = exponent_of(conv), exponent_of(embed)
+    store_scaled(coded, part, steps)
+
+
+def store_scaled(coded, part, steps):
+    rows, spare = part.shape[0], coded.shape[0] - part.shape[0]
+    conv_rows = rows * 8 // 9
+    coded[pl.ds(0, conv_rows), :] = part[:conv_rows] * jnp.exp2(-steps[0])
+    coded[pl.ds(conv_rows, rows - conv_rows), :] = part[conv_rows:] * jnp.exp2(-steps[1])
+    tail = jnp.where(iota((spare, coded.shape[1]), 0) == 0, steps[0], steps[1])
+    coded[pl.ds(rows, spare), :] = tail
+
+
+def load_coded(coded, rows):
+    conv_rows = rows * 8 // 9
+    conv_scale = jnp.exp2(coded[pl.ds(rows, 1), :])
+    embed_scale = jnp.exp2(coded[pl.ds(rows + 1, 1), :])
+    return jnp.concatenate(
+        [coded[pl.ds(0, conv_rows), :] * conv_scale, coded[pl.ds(conv_rows, rows - conv_rows), :] * embed_scale], axis=0
+    )
+
+
+def scale_kernel(keep, other, own, *coded):
     rows = keep.shape[1]
     conv_rows = rows * 8 // 9
     held = keep[...] + other[...]
-    conv, embed = held[:, :conv_rows], held[:, conv_rows:]
-    conv_step, embed_step = exponent_of(conv), exponent_of(embed)
-    coded[:, pl.ds(0, conv_rows), :] = conv * jnp.exp2(-conv_step)[None]
-    coded[:, pl.ds(conv_rows, rows - conv_rows), :] = embed * jnp.exp2(-embed_step)[None]
-    spare = coded.shape[1] - rows
-    tail = jnp.where(iota((spare, coded.shape[2]), 0) == 0, conv_step, embed_step)
-    coded[:, pl.ds(rows, spare), :] = jnp.broadcast_to(tail[None], (coded.shape[0], spare, coded.shape[2]))
+    steps = exponent_of(held[:, :conv_rows]), exponent_of(held[:, conv_rows:])
+    here = lax.axis_index("fsdp")
+    own[...] = keep[here] + other[here]
+    for place, target in enumerate(coded):
+        owner = here ^ (place + 1)
+        store_scaled(target, keep[owner] + other[owner], steps)
+
+
+def first_sum_kernel(own, *refs):
+    *received, coded = refs
+    total = own[...]
+    for part in received:
+        total = total + load_coded(part, total.shape[0])
+    store_coded(coded, total)
+
+
+def next_sum_kernel(mine, other, total, coded):
+    rows = total.shape[0]
+    summed = load_coded(mine, rows) + load_coded(other, rows)
+    total[...] = summed
+    store_coded(coded, summed)
 
 
 def output_kernel(own, other, grad_embed, grad_conv):
@@ -281,12 +324,12 @@
     return (2 * x + core) * fsdp + z
 
 
-def exchange(block, dp, fsdp, flip_x, flip_core):
+def exchange(block, dp, fsdp, flip_x, flip_core, flip_z):
     pairs = []
     for x in range(dp // 2):
         for core in range(2):
             for z in range(fsdp):
-                pairs.append((place_of(x, core, z, fsdp), place_of(x ^ flip_x, core ^ flip_core, z, fsdp)))
+                pairs.append((place_of(x, core, z, fsdp), place_of(x ^ flip_x, core ^ flip_core, z ^ flip_z, fsdp)))
     return lax.ppermute(block, GROUP, pairs)
 
 
@@ -295,28 +338,39 @@
     return lax.all_to_all(copies, GROUP, 0, 0, tiled=True)
 
 
+def local_kernel(kernel, outs, name, *operands):
+    return pl.pallas_call(
+        kernel,
+        out_shape=outs,
+        in_specs=[VMEM] * len(operands),
+        out_specs=(VMEM,) * len(outs),
+        compiler_params=pltpu.CompilerParams(vmem_limit_bytes=16 * 2**20),
+        name=name,
+    )(*operands)
+
+
+def to_half(coded):
+    rounded = lax.reduce_precision(coded, exponent_bits=5, mantissa_bits=10)
+    return rounded, rounded.astype(jnp.float16)
+
+
 def reduce_to_owner(keep, send, dp, fsdp):
     _, rows, width = keep.shape
-    conv_rows = rows * 8 // 9
-    spare = 16 * (rows // 16 + 1) - rows
-    coded = pl.pallas_call(
-        scale_kernel,
-        out_shape=jax.ShapeDtypeStruct((fsdp, rows + spare, width), F32),
-        in_specs=[VMEM] * 2,
-        out_specs=VMEM,
-        compiler_params=pltpu.CompilerParams(vmem_limit_bytes=16 * 2**20),
-        name="scale",
-    )(keep, exchange(send, dp, fsdp, 0, 1)).astype(jnp.float16)
-    got = lax.all_to_all(coded, "fsdp", 0, 0, tiled=True).astype(F32)
-    conv_scale = jnp.exp2(got[:, rows : rows + 1, :1])
-    embed_scale = jnp.exp2(got[:, rows + 1 : rows + 2, :1])
-    is_conv = jnp.arange(rows)[None, :, None] < conv_rows
-    total = jnp.sum(got[:, :rows] * jnp.where(is_conv, conv_scale, embed_scale), axis=0)
+    plain = jax.ShapeDtypeStruct((rows, width), F32)
+    scaled = jax.ShapeDtypeStruct((rows + 8, width), F32)
+    other = exchange(send, dp, fsdp, 0, 1, 0)
+    own, *coded = local_kernel(scale_kernel, (plain,) + (scaled,) * (fsdp - 1), "scale", keep, other)
+    received = [
+        exchange(to_half(part)[1], dp, fsdp, 0, 0, place + 1).astype(F32) for place, part in enumerate(coded)
+    ]
+    (coded,) = local_kernel(first_sum_kernel, (scaled,), "sum_z", own, *received)
     flip = 1
     while flip < dp // 2:
-        total = total + exchange(total, dp, fsdp, flip, 0)
+        mine, sent = to_half(coded)
+        other = exchange(sent, dp, fsdp, flip, 0, 0).astype(F32)
+        total, coded = local_kernel(next_sum_kernel, (plain, scaled), "sum_x", mine, other)
         flip *= 2
-    return total, exchange(total, dp, fsdp, 0, 1)
+    return total, exchange(total, dp, fsdp, 0, 1, 0)
 
 
 def shards(facies, prior_draws, recon_grad, w_embed, w_conv, w_head):

time: 51.3 us -> 45.9 us (0.89)
  waiting for transfers between devices: 18.1 us -> 11.8 us
  Pallas kernels: 11.2 us -> 12.2 us
  starting transfers between devices: 4.98 us -> 5.83 us
  other arithmetic: 1.18 us -> 0.39 us
    all_to_all x1 -> x0, waiting for transfers between devices: 10.9 us -> none  [reduce_to_owner(): got = lax.all_to_all(coded, 'fsdp', 0, 0, tiled=True).astype(F32)]
    ppermute x3 -> x6, waiting for transfers between devices: 7.22 us -> 11.8 us  [exchange(): return lax.ppermute(block, GROUP, pairs)]
    ppermute x3 -> x6, starting transfers between devices: 1.52 us -> 5.83 us  [exchange(): return lax.ppermute(block, GROUP, pairs)]
    all_to_all x1 -> x0, starting transfers between devices: 3.45 us -> none  [reduce_to_owner(): got = lax.all_to_all(coded, 'fsdp', 0, 0, tiled=True).astype(F32)]
    pallas_call x1 -> x3, Pallas kernels: 0.19 us -> 1.15 us  [local_kernel(): pl.pallas_call(kernel, out_shape=outs, in_specs=[VMEM] * len(operands), o...]
  transfers between devices with their start and end apart: 4 -> 6, of which waited for: 4 -> 5; matrix products, arithmetic and copies ran while one was open for 0% -> 0% of each run, Pallas kernels for 0% -> 0%
where the time goes in v4:
time: 45.9 us; the launch traced here: 45.7 us
  blocking collectives  14.8 us (32%)
  Pallas kernels  12.2 us (27%)
  waiting for transfers between devices  11.8 us (26%)
  starting transfers between devices  5.83 us (13%)
  between operations  0.72 us (2%)
    all_to_all x1, blocking collectives, gather_blocks(): return lax.all_to_all(copies, GROUP, 0, 0, tiled=True)  14.8 us
    ppermute x6, waiting for transfers between devices, exchange(): return lax.ppermute(block, GROUP, pairs)  11.8 us
    pallas_call x1, Pallas kernels, forward(): pl.pallas_call(forward_kernel, out_shape=(pltpu.VMEM((samples, 2 * latent...  6.04 us
    ppermute x6, starting transfers between devices, exchange(): return lax.ppermute(block, GROUP, pairs)  5.83 us
    pallas_call x1, Pallas kernels, backward(): pl.pallas_call(lambda *refs: backward_kernel(sizes, *refs), out_shape=(pa...  4.26 us
    pallas_call x3, Pallas kernels, local_kernel(): pl.pallas_call(kernel, out_shape=outs, in_specs=[VMEM] * len(operands), o...  1.15 us
  transfers between devices with their start and end apart: 6, of which 5 were waited for; matrix products, arithmetic and copies ran while one was open for 0% of the time, Pallas kernels for 0%

profile of v4, /device:TPU:0, one launch (start us, length us, event | category | flops | bytes accessed | tf_op | source)
XLA Modules:
  0.0 45.7 jit_solution(8918204009841974301)
XLA Ops:
  0.6 6.0 %forward.1 = (bf16[4,1280]{1,0:T(4,128)(2,1)S(1)}, bf16[4,4,512,256]{3,2,1,0:T(8,128)(2,1)S(1)}, f32[4,4,256,256]{3,2,1,0:T(8,128)S(1)}, bf16[4,4,256,256]{3,2,1...) custom-call(s32[256,2048]{1,0:T(8,128)} %bitcast.1, ...), custom_call_target="tpu_custom_call" | custom-call | tf_op jit(solution)/shard_map/forward/pallas_call | solution.py:287
  6.7 14.8 %all_to_all.5.refs_0_ = bf16[16,4,1280]{2,1,0:T(4,128)(2,1)S(1)} all-to-all(bf16[16,4,1280]{2,1,0:T(4,128)(2,1)S(1)} %broadcast_in_dim.2), channel_id=1, replica_groups=mesh['groups'=2,'dp'=4,'fsdp'=4] {'dp','fsdp'}, dimensions={0} | all-to-all | bytes 327680 | tf_op jit(solution)/shard_map/all_to_all | solution.py:338
  21.5 4.3 %backward.1 = (f32[4,144,256]{2,1,0:T(8,128)S(1)}, f32[4,144,256]{2,1,0:T(8,128)S(1)}, f32[64,512]{1,0:T(8,128)}) custom-call(bf16[16,4,1280]{2,1,0:T(4,128)(2,1)S(1)} %all_to_all.5.refs_0_, bf16[4,4,512,256]{3,2,1,0:T(8,128)(2,1)S(1)} %get-tuple-element.21.refs_1_, f32[4,4,256,256]{3,2,1,0:T(8,128)S(1)} %get-tuple-element.22.refs_2_, ...), custom_call_target="tpu_custom_call" | custom-call | tf_op jit(solution)/shard_map/backward/pallas_call | solution.py:312
  25.8 0.3 collective-permute-start
  26.1 1.8 %collective-permute-done.other = f32[4,144,256]{2,1,0:T(8,128)S(1)} collective-permute-done((f32[4,144,256]{2,1,0:T(8,128)S(1)}, f32[4,144,256]{2,1,0:T(8,128)S(1)}, u32[]{:S(2)}, u32[]{:S(2)}) %collective-permute-start) | collective-permute-done | bytes 589856 | tf_op jit(solution)/shard_map/ppermute | solution.py:333
  27.8 0.2 scale.1
  28.0 0.1 reduce-precision_convert_fusion.1
  28.1 0.1 reduce-precision_convert_fusion
  28.2 1.2 %collective-permute-start.3 = (f16[152,256]{1,0:T(8,128)(2,1)S(1)}, f16[152,256]{1,0:T(8,128)(2,1)S(1)}, u32[]{:S(2)}, u32[]{:S(2)}) collective-permute-start(f16[152,256]{1,0:T(8,128)(2,1)S(1)} %reduce-precision_convert_fusion), channel_id=1, source_target_pairs={{0,3},{1,2},{2,1},{3,0},{4,7},{5,6},{6,5},{7,4},{8,11},{9,10},{10,... | collective-permute-start | bytes 233480 | tf_op jit(solution)/shard_map/ppermute | solution.py:333
  29.5 1.2 %collective-permute-start.2 = (f16[152,256]{1,0:T(8,128)(2,1)S(1)}, f16[152,256]{1,0:T(8,128)(2,1)S(1)}, u32[]{:S(2)}, u32[]{:S(2)}) collective-permute-start(f16[152,256]{1,0:T(8,128)(2,1)S(1)} %reduce-precision_convert_fusion.1), channel_id=1, source_target_pairs={{0,2},{1,3},{2,0},{3,1},{4,6},{5,7},{6,4},{7,5},{8,10},{9,11},{10,... | collective-permute-start | bytes 233480 | tf_op jit(solution)/shard_map/ppermute | solution.py:333
  30.7 0.1 reduce-precision_convert_fusion.2
  30.8 2.1 %collective-permute-start.1 = (f16[152,256]{1,0:T(8,128)(2,1)S(1)}, f16[152,256]{1,0:T(8,128)(2,1)S(1)}, u32[]{:S(2)}, u32[]{:S(2)}) collective-permute-start(f16[152,256]{1,0:T(8,128)(2,1)S(1)} %reduce-precision_convert_fusion.2), channel_id=1, source_target_pairs={{0,1},{1,0},{2,3},{3,2},{4,5},{5,4},{6,7},{7,6},{8,9},{9,8},{10,11... | collective-permute-start | bytes 233480 | tf_op jit(solution)/shard_map/ppermute | solution.py:333
  32.8 2.5 %collective-permute-done.3 = f16[152,256]{1,0:T(8,128)(2,1)S(1)} collective-permute-done((f16[152,256]{1,0:T(8,128)(2,1)S(1)}, f16[152,256]{1,0:T(8,128)(2,1)S(1)}, u32[]{:S(2)}, u32[]{:S(2)}) %collective-permute-start.3) | collective-permute-done | bytes 77856 | tf_op jit(solution)/shard_map/ppermute | solution.py:333
  35.4 2.7 %collective-permute-done.2 = f16[152,256]{1,0:T(8,128)(2,1)S(1)} collective-permute-done((f16[152,256]{1,0:T(8,128)(2,1)S(1)}, f16[152,256]{1,0:T(8,128)(2,1)S(1)}, u32[]{:S(2)}, u32[]{:S(2)}) %collective-permute-start.2) | collective-permute-done | bytes 77856 | tf_op jit(solution)/shard_map/ppermute | solution.py:333
  38.1 0.0 collective-permute-done.1
  38.1 0.2 sum_z.1
  38.3 0.1 reduce-precision_convert_fusion.3
  38.4 1.0 %collective-permute-start.4 = (f16[152,256]{1,0:T(8,128)(2,1)S(1)}, f16[152,256]{1,0:T(8,128)(2,1)S(1)}, u32[]{:S(2)}, u32[]{:S(2)}) collective-permute-start(f16[152,256]{1,0:T(8,128)(2,1)S(1)} %get-tuple-element.37), channel_id=1, source_target_pairs={{0,8},{1,9},{2,10},{3,11},{4,12},{5,13},{6,14},{7,15},{8,0},{9,1},... | collective-permute-start | bytes 233480 | tf_op jit(solution)/shard_map/ppermute | solution.py:333
  39.4 3.5 %collective-permute-done.4 = f16[152,256]{1,0:T(8,128)(2,1)S(1)} collective-permute-done((f16[152,256]{1,0:T(8,128)(2,1)S(1)}, f16[152,256]{1,0:T(8,128)(2,1)S(1)}, u32[]{:S(2)}, u32[]{:S(2)}) %collective-permute-start.4) | collective-permute-done | bytes 77856 | tf_op jit(solution)/shard_map/ppermute | solution.py:333
  42.8 0.8 %sum_x.1 = (f32[144,256]{1,0:T(8,128)S(1)}, f32[152,256]{1,0:T(8,128)}) custom-call(f32[152,256]{1,0:T(8,128)S(1)} %get-tuple-element.38.mine, f32[152,256]{1,0:T(8,128)S(1)} %convert_element_type.31.other), custom_call_target="tpu_custom_call" | custom-call | tf_op jit(solution)/shard_map/sum_x/pallas_call | solution.py:342
  43.6 0.0 collective-permute-start.5
  43.6 1.4 %collective-permute-done.5.other = f32[144,256]{1,0:T(8,128)S(1)} collective-permute-done((f32[144,256]{1,0:T(8,128)S(1)}, f32[144,256]{1,0:T(8,128)S(1)}, u32[]{:S(2)}, u32[]{:S(2)}) %collective-permute-start.5) | collective-permute-done | bytes 147488 | tf_op jit(solution)/shard_map/ppermute | solution.py:333
  45.0 0.7 %outputs.1 = (f32[64,128]{1,0:T(8,128)}, f32[256,256]{1,0:T(8,128)}) custom-call(f32[144,256]{1,0:T(8,128)S(1)} %get-tuple-element.33.own, f32[144,256]{1,0:T(8,128)S(1)} %collective-permute-done.5.other), custom_call_target="tpu_custom_call" | custom-call | tf_op jit(solution)/shard_map/outputs/pallas_call | solution.py:382
  (5 shorter events, 0.1 us)
Async XLA Ops:
  25.8 2.1 %collective-permute-start = (f32[4,144,256]{2,1,0:T(8,128)S(1)}, f32[4,144,256]{2,1,0:T(8,128)S(1)}, u32[]{:S(2)}, u32[]{:S(2)}) collective-permute-start(f32[4,144,256]{2,1,0:T(8,128)S(1)} %get-tuple-element.28), channel_id=1, source_target_pairs={{0,4},{1,5},{2,6},{3,7},{4,0},{5,1},{6,2},{7,3},{8,12},{9,13},{10,... | collective-permute-start | bytes 1769480 | tf_op jit(solution)/shard_map/ppermute | solution.py:333
  28.2 7.2 %collective-permute-start.3 = (f16[152,256]{1,0:T(8,128)(2,1)S(1)}, f16[152,256]{1,0:T(8,128)(2,1)S(1)}, u32[]{:S(2)}, u32[]{:S(2)}) collective-permute-start(f16[152,256]{1,0:T(8,128)(2,1)S(1)} %reduce-precision_convert_fusion), channel_id=1, source_target_pairs={{0,3},{1,2},{2,1},{3,0},{4,7},{5,6},{6,5},{7,4},{8,11},{9,10},{10,... | collective-permute-start | bytes 233480 | tf_op jit(solution)/shard_map/ppermute | solution.py:333
  29.5 8.6 %collective-permute-start.2 = (f16[152,256]{1,0:T(8,128)(2,1)S(1)}, f16[152,256]{1,0:T(8,128)(2,1)S(1)}, u32[]{:S(2)}, u32[]{:S(2)}) collective-permute-start(f16[152,256]{1,0:T(8,128)(2,1)S(1)} %reduce-precision_convert_fusion.1), channel_id=1, source_target_pairs={{0,2},{1,3},{2,0},{3,1},{4,6},{5,7},{6,4},{7,5},{8,10},{9,11},{10,... | collective-permute-start | bytes 233480 | tf_op jit(solution)/shard_map/ppermute | solution.py:333
  30.8 7.3 %collective-permute-start.1 = (f16[152,256]{1,0:T(8,128)(2,1)S(1)}, f16[152,256]{1,0:T(8,128)(2,1)S(1)}, u32[]{:S(2)}, u32[]{:S(2)}) collective-permute-start(f16[152,256]{1,0:T(8,128)(2,1)S(1)} %reduce-precision_convert_fusion.2), channel_id=1, source_target_pairs={{0,1},{1,0},{2,3},{3,2},{4,5},{5,4},{6,7},{7,6},{8,9},{9,8},{10,11... | collective-permute-start | bytes 233480 | tf_op jit(solution)/shard_map/ppermute | solution.py:333
  38.4 4.5 %collective-permute-start.4 = (f16[152,256]{1,0:T(8,128)(2,1)S(1)}, f16[152,256]{1,0:T(8,128)(2,1)S(1)}, u32[]{:S(2)}, u32[]{:S(2)}) collective-permute-start(f16[152,256]{1,0:T(8,128)(2,1)S(1)} %get-tuple-element.37), channel_id=1, source_target_pairs={{0,8},{1,9},{2,10},{3,11},{4,12},{5,13},{6,14},{7,15},{8,0},{9,1},... | collective-permute-start | bytes 233480 | tf_op jit(solution)/shard_map/ppermute | solution.py:333
  43.6 1.4 %collective-permute-start.5 = (f32[144,256]{1,0:T(8,128)S(1)}, f32[144,256]{1,0:T(8,128)S(1)}, u32[]{:S(2)}, u32[]{:S(2)}) collective-permute-start(f32[144,256]{1,0:T(8,128)S(1)} %get-tuple-element.33.own), channel_id=1, source_target_pairs={{0,4},{1,5},{2,6},{3,7},{4,0},{5,1},{6,2},{7,3},{8,12},{9,13},{10,... | collective-permute-start | bytes 442376 | tf_op jit(solution)/shard_map/ppermute | solution.py:333

commit v5 on v4

--- a/solution.py
+++ b/solution.py
@@ -50,6 +50,11 @@
 
 def sigmoid(value):
     return 1.0 / (1.0 + jnp.exp(-value))
+
+
+def silu_slope(value):
+    gate = sigmoid(value)
+    return gate * (1.0 + value * (1.0 - gate))
 
 
 def forward_kernel(
@@ -121,8 +126,8 @@
 
 
 def backward_kernel(
-    sizes, gathered, one_hot, pre_embed, hidden, pre_conv, w_conv, w_head,
-    keep, send, grad_head,
+    sizes, gathered, hidden, slope_conv, w_head,
+    keep, send, grads, grad_head,
     ordered, head_full
 ):
     dp, fsdp = sizes
@@ -155,28 +160,26 @@
     lanes = mm(pick, cotangent).astype(BF16)
     back_pool = mm_nt(w_head[...], lanes) / 256.0
     back_pool = jnp.concatenate([back_pool, back_pool], axis=1)
-    grads = []
     conv_total = None
     for cp in range(4):
-        pre = pre_conv[cp]
-        gate = sigmoid(pre)
-        grads.append((back_pool * (gate * (1.0 + pre * (1.0 - gate)))).astype(BF16))
+        grads[cp] = (back_pool * slope_conv[cp]).astype(BF16)
         term = mm_nt(hidden[cp].reshape(1024, 256), grads[cp])
         conv_total = term if cp == 0 else conv_total + term
     core_zero = lax.rem(dp_here, 2) == 0
-    rows = 1024 // fsdp // 2
+    rows = keep.shape[1]
     for f in range(fsdp):
         at = 2 * f * rows
         first, second = conv_total[at : at + rows], conv_total[at + rows : at + 2 * rows]
-        keep[f, pl.ds(0, rows), :] = jnp.where(core_zero, first, second)
-        send[f, pl.ds(0, rows), :] = jnp.where(core_zero, second, first)
+        keep[f] = jnp.where(core_zero, first, second)
+        send[f] = jnp.where(core_zero, second, first)
+
+
+def embed_kernel(grads, w_conv, slope_embed, one_hot, embed_out):
     embed_total = None
     for cp in range(4):
         for j in range(4):
             back_rows = mm(w_conv[pl.ds(j * 256, 256), :], grads[cp])
-            pre = pre_embed[cp, j]
-            gate = sigmoid(pre)
-            signal = (back_rows * (gate * (1.0 + pre * (1.0 - gate)))).astype(BF16)
+            signal = (back_rows * slope_embed[cp, j]).astype(BF16)
             term = mm_nt(one_hot[cp, j], signal)
             embed_total = term if embed_total is None else embed_total + term
     embed = jnp.concatenate(
@@ -186,14 +189,18 @@
         ],
         axis=0,
     )
-    half = 256 // fsdp // 4
-    for f in range(fsdp):
+    half = embed_out.shape[1]
+    for f in range(embed_out.shape[0]):
         for side in range(2):
-            at = (4 * f + side) * half
-            first, second = embed[at : at + half], embed[at + 2 * half : at + 3 * half]
-            place = (f, pl.ds(rows, half), pl.ds(side * 128, 128))
-            keep[place] = jnp.where(core_zero, first, second)
-            send[place] = jnp.where(core_zero, second, first)
+            at = (2 * f + side) * half
+            embed_out[f, :, pl.ds(side * 128, 128)] = embed[at : at + half]
+
+
+def slope_kernel(pre_embed, pre_conv, slope_embed, slope_conv):
+    for cp in range(4):
+        for j in range(4):
+            slope_embed[cp, j] = silu_slope(pre_embed[cp, j])
+        slope_conv[cp] = silu_slope(pre_conv[cp])
 
 
 def exponent_of(part):
@@ -206,7 +213,7 @@
 
 def store_coded(coded, part):
     rows = part.shape[0]
-    conv_rows = rows * 8 // 9
+    conv_rows = rows * 4 // 5
     conv, embed = part[:conv_rows], part[conv_rows:]
     steps = exponent_of(conv), exponent_of(embed)
     store_scaled(coded, part, steps)
@@ -214,7 +221,7 @@
 
 def store_scaled(coded, part, steps):
     rows, spare = part.shape[0], coded.shape[0] - part.shape[0]
-    conv_rows = rows * 8 // 9
+    conv_rows = rows * 4 // 5
     coded[pl.ds(0, conv_rows), :] = part[:conv_rows] * jnp.exp2(-steps[0])
     coded[pl.ds(conv_rows, rows - conv_rows), :] = part[conv_rows:] * jnp.exp2(-steps[1])
     tail = jnp.where(iota((spare, coded.shape[1]), 0) == 0, steps[0], steps[1])
@@ -222,7 +229,7 @@
 
 
 def load_coded(coded, rows):
-    conv_rows = rows * 8 // 9
+    conv_rows = rows * 4 // 5
     conv_scale = jnp.exp2(coded[pl.ds(rows, 1), :])
     embed_scale = jnp.exp2(coded[pl.ds(rows + 1, 1), :])
     return jnp.concatenate(
@@ -230,16 +237,17 @@
     )
 
 
-def scale_kernel(keep, other, own, *coded):
-    rows = keep.shape[1]
-    conv_rows = rows * 8 // 9
+def scale_kernel(keep, other, embed, own, *coded):
     held = keep[...] + other[...]
-    steps = exponent_of(held[:, :conv_rows]), exponent_of(held[:, conv_rows:])
+    steps = exponent_of(held), exponent_of(embed[...])
     here = lax.axis_index("fsdp")
-    own[...] = keep[here] + other[here]
+
+    def share(z):
+        return jnp.concatenate([keep[z] + other[z], embed[z]], axis=0)
+
+    own[...] = share(here)
     for place, target in enumerate(coded):
-        owner = here ^ (place + 1)
-        store_scaled(target, keep[owner] + other[owner], steps)
+        store_scaled(target, share(here ^ (len(coded) - place)), steps)
 
 
 def first_sum_kernel(own, *refs):
@@ -250,23 +258,25 @@
     store_coded(coded, total)
 
 
-def next_sum_kernel(mine, other, total, coded):
+def next_sum_kernel(mine, other, total, *coded):
     rows = total.shape[0]
     summed = load_coded(mine, rows) + load_coded(other, rows)
     total[...] = summed
-    store_coded(coded, summed)
+    if coded:
+        store_coded(coded[0], summed)
 
 
 def output_kernel(own, other, grad_embed, grad_conv):
     rows = own.shape[0]
-    conv_rows, half = rows * 8 // 9, rows // 9
+    conv_rows, half = rows * 4 // 5, rows // 5
     core_zero = lax.rem(lax.axis_index("dp"), 2) == 0
-    first = jnp.where(core_zero, own[...], other[...])
-    second = jnp.where(core_zero, other[...], own[...])
-    for at, part in ((0, first), (1, second)):
-        grad_conv[pl.ds(at * conv_rows, conv_rows), :] = part[:conv_rows]
-        grad_embed[pl.ds(at * 2 * half, half), :] = part[conv_rows:, :128]
-        grad_embed[pl.ds((at * 2 + 1) * half, half), :] = part[conv_rows:, 128:]
+    grad_conv[pl.ds(0, conv_rows), :] = jnp.where(core_zero, own[pl.ds(0, conv_rows), :], other[pl.ds(0, conv_rows), :])
+    grad_conv[pl.ds(conv_rows, conv_rows), :] = jnp.where(
+        core_zero, other[pl.ds(0, conv_rows), :], own[pl.ds(0, conv_rows), :]
+    )
+    embed = own[pl.ds(conv_rows, half), :] + other[pl.ds(conv_rows, half), :]
+    grad_embed[pl.ds(0, half), :] = embed[:, :128]
+    grad_embed[pl.ds(half, half), :] = embed[:, 128:]
 
 
 VMEM = pl.BlockSpec(memory_space=pltpu.VMEM)
@@ -305,19 +315,46 @@
     )(*(pltpu.with_memory_space_constraint(operand, pltpu.HBM) for operand in operands))
 
 
-def backward(sizes, gathered, saved):
+def slopes(pre_embed, pre_conv):
+    return pl.pallas_call(
+        slope_kernel,
+        out_shape=(pltpu.VMEM(pre_embed.shape, F32), pltpu.VMEM(pre_conv.shape, F32)),
+        in_specs=[VMEM] * 2,
+        out_specs=(VMEM,) * 2,
+        input_output_aliases={0: 0, 1: 1},
+        compiler_params=pltpu.CompilerParams(vmem_limit_bytes=16 * 2**20),
+        cost_estimate=pl.CostEstimate(flops=12 * 10**6, bytes_accessed=10 * 2**20, transcendentals=2600000),
+        name="slopes",
+    )(pre_embed, pre_conv)
+
+
+def backward(sizes, gathered, hidden, slope_conv, w_head):
     dp, fsdp = sizes
     devices, samples, width = gathered.shape
-    payload = jax.ShapeDtypeStruct((fsdp, (1024 + 128) // fsdp // 2, 256), F32)
+    payload = pltpu.VMEM((fsdp, 1024 // fsdp // 2, 256), F32)
     return pl.pallas_call(
         lambda *refs: backward_kernel(sizes, *refs),
-        out_shape=(payload, payload, jax.ShapeDtypeStruct((256 // fsdp, 512), F32)),
-        in_specs=[VMEM] * 7,
-        out_specs=(VMEM,) * 3,
+        out_shape=(
+            payload, payload, pltpu.VMEM((4, 256, 256), BF16), jax.ShapeDtypeStruct((256 // fsdp, 512), F32)
+        ),
+        in_specs=[VMEM] * 4,
+        out_specs=(VMEM,) * 4,
         scratch_shapes=[pltpu.VMEM((devices, samples, width), F32), pltpu.VMEM((256, 512), F32)],
-        compiler_params=pltpu.CompilerParams(vmem_limit_bytes=30 * 2**20),
+        compiler_params=pltpu.CompilerParams(vmem_limit_bytes=24 * 2**20),
         name="backward",
-    )(gathered, *saved)
+    )(gathered, hidden, slope_conv, w_head)
+
+
+def embed_gradient(fsdp, grads, w_conv, slope_embed, one_hot):
+    return pl.pallas_call(
+        embed_kernel,
+        out_shape=pltpu.VMEM((fsdp, 256 // fsdp // 2, 256), F32),
+        in_specs=[VMEM] * 4,
+        out_specs=VMEM,
+        compiler_params=pltpu.CompilerParams(vmem_limit_bytes=24 * 2**20),
+        cost_estimate=pl.CostEstimate(flops=16 * 10**8, bytes_accessed=10 * 2**20, transcendentals=0),
+        name="embed_gradient",
+    )(grads, w_conv, slope_embed, one_hot)
 
 
 def place_of(x, core, z, fsdp):
@@ -354,31 +391,37 @@
     return rounded, rounded.astype(jnp.float16)
 
 
-def reduce_to_owner(keep, send, dp, fsdp):
-    _, rows, width = keep.shape
+def reduce_to_owner(keep, other, embed, dp, fsdp):
+    rows, width = keep.shape[1] + embed.shape[1], keep.shape[2]
     plain = jax.ShapeDtypeStruct((rows, width), F32)
     scaled = jax.ShapeDtypeStruct((rows + 8, width), F32)
-    other = exchange(send, dp, fsdp, 0, 1, 0)
-    own, *coded = local_kernel(scale_kernel, (plain,) + (scaled,) * (fsdp - 1), "scale", keep, other)
+    own, *coded = local_kernel(scale_kernel, (plain,) + (scaled,) * (fsdp - 1), "scale", keep, other, embed)
     received = [
-        exchange(to_half(part)[1], dp, fsdp, 0, 0, place + 1).astype(F32) for place, part in enumerate(coded)
+        exchange(to_half(part)[1], dp, fsdp, 0, 0, fsdp - 1 - place).astype(F32) for place, part in enumerate(coded)
     ]
     (coded,) = local_kernel(first_sum_kernel, (scaled,), "sum_z", own, *received)
     flip = 1
     while flip < dp // 2:
         mine, sent = to_half(coded)
         other = exchange(sent, dp, fsdp, flip, 0, 0).astype(F32)
-        total, coded = local_kernel(next_sum_kernel, (plain, scaled), "sum_x", mine, other)
         flip *= 2
+        outs = (plain, scaled) if flip < dp // 2 else (plain,)
+        total, *rest = local_kernel(next_sum_kernel, outs, "sum_x", mine, other)
+        coded = rest[0] if rest else None
     return total, exchange(total, dp, fsdp, 0, 1, 0)
 
 
 def shards(facies, prior_draws, recon_grad, w_embed, w_conv, w_head):
     dp, fsdp = lax.axis_size("dp"), lax.axis_size("fsdp")
-    block, *saved = forward(facies, prior_draws, recon_grad, w_embed, w_conv, w_head)
+    block, one_hot, pre_embed, hidden, pre_conv, w_conv, w_head = forward(
+        facies, prior_draws, recon_grad, w_embed, w_conv, w_head
+    )
     gathered = gather_blocks(block, dp * fsdp)
-    keep, send, grad_head = backward((dp, fsdp), gathered, saved)
-    own, other = reduce_to_owner(keep, send, dp, fsdp)
+    slope_embed, slope_conv = slopes(pre_embed, pre_conv)
+    keep, send, grads, grad_head = backward((dp, fsdp), gathered, hidden, slope_conv, w_head)
+    received = exchange(send, dp, fsdp, 0, 1, 0)
+    embed = embed_gradient(fsdp, grads, w_conv, slope_embed, one_hot)
+    own, other = reduce_to_owner(keep, received, embed, dp, fsdp)
     grad_embed, grad_conv = pl.pallas_call(
         output_kernel,
         out_shape=(

time: 45.9 us -> 59.3 us (1.29)
  local copies, waits for them, and re-layouts: 0.05 us -> 16.7 us
  blocking collectives: 14.8 us -> 0 us
  starting transfers between devices: 5.83 us -> 13.9 us
  Pallas kernels: 12.2 us -> 15.9 us
  waiting for transfers between devices: 11.8 us -> 11.2 us
    unnamed x0 -> x20, local copies, waits for them, and re-layouts: none -> 16 us
    all_to_all x1 -> x0, blocking collectives: 14.8 us -> none  [gather_blocks(): return lax.all_to_all(copies, GROUP, 0, 0, tiled=True)]
    all_to_all x0 -> x1, starting transfers between devices: none -> 7.37 us  [gather_blocks(): return lax.all_to_all(copies, GROUP, 0, 0, tiled=True)]
    pallas_call x0 -> x2, Pallas kernels: none -> 6.5 us  [the longest x1 3.31 us: slopes(): pl.pallas_call(slope_kernel, out_shape=(pltpu.VMEM(pre_embed.shape, F32),...]
    pallas_call x1, Pallas kernels: 4.26 us -> 2.26 us  [backward(): pl.pallas_call(lambda *refs: backward_kernel(sizes, *refs), out_shape=(pa...]
    pallas_call x3, Pallas kernels: 1.15 us -> 0.39 us  [local_kernel(): pl.pallas_call(kernel, out_shape=outs, in_specs=[VMEM] * len(operands), o...]
    ppermute x6, waiting for transfers between devices: 11.8 us -> 11.1 us  [exchange(): return lax.ppermute(block, GROUP, pairs)]
    broadcast_in_dim x1, local copies, waits for them, and re-layouts: 0.05 us -> 0.71 us  [gather_blocks(): copies = jnp.broadcast_to(block[None], (devices,) + block.shape)]
  transfers between devices with their start and end apart: 6 -> 7, of which waited for: 5 -> 5; matrix products, arithmetic and copies ran while one was open for 0% -> 0% of each run, Pallas kernels for 0% -> 11%
where the time goes in v5:
time: 59.3 us; the launch traced here: 58.9 us
  local copies, waits for them, and re-layouts  16.7 us (28%)
  Pallas kernels  15.9 us (27%)
  starting transfers between devices  13.9 us (23%)
  waiting for transfers between devices  11.2 us (19%)
  between operations  0.79 us (1%)
    unnamed x20, local copies, waits for them, and re-layouts  16 us
    ppermute x6, waiting for transfers between devices, exchange(): return lax.ppermute(block, GROUP, pairs)  11.1 us
    all_to_all x1, starting transfers between devices, gather_blocks(): return lax.all_to_all(copies, GROUP, 0, 0, tiled=True)  7.37 us
    ppermute x6, starting transfers between devices, exchange(): return lax.ppermute(block, GROUP, pairs)  6.49 us
    pallas_call x1, Pallas kernels, forward(): pl.pallas_call(forward_kernel, out_shape=(pltpu.VMEM((samples, 2 * latent...  6.04 us
    pallas_call x1, Pallas kernels, slopes(): pl.pallas_call(slope_kernel, out_shape=(pltpu.VMEM(pre_embed.shape, F32),...  3.31 us
    pallas_call x1, Pallas kernels, embed_gradient(): pl.pallas_call(embed_kernel, out_shape=pltpu.VMEM((fsdp, 256 // fsdp // 2...  3.19 us
    pallas_call x1, Pallas kernels, backward(): pl.pallas_call(lambda *refs: backward_kernel(sizes, *refs), out_shape=(pa...  2.26 us
  transfers between devices with their start and end apart: 7, of which 5 were waited for; matrix products, arithmetic and copies ran while one was open for 0% of the time, Pallas kernels for 11%

profile of v5, /device:TPU:0, one launch (start us, length us, event | category | flops | bytes accessed | tf_op | source)
XLA Modules:
  0.0 58.9 jit_solution(17492163773324634171)
XLA Ops:
  0.6 6.0 %forward.1 = (bf16[4,1280]{1,0:T(4,128)(2,1)S(1)}, bf16[4,4,512,256]{3,2,1,0:T(8,128)(2,1)S(1)}, f32[4,4,256,256]{3,2,1,0:T(8,128)S(1)}, bf16[4,4,256,256]{3,2,1...) custom-call(s32[256,2048]{1,0:T(8,128)} %bitcast.1, ...), custom_call_target="tpu_custom_call" | custom-call | tf_op jit(solution)/shard_map/forward/pallas_call | solution.py:297
  6.7 0.0 copy-start
  6.7 2.0 %copy-done = f32[4,4,256,256]{3,2,1,0:T(8,128)} copy-done((f32[4,4,256,256]{3,2,1,0:T(8,128)}, f32[4,4,256,256]{3,2,1,0:T(8,128)S(1)}, u32[]{:S(2)}) %copy-start) | copy-done | bytes 4194328
  8.7 0.0 copy-start.4
  8.7 1.9 %copy-done.4 = bf16[4,4,512,256]{3,2,1,0:T(8,128)(2,1)} copy-done((bf16[4,4,512,256]{3,2,1,0:T(8,128)(2,1)}, bf16[4,4,512,256]{3,2,1,0:T(8,128)(2,1)S(1)}, u32[]{:S(2)}) %copy-start.4) | copy-done | bytes 4194328
  10.6 0.0 copy-start.6
  10.6 0.8 %copy-done.6 = bf16[1024,256]{1,0:T(8,128)(2,1)} copy-done((bf16[1024,256]{1,0:T(8,128)(2,1)}, bf16[1024,256]{1,0:T(8,128)(2,1)S(1)}, u32[]{:S(2)}) %copy-start.6) | copy-done | bytes 524312
  11.5 0.0 copy-start.8
  11.5 0.7 %copy-done.8 = bf16[256,512]{1,0:T(8,128)(2,1)} copy-done((bf16[256,512]{1,0:T(8,128)(2,1)}, bf16[256,512]{1,0:T(8,128)(2,1)S(1)}, u32[]{:S(2)}) %copy-start.8) | copy-done | bytes 262168
  12.2 0.7 %broadcast_in_dim.2 = bf16[16,4,1280]{2,1,0:T(4,128)(2,1)} broadcast(bf16[4,1280]{1,0:T(4,128)(2,1)S(1)} %get-tuple-element.22), dimensions={1,2} | broadcast | bytes 174080 | tf_op jit(solution)/shard_map/broadcast_in_dim | solution.py:374
  12.9 7.4 %all-to-all-start = ((bf16[16,4,1280]{2,1,0:T(4,128)(2,1)}), bf16[16,4,1280]{2,1,0:T(4,128)(2,1)S(1)}, u32[]{:S(2)}, u32[]{:S(2)}) async-start(bf16[16,4,1280]{2,1,0:T(4,128)(2,1)} %broadcast_in_dim.2), calls=%async_computation | async-start | bytes 327680 | tf_op jit(solution)/shard_map/all_to_all | solution.py:375
  20.3 0.0 copy-start.1
  20.3 2.2 %copy-done.1 = f32[4,4,256,256]{3,2,1,0:T(8,128)S(1)} copy-done((f32[4,4,256,256]{3,2,1,0:T(8,128)S(1)}, f32[4,4,256,256]{3,2,1,0:T(8,128)}, u32[]{:S(2)}) %copy-start.1) | copy-done | bytes 4194328
  22.4 3.3 %slopes.1 = (f32[4,4,256,256]{3,2,1,0:T(8,128)S(1)}, f32[4,256,256]{2,1,0:T(8,128)S(1)}) custom-call(f32[4,4,256,256]{3,2,1,0:T(8,128)S(1)} %copy-done.1, f32[4,256,256]{2,1,0:T(8,128)S(1)} %get-tuple-element.25.pre_conv), custom_call_target="tpu_custom_call", output_to_operand_aliasing={{0}: (0, {}), {1}: (1, {})} | custom-call | flops 12000000 | bytes 10485760 | tf_op jit(solution)/shard_map/slopes/pallas_call | solution.py:319
  25.8 0.0 copy-start.2
  25.8 2.0 %copy-done.2 = f32[4,4,256,256]{3,2,1,0:T(8,128)} copy-done((f32[4,4,256,256]{3,2,1,0:T(8,128)}, f32[4,4,256,256]{3,2,1,0:T(8,128)S(1)}, u32[]{:S(2)}) %copy-start.2) | copy-done | bytes 4194328
  27.8 0.1 all-to-all-done.refs_0_
  27.9 0.0 copy-start.9
  27.9 0.9 %copy-done.9 = bf16[256,512]{1,0:T(8,128)(2,1)S(1)} copy-done((bf16[256,512]{1,0:T(8,128)(2,1)S(1)}, bf16[256,512]{1,0:T(8,128)(2,1)}, u32[]{:S(2)}) %copy-start.9) | copy-done | bytes 262168
  28.8 2.3 %backward.1 = (f32[4,128,256]{2,1,0:T(8,128)S(1)}, f32[4,128,256]{2,1,0:T(8,128)S(1)}, bf16[4,256,256]{2,1,0:T(8,128)(2,1)S(1)}, f32[64,512]{1,0:T(8,128)}) custom-call(bf16[16,4,1280]{2,1,0:T(4,128)(2,1)S(1)} %all-to-all-done.refs_0_, bf16[4,4,256,256]{3,2,1,0:T(8,128)(2,1)S(1)} %get-tuple-element.23.refs_1_, f32[4,256,256]{2,1,0:T(8,128)S(1)} %get-tuple-element.26.refs_2_, ...), custom_call_target="tpu_custom_call" | custom-call | tf_op jit(solution)/shard_map/backward/pallas_call | solution.py:335
  31.1 0.3 collective-permute-start
  31.4 0.0 copy-start.3
  31.4 2.2 %copy-done.3 = f32[4,4,256,256]{3,2,1,0:T(8,128)S(1)} copy-done((f32[4,4,256,256]{3,2,1,0:T(8,128)S(1)}, f32[4,4,256,256]{3,2,1,0:T(8,128)}, u32[]{:S(2)}) %copy-start.3) | copy-done | bytes 4194328
  33.6 0.0 copy-start.5
  33.6 2.2 %copy-done.5 = bf16[4,4,512,256]{3,2,1,0:T(8,128)(2,1)S(1)} copy-done((bf16[4,4,512,256]{3,2,1,0:T(8,128)(2,1)S(1)}, bf16[4,4,512,256]{3,2,1,0:T(8,128)(2,1)}, u32[]{:S(2)}) %copy-start.5) | copy-done | bytes 4194328
  35.8 0.0 copy-start.7
  35.8 1.0 %copy-done.7 = bf16[1024,256]{1,0:T(8,128)(2,1)S(1)} copy-done((bf16[1024,256]{1,0:T(8,128)(2,1)S(1)}, bf16[1024,256]{1,0:T(8,128)(2,1)}, u32[]{:S(2)}) %copy-start.7) | copy-done | bytes 524312
  36.8 3.2 %embed_gradient.1.embed = f32[4,32,256]{2,1,0:T(8,128)S(1)} custom-call(bf16[4,256,256]{2,1,0:T(8,128)(2,1)S(1)} %get-tuple-element.30.grads, bf16[1024,256]{1,0:T(8,128)(2,1)S(1)} %copy-done.7, f32[4,4,256,256]{3,2,1,0:T(8,128)S(1)} %copy-done.3, bf16[4,4,512,256]{3,2,1,0:T(8,128)(2,1)S(1)} %copy-done.5), custom_call_target="tpu_custom_call" | custom-call | flops 1600000000 | bytes 10485760 | tf_op jit(solution)/shard_map/embed_gradient/pallas_call | solution.py:349
  40.0 0.0 collective-permute-done.other
  40.0 0.2 scale.1
  40.2 0.1 reduce-precision_convert_fusion.2
  40.3 3.6 %collective-permute-start.1 = (f16[168,256]{1,0:T(8,128)(2,1)S(1)}, f16[168,256]{1,0:T(8,128)(2,1)S(1)}, u32[]{:S(2)}, u32[]{:S(2)}) collective-permute-start(f16[168,256]{1,0:T(8,128)(2,1)S(1)} %reduce-precision_convert_fusion.2), channel_id=1, source_target_pairs={{0,3},{1,2},{2,1},{3,0},{4,7},{5,6},{6,5},{7,4},{8,11},{9,10},{10,... | collective-permute-start | bytes 258056 | tf_op jit(solution)/shard_map/ppermute | solution.py:370
  43.9 0.1 reduce-precision_convert_fusion.1
  44.0 0.1 collective-permute-start.2
  44.0 0.1 reduce-precision_convert_fusion
  44.1 0.9 %collective-permute-start.3 = (f16[168,256]{1,0:T(8,128)(2,1)S(1)}, f16[168,256]{1,0:T(8,128)(2,1)S(1)}, u32[]{:S(2)}, u32[]{:S(2)}) collective-permute-start(f16[168,256]{1,0:T(8,128)(2,1)S(1)} %reduce-precision_convert_fusion), channel_id=1, source_target_pairs={{0,1},{1,0},{2,3},{3,2},{4,5},{5,4},{6,7},{7,6},{8,9},{9,8},{10,11... | collective-permute-start | bytes 258056 | tf_op jit(solution)/shard_map/ppermute | solution.py:370
  45.1 2.2 %collective-permute-done.1 = f16[168,256]{1,0:T(8,128)(2,1)S(1)} collective-permute-done((f16[168,256]{1,0:T(8,128)(2,1)S(1)}, f16[168,256]{1,0:T(8,128)(2,1)S(1)}, u32[]{:S(2)}, u32[]{:S(2)}) %collective-permute-start.1) | collective-permute-done | bytes 86048 | tf_op jit(solution)/shard_map/ppermute | solution.py:370
  47.3 4.5 %collective-permute-done.2 = f16[168,256]{1,0:T(8,128)(2,1)S(1)} collective-permute-done((f16[168,256]{1,0:T(8,128)(2,1)S(1)}, f16[168,256]{1,0:T(8,128)(2,1)S(1)}, u32[]{:S(2)}, u32[]{:S(2)}) %collective-permute-start.2) | collective-permute-done | bytes 86048 | tf_op jit(solution)/shard_map/ppermute | solution.py:370
  51.8 0.0 collective-permute-done.3
  51.9 0.2 sum_z.1
  52.0 0.1 reduce-precision_convert_fusion.3
  52.1 1.5 %collective-permute-start.4 = (f16[168,256]{1,0:T(8,128)(2,1)S(1)}, f16[168,256]{1,0:T(8,128)(2,1)S(1)}, u32[]{:S(2)}, u32[]{:S(2)}) collective-permute-start(f16[168,256]{1,0:T(8,128)(2,1)S(1)} %get-tuple-element.41), channel_id=1, source_target_pairs={{0,8},{1,9},{2,10},{3,11},{4,12},{5,13},{6,14},{7,15},{8,0},{9,1},... | collective-permute-start | bytes 258056 | tf_op jit(solution)/shard_map/ppermute | solution.py:370
  53.7 3.0 %collective-permute-done.4 = f16[168,256]{1,0:T(8,128)(2,1)S(1)} collective-permute-done((f16[168,256]{1,0:T(8,128)(2,1)S(1)}, f16[168,256]{1,0:T(8,128)(2,1)S(1)}, u32[]{:S(2)}, u32[]{:S(2)}) %collective-permute-start.4) | collective-permute-done | bytes 86048 | tf_op jit(solution)/shard_map/ppermute | solution.py:370
  56.7 0.1 collective-permute-start.5
  56.8 1.4 %collective-permute-done.5.other = f32[160,256]{1,0:T(8,128)S(1)} collective-permute-done((f32[160,256]{1,0:T(8,128)S(1)}, f32[160,256]{1,0:T(8,128)S(1)}, u32[]{:S(2)}, u32[]{:S(2)}) %collective-permute-start.5) | collective-permute-done | bytes 163872 | tf_op jit(solution)/shard_map/ppermute | solution.py:370
  58.2 0.7 %outputs.1 = (f32[64,128]{1,0:T(8,128)}, f32[256,256]{1,0:T(8,128)}) custom-call(f32[160,256]{1,0:T(8,128)S(1)} %sum_x.1.own, f32[160,256]{1,0:T(8,128)S(1)} %collective-permute-done.5.other), custom_call_target="tpu_custom_call" | custom-call | tf_op jit(solution)/shard_map/outputs/pallas_call | solution.py:425
  (5 shorter events, 0.1 us)
Async XLA Ops:
  6.7 2.0 %copy-start = (f32[4,4,256,256]{3,2,1,0:T(8,128)}, f32[4,4,256,256]{3,2,1,0:T(8,128)S(1)}, u32[]{:S(2)}) copy-start(f32[4,4,256,256]{3,2,1,0:T(8,128)S(1)} %get-tuple-element.24.pre_embed) | copy-start | bytes 12582916
  8.7 1.9 %copy-start.4 = (bf16[4,4,512,256]{3,2,1,0:T(8,128)(2,1)}, bf16[4,4,512,256]{3,2,1,0:T(8,128)(2,1)S(1)}, u32[]{:S(2)}) copy-start(bf16[4,4,512,256]{3,2,1,0:T(8,128)(2,1)S(1)} %get-tuple-element.33.one_hot) | copy-start | bytes 12582916
  10.6 0.9 %copy-start.6 = (bf16[1024,256]{1,0:T(8,128)(2,1)}, bf16[1024,256]{1,0:T(8,128)(2,1)S(1)}, u32[]{:S(2)}) copy-start(bf16[1024,256]{1,0:T(8,128)(2,1)S(1)} %get-tuple-element.31.w_conv) | copy-start | bytes 1572868
  11.5 0.7 %copy-start.8 = (bf16[256,512]{1,0:T(8,128)(2,1)}, bf16[256,512]{1,0:T(8,128)(2,1)S(1)}, u32[]{:S(2)}) copy-start(bf16[256,512]{1,0:T(8,128)(2,1)S(1)} %get-tuple-element.27.refs_3_) | copy-start | bytes 786436
  12.9 15.0 %all-to-all-start = ((bf16[16,4,1280]{2,1,0:T(4,128)(2,1)}), bf16[16,4,1280]{2,1,0:T(4,128)(2,1)S(1)}, u32[]{:S(2)}, u32[]{:S(2)}) async-start(bf16[16,4,1280]{2,1,0:T(4,128)(2,1)} %broadcast_in_dim.2), calls=%async_computation | async-start | bytes 327680 | tf_op jit(solution)/shard_map/all_to_all | solution.py:375
  20.3 2.2 %copy-start.1 = (f32[4,4,256,256]{3,2,1,0:T(8,128)S(1)}, f32[4,4,256,256]{3,2,1,0:T(8,128)}, u32[]{:S(2)}) copy-start(f32[4,4,256,256]{3,2,1,0:T(8,128)} %copy-done) | copy-start | bytes 12582916
  25.8 2.0 %copy-start.2 = (f32[4,4,256,256]{3,2,1,0:T(8,128)}, f32[4,4,256,256]{3,2,1,0:T(8,128)S(1)}, u32[]{:S(2)}) copy-start(f32[4,4,256,256]{3,2,1,0:T(8,128)S(1)} %get-tuple-element.32.slope_embed) | copy-start | bytes 12582916
  27.9 1.0 %copy-start.9 = (bf16[256,512]{1,0:T(8,128)(2,1)S(1)}, bf16[256,512]{1,0:T(8,128)(2,1)}, u32[]{:S(2)}) copy-start(bf16[256,512]{1,0:T(8,128)(2,1)} %copy-done.8) | copy-start | bytes 786436
  31.1 8.9 %collective-permute-start = (f32[4,128,256]{2,1,0:T(8,128)S(1)}, f32[4,128,256]{2,1,0:T(8,128)S(1)}, u32[]{:S(2)}, u32[]{:S(2)}) collective-permute-start(f32[4,128,256]{2,1,0:T(8,128)S(1)} %get-tuple-element.29), channel_id=1, source_target_pairs={{0,4},{1,5},{2,6},{3,7},{4,0},{5,1},{6,2},{7,3},{8,12},{9,13},{10,... | collective-permute-start | bytes 1572872 | tf_op jit(solution)/shard_map/ppermute | solution.py:370
  31.4 2.2 %copy-start.3 = (f32[4,4,256,256]{3,2,1,0:T(8,128)S(1)}, f32[4,4,256,256]{3,2,1,0:T(8,128)}, u32[]{:S(2)}) copy-start(f32[4,4,256,256]{3,2,1,0:T(8,128)} %copy-done.2) | copy-start | bytes 12582916
  33.6 2.2 %copy-start.5 = (bf16[4,4,512,256]{3,2,1,0:T(8,128)(2,1)S(1)}, bf16[4,4,512,256]{3,2,1,0:T(8,128)(2,1)}, u32[]{:S(2)}) copy-start(bf16[4,4,512,256]{3,2,1,0:T(8,128)(2,1)} %copy-done.4) | copy-start | bytes 12582916
  35.8 1.0 %copy-start.7 = (bf16[1024,256]{1,0:T(8,128)(2,1)S(1)}, bf16[1024,256]{1,0:T(8,128)(2,1)}, u32[]{:S(2)}) copy-start(bf16[1024,256]{1,0:T(8,128)(2,1)} %copy-done.6) | copy-start | bytes 1572868
  40.3 7.0 %collective-permute-start.1 = (f16[168,256]{1,0:T(8,128)(2,1)S(1)}, f16[168,256]{1,0:T(8,128)(2,1)S(1)}, u32[]{:S(2)}, u32[]{:S(2)}) collective-permute-start(f16[168,256]{1,0:T(8,128)(2,1)S(1)} %reduce-precision_convert_fusion.2), channel_id=1, source_target_pairs={{0,3},{1,2},{2,1},{3,0},{4,7},{5,6},{6,5},{7,4},{8,11},{9,10},{10,... | collective-permute-start | bytes 258056 | tf_op jit(solution)/shard_map/ppermute | solution.py:370
  44.0 7.9 %collective-permute-start.2 = (f16[168,256]{1,0:T(8,128)(2,1)S(1)}, f16[168,256]{1,0:T(8,128)(2,1)S(1)}, u32[]{:S(2)}, u32[]{:S(2)}) collective-permute-start(f16[168,256]{1,0:T(8,128)(2,1)S(1)} %reduce-precision_convert_fusion.1), channel_id=1, source_target_pairs={{0,2},{1,3},{2,0},{3,1},{4,6},{5,7},{6,4},{7,5},{8,10},{9,11},{10,... | collective-permute-start | bytes 258056 | tf_op jit(solution)/shard_map/ppermute | solution.py:370
  44.1 7.7 %collective-permute-start.3 = (f16[168,256]{1,0:T(8,128)(2,1)S(1)}, f16[168,256]{1,0:T(8,128)(2,1)S(1)}, u32[]{:S(2)}, u32[]{:S(2)}) collective-permute-start(f16[168,256]{1,0:T(8,128)(2,1)S(1)} %reduce-precision_convert_fusion), channel_id=1, source_target_pairs={{0,1},{1,0},{2,3},{3,2},{4,5},{5,4},{6,7},{7,6},{8,9},{9,8},{10,11... | collective-permute-start | bytes 258056 | tf_op jit(solution)/shard_map/ppermute | solution.py:370
  52.1 4.6 %collective-permute-start.4 = (f16[168,256]{1,0:T(8,128)(2,1)S(1)}, f16[168,256]{1,0:T(8,128)(2,1)S(1)}, u32[]{:S(2)}, u32[]{:S(2)}) collective-permute-start(f16[168,256]{1,0:T(8,128)(2,1)S(1)} %get-tuple-element.41), channel_id=1, source_target_pairs={{0,8},{1,9},{2,10},{3,11},{4,12},{5,13},{6,14},{7,15},{8,0},{9,1},... | collective-permute-start | bytes 258056 | tf_op jit(solution)/shard_map/ppermute | solution.py:370
  56.7 1.5 %collective-permute-start.5 = (f32[160,256]{1,0:T(8,128)S(1)}, f32[160,256]{1,0:T(8,128)S(1)}, u32[]{:S(2)}, u32[]{:S(2)}) collective-permute-start(f32[160,256]{1,0:T(8,128)S(1)} %sum_x.1.own), channel_id=1, source_target_pairs={{0,4},{1,5},{2,6},{3,7},{4,0},{5,1},{6,2},{7,3},{8,12},{9,13},{10,... | collective-permute-start | bytes 491528 | tf_op jit(solution)/shard_map/ppermute | solution.py:370

commit v6 on v5

--- a/solution.py
+++ b/solution.py
@@ -126,7 +126,7 @@
 
 
 def backward_kernel(
-    sizes, gathered, hidden, slope_conv, w_head,
+    sizes, gathered, hidden, pre_conv, w_head,
     keep, send, grads, grad_head,
     ordered, head_full
 ):
@@ -134,8 +134,10 @@
     devices = dp * fsdp
     dp_here, fsdp_here = lax.axis_index("dp"), lax.axis_index("fsdp")
     here = dp_here * fsdp + fsdp_here
-    for owner in range(devices):
-        ordered[owner] = gathered[owner].astype(F32)
+    for place in range(devices):
+        core_flip, x_flip, z_flip = place // (devices // 2), place // fsdp % (dp // 2), place % fsdp
+        owner = (dp_here ^ (2 * x_flip + core_flip)) * fsdp + (fsdp_here ^ z_flip)
+        ordered[owner] = gathered[place].astype(F32)
     samples = ordered.shape[1]
     count = devices * samples
     full = ordered[...].reshape(count, ordered.shape[2])
@@ -162,7 +164,7 @@
     back_pool = jnp.concatenate([back_pool, back_pool], axis=1)
     conv_total = None
     for cp in range(4):
-        grads[cp] = (back_pool * slope_conv[cp]).astype(BF16)
+        grads[cp] = (back_pool * silu_slope(pre_conv[cp])).astype(BF16)
         term = mm_nt(hidden[cp].reshape(1024, 256), grads[cp])
         conv_total = term if cp == 0 else conv_total + term
     core_zero = lax.rem(dp_here, 2) == 0
@@ -174,12 +176,12 @@
         send[f] = jnp.where(core_zero, second, first)
 
 
-def embed_kernel(grads, w_conv, slope_embed, one_hot, embed_out):
+def embed_kernel(grads, w_conv, pre_embed, one_hot, embed_out):
     embed_total = None
     for cp in range(4):
         for j in range(4):
             back_rows = mm(w_conv[pl.ds(j * 256, 256), :], grads[cp])
-            signal = (back_rows * slope_embed[cp, j]).astype(BF16)
+            signal = (back_rows * silu_slope(pre_embed[cp, j])).astype(BF16)
             term = mm_nt(one_hot[cp, j], signal)
             embed_total = term if embed_total is None else embed_total + term
     embed = jnp.concatenate(
@@ -196,13 +198,6 @@
             embed_out[f, :, pl.ds(side * 128, 128)] = embed[at : at + half]
 
 
-def slope_kernel(pre_embed, pre_conv, slope_embed, slope_conv):
-    for cp in range(4):
-        for j in range(4):
-            slope_embed[cp, j] = silu_slope(pre_embed[cp, j])
-        slope_conv[cp] = silu_slope(pre_conv[cp])
-
-
 def exponent_of(part):
     top = jnp.abs(part)
     while top.ndim > 2:
@@ -247,7 +242,7 @@
 
     own[...] = share(here)
     for place, target in enumerate(coded):
-        store_scaled(target, share(here ^ (len(coded) - place)), steps)
+        store_scaled(target, share(here ^ (place + 1)), steps)
 
 
 def first_sum_kernel(own, *refs):
@@ -315,20 +310,7 @@
     )(*(pltpu.with_memory_space_constraint(operand, pltpu.HBM) for operand in operands))
 
 
-def slopes(pre_embed, pre_conv):
-    return pl.pallas_call(
-        slope_kernel,
-        out_shape=(pltpu.VMEM(pre_embed.shape, F32), pltpu.VMEM(pre_conv.shape, F32)),
-        in_specs=[VMEM] * 2,
-        out_specs=(VMEM,) * 2,
-        input_output_aliases={0: 0, 1: 1},
-        compiler_params=pltpu.CompilerParams(vmem_limit_bytes=16 * 2**20),
-        cost_estimate=pl.CostEstimate(flops=12 * 10**6, bytes_accessed=10 * 2**20, transcendentals=2600000),
-        name="slopes",
-    )(pre_embed, pre_conv)
-
-
-def backward(sizes, gathered, hidden, slope_conv, w_head):
+def backward(sizes, gathered, hidden, pre_conv, w_head):
     dp, fsdp = sizes
     devices, samples, width = gathered.shape
     payload = pltpu.VMEM((fsdp, 1024 // fsdp // 2, 256), F32)
@@ -342,10 +324,10 @@
         scratch_shapes=[pltpu.VMEM((devices, samples, width), F32), pltpu.VMEM((256, 512), F32)],
         compiler_params=pltpu.CompilerParams(vmem_limit_bytes=24 * 2**20),
         name="backward",
-    )(gathered, hidden, slope_conv, w_head)
-
-
-def embed_gradient(fsdp, grads, w_conv, slope_embed, one_hot):
+    )(gathered, hidden, pre_conv, w_head)
+
+
+def embed_gradient(fsdp, grads, w_conv, pre_embed, one_hot):
     return pl.pallas_call(
         embed_kernel,
         out_shape=pltpu.VMEM((fsdp, 256 // fsdp // 2, 256), F32),
@@ -354,7 +336,7 @@
         compiler_params=pltpu.CompilerParams(vmem_limit_bytes=24 * 2**20),
         cost_estimate=pl.CostEstimate(flops=16 * 10**8, bytes_accessed=10 * 2**20, transcendentals=0),
         name="embed_gradient",
-    )(grads, w_conv, slope_embed, one_hot)
+    )(grads, w_conv, pre_embed, one_hot)
 
 
 def place_of(x, core, z, fsdp):
@@ -370,9 +352,14 @@
     return lax.ppermute(block, GROUP, pairs)
 
 
-def gather_blocks(block, devices):
-    copies = jnp.broadcast_to(block[None], (devices,) + block.shape)
-    return lax.all_to_all(copies, GROUP, 0, 0, tiled=True)
+def gather_blocks(block, dp, fsdp):
+    blocks = [block] + [exchange(block, dp, fsdp, 0, 0, flip) for flip in range(1, fsdp)]
+    stacked = jnp.stack(blocks)
+    flip = 1
+    while flip < dp // 2:
+        stacked = jnp.concatenate([stacked, exchange(stacked, dp, fsdp, flip, 0, 0)], axis=0)
+        flip *= 2
+    return jnp.concatenate([stacked, exchange(stacked, dp, fsdp, 0, 1, 0)], axis=0)
 
 
 def local_kernel(kernel, outs, name, *operands):
@@ -397,7 +384,7 @@
     scaled = jax.ShapeDtypeStruct((rows + 8, width), F32)
     own, *coded = local_kernel(scale_kernel, (plain,) + (scaled,) * (fsdp - 1), "scale", keep, other, embed)
     received = [
-        exchange(to_half(part)[1], dp, fsdp, 0, 0, fsdp - 1 - place).astype(F32) for place, part in enumerate(coded)
+        exchange(to_half(part)[1], dp, fsdp, 0, 0, place + 1).astype(F32) for place, part in enumerate(coded)
     ]
     (coded,) = local_kernel(first_sum_kernel, (scaled,), "sum_z", own, *received)
     flip = 1
@@ -416,11 +403,10 @@
     block, one_hot, pre_embed, hidden, pre_conv, w_conv, w_head = forward(
         facies, prior_draws, recon_grad, w_embed, w_conv, w_head
     )
-    gathered = gather_blocks(block, dp * fsdp)
-    slope_embed, slope_conv = slopes(pre_embed, pre_conv)
-    keep, send, grads, grad_head = backward((dp, fsdp), gathered, hidden, slope_conv, w_head)
+    gathered = gather_blocks(block, dp, fsdp)
+    keep, send, grads, grad_head = backward((dp, fsdp), gathered, hidden, pre_conv, w_head)
     received = exchange(send, dp, fsdp, 0, 1, 0)
-    embed = embed_gradient(fsdp, grads, w_conv, slope_embed, one_hot)
+    embed = embed_gradient(fsdp, grads, w_conv, pre_embed, one_hot)
     own, other = reduce_to_owner(keep, received, embed, dp, fsdp)
     grad_embed, grad_conv = pl.pallas_call(
         output_kernel,

time: 59.3 us -> 45.7 us (0.77)
  local copies, waits for them, and re-layouts: 16.7 us -> 0.13 us
  waiting for transfers between devices: 11.2 us -> 18.1 us
  Pallas kernels: 15.9 us -> 12.4 us
    unnamed x20 -> x4, local copies, waits for them, and re-layouts: 16 us -> 0.06 us
    all_to_all x1 -> x0, starting transfers between devices: 7.37 us -> none  [gather_blocks(): return lax.all_to_all(copies, GROUP, 0, 0, tiled=True)]
    ppermute x6 -> x11, starting transfers between devices: 6.49 us -> 13.7 us  [exchange(): return lax.ppermute(block, GROUP, pairs)]
    ppermute x6 -> x11, waiting for transfers between devices: 11.1 us -> 18.1 us  [exchange(): return lax.ppermute(block, GROUP, pairs)]
    pallas_call x1 -> x0, Pallas kernels: 3.31 us -> none  [slopes(): pl.pallas_call(slope_kernel, out_shape=(pltpu.VMEM(pre_embed.shape, F32),...]
    broadcast_in_dim x1 -> x0, local copies, waits for them, and re-layouts: 0.71 us -> none  [gather_blocks(): copies = jnp.broadcast_to(block[None], (devices,) + block.shape)]
  transfers between devices with their start and end apart: 7 -> 11, of which waited for: 5 -> 8; matrix products, arithmetic and copies ran while one was open for 0% -> 0% of each run, Pallas kernels for 11% -> 7%
where the time goes in v6:
time: 45.7 us; the launch traced here: 45.5 us
  waiting for transfers between devices  18.1 us (40%)
  starting transfers between devices  13.7 us (30%)
  Pallas kernels  12.4 us (27%)
  between operations  0.77 us (2%)
  other arithmetic  0.46 us (1%)
    ppermute x11, waiting for transfers between devices, exchange(): return lax.ppermute(block, GROUP, pairs)  18.1 us
    ppermute x11, starting transfers between devices, exchange(): return lax.ppermute(block, GROUP, pairs)  13.7 us
    pallas_call x1, Pallas kernels, forward(): pl.pallas_call(forward_kernel, out_shape=(pltpu.VMEM((samples, 2 * latent...  6.03 us
    pallas_call x1, Pallas kernels, embed_gradient(): pl.pallas_call(embed_kernel, out_shape=pltpu.VMEM((fsdp, 256 // fsdp // 2...  3.24 us
    pallas_call x1, Pallas kernels, backward(): pl.pallas_call(lambda *refs: backward_kernel(sizes, *refs), out_shape=(pa...  1.99 us
  transfers between devices with their start and end apart: 11, of which 8 were waited for; matrix products, arithmetic and copies ran while one was open for 0% of the time, Pallas kernels for 7%

profile of v6, /device:TPU:0, one launch (start us, length us, event | category | flops | bytes accessed | tf_op | source)
XLA Modules:
  0.0 45.5 jit_solution(1324191637306532235)
XLA Ops:
  0.6 6.0 %forward.1 = (bf16[4,1280]{1,0:T(4,128)(2,1)S(1)}, bf16[4,4,512,256]{3,2,1,0:T(8,128)(2,1)S(1)}, f32[4,4,256,256]{3,2,1,0:T(8,128)S(1)}, bf16[4,4,256,256]{3,2,1...) custom-call(s32[256,2048]{1,0:T(8,128)} %bitcast.14, ...), custom_call_target="tpu_custom_call" | custom-call | tf_op jit(solution)/shard_map/forward/pallas_call | solution.py:292
  6.7 5.1 %collective-permute-start.2 = (bf16[4,1280]{1,0:T(4,128)(2,1)S(1)}, bf16[4,1280]{1,0:T(4,128)(2,1)S(1)}, u32[]{:S(2)}, u32[]{:S(2)}) collective-permute-start(bf16[4,1280]{1,0:T(4,128)(2,1)S(1)} %get-tuple-element.20), channel_id=1, source_target_pairs={{0,3},{1,2},{2,1},{3,0},{4,7},{5,6},{6,5},{7,4},{8,11},{9,10},{10,... | collective-permute-start | bytes 30728 | tf_op jit(solution)/shard_map/ppermute | solution.py:352
  11.8 0.0 collective-permute-start.1
  11.8 0.6 %collective-permute-start = (bf16[4,1280]{1,0:T(4,128)(2,1)S(1)}, bf16[4,1280]{1,0:T(4,128)(2,1)S(1)}, u32[]{:S(2)}, u32[]{:S(2)}) collective-permute-start(bf16[4,1280]{1,0:T(4,128)(2,1)S(1)} %get-tuple-element.20), channel_id=1, source_target_pairs={{0,1},{1,0},{2,3},{3,2},{4,5},{5,4},{6,7},{7,6},{8,9},{9,8},{10,11... | collective-permute-start | bytes 30728 | tf_op jit(solution)/shard_map/ppermute | solution.py:352
  12.4 1.0 %collective-permute-done.2 = bf16[4,1280]{1,0:T(4,128)(2,1)S(1)} collective-permute-done((bf16[4,1280]{1,0:T(4,128)(2,1)S(1)}, bf16[4,1280]{1,0:T(4,128)(2,1)S(1)}, u32[]{:S(2)}, u32[]{:S(2)}) %collective-permute-start.2) | collective-permute-done | bytes 10272 | tf_op jit(solution)/shard_map/ppermute | solution.py:352
  13.4 2.9 %collective-permute-done.1 = bf16[4,1280]{1,0:T(4,128)(2,1)S(1)} collective-permute-done((bf16[4,1280]{1,0:T(4,128)(2,1)S(1)}, bf16[4,1280]{1,0:T(4,128)(2,1)S(1)}, u32[]{:S(2)}, u32[]{:S(2)}) %collective-permute-start.1) | collective-permute-done | bytes 10272 | tf_op jit(solution)/shard_map/ppermute | solution.py:352
  16.4 0.0 collective-permute-done
  16.4 1.5 %collective-permute-start.3 = (bf16[4,4,1280]{2,1,0:T(4,128)(2,1)S(1)}, bf16[4,4,1280]{2,1,0:T(4,128)(2,1)S(1)}, u32[]{:S(2)}, u32[]{:S(2)}) collective-permute-start(bf16[4,4,1280]{2,1,0:T(4,128)(2,1)S(1)} %pad_maximum_fusion), channel_id=1, source_target_pairs={{0,8},{1,9},{2,10},{3,11},{4,12},{5,13},{6,14},{7,15},{8,0},{9,1},... | collective-permute-start | bytes 122888 | tf_op jit(solution)/shard_map/ppermute | solution.py:352
  18.0 2.5 %collective-permute-done.3 = bf16[4,4,1280]{2,1,0:T(4,128)(2,1)S(1)} collective-permute-done((bf16[4,4,1280]{2,1,0:T(4,128)(2,1)S(1)}, bf16[4,4,1280]{2,1,0:T(4,128)(2,1)S(1)}, u32[]{:S(2)}, u32[]{:S(2)}) %collective-permute-start.3) | collective-permute-done | bytes 40992 | tf_op jit(solution)/shard_map/ppermute | solution.py:352
  20.5 0.1 collective-permute-start.4
  20.6 1.3 %collective-permute-done.4 = bf16[8,4,1280]{2,1,0:T(4,128)(2,1)S(1)} collective-permute-done((bf16[8,4,1280]{2,1,0:T(4,128)(2,1)S(1)}, bf16[8,4,1280]{2,1,0:T(4,128)(2,1)S(1)}, u32[]{:S(2)}, u32[]{:S(2)}) %collective-permute-start.4) | collective-permute-done | bytes 81952 | tf_op jit(solution)/shard_map/ppermute | solution.py:352
  21.9 2.0 %backward.1 = (f32[4,128,256]{2,1,0:T(8,128)S(1)}, f32[4,128,256]{2,1,0:T(8,128)S(1)}, bf16[4,256,256]{2,1,0:T(8,128)(2,1)S(1)}, f32[64,512]{1,0:T(8,128)}) custom-call(bf16[16,4,1280]{2,1,0:T(4,128)(2,1)S(1)} %constant_dynamic-update-slice_fusion.5.refs_0_, bf16[4,4,256,256]{3,2,1,0:T(8,128)(2,1)S(1)} %get-tuple-element.21.refs_1_, ...), custom_call_target="tpu_custom_call" | custom-call | tf_op jit(solution)/shard_map/backward/pallas_call | solution.py:317
  23.9 0.2 collective-permute-start.5
  24.1 3.2 %embed_gradient.1.embed = f32[4,32,256]{2,1,0:T(8,128)S(1)} custom-call(bf16[4,256,256]{2,1,0:T(8,128)(2,1)S(1)} %get-tuple-element.26.grads, bf16[1024,256]{1,0:T(8,128)(2,1)S(1)} %get-tuple-element.27.w_conv, f32[4,4,256,256]{3,2,1,0:T(8,128)S(1)} %get-tuple-element.28.pre_embed, bf16[4,4,512,256]{3,2,1,0:T(8,128)(2,1)S(1)} %get-tuple-element.29.one_hot), custom_call_target="tpu_custom_call" | custom-call | flops 1600000000 | bytes 10485760 | tf_op jit(solution)/shard_map/embed_gradient/pallas_call | solution.py:331
  27.4 0.0 collective-permute-done.5.other
  27.4 0.2 scale.1
  27.6 0.1 reduce-precision_convert_fusion.1
  27.7 0.1 reduce-precision_convert_fusion
  27.8 1.5 %collective-permute-start.8 = (f16[168,256]{1,0:T(8,128)(2,1)S(1)}, f16[168,256]{1,0:T(8,128)(2,1)S(1)}, u32[]{:S(2)}, u32[]{:S(2)}) collective-permute-start(f16[168,256]{1,0:T(8,128)(2,1)S(1)} %reduce-precision_convert_fusion), channel_id=1, source_target_pairs={{0,3},{1,2},{2,1},{3,0},{4,7},{5,6},{6,5},{7,4},{8,11},{9,10},{10,... | collective-permute-start | bytes 258056 | tf_op jit(solution)/shard_map/ppermute | solution.py:352
  29.3 0.6 %collective-permute-start.7 = (f16[168,256]{1,0:T(8,128)(2,1)S(1)}, f16[168,256]{1,0:T(8,128)(2,1)S(1)}, u32[]{:S(2)}, u32[]{:S(2)}) collective-permute-start(f16[168,256]{1,0:T(8,128)(2,1)S(1)} %reduce-precision_convert_fusion.1), channel_id=1, source_target_pairs={{0,2},{1,3},{2,0},{3,1},{4,6},{5,7},{6,4},{7,5},{8,10},{9,11},{10,... | collective-permute-start | bytes 258056 | tf_op jit(solution)/shard_map/ppermute | solution.py:352
  29.9 0.1 reduce-precision_convert_fusion.2
  30.0 2.4 %collective-permute-start.6 = (f16[168,256]{1,0:T(8,128)(2,1)S(1)}, f16[168,256]{1,0:T(8,128)(2,1)S(1)}, u32[]{:S(2)}, u32[]{:S(2)}) collective-permute-start(f16[168,256]{1,0:T(8,128)(2,1)S(1)} %reduce-precision_convert_fusion.2), channel_id=1, source_target_pairs={{0,1},{1,0},{2,3},{3,2},{4,5},{5,4},{6,7},{7,6},{8,9},{9,8},{10,11... | collective-permute-start | bytes 258056 | tf_op jit(solution)/shard_map/ppermute | solution.py:352
  32.4 2.7 %collective-permute-done.8 = f16[168,256]{1,0:T(8,128)(2,1)S(1)} collective-permute-done((f16[168,256]{1,0:T(8,128)(2,1)S(1)}, f16[168,256]{1,0:T(8,128)(2,1)S(1)}, u32[]{:S(2)}, u32[]{:S(2)}) %collective-permute-start.8) | collective-permute-done | bytes 86048 | tf_op jit(solution)/shard_map/ppermute | solution.py:352
  35.1 3.3 %collective-permute-done.7 = f16[168,256]{1,0:T(8,128)(2,1)S(1)} collective-permute-done((f16[168,256]{1,0:T(8,128)(2,1)S(1)}, f16[168,256]{1,0:T(8,128)(2,1)S(1)}, u32[]{:S(2)}, u32[]{:S(2)}) %collective-permute-start.7) | collective-permute-done | bytes 86048 | tf_op jit(solution)/shard_map/ppermute | solution.py:352
  38.4 0.0 collective-permute-done.6
  38.5 0.2 sum_z.1
  38.6 0.1 reduce-precision_convert_fusion.3
  38.7 1.5 %collective-permute-start.9 = (f16[168,256]{1,0:T(8,128)(2,1)S(1)}, f16[168,256]{1,0:T(8,128)(2,1)S(1)}, u32[]{:S(2)}, u32[]{:S(2)}) collective-permute-start(f16[168,256]{1,0:T(8,128)(2,1)S(1)} %get-tuple-element.37), channel_id=1, source_target_pairs={{0,8},{1,9},{2,10},{3,11},{4,12},{5,13},{6,14},{7,15},{8,0},{9,1},... | collective-permute-start | bytes 258056 | tf_op jit(solution)/shard_map/ppermute | solution.py:352
  40.3 3.0 %collective-permute-done.9 = f16[168,256]{1,0:T(8,128)(2,1)S(1)} collective-permute-done((f16[168,256]{1,0:T(8,128)(2,1)S(1)}, f16[168,256]{1,0:T(8,128)(2,1)S(1)}, u32[]{:S(2)}, u32[]{:S(2)}) %collective-permute-start.9) | collective-permute-done | bytes 86048 | tf_op jit(solution)/shard_map/ppermute | solution.py:352
  43.4 0.1 collective-permute-start.10
  43.4 1.4 %collective-permute-done.10.other = f32[160,256]{1,0:T(8,128)S(1)} collective-permute-done((f32[160,256]{1,0:T(8,128)S(1)}, f32[160,256]{1,0:T(8,128)S(1)}, u32[]{:S(2)}, u32[]{:S(2)}) %collective-permute-start.10) | collective-permute-done | bytes 163872 | tf_op jit(solution)/shard_map/ppermute | solution.py:352
  44.8 0.7 %outputs.1 = (f32[64,128]{1,0:T(8,128)}, f32[256,256]{1,0:T(8,128)}) custom-call(f32[160,256]{1,0:T(8,128)S(1)} %sum_x.1.own, f32[160,256]{1,0:T(8,128)S(1)} %collective-permute-done.10.other), custom_call_target="tpu_custom_call" | custom-call | tf_op jit(solution)/shard_map/outputs/pallas_call | solution.py:411
  (12 shorter events, 0.3 us)
Async XLA Ops:
  6.7 6.8 %collective-permute-start.2 = (bf16[4,1280]{1,0:T(4,128)(2,1)S(1)}, bf16[4,1280]{1,0:T(4,128)(2,1)S(1)}, u32[]{:S(2)}, u32[]{:S(2)}) collective-permute-start(bf16[4,1280]{1,0:T(4,128)(2,1)S(1)} %get-tuple-element.20), channel_id=1, source_target_pairs={{0,3},{1,2},{2,1},{3,0},{4,7},{5,6},{6,5},{7,4},{8,11},{9,10},{10,... | collective-permute-start | bytes 30728 | tf_op jit(solution)/shard_map/ppermute | solution.py:352
  11.8 4.6 %collective-permute-start.1 = (bf16[4,1280]{1,0:T(4,128)(2,1)S(1)}, bf16[4,1280]{1,0:T(4,128)(2,1)S(1)}, u32[]{:S(2)}, u32[]{:S(2)}) collective-permute-start(bf16[4,1280]{1,0:T(4,128)(2,1)S(1)} %get-tuple-element.20), channel_id=1, source_target_pairs={{0,2},{1,3},{2,0},{3,1},{4,6},{5,7},{6,4},{7,5},{8,10},{9,11},{10,... | collective-permute-start | bytes 30728 | tf_op jit(solution)/shard_map/ppermute | solution.py:352
  11.8 4.6 %collective-permute-start = (bf16[4,1280]{1,0:T(4,128)(2,1)S(1)}, bf16[4,1280]{1,0:T(4,128)(2,1)S(1)}, u32[]{:S(2)}, u32[]{:S(2)}) collective-permute-start(bf16[4,1280]{1,0:T(4,128)(2,1)S(1)} %get-tuple-element.20), channel_id=1, source_target_pairs={{0,1},{1,0},{2,3},{3,2},{4,5},{5,4},{6,7},{7,6},{8,9},{9,8},{10,11... | collective-permute-start | bytes 30728 | tf_op jit(solution)/shard_map/ppermute | solution.py:352
  16.4 4.1 %collective-permute-start.3 = (bf16[4,4,1280]{2,1,0:T(4,128)(2,1)S(1)}, bf16[4,4,1280]{2,1,0:T(4,128)(2,1)S(1)}, u32[]{:S(2)}, u32[]{:S(2)}) collective-permute-start(bf16[4,4,1280]{2,1,0:T(4,128)(2,1)S(1)} %pad_maximum_fusion), channel_id=1, source_target_pairs={{0,8},{1,9},{2,10},{3,11},{4,12},{5,13},{6,14},{7,15},{8,0},{9,1},... | collective-permute-start | bytes 122888 | tf_op jit(solution)/shard_map/ppermute | solution.py:352
  20.5 1.3 %collective-permute-start.4 = (bf16[8,4,1280]{2,1,0:T(4,128)(2,1)S(1)}, bf16[8,4,1280]{2,1,0:T(4,128)(2,1)S(1)}, u32[]{:S(2)}, u32[]{:S(2)}) collective-permute-start(bf16[8,4,1280]{2,1,0:T(4,128)(2,1)S(1)} %get-tuple-element.39), channel_id=1, source_target_pairs={{0,4},{1,5},{2,6},{3,7},{4,0},{5,1},{6,2},{7,3},{8,12},{9,13},{10,... | collective-permute-start | bytes 245768 | tf_op jit(solution)/shard_map/ppermute | solution.py:352
  23.9 3.5 %collective-permute-start.5 = (f32[4,128,256]{2,1,0:T(8,128)S(1)}, f32[4,128,256]{2,1,0:T(8,128)S(1)}, u32[]{:S(2)}, u32[]{:S(2)}) collective-permute-start(f32[4,128,256]{2,1,0:T(8,128)S(1)} %get-tuple-element.25), channel_id=1, source_target_pairs={{0,4},{1,5},{2,6},{3,7},{4,0},{5,1},{6,2},{7,3},{8,12},{9,13},{10,... | collective-permute-start | bytes 1572872 | tf_op jit(solution)/shard_map/ppermute | solution.py:352
  27.8 7.3 %collective-permute-start.8 = (f16[168,256]{1,0:T(8,128)(2,1)S(1)}, f16[168,256]{1,0:T(8,128)(2,1)S(1)}, u32[]{:S(2)}, u32[]{:S(2)}) collective-permute-start(f16[168,256]{1,0:T(8,128)(2,1)S(1)} %reduce-precision_convert_fusion), channel_id=1, source_target_pairs={{0,3},{1,2},{2,1},{3,0},{4,7},{5,6},{6,5},{7,4},{8,11},{9,10},{10,... | collective-permute-start | bytes 258056 | tf_op jit(solution)/shard_map/ppermute | solution.py:352
  29.3 9.1 %collective-permute-start.7 = (f16[168,256]{1,0:T(8,128)(2,1)S(1)}, f16[168,256]{1,0:T(8,128)(2,1)S(1)}, u32[]{:S(2)}, u32[]{:S(2)}) collective-permute-start(f16[168,256]{1,0:T(8,128)(2,1)S(1)} %reduce-precision_convert_fusion.1), channel_id=1, source_target_pairs={{0,2},{1,3},{2,0},{3,1},{4,6},{5,7},{6,4},{7,5},{8,10},{9,11},{10,... | collective-permute-start | bytes 258056 | tf_op jit(solution)/shard_map/ppermute | solution.py:352
  30.0 8.4 %collective-permute-start.6 = (f16[168,256]{1,0:T(8,128)(2,1)S(1)}, f16[168,256]{1,0:T(8,128)(2,1)S(1)}, u32[]{:S(2)}, u32[]{:S(2)}) collective-permute-start(f16[168,256]{1,0:T(8,128)(2,1)S(1)} %reduce-precision_convert_fusion.2), channel_id=1, source_target_pairs={{0,1},{1,0},{2,3},{3,2},{4,5},{5,4},{6,7},{7,6},{8,9},{9,8},{10,11... | collective-permute-start | bytes 258056 | tf_op jit(solution)/shard_map/ppermute | solution.py:352
  38.7 4.6 %collective-permute-start.9 = (f16[168,256]{1,0:T(8,128)(2,1)S(1)}, f16[168,256]{1,0:T(8,128)(2,1)S(1)}, u32[]{:S(2)}, u32[]{:S(2)}) collective-permute-start(f16[168,256]{1,0:T(8,128)(2,1)S(1)} %get-tuple-element.37), channel_id=1, source_target_pairs={{0,8},{1,9},{2,10},{3,11},{4,12},{5,13},{6,14},{7,15},{8,0},{9,1},... | collective-permute-start | bytes 258056 | tf_op jit(solution)/shard_map/ppermute | solution.py:352
  43.4 1.5 %collective-permute-start.10 = (f32[160,256]{1,0:T(8,128)S(1)}, f32[160,256]{1,0:T(8,128)S(1)}, u32[]{:S(2)}, u32[]{:S(2)}) collective-permute-start(f32[160,256]{1,0:T(8,128)S(1)} %sum_x.1.own), channel_id=1, source_target_pairs={{0,4},{1,5},{2,6},{3,7},{4,0},{5,1},{6,2},{7,3},{8,12},{9,13},{10,... | collective-permute-start | bytes 491528 | tf_op jit(solution)/shard_map/ppermute | solution.py:352

commit v7 on v6

--- a/solution.py
+++ b/solution.py
@@ -62,53 +62,61 @@
     block, one_hot, pre_embed, hidden, pre_conv, w_conv, w_head,
     facies, prior, recon, w_embed, packed, sorted_rows, sem
 ):
-    parts = 4
-    width = facies.shape[1] // parts
-    loads = [
-        pltpu.make_async_copy(
-            facies_hbm.at[:, pl.ds(i * width, width)], facies.at[:, pl.ds(i * width, width)], sem.at[i]
-        )
-        for i in range(parts)
-    ]
+    width = facies.shape[1] // 2
+    halves = [pl.ds(half * width, width) for half in range(2)]
+    loads = [pltpu.make_async_copy(facies_hbm.at[:, at], facies.at[:, at], sem.at[i]) for i, at in enumerate(halves)]
+    for load in loads:
+        load.start()
     for source, target in (
         (w_embed_hbm, w_embed), (w_conv_hbm, w_conv), (prior_hbm, prior), (recon_hbm, recon), (w_head_hbm, w_head)
     ):
         loads.append(pltpu.make_async_copy(source, target, sem.at[len(loads)]))
-    for load in loads:
-        load.start()
     row, lane = iota((256, 256), 0), iota((256, 256), 1)
     order = jnp.where((row // 32 == lane % 8) & (row % 32 == lane // 8), 1.0, 0.0).astype(BF16)
     spread = spread_matrix()
     level = (iota((512, 256), 0) % 4).astype(F32)
-    for i in range(parts):
-        loads[i].wait()
-        part = facies[:, pl.ds(i * width, width)].astype(F32).astype(BF16)
-        sorted_rows[:, pl.ds(i * width, width)] = mm(order, part).astype(BF16)
-    for t in range(8):
-        for dy2 in range(2):
-            j, dx = 2 * (t // 4) + dy2, t % 4
-            rows = [sorted_rows[pl.ds(t * 32, 32), pl.ds((2 * b2 + dy2) * 128, 128)] for b2 in range(8)]
+    for half in range(2):
+        loads[half].wait()
+        if half == 0:
+            for load in loads[2:]:
+                load.start()
+        for at in range(half * width, half * width + width, 512):
+            part = facies[:, pl.ds(at, 512)].astype(F32).astype(BF16)
+            sorted_rows[:, pl.ds(at, 512)] = mm(order, part).astype(BF16)
+        for t in range(8):
+            dx2, dx = t // 4, t % 4
+            rows = [
+                sorted_rows[pl.ds(t * 32, 32), pl.ds((2 * b2 + dy2) * 128, 128)]
+                for dy2 in range(2)
+                for b2 in range(4 * half, 4 * half + 4)
+            ]
             copied = mm_nt(spread, jnp.concatenate(rows, axis=0))
             hot = jnp.where(copied == level, 1.0, 0.0).astype(BF16)
             for cp in range(4):
-                one_hot[cp, j, pl.ds(dx * 128, 128), :] = hot[cp * 128 : (cp + 1) * 128]
-    loads[4].wait()
+                for dy2 in range(2):
+                    one_hot[cp, pl.ds(dx * 128, 128), pl.ds((2 * dx2 + dy2) * 256 + half * 128, 128)] = hot[
+                        cp * 128 : cp * 128 + 128, dy2 * 128 : dy2 * 128 + 128
+                    ]
+    loads[2].wait()
     packed[...] = pair_weights(w_embed[...])
-    loads[5].wait()
+    loads[3].wait()
     conv_turned = jnp.transpose(w_conv[...].astype(F32)).astype(BF16)
     sums = jnp.zeros((256, 128), F32)
     for cp in range(4):
-        for j in range(4):
-            pre = mm(packed[...], one_hot[cp, j])
-            pre_embed[cp, j] = pre
-            hidden[cp, j] = (pre * sigmoid(pre)).astype(BF16)
+        for dx2 in range(2):
+            at = pl.ds(dx2 * 512, 512)
+            pre = mm(packed[...], one_hot[cp, :, at])
+            pre_embed[cp, :, at] = pre
+            act = (pre * sigmoid(pre)).astype(BF16)
+            hidden[cp, 2 * dx2] = act[:, :256]
+            hidden[cp, 2 * dx2 + 1] = act[:, 256:]
         pre = mm(conv_turned, hidden[cp].reshape(1024, 256))
         pre_conv[cp] = pre
         act = pre * sigmoid(pre)
         sums = sums + act[:, :128] + act[:, 128:]
     pick = jnp.where(iota((8, 128), 1) // 8 % 4 == iota((8, 128), 0), 1.0, 0.0)
     total = lax.dot_general(pick, sums, NT, precision=lax.Precision.HIGHEST, preferred_element_type=F32)
-    for load in loads[6:]:
+    for load in loads[4:]:
         load.wait()
     block[:, pl.ds(0, 512)] = prior[...]
     block[:, pl.ds(512, 512)] = recon[...]
@@ -134,10 +142,8 @@
     devices = dp * fsdp
     dp_here, fsdp_here = lax.axis_index("dp"), lax.axis_index("fsdp")
     here = dp_here * fsdp + fsdp_here
-    for place in range(devices):
-        core_flip, x_flip, z_flip = place // (devices // 2), place // fsdp % (dp // 2), place % fsdp
-        owner = (dp_here ^ (2 * x_flip + core_flip)) * fsdp + (fsdp_here ^ z_flip)
-        ordered[owner] = gathered[place].astype(F32)
+    for owner in range(devices):
+        ordered[owner] = gathered[owner].astype(F32)
     samples = ordered.shape[1]
     count = devices * samples
     full = ordered[...].reshape(count, ordered.shape[2])
@@ -179,11 +185,13 @@
 def embed_kernel(grads, w_conv, pre_embed, one_hot, embed_out):
     embed_total = None
     for cp in range(4):
-        for j in range(4):
-            back_rows = mm(w_conv[pl.ds(j * 256, 256), :], grads[cp])
-            signal = (back_rows * silu_slope(pre_embed[cp, j])).astype(BF16)
-            term = mm_nt(one_hot[cp, j], signal)
-            embed_total = term if embed_total is None else embed_total + term
+        signals = []
+        for dx2 in range(2):
+            back_rows = mm(w_conv[pl.ds(dx2 * 512, 512), :], grads[cp])
+            back_rows = jnp.concatenate([back_rows[:256], back_rows[256:]], axis=1)
+            signals.append((back_rows * silu_slope(pre_embed[cp, :, pl.ds(dx2 * 512, 512)])).astype(BF16))
+        term = mm_nt(one_hot[cp], jnp.concatenate(signals, axis=1))
+        embed_total = term if cp == 0 else embed_total + term
     embed = jnp.concatenate(
         [
             embed_total[dx * 128 : dx * 128 + 64, :128] + embed_total[dx * 128 + 64 : dx * 128 + 128, 128:]
@@ -277,8 +285,8 @@
 VMEM = pl.BlockSpec(memory_space=pltpu.VMEM)
 HBM = pl.BlockSpec(memory_space=pltpu.HBM)
 SAVED = (
-    ((4, 4, 512, 256), BF16),
-    ((4, 4, 256, 256), F32),
+    ((4, 512, 1024), BF16),
+    ((4, 256, 1024), F32),
     ((4, 4, 256, 256), BF16),
     ((4, 256, 256), F32),
 )
@@ -303,7 +311,7 @@
             pltpu.VMEM(w_embed.shape, BF16),
             pltpu.VMEM((256, 512), BF16),
             pltpu.VMEM((rows, lanes), BF16),
-            pltpu.SemaphoreType.DMA((9,)),
+            pltpu.SemaphoreType.DMA((7,)),
         ],
         compiler_params=pltpu.CompilerParams(vmem_limit_bytes=30 * 2**20),
         name="forward",
@@ -352,14 +360,9 @@
     return lax.ppermute(block, GROUP, pairs)
 
 
-def gather_blocks(block, dp, fsdp):
-    blocks = [block] + [exchange(block, dp, fsdp, 0, 0, flip) for flip in range(1, fsdp)]
-    stacked = jnp.stack(blocks)
-    flip = 1
-    while flip < dp // 2:
-        stacked = jnp.concatenate([stacked, exchange(stacked, dp, fsdp, flip, 0, 0)], axis=0)
-        flip *= 2
-    return jnp.concatenate([stacked, exchange(stacked, dp, fsdp, 0, 1, 0)], axis=0)
+def gather_blocks(block, devices):
+    copies = jnp.broadcast_to(block[None], (devices,) + block.shape)
+    return lax.all_to_all(copies, GROUP, 0, 0, tiled=True)
 
 
 def local_kernel(kernel, outs, name, *operands):
@@ -403,7 +406,7 @@
     block, one_hot, pre_embed, hidden, pre_conv, w_conv, w_head = forward(
         facies, prior_draws, recon_grad, w_embed, w_conv, w_head
     )
-    gathered = gather_blocks(block, dp, fsdp)
+    gathered = gather_blocks(block, dp * fsdp)
     keep, send, grads, grad_head = backward((dp, fsdp), gathered, hidden, pre_conv, w_head)
     received = exchange(send, dp, fsdp, 0, 1, 0)
     embed = embed_gradient(fsdp, grads, w_conv, pre_embed, one_hot)

time: 45.7 us -> 45.1 us (0.987)
  blocking collectives: 0 us -> 14.8 us
  starting transfers between devices: 13.7 us -> 5.76 us
  waiting for transfers between devices: 18.1 us -> 11.1 us
    all_to_all x0 -> x1, blocking collectives: none -> 14.8 us  [gather_blocks(): return lax.all_to_all(copies, GROUP, 0, 0, tiled=True)]
    ppermute x11 -> x6, starting transfers between devices: 13.7 us -> 5.76 us  [exchange(): return lax.ppermute(block, GROUP, pairs)]
    ppermute x11 -> x6, waiting for transfers between devices: 18.1 us -> 11.1 us  [exchange(): return lax.ppermute(block, GROUP, pairs)]
  transfers between devices with their start and end apart: 11 -> 6, of which waited for: 8 -> 4; matrix products, arithmetic and copies ran while one was open for 0% -> 0% of each run, Pallas kernels for 7% -> 6%
where the time goes in v7:
time: 45.1 us; the launch traced here: 44.9 us
  blocking collectives  14.8 us (33%)
  Pallas kernels  12.1 us (27%)
  waiting for transfers between devices  11.1 us (25%)
  starting transfers between devices  5.76 us (13%)
  between operations  0.75 us (2%)
    all_to_all x1, blocking collectives, gather_blocks(): return lax.all_to_all(copies, GROUP, 0, 0, tiled=True)  14.8 us
    ppermute x6, waiting for transfers between devices, exchange(): return lax.ppermute(block, GROUP, pairs)  11.1 us
    pallas_call x1, Pallas kernels, forward(): pl.pallas_call(forward_kernel, out_shape=(pltpu.VMEM((samples, 2 * latent...  6.18 us
    ppermute x6, starting transfers between devices, exchange(): return lax.ppermute(block, GROUP, pairs)  5.76 us
    pallas_call x1, Pallas kernels, embed_gradient(): pl.pallas_call(embed_kernel, out_shape=pltpu.VMEM((fsdp, 256 // fsdp // 2...  2.79 us
    pallas_call x1, Pallas kernels, backward(): pl.pallas_call(lambda *refs: backward_kernel(sizes, *refs), out_shape=(pa...  1.97 us
  transfers between devices with their start and end apart: 6, of which 4 were waited for; matrix products, arithmetic and copies ran while one was open for 0% of the time, Pallas kernels for 6%

profile of v7, /device:TPU:0, one launch (start us, length us, event | category | flops | bytes accessed | tf_op | source)
XLA Modules:
  0.0 44.9 jit_solution(5620438403928949779)
XLA Ops:
  0.6 6.2 %forward.1 = (bf16[4,1280]{1,0:T(4,128)(2,1)S(1)}, bf16[4,512,1024]{2,1,0:T(8,128)(2,1)S(1)}, f32[4,256,1024]{2,1,0:T(8,128)S(1)}, bf16[4,4,256,256]{3,2,1,0:T(8...) custom-call(s32[256,2048]{1,0:T(8,128)} %bitcast.1, ...), custom_call_target="tpu_custom_call" | custom-call | tf_op jit(solution)/shard_map/forward/pallas_call | solution.py:300
  6.9 14.8 %all_to_all.5.refs_0_ = bf16[16,4,1280]{2,1,0:T(4,128)(2,1)S(1)} all-to-all(bf16[16,4,1280]{2,1,0:T(4,128)(2,1)S(1)} %broadcast_in_dim.2), channel_id=1, replica_groups=mesh['groups'=2,'dp'=4,'fsdp'=4] {'dp','fsdp'}, dimensions={0} | all-to-all | bytes 327680 | tf_op jit(solution)/shard_map/all_to_all | solution.py:365
  21.6 2.0 %backward.1 = (f32[4,128,256]{2,1,0:T(8,128)S(1)}, f32[4,128,256]{2,1,0:T(8,128)S(1)}, bf16[4,256,256]{2,1,0:T(8,128)(2,1)S(1)}, f32[64,512]{1,0:T(8,128)}) custom-call(bf16[16,4,1280]{2,1,0:T(4,128)(2,1)S(1)} %all_to_all.5.refs_0_, bf16[4,4,256,256]{3,2,1,0:T(8,128)(2,1)S(1)} %get-tuple-element.21.refs_1_, f32[4,256,256]{2,1,0:T(8,128)S(1)} %get-tuple-element.22.refs_2_, ...), custom_call_target="tpu_custom_call" | custom-call | tf_op jit(solution)/shard_map/backward/pallas_call | solution.py:325
  23.6 0.3 collective-permute-start
  23.9 2.8 %embed_gradient.1.embed = f32[4,32,256]{2,1,0:T(8,128)S(1)} custom-call(bf16[4,256,256]{2,1,0:T(8,128)(2,1)S(1)} %get-tuple-element.26.grads, bf16[1024,256]{1,0:T(8,128)(2,1)S(1)} %get-tuple-element.27.w_conv, f32[4,256,1024]{2,1,0:T(8,128)S(1)} %get-tuple-element.28.pre_embed, bf16[4,512,1024]{2,1,0:T(8,128)(2,1)S(1)} %get-tuple-element.29.one_hot), custom_call_target="tpu_custom_call" | custom-call | flops 1600000000 | bytes 10485760 | tf_op jit(solution)/shard_map/embed_gradient/pallas_call | solution.py:339
  26.7 0.0 collective-permute-done.other
  26.7 0.2 scale.1
  26.9 0.1 reduce-precision_convert_fusion.1
  27.0 0.1 reduce-precision_convert_fusion
  27.1 1.0 %collective-permute-start.3 = (f16[168,256]{1,0:T(8,128)(2,1)S(1)}, f16[168,256]{1,0:T(8,128)(2,1)S(1)}, u32[]{:S(2)}, u32[]{:S(2)}) collective-permute-start(f16[168,256]{1,0:T(8,128)(2,1)S(1)} %reduce-precision_convert_fusion), channel_id=1, source_target_pairs={{0,3},{1,2},{2,1},{3,0},{4,7},{5,6},{6,5},{7,4},{8,11},{9,10},{10,... | collective-permute-start | bytes 258056 | tf_op jit(solution)/shard_map/ppermute | solution.py:360
  28.2 1.2 %collective-permute-start.2 = (f16[168,256]{1,0:T(8,128)(2,1)S(1)}, f16[168,256]{1,0:T(8,128)(2,1)S(1)}, u32[]{:S(2)}, u32[]{:S(2)}) collective-permute-start(f16[168,256]{1,0:T(8,128)(2,1)S(1)} %reduce-precision_convert_fusion.1), channel_id=1, source_target_pairs={{0,2},{1,3},{2,0},{3,1},{4,6},{5,7},{6,4},{7,5},{8,10},{9,11},{10,... | collective-permute-start | bytes 258056 | tf_op jit(solution)/shard_map/ppermute | solution.py:360
  29.4 0.1 reduce-precision_convert_fusion.2
  29.5 2.3 %collective-permute-start.1 = (f16[168,256]{1,0:T(8,128)(2,1)S(1)}, f16[168,256]{1,0:T(8,128)(2,1)S(1)}, u32[]{:S(2)}, u32[]{:S(2)}) collective-permute-start(f16[168,256]{1,0:T(8,128)(2,1)S(1)} %reduce-precision_convert_fusion.2), channel_id=1, source_target_pairs={{0,1},{1,0},{2,3},{3,2},{4,5},{5,4},{6,7},{7,6},{8,9},{9,8},{10,11... | collective-permute-start | bytes 258056 | tf_op jit(solution)/shard_map/ppermute | solution.py:360
  31.7 2.7 %collective-permute-done.3 = f16[168,256]{1,0:T(8,128)(2,1)S(1)} collective-permute-done((f16[168,256]{1,0:T(8,128)(2,1)S(1)}, f16[168,256]{1,0:T(8,128)(2,1)S(1)}, u32[]{:S(2)}, u32[]{:S(2)}) %collective-permute-start.3) | collective-permute-done | bytes 86048 | tf_op jit(solution)/shard_map/ppermute | solution.py:360
  34.5 3.3 %collective-permute-done.2 = f16[168,256]{1,0:T(8,128)(2,1)S(1)} collective-permute-done((f16[168,256]{1,0:T(8,128)(2,1)S(1)}, f16[168,256]{1,0:T(8,128)(2,1)S(1)}, u32[]{:S(2)}, u32[]{:S(2)}) %collective-permute-start.2) | collective-permute-done | bytes 86048 | tf_op jit(solution)/shard_map/ppermute | solution.py:360
  37.8 0.0 collective-permute-done.1
  37.9 0.2 sum_z.1
  38.0 0.1 reduce-precision_convert_fusion.3
  38.1 0.9 %collective-permute-start.4 = (f16[168,256]{1,0:T(8,128)(2,1)S(1)}, f16[168,256]{1,0:T(8,128)(2,1)S(1)}, u32[]{:S(2)}, u32[]{:S(2)}) collective-permute-start(f16[168,256]{1,0:T(8,128)(2,1)S(1)} %get-tuple-element.37), channel_id=1, source_target_pairs={{0,8},{1,9},{2,10},{3,11},{4,12},{5,13},{6,14},{7,15},{8,0},{9,1},... | collective-permute-start | bytes 258056 | tf_op jit(solution)/shard_map/ppermute | solution.py:360
  39.0 3.7 %collective-permute-done.4 = f16[168,256]{1,0:T(8,128)(2,1)S(1)} collective-permute-done((f16[168,256]{1,0:T(8,128)(2,1)S(1)}, f16[168,256]{1,0:T(8,128)(2,1)S(1)}, u32[]{:S(2)}, u32[]{:S(2)}) %collective-permute-start.4) | collective-permute-done | bytes 86048 | tf_op jit(solution)/shard_map/ppermute | solution.py:360
  42.7 0.1 collective-permute-start.5
  42.8 1.4 %collective-permute-done.5.other = f32[160,256]{1,0:T(8,128)S(1)} collective-permute-done((f32[160,256]{1,0:T(8,128)S(1)}, f32[160,256]{1,0:T(8,128)S(1)}, u32[]{:S(2)}, u32[]{:S(2)}) %collective-permute-start.5) | collective-permute-done | bytes 163872 | tf_op jit(solution)/shard_map/ppermute | solution.py:360
  44.2 0.7 %outputs.1 = (f32[64,128]{1,0:T(8,128)}, f32[256,256]{1,0:T(8,128)}) custom-call(f32[160,256]{1,0:T(8,128)S(1)} %sum_x.1.own, f32[160,256]{1,0:T(8,128)S(1)} %collective-permute-done.5.other), custom_call_target="tpu_custom_call" | custom-call | tf_op jit(solution)/shard_map/outputs/pallas_call | solution.py:414
  (6 shorter events, 0.1 us)
Async XLA Ops:
  23.6 3.1 %collective-permute-start = (f32[4,128,256]{2,1,0:T(8,128)S(1)}, f32[4,128,256]{2,1,0:T(8,128)S(1)}, u32[]{:S(2)}, u32[]{:S(2)}) collective-permute-start(f32[4,128,256]{2,1,0:T(8,128)S(1)} %get-tuple-element.25), channel_id=1, source_target_pairs={{0,4},{1,5},{2,6},{3,7},{4,0},{5,1},{6,2},{7,3},{8,12},{9,13},{10,... | collective-permute-start | bytes 1572872 | tf_op jit(solution)/shard_map/ppermute | solution.py:360
  27.1 7.3 %collective-permute-start.3 = (f16[168,256]{1,0:T(8,128)(2,1)S(1)}, f16[168,256]{1,0:T(8,128)(2,1)S(1)}, u32[]{:S(2)}, u32[]{:S(2)}) collective-permute-start(f16[168,256]{1,0:T(8,128)(2,1)S(1)} %reduce-precision_convert_fusion), channel_id=1, source_target_pairs={{0,3},{1,2},{2,1},{3,0},{4,7},{5,6},{6,5},{7,4},{8,11},{9,10},{10,... | collective-permute-start | bytes 258056 | tf_op jit(solution)/shard_map/ppermute | solution.py:360
  28.2 9.6 %collective-permute-start.2 = (f16[168,256]{1,0:T(8,128)(2,1)S(1)}, f16[168,256]{1,0:T(8,128)(2,1)S(1)}, u32[]{:S(2)}, u32[]{:S(2)}) collective-permute-start(f16[168,256]{1,0:T(8,128)(2,1)S(1)} %reduce-precision_convert_fusion.1), channel_id=1, source_target_pairs={{0,2},{1,3},{2,0},{3,1},{4,6},{5,7},{6,4},{7,5},{8,10},{9,11},{10,... | collective-permute-start | bytes 258056 | tf_op jit(solution)/shard_map/ppermute | solution.py:360
  29.5 8.4 %collective-permute-start.1 = (f16[168,256]{1,0:T(8,128)(2,1)S(1)}, f16[168,256]{1,0:T(8,128)(2,1)S(1)}, u32[]{:S(2)}, u32[]{:S(2)}) collective-permute-start(f16[168,256]{1,0:T(8,128)(2,1)S(1)} %reduce-precision_convert_fusion.2), channel_id=1, source_target_pairs={{0,1},{1,0},{2,3},{3,2},{4,5},{5,4},{6,7},{7,6},{8,9},{9,8},{10,11... | collective-permute-start | bytes 258056 | tf_op jit(solution)/shard_map/ppermute | solution.py:360
  38.1 4.6 %collective-permute-start.4 = (f16[168,256]{1,0:T(8,128)(2,1)S(1)}, f16[168,256]{1,0:T(8,128)(2,1)S(1)}, u32[]{:S(2)}, u32[]{:S(2)}) collective-permute-start(f16[168,256]{1,0:T(8,128)(2,1)S(1)} %get-tuple-element.37), channel_id=1, source_target_pairs={{0,8},{1,9},{2,10},{3,11},{4,12},{5,13},{6,14},{7,15},{8,0},{9,1},... | collective-permute-start | bytes 258056 | tf_op jit(solution)/shard_map/ppermute | solution.py:360
  42.7 1.5 %collective-permute-start.5 = (f32[160,256]{1,0:T(8,128)S(1)}, f32[160,256]{1,0:T(8,128)S(1)}, u32[]{:S(2)}, u32[]{:S(2)}) collective-permute-start(f32[160,256]{1,0:T(8,128)S(1)} %sum_x.1.own), channel_id=1, source_target_pairs={{0,4},{1,5},{2,6},{3,7},{4,0},{5,1},{6,2},{7,3},{8,12},{9,13},{10,... | collective-permute-start | bytes 491528 | tf_op jit(solution)/shard_map/ppermute | solution.py:360

commit v8 on v7

--- a/solution.py
+++ b/solution.py
@@ -49,7 +49,7 @@
 
 
 def sigmoid(value):
-    return 1.0 / (1.0 + jnp.exp(-value))
+    return pltpu.reciprocal(1.0 + jnp.exp2(value * -1.4426950408889634), approx=True)
 
 
 def silu_slope(value):
@@ -74,7 +74,7 @@
     row, lane = iota((256, 256), 0), iota((256, 256), 1)
     order = jnp.where((row // 32 == lane % 8) & (row % 32 == lane // 8), 1.0, 0.0).astype(BF16)
     spread = spread_matrix()
-    level = (iota((512, 256), 0) % 4).astype(F32)
+    level = (iota((512, 256), 0) % 4).astype(F32).astype(BF16)
     for half in range(2):
         loads[half].wait()
         if half == 0:
@@ -91,7 +91,7 @@
                 for b2 in range(4 * half, 4 * half + 4)
             ]
             copied = mm_nt(spread, jnp.concatenate(rows, axis=0))
-            hot = jnp.where(copied == level, 1.0, 0.0).astype(BF16)
+            hot = jnp.where(copied.astype(BF16) == level, BF16(1.0), BF16(0.0))
             for cp in range(4):
                 for dy2 in range(2):
                     one_hot[cp, pl.ds(dx * 128, 128), pl.ds((2 * dx2 + dy2) * 256 + half * 128, 128)] = hot[
@@ -136,20 +136,17 @@
 def backward_kernel(
     sizes, gathered, hidden, pre_conv, w_head,
     keep, send, grads, grad_head,
-    ordered, head_full
+    head_full
 ):
     dp, fsdp = sizes
     devices = dp * fsdp
     dp_here, fsdp_here = lax.axis_index("dp"), lax.axis_index("fsdp")
     here = dp_here * fsdp + fsdp_here
-    for owner in range(devices):
-        ordered[owner] = gathered[owner].astype(F32)
-    samples = ordered.shape[1]
-    count = devices * samples
-    full = ordered[...].reshape(count, ordered.shape[2])
-    prior = full[:, :512].astype(BF16)
-    recon = full[:, 512:1024]
-    pooled = full[:, 1024:].astype(BF16)
+    count = gathered.shape[0]
+    samples = count // devices
+    prior = gathered[:, pl.ds(0, 512)]
+    recon = gathered[:, pl.ds(512, 512)].astype(F32)
+    pooled = gathered[:, pl.ds(1024, 256)]
     latent = mm(pooled, w_head[...]).astype(BF16)
     latent_float = latent.astype(F32)
     square = jnp.sum(latent_float * latent_float, axis=1, keepdims=True)
@@ -157,7 +154,7 @@
     cross_sum, cross_mix = pair_kernel(latent, square, prior)
     pull = -32.0 / count * ((self_sum - cross_sum) * latent_float - self_mix + cross_mix)
     cotangent = (recon + pull).astype(BF16)
-    turned = jnp.transpose(full[:, 1024:]).astype(BF16)
+    turned = jnp.transpose(pooled.astype(F32)).astype(BF16)
     head_full[...] = mm(turned, cotangent)
     share = grad_head.shape[0]
     start = pl.multiple_of(fsdp_here * share, share)
@@ -261,23 +258,20 @@
     store_coded(coded, total)
 
 
-def next_sum_kernel(mine, other, total, *coded):
-    rows = total.shape[0]
-    summed = load_coded(mine, rows) + load_coded(other, rows)
-    total[...] = summed
-    if coded:
-        store_coded(coded[0], summed)
-
-
-def output_kernel(own, other, grad_embed, grad_conv):
-    rows = own.shape[0]
+def next_sum_kernel(mine, other, coded):
+    rows = mine.shape[0] - 8
+    store_coded(coded, load_coded(mine, rows) + load_coded(other, rows))
+
+
+def output_kernel(mine, across, sibling, diagonal, grad_embed, grad_conv):
+    rows = mine.shape[0] - 8
     conv_rows, half = rows * 4 // 5, rows // 5
     core_zero = lax.rem(lax.axis_index("dp"), 2) == 0
-    grad_conv[pl.ds(0, conv_rows), :] = jnp.where(core_zero, own[pl.ds(0, conv_rows), :], other[pl.ds(0, conv_rows), :])
-    grad_conv[pl.ds(conv_rows, conv_rows), :] = jnp.where(
-        core_zero, other[pl.ds(0, conv_rows), :], own[pl.ds(0, conv_rows), :]
-    )
-    embed = own[pl.ds(conv_rows, half), :] + other[pl.ds(conv_rows, half), :]
+    own = load_coded(mine, rows) + load_coded(across, rows)
+    other = load_coded(sibling, rows) + load_coded(diagonal, rows)
+    grad_conv[pl.ds(0, conv_rows), :] = jnp.where(core_zero, own[:conv_rows], other[:conv_rows])
+    grad_conv[pl.ds(conv_rows, conv_rows), :] = jnp.where(core_zero, other[:conv_rows], own[:conv_rows])
+    embed = own[conv_rows:] + other[conv_rows:]
     grad_embed[pl.ds(0, half), :] = embed[:, :128]
     grad_embed[pl.ds(half, half), :] = embed[:, 128:]
 
@@ -320,7 +314,6 @@
 
 def backward(sizes, gathered, hidden, pre_conv, w_head):
     dp, fsdp = sizes
-    devices, samples, width = gathered.shape
     payload = pltpu.VMEM((fsdp, 1024 // fsdp // 2, 256), F32)
     return pl.pallas_call(
         lambda *refs: backward_kernel(sizes, *refs),
@@ -329,7 +322,7 @@
         ),
         in_specs=[VMEM] * 4,
         out_specs=(VMEM,) * 4,
-        scratch_shapes=[pltpu.VMEM((devices, samples, width), F32), pltpu.VMEM((256, 512), F32)],
+        scratch_shapes=[pltpu.VMEM((256, 512), F32)],
         compiler_params=pltpu.CompilerParams(vmem_limit_bytes=24 * 2**20),
         name="backward",
     )(gathered, hidden, pre_conv, w_head)
@@ -362,7 +355,7 @@
 
 def gather_blocks(block, devices):
     copies = jnp.broadcast_to(block[None], (devices,) + block.shape)
-    return lax.all_to_all(copies, GROUP, 0, 0, tiled=True)
+    return lax.all_to_all(copies, GROUP, 0, 0, tiled=True).reshape(-1, block.shape[1])
 
 
 def local_kernel(kernel, outs, name, *operands):
@@ -390,15 +383,14 @@
         exchange(to_half(part)[1], dp, fsdp, 0, 0, place + 1).astype(F32) for place, part in enumerate(coded)
     ]
     (coded,) = local_kernel(first_sum_kernel, (scaled,), "sum_z", own, *received)
-    flip = 1
-    while flip < dp // 2:
+    flip = dp // 4
+    for bit in range(flip.bit_length() - 1):
         mine, sent = to_half(coded)
-        other = exchange(sent, dp, fsdp, flip, 0, 0).astype(F32)
-        flip *= 2
-        outs = (plain, scaled) if flip < dp // 2 else (plain,)
-        total, *rest = local_kernel(next_sum_kernel, outs, "sum_x", mine, other)
-        coded = rest[0] if rest else None
-    return total, exchange(total, dp, fsdp, 0, 1, 0)
+        other = exchange(sent, dp, fsdp, 2**bit, 0, 0).astype(F32)
+        (coded,) = local_kernel(next_sum_kernel, (scaled,), "sum_x", mine, other)
+    mine, sent = to_half(coded)
+    flips = (flip, 0), (0, 1), (flip, 1)
+    return mine, *(exchange(sent, dp, fsdp, x, core, 0).astype(F32) for x, core in flips)
 
 
 def shards(facies, prior_draws, recon_grad, w_embed, w_conv, w_head):
@@ -410,18 +402,18 @@
     keep, send, grads, grad_head = backward((dp, fsdp), gathered, hidden, pre_conv, w_head)
     received = exchange(send, dp, fsdp, 0, 1, 0)
     embed = embed_gradient(fsdp, grads, w_conv, pre_embed, one_hot)
-    own, other = reduce_to_owner(keep, received, embed, dp, fsdp)
+    sums = reduce_to_owner(keep, received, embed, dp, fsdp)
     grad_embed, grad_conv = pl.pallas_call(
         output_kernel,
         out_shape=(
             jax.ShapeDtypeStruct((256 // fsdp, 128), F32),
             jax.ShapeDtypeStruct((1024 // fsdp, 256), F32),
         ),
-        in_specs=[VMEM] * 2,
+        in_specs=[VMEM] * 4,
         out_specs=(VMEM,) * 2,
         compiler_params=pltpu.CompilerParams(vmem_limit_bytes=16 * 2**20),
         name="outputs",
-    )(own, other)
+    )(*sums)
     return (grad_embed, grad_conv, grad_head)
 
 

time: 45.1 us -> 57.5 us (1.27)
  local copies, waits for them, and re-layouts: 0.05 us -> 11.9 us
  starting transfers between devices: 5.76 us -> 7.04 us
  waiting for transfers between devices: 11.1 us -> 10.3 us
    unnamed x0 -> x16, local copies, waits for them, and re-layouts: none -> 11.8 us
    ppermute x6 -> x7, starting transfers between devices: 5.76 us -> 7.04 us  [exchange(): return lax.ppermute(block, GROUP, pairs)]
    ppermute x6 -> x7, waiting for transfers between devices: 11.1 us -> 10.3 us  [exchange(): return lax.ppermute(block, GROUP, pairs)]
  transfers between devices with their start and end apart: 6 -> 7, of which waited for: 4 -> 4; matrix products, arithmetic and copies ran while one was open for 0% -> 0% of each run, Pallas kernels for 6% -> 5%
where the time goes in v8:
time: 57.5 us; the launch traced here: 57.2 us
  blocking collectives  14.8 us (26%)
  Pallas kernels  11.9 us (21%)
  local copies, waits for them, and re-layouts  11.9 us (21%)
  waiting for transfers between devices  10.3 us (18%)
  starting transfers between devices  7.04 us (12%)
  between operations  0.78 us (1%)
    all_to_all x1, blocking collectives, gather_blocks(): lax.all_to_all(copies, GROUP, 0, 0, tiled=True).reshape(-1, block.shape[1])  14.8 us
    unnamed x16, local copies, waits for them, and re-layouts  11.8 us
    ppermute x7, waiting for transfers between devices, exchange(): return lax.ppermute(block, GROUP, pairs)  10.3 us
    ppermute x7, starting transfers between devices, exchange(): return lax.ppermute(block, GROUP, pairs)  7.04 us
    pallas_call x1, Pallas kernels, forward(): pl.pallas_call(forward_kernel, out_shape=(pltpu.VMEM((samples, 2 * latent...  6.09 us
    pallas_call x1, Pallas kernels, embed_gradient(): pl.pallas_call(embed_kernel, out_shape=pltpu.VMEM((fsdp, 256 // fsdp // 2...  2.72 us
    pallas_call x1, Pallas kernels, backward(): pl.pallas_call(lambda *refs: backward_kernel(sizes, *refs), out_shape=(pa...  1.98 us
  transfers between devices with their start and end apart: 7, of which 4 were waited for; matrix products, arithmetic and copies ran while one was open for 0% of the time, Pallas kernels for 5%

profile of v8, /device:TPU:0, one launch (start us, length us, event | category | flops | bytes accessed | tf_op | source)
XLA Modules:
  0.0 57.2 jit_solution(13778754137707736914)
XLA Ops:
  0.6 6.1 %forward.1 = (bf16[4,1280]{1,0:T(4,128)(2,1)S(1)}, bf16[4,512,1024]{2,1,0:T(8,128)(2,1)S(1)}, f32[4,256,1024]{2,1,0:T(8,128)S(1)}, bf16[4,4,256,256]{3,2,1,0:T(8...) custom-call(s32[256,2048]{1,0:T(8,128)} %bitcast.1, ...), custom_call_target="tpu_custom_call" | custom-call | tf_op jit(solution)/shard_map/forward/pallas_call | solution.py:294
  6.7 0.0 copy-start
  6.7 2.0 %copy-done = bf16[4,512,1024]{2,1,0:T(8,128)(2,1)} copy-done((bf16[4,512,1024]{2,1,0:T(8,128)(2,1)}, bf16[4,512,1024]{2,1,0:T(8,128)(2,1)S(1)}, u32[]{:S(2)}) %copy-start) | copy-done | bytes 4194328
  8.7 0.0 copy-start.2
  8.7 2.0 %copy-done.2 = f32[4,256,1024]{2,1,0:T(8,128)} copy-done((f32[4,256,1024]{2,1,0:T(8,128)}, f32[4,256,1024]{2,1,0:T(8,128)S(1)}, u32[]{:S(2)}) %copy-start.2) | copy-done | bytes 4194328
  10.7 0.0 copy-start.4
  10.7 0.8 %copy-done.4 = bf16[1024,256]{1,0:T(8,128)(2,1)} copy-done((bf16[1024,256]{1,0:T(8,128)(2,1)}, bf16[1024,256]{1,0:T(8,128)(2,1)S(1)}, u32[]{:S(2)}) %copy-start.4) | copy-done | bytes 524312
  11.5 0.0 copy-start.6
  11.5 0.7 %copy-done.6 = bf16[256,512]{1,0:T(8,128)(2,1)} copy-done((bf16[256,512]{1,0:T(8,128)(2,1)}, bf16[256,512]{1,0:T(8,128)(2,1)S(1)}, u32[]{:S(2)}) %copy-start.6) | copy-done | bytes 262168
  12.3 14.8 %all_to_all.5 = bf16[16,4,1280]{2,1,0:T(4,128)(2,1)S(1)} all-to-all(bf16[16,4,1280]{2,1,0:T(4,128)(2,1)S(1)} %broadcast_in_dim.2), channel_id=1, replica_groups=mesh['groups'=2,'dp'=4,'fsdp'=4] {'dp','fsdp'}, dimensions={0} | all-to-all | bytes 327680 | tf_op jit(solution)/shard_map/all_to_all | solution.py:358
  27.1 0.0 copy-start.7
  27.1 0.9 %copy-done.7 = bf16[256,512]{1,0:T(8,128)(2,1)S(1)} copy-done((bf16[256,512]{1,0:T(8,128)(2,1)S(1)}, bf16[256,512]{1,0:T(8,128)(2,1)}, u32[]{:S(2)}) %copy-start.7) | copy-done | bytes 262168
  28.1 2.0 %backward.1 = (f32[4,128,256]{2,1,0:T(8,128)S(1)}, f32[4,128,256]{2,1,0:T(8,128)S(1)}, bf16[4,256,256]{2,1,0:T(8,128)(2,1)S(1)}, f32[64,512]{1,0:T(8,128)}) custom-call(bf16[64,1280]{1,0:T(8,128)(2,1)S(1)} %reshape.14.refs_0_, bf16[4,4,256,256]{3,2,1,0:T(8,128)(2,1)S(1)} %get-tuple-element.21.refs_1_, f32[4,256,256]{2,1,0:T(8,128)S(1)} %get-tuple-element.22.refs_2_, ...), custom_call_target="tpu_custom_call" | custom-call | tf_op jit(solution)/shard_map/backward/pallas_call | solution.py:318
  30.0 0.3 collective-permute-start
  30.4 0.0 copy-start.1
  30.4 2.2 %copy-done.1 = bf16[4,512,1024]{2,1,0:T(8,128)(2,1)S(1)} copy-done((bf16[4,512,1024]{2,1,0:T(8,128)(2,1)S(1)}, bf16[4,512,1024]{2,1,0:T(8,128)(2,1)}, u32[]{:S(2)}) %copy-start.1) | copy-done | bytes 4194328
  32.5 0.0 copy-start.3
  32.5 2.2 %copy-done.3 = f32[4,256,1024]{2,1,0:T(8,128)S(1)} copy-done((f32[4,256,1024]{2,1,0:T(8,128)S(1)}, f32[4,256,1024]{2,1,0:T(8,128)}, u32[]{:S(2)}) %copy-start.3) | copy-done | bytes 4194328
  34.7 0.0 copy-start.5
  34.7 1.0 %copy-done.5 = bf16[1024,256]{1,0:T(8,128)(2,1)S(1)} copy-done((bf16[1024,256]{1,0:T(8,128)(2,1)S(1)}, bf16[1024,256]{1,0:T(8,128)(2,1)}, u32[]{:S(2)}) %copy-start.5) | copy-done | bytes 524312
  35.8 2.7 %embed_gradient.1.embed = f32[4,32,256]{2,1,0:T(8,128)S(1)} custom-call(bf16[4,256,256]{2,1,0:T(8,128)(2,1)S(1)} %get-tuple-element.26.grads, bf16[1024,256]{1,0:T(8,128)(2,1)S(1)} %copy-done.5, f32[4,256,1024]{2,1,0:T(8,128)S(1)} %copy-done.3, bf16[4,512,1024]{2,1,0:T(8,128)(2,1)S(1)} %copy-done.1), custom_call_target="tpu_custom_call" | custom-call | flops 1600000000 | bytes 10485760 | tf_op jit(solution)/shard_map/embed_gradient/pallas_call | solution.py:332
  38.5 0.0 collective-permute-done.other
  38.5 0.2 scale.1
  38.7 0.1 reduce-precision_convert_fusion.1
  38.8 0.1 reduce-precision_convert_fusion
  38.9 1.0 %collective-permute-start.3 = (f16[168,256]{1,0:T(8,128)(2,1)S(1)}, f16[168,256]{1,0:T(8,128)(2,1)S(1)}, u32[]{:S(2)}, u32[]{:S(2)}) collective-permute-start(f16[168,256]{1,0:T(8,128)(2,1)S(1)} %reduce-precision_convert_fusion), channel_id=1, source_target_pairs={{0,3},{1,2},{2,1},{3,0},{4,7},{5,6},{6,5},{7,4},{8,11},{9,10},{10,... | collective-permute-start | bytes 258056 | tf_op jit(solution)/shard_map/ppermute | solution.py:353
  39.9 1.2 %collective-permute-start.2 = (f16[168,256]{1,0:T(8,128)(2,1)S(1)}, f16[168,256]{1,0:T(8,128)(2,1)S(1)}, u32[]{:S(2)}, u32[]{:S(2)}) collective-permute-start(f16[168,256]{1,0:T(8,128)(2,1)S(1)} %reduce-precision_convert_fusion.1), channel_id=1, source_target_pairs={{0,2},{1,3},{2,0},{3,1},{4,6},{5,7},{6,4},{7,5},{8,10},{9,11},{10,... | collective-permute-start | bytes 258056 | tf_op jit(solution)/shard_map/ppermute | solution.py:353
  41.1 0.1 reduce-precision_convert_fusion.2
  41.2 2.3 %collective-permute-start.1 = (f16[168,256]{1,0:T(8,128)(2,1)S(1)}, f16[168,256]{1,0:T(8,128)(2,1)S(1)}, u32[]{:S(2)}, u32[]{:S(2)}) collective-permute-start(f16[168,256]{1,0:T(8,128)(2,1)S(1)} %reduce-precision_convert_fusion.2), channel_id=1, source_target_pairs={{0,1},{1,0},{2,3},{3,2},{4,5},{5,4},{6,7},{7,6},{8,9},{9,8},{10,11... | collective-permute-start | bytes 258056 | tf_op jit(solution)/shard_map/ppermute | solution.py:353
  43.5 2.7 %collective-permute-done.3 = f16[168,256]{1,0:T(8,128)(2,1)S(1)} collective-permute-done((f16[168,256]{1,0:T(8,128)(2,1)S(1)}, f16[168,256]{1,0:T(8,128)(2,1)S(1)}, u32[]{:S(2)}, u32[]{:S(2)}) %collective-permute-start.3) | collective-permute-done | bytes 86048 | tf_op jit(solution)/shard_map/ppermute | solution.py:353
  46.3 3.3 %collective-permute-done.2 = f16[168,256]{1,0:T(8,128)(2,1)S(1)} collective-permute-done((f16[168,256]{1,0:T(8,128)(2,1)S(1)}, f16[168,256]{1,0:T(8,128)(2,1)S(1)}, u32[]{:S(2)}, u32[]{:S(2)}) %collective-permute-start.2) | collective-permute-done | bytes 86048 | tf_op jit(solution)/shard_map/ppermute | solution.py:353
  49.6 0.0 collective-permute-done.1
  49.6 0.2 sum_z.1
  49.8 0.1 reduce-precision_convert_fusion.3
  49.9 0.5 collective-permute-start.6
  50.4 0.5 collective-permute-start.5
  50.8 1.3 %collective-permute-start.4 = (f16[168,256]{1,0:T(8,128)(2,1)S(1)}, f16[168,256]{1,0:T(8,128)(2,1)S(1)}, u32[]{:S(2)}, u32[]{:S(2)}) collective-permute-start(f16[168,256]{1,0:T(8,128)(2,1)S(1)} %get-tuple-element.37), channel_id=1, source_target_pairs={{0,8},{1,9},{2,10},{3,11},{4,12},{5,13},{6,14},{7,15},{8,0},{9,1},... | collective-permute-start | bytes 258056 | tf_op jit(solution)/shard_map/ppermute | solution.py:353
  52.1 2.7 %collective-permute-done.6 = f16[168,256]{1,0:T(8,128)(2,1)S(1)} collective-permute-done((f16[168,256]{1,0:T(8,128)(2,1)S(1)}, f16[168,256]{1,0:T(8,128)(2,1)S(1)}, u32[]{:S(2)}, u32[]{:S(2)}) %collective-permute-start.6) | collective-permute-done | bytes 86048 | tf_op jit(solution)/shard_map/ppermute | solution.py:353
  54.8 0.0 collective-permute-done.5
  54.8 1.6 %collective-permute-done.4 = f16[168,256]{1,0:T(8,128)(2,1)S(1)} collective-permute-done((f16[168,256]{1,0:T(8,128)(2,1)S(1)}, f16[168,256]{1,0:T(8,128)(2,1)S(1)}, u32[]{:S(2)}, u32[]{:S(2)}) %collective-permute-start.4) | collective-permute-done | bytes 86048 | tf_op jit(solution)/shard_map/ppermute | solution.py:353
  56.4 0.8 %outputs.1 = (f32[64,128]{1,0:T(8,128)}, f32[256,256]{1,0:T(8,128)}) custom-call(f32[168,256]{1,0:T(8,128)S(1)} %get-tuple-element.38.mine, f32[168,256]{1,0:T(8,128)S(1)} %convert_element_type.37.across, f32[168,256]{1,0:T(8,128)S(1)} %convert_element_type.38.sibling, f32[168,256]{1,0:T(8,128)S(1)} %convert_element_type.39.diagonal), custom_call_target="tpu_custom_call" | custom-call | tf_op jit(solution)/shard_map/outputs/pallas_call | solution.py:406
  (8 shorter events, 0.2 us)
Async XLA Ops:
  6.7 2.0 %copy-start = (bf16[4,512,1024]{2,1,0:T(8,128)(2,1)}, bf16[4,512,1024]{2,1,0:T(8,128)(2,1)S(1)}, u32[]{:S(2)}) copy-start(bf16[4,512,1024]{2,1,0:T(8,128)(2,1)S(1)} %get-tuple-element.29.one_hot) | copy-start | bytes 12582916
  8.7 2.0 %copy-start.2 = (f32[4,256,1024]{2,1,0:T(8,128)}, f32[4,256,1024]{2,1,0:T(8,128)S(1)}, u32[]{:S(2)}) copy-start(f32[4,256,1024]{2,1,0:T(8,128)S(1)} %get-tuple-element.28.pre_embed) | copy-start | bytes 12582916
  10.7 0.8 %copy-start.4 = (bf16[1024,256]{1,0:T(8,128)(2,1)}, bf16[1024,256]{1,0:T(8,128)(2,1)S(1)}, u32[]{:S(2)}) copy-start(bf16[1024,256]{1,0:T(8,128)(2,1)S(1)} %get-tuple-element.27.w_conv) | copy-start | bytes 1572868
  11.5 0.7 %copy-start.6 = (bf16[256,512]{1,0:T(8,128)(2,1)}, bf16[256,512]{1,0:T(8,128)(2,1)S(1)}, u32[]{:S(2)}) copy-start(bf16[256,512]{1,0:T(8,128)(2,1)S(1)} %get-tuple-element.23.refs_3_) | copy-start | bytes 786436
  27.1 1.0 %copy-start.7 = (bf16[256,512]{1,0:T(8,128)(2,1)S(1)}, bf16[256,512]{1,0:T(8,128)(2,1)}, u32[]{:S(2)}) copy-start(bf16[256,512]{1,0:T(8,128)(2,1)} %copy-done.6) | copy-start | bytes 786436
  30.0 8.5 %collective-permute-start = (f32[4,128,256]{2,1,0:T(8,128)S(1)}, f32[4,128,256]{2,1,0:T(8,128)S(1)}, u32[]{:S(2)}, u32[]{:S(2)}) collective-permute-start(f32[4,128,256]{2,1,0:T(8,128)S(1)} %get-tuple-element.25), channel_id=1, source_target_pairs={{0,4},{1,5},{2,6},{3,7},{4,0},{5,1},{6,2},{7,3},{8,12},{9,13},{10,... | collective-permute-start | bytes 1572872 | tf_op jit(solution)/shard_map/ppermute | solution.py:353
  30.4 2.2 %copy-start.1 = (bf16[4,512,1024]{2,1,0:T(8,128)(2,1)S(1)}, bf16[4,512,1024]{2,1,0:T(8,128)(2,1)}, u32[]{:S(2)}) copy-start(bf16[4,512,1024]{2,1,0:T(8,128)(2,1)} %copy-done) | copy-start | bytes 12582916
  32.5 2.2 %copy-start.3 = (f32[4,256,1024]{2,1,0:T(8,128)S(1)}, f32[4,256,1024]{2,1,0:T(8,128)}, u32[]{:S(2)}) copy-start(f32[4,256,1024]{2,1,0:T(8,128)} %copy-done.2) | copy-start | bytes 12582916
  34.7 1.0 %copy-start.5 = (bf16[1024,256]{1,0:T(8,128)(2,1)S(1)}, bf16[1024,256]{1,0:T(8,128)(2,1)}, u32[]{:S(2)}) copy-start(bf16[1024,256]{1,0:T(8,128)(2,1)} %copy-done.4) | copy-start | bytes 1572868
  38.9 7.3 %collective-permute-start.3 = (f16[168,256]{1,0:T(8,128)(2,1)S(1)}, f16[168,256]{1,0:T(8,128)(2,1)S(1)}, u32[]{:S(2)}, u32[]{:S(2)}) collective-permute-start(f16[168,256]{1,0:T(8,128)(2,1)S(1)} %reduce-precision_convert_fusion), channel_id=1, source_target_pairs={{0,3},{1,2},{2,1},{3,0},{4,7},{5,6},{6,5},{7,4},{8,11},{9,10},{10,... | collective-permute-start | bytes 258056 | tf_op jit(solution)/shard_map/ppermute | solution.py:353
  39.9 9.6 %collective-permute-start.2 = (f16[168,256]{1,0:T(8,128)(2,1)S(1)}, f16[168,256]{1,0:T(8,128)(2,1)S(1)}, u32[]{:S(2)}, u32[]{:S(2)}) collective-permute-start(f16[168,256]{1,0:T(8,128)(2,1)S(1)} %reduce-precision_convert_fusion.1), channel_id=1, source_target_pairs={{0,2},{1,3},{2,0},{3,1},{4,6},{5,7},{6,4},{7,5},{8,10},{9,11},{10,... | collective-permute-start | bytes 258056 | tf_op jit(solution)/shard_map/ppermute | solution.py:353
  41.2 8.4 %collective-permute-start.1 = (f16[168,256]{1,0:T(8,128)(2,1)S(1)}, f16[168,256]{1,0:T(8,128)(2,1)S(1)}, u32[]{:S(2)}, u32[]{:S(2)}) collective-permute-start(f16[168,256]{1,0:T(8,128)(2,1)S(1)} %reduce-precision_convert_fusion.2), channel_id=1, source_target_pairs={{0,1},{1,0},{2,3},{3,2},{4,5},{5,4},{6,7},{7,6},{8,9},{9,8},{10,11... | collective-permute-start | bytes 258056 | tf_op jit(solution)/shard_map/ppermute | solution.py:353
  49.9 4.9 %collective-permute-start.6 = (f16[168,256]{1,0:T(8,128)(2,1)S(1)}, f16[168,256]{1,0:T(8,128)(2,1)S(1)}, u32[]{:S(2)}, u32[]{:S(2)}) collective-permute-start(f16[168,256]{1,0:T(8,128)(2,1)S(1)} %get-tuple-element.37), channel_id=1, source_target_pairs={{0,12},{1,13},{2,14},{3,15},{4,8},{5,9},{6,10},{7,11},{8,4},{9,5},... | collective-permute-start | bytes 258056 | tf_op jit(solution)/shard_map/ppermute | solution.py:353
  50.4 4.4 %collective-permute-start.5 = (f16[168,256]{1,0:T(8,128)(2,1)S(1)}, f16[168,256]{1,0:T(8,128)(2,1)S(1)}, u32[]{:S(2)}, u32[]{:S(2)}) collective-permute-start(f16[168,256]{1,0:T(8,128)(2,1)S(1)} %get-tuple-element.37), channel_id=1, source_target_pairs={{0,4},{1,5},{2,6},{3,7},{4,0},{5,1},{6,2},{7,3},{8,12},{9,13},{10,... | collective-permute-start | bytes 258056 | tf_op jit(solution)/shard_map/ppermute | solution.py:353
  50.8 5.6 %collective-permute-start.4 = (f16[168,256]{1,0:T(8,128)(2,1)S(1)}, f16[168,256]{1,0:T(8,128)(2,1)S(1)}, u32[]{:S(2)}, u32[]{:S(2)}) collective-permute-start(f16[168,256]{1,0:T(8,128)(2,1)S(1)} %get-tuple-element.37), channel_id=1, source_target_pairs={{0,8},{1,9},{2,10},{3,11},{4,12},{5,13},{6,14},{7,15},{8,0},{9,1},... | collective-permute-start | bytes 258056 | tf_op jit(solution)/shard_map/ppermute | solution.py:353

commit v9 on v7

--- a/solution.py
+++ b/solution.py
@@ -27,29 +27,19 @@
     return lax.dot_general(left, right, NT, preferred_element_type=F32)
 
 
-def spread_matrix():
-    out_row = iota((512, 128), 0)
-    lane = iota((512, 128), 1)
-    pair, half = out_row // 128, out_row // 64 % 2
-    row_dy, row_dz = out_row // 16 % 4, out_row // 4 % 4
-    lane_dy, lane_c, lane_dz = lane // 32, lane // 4 % 8, lane % 4
-    hit = (row_dy == lane_dy) & (row_dz == lane_dz) & (lane_c == 2 * pair + half)
-    return jnp.where(hit, 1.0, 0.0).astype(BF16)
-
-
 def pair_weights(w_embed):
     turned = jnp.transpose(w_embed.astype(F32)).astype(BF16)
+    row, lane = iota((256, 512), 0), iota((256, 512), 1)
+    same = (row // 64 == lane // 128) & (row % 4 == lane // 32 % 4)
+    same = same & (row // 16 % 4 == lane // 8 % 4) & (row // 4 % 4 == lane % 4)
     halves = []
     for half in range(2):
-        row = iota((256, 512), 0)
-        lane = iota((256, 512), 1)
-        hit = (row // 64 == lane // 128) & (row % 64 == lane % 64) & (lane // 64 % 2 == half)
-        halves.append(mm(turned, jnp.where(hit, 1.0, 0.0).astype(BF16)))
+        halves.append(mm(turned, jnp.where(same & (lane // 4 % 2 == half), 1.0, 0.0).astype(BF16)))
     return jnp.concatenate(halves, axis=0).astype(BF16)
 
 
 def sigmoid(value):
-    return 1.0 / (1.0 + jnp.exp(-value))
+    return pltpu.reciprocal(1.0 + jnp.exp2(value * -1.4426950408889634), approx=True)
 
 
 def silu_slope(value):
@@ -60,46 +50,44 @@
 def forward_kernel(
     facies_hbm, prior_hbm, recon_hbm, w_embed_hbm, w_conv_hbm, w_head_hbm,
     block, one_hot, pre_embed, hidden, pre_conv, w_conv, w_head,
-    facies, prior, recon, w_embed, packed, sorted_rows, sem
+    facies, prior, recon, w_embed, packed, sem
 ):
-    width = facies.shape[1] // 2
-    halves = [pl.ds(half * width, width) for half in range(2)]
-    loads = [pltpu.make_async_copy(facies_hbm.at[:, at], facies.at[:, at], sem.at[i]) for i, at in enumerate(halves)]
+    blocks = facies.shape[0]
+    loads = [
+        pltpu.make_async_copy(facies_hbm.at[:, pl.ds(b * 128, 128)], facies.at[b], sem.at[b]) for b in range(blocks)
+    ]
     for load in loads:
         load.start()
+    others = []
     for source, target in (
         (w_embed_hbm, w_embed), (w_conv_hbm, w_conv), (prior_hbm, prior), (recon_hbm, recon), (w_head_hbm, w_head)
     ):
-        loads.append(pltpu.make_async_copy(source, target, sem.at[len(loads)]))
-    row, lane = iota((256, 256), 0), iota((256, 256), 1)
-    order = jnp.where((row // 32 == lane % 8) & (row % 32 == lane // 8), 1.0, 0.0).astype(BF16)
-    spread = spread_matrix()
-    level = (iota((512, 256), 0) % 4).astype(F32)
+        others.append(pltpu.make_async_copy(source, target, sem.at[blocks + len(others)]))
     for half in range(2):
-        loads[half].wait()
+        for load in loads[half * blocks // 2 : (half + 1) * blocks // 2]:
+            load.wait()
         if half == 0:
-            for load in loads[2:]:
+            for load in others:
                 load.start()
-        for at in range(half * width, half * width + width, 512):
-            part = facies[:, pl.ds(at, 512)].astype(F32).astype(BF16)
-            sorted_rows[:, pl.ds(at, 512)] = mm(order, part).astype(BF16)
         for t in range(8):
             dx2, dx = t // 4, t % 4
             rows = [
-                sorted_rows[pl.ds(t * 32, 32), pl.ds((2 * b2 + dy2) * 128, 128)]
+                facies[2 * b2 + dy2, pl.ds(t, 32, stride=8), :]
                 for dy2 in range(2)
                 for b2 in range(4 * half, 4 * half + 4)
             ]
-            copied = mm_nt(spread, jnp.concatenate(rows, axis=0))
-            hot = jnp.where(copied == level, 1.0, 0.0).astype(BF16)
+            turned = jnp.transpose(jnp.concatenate(rows, axis=0).astype(F32))
             for cp in range(4):
-                for dy2 in range(2):
-                    one_hot[cp, pl.ds(dx * 128, 128), pl.ds((2 * dx2 + dy2) * 256 + half * 128, 128)] = hot[
-                        cp * 128 : cp * 128 + 128, dy2 * 128 : dy2 * 128 + 128
-                    ]
-    loads[2].wait()
+                part = jnp.concatenate([turned[dy * 32 + cp * 8 : dy * 32 + cp * 8 + 8] for dy in range(4)], axis=0)
+                part = part.astype(BF16)
+                for k in range(LEVELS):
+                    hot = jnp.where(part == BF16(k), BF16(1.0), BF16(0.0))
+                    for dy2 in range(2):
+                        at = (2 * dx2 + dy2) * 256 + half * 128
+                        one_hot[cp, pl.ds(dx * 128 + k * 32, 32), pl.ds(at, 128)] = hot[:, dy2 * 128 : dy2 * 128 + 128]
+    others[0].wait()
     packed[...] = pair_weights(w_embed[...])
-    loads[3].wait()
+    others[1].wait()
     conv_turned = jnp.transpose(w_conv[...].astype(F32)).astype(BF16)
     sums = jnp.zeros((256, 128), F32)
     for cp in range(4):
@@ -116,7 +104,7 @@
         sums = sums + act[:, :128] + act[:, 128:]
     pick = jnp.where(iota((8, 128), 1) // 8 % 4 == iota((8, 128), 0), 1.0, 0.0)
     total = lax.dot_general(pick, sums, NT, precision=lax.Precision.HIGHEST, preferred_element_type=F32)
-    for load in loads[4:]:
+    for load in others[2:]:
         load.wait()
     block[:, pl.ds(0, 512)] = prior[...]
     block[:, pl.ds(512, 512)] = recon[...]
@@ -192,18 +180,15 @@
             signals.append((back_rows * silu_slope(pre_embed[cp, :, pl.ds(dx2 * 512, 512)])).astype(BF16))
         term = mm_nt(one_hot[cp], jnp.concatenate(signals, axis=1))
         embed_total = term if cp == 0 else embed_total + term
-    embed = jnp.concatenate(
-        [
-            embed_total[dx * 128 : dx * 128 + 64, :128] + embed_total[dx * 128 + 64 : dx * 128 + 128, 128:]
-            for dx in range(4)
-        ],
-        axis=0,
-    )
+    pairs = embed_total.reshape(64, 8, 256)
+    embed = (pairs[:, :4, :128] + pairs[:, 4:, 128:]).reshape(256, 128)
     half = embed_out.shape[1]
+    depth = 2 * half // LEVELS
     for f in range(embed_out.shape[0]):
+        dx, at = f * 2 * half // 64, f * 2 * half % 64 // LEVELS
+        share = jnp.concatenate([embed[dx * 64 + k * 16 + at :][:depth] for k in range(LEVELS)], axis=0)
         for side in range(2):
-            at = (2 * f + side) * half
-            embed_out[f, :, pl.ds(side * 128, 128)] = embed[at : at + half]
+            embed_out[f, :, pl.ds(side * 128, 128)] = share[side * half : (side + 1) * half]
 
 
 def exponent_of(part):
@@ -278,8 +263,16 @@
         core_zero, other[pl.ds(0, conv_rows), :], own[pl.ds(0, conv_rows), :]
     )
     embed = own[pl.ds(conv_rows, half), :] + other[pl.ds(conv_rows, half), :]
-    grad_embed[pl.ds(0, half), :] = embed[:, :128]
-    grad_embed[pl.ds(half, half), :] = embed[:, 128:]
+    embed = jnp.concatenate([embed[:, :128], embed[:, 128:]], axis=0)
+    count = 2 * half
+    row, lane = iota((count, count), 0), iota((count, count), 1)
+    order = jnp.where(lane == row % LEVELS * (count // LEVELS) + row // LEVELS, 1.0, 0.0).astype(BF16)
+    result = None
+    for _ in range(3):
+        term = embed.astype(BF16)
+        embed = embed - term.astype(F32)
+        result = mm(order, term) if result is None else result + mm(order, term)
+    grad_embed[...] = result
 
 
 VMEM = pl.BlockSpec(memory_space=pltpu.VMEM)
@@ -305,13 +298,12 @@
         in_specs=[HBM] * 6,
         out_specs=(VMEM,) * 7,
         scratch_shapes=[
-            pltpu.VMEM((rows, lanes), jnp.int32),
+            pltpu.VMEM((lanes // 128, rows, 128), jnp.int32),
             pltpu.VMEM(prior_draws.shape, BF16),
             pltpu.VMEM(recon_grad.shape, BF16),
             pltpu.VMEM(w_embed.shape, BF16),
             pltpu.VMEM((256, 512), BF16),
-            pltpu.VMEM((rows, lanes), BF16),
-            pltpu.SemaphoreType.DMA((7,)),
+            pltpu.SemaphoreType.DMA((lanes // 128 + 5,)),
         ],
         compiler_params=pltpu.CompilerParams(vmem_limit_bytes=30 * 2**20),
         name="forward",

time: 45.1 us -> 44.3 us (0.982)
  Pallas kernels: 12.1 us -> 11.3 us
    pallas_call x1, Pallas kernels: 6.18 us -> 5.34 us  [forward(): pl.pallas_call(forward_kernel, out_shape=(pltpu.VMEM((samples, 2 * latent...]
where the time goes in v9:
time: 44.3 us; the launch traced here: 44.1 us
  blocking collectives  14.8 us (33%)
  Pallas kernels  11.3 us (26%)
  waiting for transfers between devices  11.1 us (25%)
  starting transfers between devices  5.77 us (13%)
  between operations  0.74 us (2%)
    all_to_all x1, blocking collectives, gather_blocks(): return lax.all_to_all(copies, GROUP, 0, 0, tiled=True)  14.8 us
    ppermute x6, waiting for transfers between devices, exchange(): return lax.ppermute(block, GROUP, pairs)  11.1 us
    ppermute x6, starting transfers between devices, exchange(): return lax.ppermute(block, GROUP, pairs)  5.77 us
    pallas_call x1, Pallas kernels, forward(): pl.pallas_call(forward_kernel, out_shape=(pltpu.VMEM((samples, 2 * latent...  5.34 us
    pallas_call x1, Pallas kernels, embed_gradient(): pl.pallas_call(embed_kernel, out_shape=pltpu.VMEM((fsdp, 256 // fsdp // 2...  2.78 us
    pallas_call x1, Pallas kernels, backward(): pl.pallas_call(lambda *refs: backward_kernel(sizes, *refs), out_shape=(pa...  1.98 us
  transfers between devices with their start and end apart: 6, of which 4 were waited for; matrix products, arithmetic and copies ran while one was open for 0% of the time, Pallas kernels for 6%

profile of v9, /device:TPU:0, one launch (start us, length us, event | category | flops | bytes accessed | tf_op | source)
XLA Modules:
  0.0 44.1 jit_solution(10950773403705347432)
XLA Ops:
  0.6 5.3 %forward.1 = (bf16[4,1280]{1,0:T(4,128)(2,1)S(1)}, bf16[4,512,1024]{2,1,0:T(8,128)(2,1)S(1)}, f32[4,256,1024]{2,1,0:T(8,128)S(1)}, bf16[4,4,256,256]{3,2,1,0:T(8...) custom-call(s32[256,2048]{1,0:T(8,128)} %bitcast.1, ...), custom_call_target="tpu_custom_call" | custom-call | tf_op jit(solution)/shard_map/forward/pallas_call | solution.py:293
  6.0 14.8 %all_to_all.5.refs_0_ = bf16[16,4,1280]{2,1,0:T(4,128)(2,1)S(1)} all-to-all(bf16[16,4,1280]{2,1,0:T(4,128)(2,1)S(1)} %broadcast_in_dim.2), channel_id=1, replica_groups=mesh['groups'=2,'dp'=4,'fsdp'=4] {'dp','fsdp'}, dimensions={0} | all-to-all | bytes 327680 | tf_op jit(solution)/shard_map/all_to_all | solution.py:357
  20.8 2.0 %backward.1 = (f32[4,128,256]{2,1,0:T(8,128)S(1)}, f32[4,128,256]{2,1,0:T(8,128)S(1)}, bf16[4,256,256]{2,1,0:T(8,128)(2,1)S(1)}, f32[64,512]{1,0:T(8,128)}) custom-call(bf16[16,4,1280]{2,1,0:T(4,128)(2,1)S(1)} %all_to_all.5.refs_0_, bf16[4,4,256,256]{3,2,1,0:T(8,128)(2,1)S(1)} %get-tuple-element.21.refs_1_, f32[4,256,256]{2,1,0:T(8,128)S(1)} %get-tuple-element.22.refs_2_, ...), custom_call_target="tpu_custom_call" | custom-call | tf_op jit(solution)/shard_map/backward/pallas_call | solution.py:317
  22.8 0.3 collective-permute-start
  23.1 2.8 %embed_gradient.1.embed = f32[4,32,256]{2,1,0:T(8,128)S(1)} custom-call(bf16[4,256,256]{2,1,0:T(8,128)(2,1)S(1)} %get-tuple-element.26.grads, bf16[1024,256]{1,0:T(8,128)(2,1)S(1)} %get-tuple-element.27.w_conv, f32[4,256,1024]{2,1,0:T(8,128)S(1)} %get-tuple-element.28.pre_embed, bf16[4,512,1024]{2,1,0:T(8,128)(2,1)S(1)} %get-tuple-element.29.one_hot), custom_call_target="tpu_custom_call" | custom-call | flops 1600000000 | bytes 10485760 | tf_op jit(solution)/shard_map/embed_gradient/pallas_call | solution.py:331
  25.9 0.0 collective-permute-done.other
  25.9 0.2 scale.1
  26.1 0.1 reduce-precision_convert_fusion.1
  26.2 0.1 reduce-precision_convert_fusion
  26.3 1.0 %collective-permute-start.3 = (f16[168,256]{1,0:T(8,128)(2,1)S(1)}, f16[168,256]{1,0:T(8,128)(2,1)S(1)}, u32[]{:S(2)}, u32[]{:S(2)}) collective-permute-start(f16[168,256]{1,0:T(8,128)(2,1)S(1)} %reduce-precision_convert_fusion), channel_id=1, source_target_pairs={{0,3},{1,2},{2,1},{3,0},{4,7},{5,6},{6,5},{7,4},{8,11},{9,10},{10,... | collective-permute-start | bytes 258056 | tf_op jit(solution)/shard_map/ppermute | solution.py:352
  27.3 1.2 %collective-permute-start.2 = (f16[168,256]{1,0:T(8,128)(2,1)S(1)}, f16[168,256]{1,0:T(8,128)(2,1)S(1)}, u32[]{:S(2)}, u32[]{:S(2)}) collective-permute-start(f16[168,256]{1,0:T(8,128)(2,1)S(1)} %reduce-precision_convert_fusion.1), channel_id=1, source_target_pairs={{0,2},{1,3},{2,0},{3,1},{4,6},{5,7},{6,4},{7,5},{8,10},{9,11},{10,... | collective-permute-start | bytes 258056 | tf_op jit(solution)/shard_map/ppermute | solution.py:352
  28.5 0.1 reduce-precision_convert_fusion.2
  28.6 2.3 %collective-permute-start.1 = (f16[168,256]{1,0:T(8,128)(2,1)S(1)}, f16[168,256]{1,0:T(8,128)(2,1)S(1)}, u32[]{:S(2)}, u32[]{:S(2)}) collective-permute-start(f16[168,256]{1,0:T(8,128)(2,1)S(1)} %reduce-precision_convert_fusion.2), channel_id=1, source_target_pairs={{0,1},{1,0},{2,3},{3,2},{4,5},{5,4},{6,7},{7,6},{8,9},{9,8},{10,11... | collective-permute-start | bytes 258056 | tf_op jit(solution)/shard_map/ppermute | solution.py:352
  30.9 2.7 %collective-permute-done.3 = f16[168,256]{1,0:T(8,128)(2,1)S(1)} collective-permute-done((f16[168,256]{1,0:T(8,128)(2,1)S(1)}, f16[168,256]{1,0:T(8,128)(2,1)S(1)}, u32[]{:S(2)}, u32[]{:S(2)}) %collective-permute-start.3) | collective-permute-done | bytes 86048 | tf_op jit(solution)/shard_map/ppermute | solution.py:352
  33.6 3.3 %collective-permute-done.2 = f16[168,256]{1,0:T(8,128)(2,1)S(1)} collective-permute-done((f16[168,256]{1,0:T(8,128)(2,1)S(1)}, f16[168,256]{1,0:T(8,128)(2,1)S(1)}, u32[]{:S(2)}, u32[]{:S(2)}) %collective-permute-start.2) | collective-permute-done | bytes 86048 | tf_op jit(solution)/shard_map/ppermute | solution.py:352
  37.0 0.0 collective-permute-done.1
  37.0 0.2 sum_z.1
  37.2 0.1 reduce-precision_convert_fusion.3
  37.3 0.9 %collective-permute-start.4 = (f16[168,256]{1,0:T(8,128)(2,1)S(1)}, f16[168,256]{1,0:T(8,128)(2,1)S(1)}, u32[]{:S(2)}, u32[]{:S(2)}) collective-permute-start(f16[168,256]{1,0:T(8,128)(2,1)S(1)} %get-tuple-element.37), channel_id=1, source_target_pairs={{0,8},{1,9},{2,10},{3,11},{4,12},{5,13},{6,14},{7,15},{8,0},{9,1},... | collective-permute-start | bytes 258056 | tf_op jit(solution)/shard_map/ppermute | solution.py:352
  38.2 3.7 %collective-permute-done.4 = f16[168,256]{1,0:T(8,128)(2,1)S(1)} collective-permute-done((f16[168,256]{1,0:T(8,128)(2,1)S(1)}, f16[168,256]{1,0:T(8,128)(2,1)S(1)}, u32[]{:S(2)}, u32[]{:S(2)}) %collective-permute-start.4) | collective-permute-done | bytes 86048 | tf_op jit(solution)/shard_map/ppermute | solution.py:352
  41.9 0.1 collective-permute-start.5
  42.0 1.4 %collective-permute-done.5.other = f32[160,256]{1,0:T(8,128)S(1)} collective-permute-done((f32[160,256]{1,0:T(8,128)S(1)}, f32[160,256]{1,0:T(8,128)S(1)}, u32[]{:S(2)}, u32[]{:S(2)}) %collective-permute-start.5) | collective-permute-done | bytes 163872 | tf_op jit(solution)/shard_map/ppermute | solution.py:352
  43.4 0.8 %outputs.1 = (f32[64,128]{1,0:T(8,128)}, f32[256,256]{1,0:T(8,128)}) custom-call(f32[160,256]{1,0:T(8,128)S(1)} %sum_x.1.own, f32[160,256]{1,0:T(8,128)S(1)} %collective-permute-done.5.other), custom_call_target="tpu_custom_call" | custom-call | tf_op jit(solution)/shard_map/outputs/pallas_call | solution.py:406
  (6 shorter events, 0.1 us)
Async XLA Ops:
  22.8 3.1 %collective-permute-start = (f32[4,128,256]{2,1,0:T(8,128)S(1)}, f32[4,128,256]{2,1,0:T(8,128)S(1)}, u32[]{:S(2)}, u32[]{:S(2)}) collective-permute-start(f32[4,128,256]{2,1,0:T(8,128)S(1)} %get-tuple-element.25), channel_id=1, source_target_pairs={{0,4},{1,5},{2,6},{3,7},{4,0},{5,1},{6,2},{7,3},{8,12},{9,13},{10,... | collective-permute-start | bytes 1572872 | tf_op jit(solution)/shard_map/ppermute | solution.py:352
  26.3 7.3 %collective-permute-start.3 = (f16[168,256]{1,0:T(8,128)(2,1)S(1)}, f16[168,256]{1,0:T(8,128)(2,1)S(1)}, u32[]{:S(2)}, u32[]{:S(2)}) collective-permute-start(f16[168,256]{1,0:T(8,128)(2,1)S(1)} %reduce-precision_convert_fusion), channel_id=1, source_target_pairs={{0,3},{1,2},{2,1},{3,0},{4,7},{5,6},{6,5},{7,4},{8,11},{9,10},{10,... | collective-permute-start | bytes 258056 | tf_op jit(solution)/shard_map/ppermute | solution.py:352
  27.3 9.7 %collective-permute-start.2 = (f16[168,256]{1,0:T(8,128)(2,1)S(1)}, f16[168,256]{1,0:T(8,128)(2,1)S(1)}, u32[]{:S(2)}, u32[]{:S(2)}) collective-permute-start(f16[168,256]{1,0:T(8,128)(2,1)S(1)} %reduce-precision_convert_fusion.1), channel_id=1, source_target_pairs={{0,2},{1,3},{2,0},{3,1},{4,6},{5,7},{6,4},{7,5},{8,10},{9,11},{10,... | collective-permute-start | bytes 258056 | tf_op jit(solution)/shard_map/ppermute | solution.py:352
  28.6 8.4 %collective-permute-start.1 = (f16[168,256]{1,0:T(8,128)(2,1)S(1)}, f16[168,256]{1,0:T(8,128)(2,1)S(1)}, u32[]{:S(2)}, u32[]{:S(2)}) collective-permute-start(f16[168,256]{1,0:T(8,128)(2,1)S(1)} %reduce-precision_convert_fusion.2), channel_id=1, source_target_pairs={{0,1},{1,0},{2,3},{3,2},{4,5},{5,4},{6,7},{7,6},{8,9},{9,8},{10,11... | collective-permute-start | bytes 258056 | tf_op jit(solution)/shard_map/ppermute | solution.py:352
  37.3 4.6 %collective-permute-start.4 = (f16[168,256]{1,0:T(8,128)(2,1)S(1)}, f16[168,256]{1,0:T(8,128)(2,1)S(1)}, u32[]{:S(2)}, u32[]{:S(2)}) collective-permute-start(f16[168,256]{1,0:T(8,128)(2,1)S(1)} %get-tuple-element.37), channel_id=1, source_target_pairs={{0,8},{1,9},{2,10},{3,11},{4,12},{5,13},{6,14},{7,15},{8,0},{9,1},... | collective-permute-start | bytes 258056 | tf_op jit(solution)/shard_map/ppermute | solution.py:352
  41.9 1.5 %collective-permute-start.5 = (f32[160,256]{1,0:T(8,128)S(1)}, f32[160,256]{1,0:T(8,128)S(1)}, u32[]{:S(2)}, u32[]{:S(2)}) collective-permute-start(f32[160,256]{1,0:T(8,128)S(1)} %sum_x.1.own), channel_id=1, source_target_pairs={{0,4},{1,5},{2,6},{3,7},{4,0},{5,1},{6,2},{7,3},{8,12},{9,13},{10,... | collective-permute-start | bytes 491528 | tf_op jit(solution)/shard_map/ppermute | solution.py:352

commit v10 on v9

--- a/solution.py
+++ b/solution.py
@@ -27,15 +27,11 @@
     return lax.dot_general(left, right, NT, preferred_element_type=F32)
 
 
-def pair_weights(w_embed):
+def turned_weights(w_embed):
     turned = jnp.transpose(w_embed.astype(F32)).astype(BF16)
-    row, lane = iota((256, 512), 0), iota((256, 512), 1)
-    same = (row // 64 == lane // 128) & (row % 4 == lane // 32 % 4)
-    same = same & (row // 16 % 4 == lane // 8 % 4) & (row // 4 % 4 == lane % 4)
-    halves = []
-    for half in range(2):
-        halves.append(mm(turned, jnp.where(same & (lane // 4 % 2 == half), 1.0, 0.0).astype(BF16)))
-    return jnp.concatenate(halves, axis=0).astype(BF16)
+    row, lane = iota((256, 256), 0), iota((256, 256), 1)
+    same = (row // 64 == lane // 64) & (row % 4 == lane // 16 % 4) & (row // 4 % 16 == lane % 16)
+    return mm(turned, jnp.where(same, 1.0, 0.0).astype(BF16)).astype(BF16)
 
 
 def sigmoid(value):
@@ -50,24 +46,29 @@
 def forward_kernel(
     facies_hbm, prior_hbm, recon_hbm, w_embed_hbm, w_conv_hbm, w_head_hbm,
     block, one_hot, pre_embed, hidden, pre_conv, w_conv, w_head,
-    facies, prior, recon, w_embed, packed, sem
+    facies, prior, recon, w_embed, packed, conv_turned, sem
 ):
     blocks = facies.shape[0]
     loads = [
         pltpu.make_async_copy(facies_hbm.at[:, pl.ds(b * 128, 128)], facies.at[b], sem.at[b]) for b in range(blocks)
     ]
-    for load in loads:
-        load.start()
     others = []
     for source, target in (
         (w_embed_hbm, w_embed), (w_conv_hbm, w_conv), (prior_hbm, prior), (recon_hbm, recon), (w_head_hbm, w_head)
     ):
         others.append(pltpu.make_async_copy(source, target, sem.at[blocks + len(others)]))
+    for load in others[:2] + loads:
+        load.start()
+    others[0].wait()
+    packed[...] = turned_weights(w_embed[...])
+    others[1].wait()
+    conv_turned[...] = jnp.transpose(w_conv[...].astype(F32)).astype(BF16)
+    low = iota((8, 256), 0) < 4
     for half in range(2):
         for load in loads[half * blocks // 2 : (half + 1) * blocks // 2]:
             load.wait()
         if half == 0:
-            for load in others:
+            for load in others[2:]:
                 load.start()
         for t in range(8):
             dx2, dx = t // 4, t % 4
@@ -78,27 +79,33 @@
             ]
             turned = jnp.transpose(jnp.concatenate(rows, axis=0).astype(F32))
             for cp in range(4):
-                part = jnp.concatenate([turned[dy * 32 + cp * 8 : dy * 32 + cp * 8 + 8] for dy in range(4)], axis=0)
-                part = part.astype(BF16)
-                for k in range(LEVELS):
-                    hot = jnp.where(part == BF16(k), BF16(1.0), BF16(0.0))
-                    for dy2 in range(2):
-                        at = (2 * dx2 + dy2) * 256 + half * 128
-                        one_hot[cp, pl.ds(dx * 128 + k * 32, 32), pl.ds(at, 128)] = hot[:, dy2 * 128 : dy2 * 128 + 128]
-    others[0].wait()
-    packed[...] = pair_weights(w_embed[...])
-    others[1].wait()
-    conv_turned = jnp.transpose(w_conv[...].astype(F32)).astype(BF16)
+                part = [turned[dy * 32 + cp * 8 : dy * 32 + cp * 8 + 8] for dy in range(4)]
+                swapped = [pltpu.roll(piece, 4, 0) for piece in part]
+                for dz2 in range(2):
+                    pieces = [
+                        jnp.where(low, part[dy], swapped[dy + 1]) if dz2 == 0 else jnp.where(low, swapped[dy], part[dy + 1])
+                        for dy in (0, 2)
+                    ]
+                    cells = jnp.concatenate(pieces, axis=0).astype(BF16)
+                    for k in range(LEVELS):
+                        hot = jnp.where(cells == BF16(k), BF16(1.0), BF16(0.0))
+                        for dy2 in range(2):
+                            at = (2 * dx2 + dy2) * 256 + half * 128
+                            one_hot[2 * cp + dz2, pl.ds(dx * 64 + k * 16, 16), pl.ds(at, 128)] = hot[
+                                :, dy2 * 128 : dy2 * 128 + 128
+                            ]
     sums = jnp.zeros((256, 128), F32)
     for cp in range(4):
-        for dx2 in range(2):
-            at = pl.ds(dx2 * 512, 512)
-            pre = mm(packed[...], one_hot[cp, :, at])
-            pre_embed[cp, :, at] = pre
-            act = (pre * sigmoid(pre)).astype(BF16)
-            hidden[cp, 2 * dx2] = act[:, :256]
-            hidden[cp, 2 * dx2 + 1] = act[:, 256:]
-        pre = mm(conv_turned, hidden[cp].reshape(1024, 256))
+        for dz2 in range(2):
+            rows = pl.ds(dz2 * 128, 128)
+            for dx2 in range(2):
+                at = pl.ds(dx2 * 512, 512)
+                pre = mm(packed[...], one_hot[2 * cp + dz2, :, at])
+                pre_embed[cp, rows, at] = pre
+                act = (pre * sigmoid(pre)).astype(BF16)
+                hidden[cp, 2 * dx2, rows, :] = act[:, :256]
+                hidden[cp, 2 * dx2 + 1, rows, :] = act[:, 256:]
+        pre = mm(conv_turned[...], hidden[cp].reshape(1024, 256))
         pre_conv[cp] = pre
         act = pre * sigmoid(pre)
         sums = sums + act[:, :128] + act[:, 128:]
@@ -171,17 +178,17 @@
 
 
 def embed_kernel(grads, w_conv, pre_embed, one_hot, embed_out):
-    embed_total = None
+    embed = None
     for cp in range(4):
         signals = []
         for dx2 in range(2):
             back_rows = mm(w_conv[pl.ds(dx2 * 512, 512), :], grads[cp])
             back_rows = jnp.concatenate([back_rows[:256], back_rows[256:]], axis=1)
             signals.append((back_rows * silu_slope(pre_embed[cp, :, pl.ds(dx2 * 512, 512)])).astype(BF16))
-        term = mm_nt(one_hot[cp], jnp.concatenate(signals, axis=1))
-        embed_total = term if cp == 0 else embed_total + term
-    pairs = embed_total.reshape(64, 8, 256)
-    embed = (pairs[:, :4, :128] + pairs[:, 4:, 128:]).reshape(256, 128)
+        signal = jnp.concatenate(signals, axis=1)
+        for dz2 in range(2):
+            term = mm_nt(one_hot[2 * cp + dz2], signal[dz2 * 128 : dz2 * 128 + 128])
+            embed = term if embed is None else embed + term
     half = embed_out.shape[1]
     depth = 2 * half // LEVELS
     for f in range(embed_out.shape[0]):
@@ -278,7 +285,7 @@
 VMEM = pl.BlockSpec(memory_space=pltpu.VMEM)
 HBM = pl.BlockSpec(memory_space=pltpu.HBM)
 SAVED = (
-    ((4, 512, 1024), BF16),
+    ((8, 256, 1024), BF16),
     ((4, 256, 1024), F32),
     ((4, 4, 256, 256), BF16),
     ((4, 256, 256), F32),
@@ -302,7 +309,8 @@
             pltpu.VMEM(prior_draws.shape, BF16),
             pltpu.VMEM(recon_grad.shape, BF16),
             pltpu.VMEM(w_embed.shape, BF16),
-            pltpu.VMEM((256, 512), BF16),
+            pltpu.VMEM((128, 256), BF16),
+            pltpu.VMEM((256, 1024), BF16),
             pltpu.SemaphoreType.DMA((lanes // 128 + 5,)),
         ],
         compiler_params=pltpu.CompilerParams(vmem_limit_bytes=30 * 2**20),

time: 44.3 us -> 44.1 us (level)
  transfers between devices with their start and end apart: 6 -> 6, of which waited for: 4 -> 4; matrix products, arithmetic and copies ran while one was open for 0% -> 0% of each run, Pallas kernels for 6% -> 7%
where the time goes in v10:
time: 44.1 us; the launch traced here: 43.9 us
  blocking collectives  14.8 us (34%)
  waiting for transfers between devices  11.2 us (25%)
  Pallas kernels  11 us (25%)
  starting transfers between devices  5.72 us (13%)
  between operations  0.75 us (2%)
    all_to_all x1, blocking collectives, gather_blocks(): return lax.all_to_all(copies, GROUP, 0, 0, tiled=True)  14.8 us
    ppermute x6, waiting for transfers between devices, exchange(): return lax.ppermute(block, GROUP, pairs)  11.2 us
    ppermute x6, starting transfers between devices, exchange(): return lax.ppermute(block, GROUP, pairs)  5.72 us
    pallas_call x1, Pallas kernels, forward(): pl.pallas_call(forward_kernel, out_shape=(pltpu.VMEM((samples, 2 * latent...  4.96 us
    pallas_call x1, Pallas kernels, embed_gradient(): pl.pallas_call(embed_kernel, out_shape=pltpu.VMEM((fsdp, 256 // fsdp // 2...  2.94 us
    pallas_call x1, Pallas kernels, backward(): pl.pallas_call(lambda *refs: backward_kernel(sizes, *refs), out_shape=(pa...  1.98 us
  transfers between devices with their start and end apart: 6, of which 4 were waited for; matrix products, arithmetic and copies ran while one was open for 0% of the time, Pallas kernels for 7%

profile of v10, /device:TPU:0, one launch (start us, length us, event | category | flops | bytes accessed | tf_op | source)
XLA Modules:
  0.0 43.9 jit_solution(4028767084681257395)
XLA Ops:
  0.6 5.0 %forward.1 = (bf16[4,1280]{1,0:T(4,128)(2,1)S(1)}, bf16[8,256,1024]{2,1,0:T(8,128)(2,1)S(1)}, f32[4,256,1024]{2,1,0:T(8,128)S(1)}, bf16[4,4,256,256]{3,2,1,0:T(8...) custom-call(s32[256,2048]{1,0:T(8,128)} %bitcast.1, ...), custom_call_target="tpu_custom_call" | custom-call | tf_op jit(solution)/shard_map/forward/pallas_call | solution.py:300
  5.7 14.8 %all_to_all.5.refs_0_ = bf16[16,4,1280]{2,1,0:T(4,128)(2,1)S(1)} all-to-all(bf16[16,4,1280]{2,1,0:T(4,128)(2,1)S(1)} %broadcast_in_dim.2), channel_id=1, replica_groups=mesh['groups'=2,'dp'=4,'fsdp'=4] {'dp','fsdp'}, dimensions={0} | all-to-all | bytes 327680 | tf_op jit(solution)/shard_map/all_to_all | solution.py:365
  20.4 2.0 %backward.1 = (f32[4,128,256]{2,1,0:T(8,128)S(1)}, f32[4,128,256]{2,1,0:T(8,128)S(1)}, bf16[4,256,256]{2,1,0:T(8,128)(2,1)S(1)}, f32[64,512]{1,0:T(8,128)}) custom-call(bf16[16,4,1280]{2,1,0:T(4,128)(2,1)S(1)} %all_to_all.5.refs_0_, bf16[4,4,256,256]{3,2,1,0:T(8,128)(2,1)S(1)} %get-tuple-element.21.refs_1_, f32[4,256,256]{2,1,0:T(8,128)S(1)} %get-tuple-element.22.refs_2_, ...), custom_call_target="tpu_custom_call" | custom-call | tf_op jit(solution)/shard_map/backward/pallas_call | solution.py:325
  22.4 0.3 collective-permute-start
  22.7 2.9 %embed_gradient.1.embed = f32[4,32,256]{2,1,0:T(8,128)S(1)} custom-call(bf16[4,256,256]{2,1,0:T(8,128)(2,1)S(1)} %get-tuple-element.26.grads, bf16[1024,256]{1,0:T(8,128)(2,1)S(1)} %get-tuple-element.27.w_conv, f32[4,256,1024]{2,1,0:T(8,128)S(1)} %get-tuple-element.28.pre_embed, bf16[8,256,1024]{2,1,0:T(8,128)(2,1)S(1)} %get-tuple-element.29.one_hot), custom_call_target="tpu_custom_call" | custom-call | flops 1600000000 | bytes 10485760 | tf_op jit(solution)/shard_map/embed_gradient/pallas_call | solution.py:339
  25.7 0.0 collective-permute-done.other
  25.7 0.2 scale.1
  25.9 0.1 reduce-precision_convert_fusion.1
  26.0 0.1 reduce-precision_convert_fusion
  26.1 1.0 %collective-permute-start.3 = (f16[168,256]{1,0:T(8,128)(2,1)S(1)}, f16[168,256]{1,0:T(8,128)(2,1)S(1)}, u32[]{:S(2)}, u32[]{:S(2)}) collective-permute-start(f16[168,256]{1,0:T(8,128)(2,1)S(1)} %reduce-precision_convert_fusion), channel_id=1, source_target_pairs={{0,3},{1,2},{2,1},{3,0},{4,7},{5,6},{6,5},{7,4},{8,11},{9,10},{10,... | collective-permute-start | bytes 258056 | tf_op jit(solution)/shard_map/ppermute | solution.py:360
  27.1 1.2 %collective-permute-start.2 = (f16[168,256]{1,0:T(8,128)(2,1)S(1)}, f16[168,256]{1,0:T(8,128)(2,1)S(1)}, u32[]{:S(2)}, u32[]{:S(2)}) collective-permute-start(f16[168,256]{1,0:T(8,128)(2,1)S(1)} %reduce-precision_convert_fusion.1), channel_id=1, source_target_pairs={{0,2},{1,3},{2,0},{3,1},{4,6},{5,7},{6,4},{7,5},{8,10},{9,11},{10,... | collective-permute-start | bytes 258056 | tf_op jit(solution)/shard_map/ppermute | solution.py:360
  28.3 0.1 reduce-precision_convert_fusion.2
  28.4 2.3 %collective-permute-start.1 = (f16[168,256]{1,0:T(8,128)(2,1)S(1)}, f16[168,256]{1,0:T(8,128)(2,1)S(1)}, u32[]{:S(2)}, u32[]{:S(2)}) collective-permute-start(f16[168,256]{1,0:T(8,128)(2,1)S(1)} %reduce-precision_convert_fusion.2), channel_id=1, source_target_pairs={{0,1},{1,0},{2,3},{3,2},{4,5},{5,4},{6,7},{7,6},{8,9},{9,8},{10,11... | collective-permute-start | bytes 258056 | tf_op jit(solution)/shard_map/ppermute | solution.py:360
  30.7 2.7 %collective-permute-done.3 = f16[168,256]{1,0:T(8,128)(2,1)S(1)} collective-permute-done((f16[168,256]{1,0:T(8,128)(2,1)S(1)}, f16[168,256]{1,0:T(8,128)(2,1)S(1)}, u32[]{:S(2)}, u32[]{:S(2)}) %collective-permute-start.3) | collective-permute-done | bytes 86048 | tf_op jit(solution)/shard_map/ppermute | solution.py:360
  33.4 3.3 %collective-permute-done.2 = f16[168,256]{1,0:T(8,128)(2,1)S(1)} collective-permute-done((f16[168,256]{1,0:T(8,128)(2,1)S(1)}, f16[168,256]{1,0:T(8,128)(2,1)S(1)}, u32[]{:S(2)}, u32[]{:S(2)}) %collective-permute-start.2) | collective-permute-done | bytes 86048 | tf_op jit(solution)/shard_map/ppermute | solution.py:360
  36.8 0.0 collective-permute-done.1
  36.8 0.2 sum_z.1
  37.0 0.1 reduce-precision_convert_fusion.3
  37.1 0.8 %collective-permute-start.4 = (f16[168,256]{1,0:T(8,128)(2,1)S(1)}, f16[168,256]{1,0:T(8,128)(2,1)S(1)}, u32[]{:S(2)}, u32[]{:S(2)}) collective-permute-start(f16[168,256]{1,0:T(8,128)(2,1)S(1)} %get-tuple-element.37), channel_id=1, source_target_pairs={{0,8},{1,9},{2,10},{3,11},{4,12},{5,13},{6,14},{7,15},{8,0},{9,1},... | collective-permute-start | bytes 258056 | tf_op jit(solution)/shard_map/ppermute | solution.py:360
  37.9 3.7 %collective-permute-done.4 = f16[168,256]{1,0:T(8,128)(2,1)S(1)} collective-permute-done((f16[168,256]{1,0:T(8,128)(2,1)S(1)}, f16[168,256]{1,0:T(8,128)(2,1)S(1)}, u32[]{:S(2)}, u32[]{:S(2)}) %collective-permute-start.4) | collective-permute-done | bytes 86048 | tf_op jit(solution)/shard_map/ppermute | solution.py:360
  41.7 0.1 collective-permute-start.5
  41.8 1.4 %collective-permute-done.5.other = f32[160,256]{1,0:T(8,128)S(1)} collective-permute-done((f32[160,256]{1,0:T(8,128)S(1)}, f32[160,256]{1,0:T(8,128)S(1)}, u32[]{:S(2)}, u32[]{:S(2)}) %collective-permute-start.5) | collective-permute-done | bytes 163872 | tf_op jit(solution)/shard_map/ppermute | solution.py:360
  43.1 0.8 %outputs.1 = (f32[64,128]{1,0:T(8,128)}, f32[256,256]{1,0:T(8,128)}) custom-call(f32[160,256]{1,0:T(8,128)S(1)} %sum_x.1.own, f32[160,256]{1,0:T(8,128)S(1)} %collective-permute-done.5.other), custom_call_target="tpu_custom_call" | custom-call | tf_op jit(solution)/shard_map/outputs/pallas_call | solution.py:414
  (6 shorter events, 0.1 us)
Async XLA Ops:
  22.4 3.3 %collective-permute-start = (f32[4,128,256]{2,1,0:T(8,128)S(1)}, f32[4,128,256]{2,1,0:T(8,128)S(1)}, u32[]{:S(2)}, u32[]{:S(2)}) collective-permute-start(f32[4,128,256]{2,1,0:T(8,128)S(1)} %get-tuple-element.25), channel_id=1, source_target_pairs={{0,4},{1,5},{2,6},{3,7},{4,0},{5,1},{6,2},{7,3},{8,12},{9,13},{10,... | collective-permute-start | bytes 1572872 | tf_op jit(solution)/shard_map/ppermute | solution.py:360
  26.1 7.3 %collective-permute-start.3 = (f16[168,256]{1,0:T(8,128)(2,1)S(1)}, f16[168,256]{1,0:T(8,128)(2,1)S(1)}, u32[]{:S(2)}, u32[]{:S(2)}) collective-permute-start(f16[168,256]{1,0:T(8,128)(2,1)S(1)} %reduce-precision_convert_fusion), channel_id=1, source_target_pairs={{0,3},{1,2},{2,1},{3,0},{4,7},{5,6},{6,5},{7,4},{8,11},{9,10},{10,... | collective-permute-start | bytes 258056 | tf_op jit(solution)/shard_map/ppermute | solution.py:360
  27.1 9.7 %collective-permute-start.2 = (f16[168,256]{1,0:T(8,128)(2,1)S(1)}, f16[168,256]{1,0:T(8,128)(2,1)S(1)}, u32[]{:S(2)}, u32[]{:S(2)}) collective-permute-start(f16[168,256]{1,0:T(8,128)(2,1)S(1)} %reduce-precision_convert_fusion.1), channel_id=1, source_target_pairs={{0,2},{1,3},{2,0},{3,1},{4,6},{5,7},{6,4},{7,5},{8,10},{9,11},{10,... | collective-permute-start | bytes 258056 | tf_op jit(solution)/shard_map/ppermute | solution.py:360
  28.4 8.4 %collective-permute-start.1 = (f16[168,256]{1,0:T(8,128)(2,1)S(1)}, f16[168,256]{1,0:T(8,128)(2,1)S(1)}, u32[]{:S(2)}, u32[]{:S(2)}) collective-permute-start(f16[168,256]{1,0:T(8,128)(2,1)S(1)} %reduce-precision_convert_fusion.2), channel_id=1, source_target_pairs={{0,1},{1,0},{2,3},{3,2},{4,5},{5,4},{6,7},{7,6},{8,9},{9,8},{10,11... | collective-permute-start | bytes 258056 | tf_op jit(solution)/shard_map/ppermute | solution.py:360
  37.1 4.6 %collective-permute-start.4 = (f16[168,256]{1,0:T(8,128)(2,1)S(1)}, f16[168,256]{1,0:T(8,128)(2,1)S(1)}, u32[]{:S(2)}, u32[]{:S(2)}) collective-permute-start(f16[168,256]{1,0:T(8,128)(2,1)S(1)} %get-tuple-element.37), channel_id=1, source_target_pairs={{0,8},{1,9},{2,10},{3,11},{4,12},{5,13},{6,14},{7,15},{8,0},{9,1},... | collective-permute-start | bytes 258056 | tf_op jit(solution)/shard_map/ppermute | solution.py:360
  41.7 1.5 %collective-permute-start.5 = (f32[160,256]{1,0:T(8,128)S(1)}, f32[160,256]{1,0:T(8,128)S(1)}, u32[]{:S(2)}, u32[]{:S(2)}) collective-permute-start(f32[160,256]{1,0:T(8,128)S(1)} %sum_x.1.own), channel_id=1, source_target_pairs={{0,4},{1,5},{2,6},{3,7},{4,0},{5,1},{6,2},{7,3},{8,12},{9,13},{10,... | collective-permute-start | bytes 491528 | tf_op jit(solution)/shard_map/ppermute | solution.py:360

commit v11 on v10

--- a/solution.py
+++ b/solution.py
@@ -1,3 +1,5 @@
+import functools
+
 import jax
 import jax.numpy as jnp
 from jax import lax
@@ -30,7 +32,8 @@
 def turned_weights(w_embed):
     turned = jnp.transpose(w_embed.astype(F32)).astype(BF16)
     row, lane = iota((256, 256), 0), iota((256, 256), 1)
-    same = (row // 64 == lane // 64) & (row % 4 == lane // 16 % 4) & (row // 4 % 16 == lane % 16)
+    dx, k = row // 64, row % 4
+    same = lane == jnp.where(k < 3, dx * 48 + k * 16, 192 + dx * 16) + row // 4 % 16
     return mm(turned, jnp.where(same, 1.0, 0.0).astype(BF16)).astype(BF16)
 
 
@@ -89,11 +92,10 @@
                     cells = jnp.concatenate(pieces, axis=0).astype(BF16)
                     for k in range(LEVELS):
                         hot = jnp.where(cells == BF16(k), BF16(1.0), BF16(0.0))
+                        first = dx * 48 + k * 16 if k < 3 else 192 + dx * 16
                         for dy2 in range(2):
                             at = (2 * dx2 + dy2) * 256 + half * 128
-                            one_hot[2 * cp + dz2, pl.ds(dx * 64 + k * 16, 16), pl.ds(at, 128)] = hot[
-                                :, dy2 * 128 : dy2 * 128 + 128
-                            ]
+                            one_hot[2 * cp + dz2, pl.ds(first, 16), pl.ds(at, 128)] = hot[:, dy2 * 128 : dy2 * 128 + 128]
     sums = jnp.zeros((256, 128), F32)
     for cp in range(4):
         for dz2 in range(2):
@@ -179,6 +181,7 @@
 
 def embed_kernel(grads, w_conv, pre_embed, one_hot, embed_out):
     embed = None
+    ones = jnp.ones((16, 1024), BF16)
     for cp in range(4):
         signals = []
         for dx2 in range(2):
@@ -187,15 +190,19 @@
             signals.append((back_rows * silu_slope(pre_embed[cp, :, pl.ds(dx2 * 512, 512)])).astype(BF16))
         signal = jnp.concatenate(signals, axis=1)
         for dz2 in range(2):
-            term = mm_nt(one_hot[2 * cp + dz2], signal[dz2 * 128 : dz2 * 128 + 128])
+            rows = jnp.concatenate([one_hot[2 * cp + dz2, pl.ds(0, 192), :], ones], axis=0)
+            term = mm_nt(rows, signal[dz2 * 128 : dz2 * 128 + 128])
             embed = term if embed is None else embed + term
-    half = embed_out.shape[1]
-    depth = 2 * half // LEVELS
-    for f in range(embed_out.shape[0]):
-        dx, at = f * 2 * half // 64, f * 2 * half % 64 // LEVELS
-        share = jnp.concatenate([embed[dx * 64 + k * 16 + at :][:depth] for k in range(LEVELS)], axis=0)
+    shares = embed_out.shape[0]
+    depth = 64 // shares
+    half = 3 * depth // 2
+    embed_out[...] = jnp.zeros(embed_out.shape, F32)
+    for f in range(shares):
+        dx, at = f * 4 // shares, f * depth % 16
+        share = jnp.concatenate([embed[dx * 48 + k * 16 + at :][:depth] for k in range(3)], axis=0)
         for side in range(2):
-            embed_out[f, :, pl.ds(side * 128, 128)] = share[side * half : (side + 1) * half]
+            embed_out[f, pl.ds(0, half), pl.ds(side * 128, 128)] = share[side * half : (side + 1) * half]
+        embed_out[f, pl.ds(embed_out.shape[1] - 8, 8), pl.ds(0, 128)] = embed[192:200]
 
 
 def exponent_of(part):
@@ -206,30 +213,28 @@
     return jnp.clip(jnp.floor(jnp.log2(jnp.maximum(top, 1e-37))) - 14.0, -124.0, 114.0)
 
 
-def store_coded(coded, part):
-    rows = part.shape[0]
-    conv_rows = rows * 4 // 5
-    conv, embed = part[:conv_rows], part[conv_rows:]
-    steps = exponent_of(conv), exponent_of(embed)
-    store_scaled(coded, part, steps)
-
-
-def store_scaled(coded, part, steps):
-    rows, spare = part.shape[0], coded.shape[0] - part.shape[0]
-    conv_rows = rows * 4 // 5
+def store_coded(coded, part, conv_rows):
+    store_scaled(coded, part, (exponent_of(part[:conv_rows]), exponent_of(part[conv_rows:])), conv_rows)
+
+
+def store_scaled(coded, part, steps, conv_rows):
+    last = part.shape[0] - 8
     coded[pl.ds(0, conv_rows), :] = part[:conv_rows] * jnp.exp2(-steps[0])
-    coded[pl.ds(conv_rows, rows - conv_rows), :] = part[conv_rows:] * jnp.exp2(-steps[1])
-    tail = jnp.where(iota((spare, coded.shape[1]), 0) == 0, steps[0], steps[1])
-    coded[pl.ds(rows, spare), :] = tail
-
-
-def load_coded(coded, rows):
-    conv_rows = rows * 4 // 5
-    conv_scale = jnp.exp2(coded[pl.ds(rows, 1), :])
-    embed_scale = jnp.exp2(coded[pl.ds(rows + 1, 1), :])
-    return jnp.concatenate(
-        [coded[pl.ds(0, conv_rows), :] * conv_scale, coded[pl.ds(conv_rows, rows - conv_rows), :] * embed_scale], axis=0
-    )
+    coded[pl.ds(conv_rows, last - conv_rows), :] = part[conv_rows:last] * jnp.exp2(-steps[1])
+    total = part[last:, :128] * jnp.exp2(-steps[1])
+    high = total.astype(BF16).astype(F32)
+    row = iota((8, 256), 0)
+    tail = jnp.where(row == 1, steps[0], steps[1])
+    coded[pl.ds(last, 8), :] = jnp.where(row == 0, jnp.concatenate([high, total - high], axis=1), tail)
+
+
+def load_coded(coded, conv_rows):
+    last = coded.shape[0] - 8
+    embed_scale = jnp.exp2(coded[pl.ds(last + 2, 1), :])
+    total = coded[pl.ds(last, 8), pl.ds(0, 128)] + coded[pl.ds(last, 8), pl.ds(128, 128)]
+    total = jnp.where(iota((8, 256), 0) == 0, jnp.concatenate([total, jnp.zeros((8, 128), F32)], axis=1), 0.0)
+    embed = jnp.concatenate([coded[pl.ds(conv_rows, last - conv_rows), :], total], axis=0) * embed_scale
+    return jnp.concatenate([coded[pl.ds(0, conv_rows), :] * jnp.exp2(coded[pl.ds(last + 1, 1), :]), embed], axis=0)
 
 
 def scale_kernel(keep, other, embed, own, *coded):
@@ -242,38 +247,40 @@
 
     own[...] = share(here)
     for place, target in enumerate(coded):
-        store_scaled(target, share(here ^ (place + 1)), steps)
-
-
-def first_sum_kernel(own, *refs):
+        store_scaled(target, share(here ^ (place + 1)), steps, keep.shape[1])
+
+
+def first_sum_kernel(conv_rows, own, *refs):
     *received, coded = refs
     total = own[...]
     for part in received:
-        total = total + load_coded(part, total.shape[0])
-    store_coded(coded, total)
-
-
-def next_sum_kernel(mine, other, total, *coded):
-    rows = total.shape[0]
-    summed = load_coded(mine, rows) + load_coded(other, rows)
+        total = total + load_coded(part, conv_rows)
+    store_coded(coded, total, conv_rows)
+
+
+def next_sum_kernel(conv_rows, mine, other, total, *coded):
+    summed = load_coded(mine, conv_rows) + load_coded(other, conv_rows)
     total[...] = summed
     if coded:
-        store_coded(coded[0], summed)
+        store_coded(coded[0], summed, conv_rows)
 
 
 def output_kernel(own, other, grad_embed, grad_conv):
-    rows = own.shape[0]
-    conv_rows, half = rows * 4 // 5, rows // 5
+    conv_rows, count = grad_conv.shape[0] // 2, grad_embed.shape[0]
     core_zero = lax.rem(lax.axis_index("dp"), 2) == 0
     grad_conv[pl.ds(0, conv_rows), :] = jnp.where(core_zero, own[pl.ds(0, conv_rows), :], other[pl.ds(0, conv_rows), :])
     grad_conv[pl.ds(conv_rows, conv_rows), :] = jnp.where(
         core_zero, other[pl.ds(0, conv_rows), :], own[pl.ds(0, conv_rows), :]
     )
+    half, depth = 3 * count // 8, count // LEVELS
     embed = own[pl.ds(conv_rows, half), :] + other[pl.ds(conv_rows, half), :]
     embed = jnp.concatenate([embed[:, :128], embed[:, 128:]], axis=0)
-    count = 2 * half
+    last = own.shape[0] - 8
+    total = own[pl.ds(last, 1), pl.ds(0, 128)] + other[pl.ds(last, 1), pl.ds(0, 128)]
+    fourth = total - (embed[:depth] + embed[depth : 2 * depth] + embed[2 * depth :])
+    embed = jnp.concatenate([embed, fourth], axis=0)
     row, lane = iota((count, count), 0), iota((count, count), 1)
-    order = jnp.where(lane == row % LEVELS * (count // LEVELS) + row // LEVELS, 1.0, 0.0).astype(BF16)
+    order = jnp.where(lane == row % LEVELS * depth + row // LEVELS, 1.0, 0.0).astype(BF16)
     result = None
     for _ in range(3):
         term = embed.astype(BF16)
@@ -338,7 +345,7 @@
 def embed_gradient(fsdp, grads, w_conv, pre_embed, one_hot):
     return pl.pallas_call(
         embed_kernel,
-        out_shape=pltpu.VMEM((fsdp, 256 // fsdp // 2, 256), F32),
+        out_shape=pltpu.VMEM((fsdp, (96 // fsdp + 7) // 8 * 8 + 8, 256), F32),
         in_specs=[VMEM] * 4,
         out_specs=VMEM,
         compiler_params=pltpu.CompilerParams(vmem_limit_bytes=24 * 2**20),
@@ -382,21 +389,21 @@
 
 
 def reduce_to_owner(keep, other, embed, dp, fsdp):
-    rows, width = keep.shape[1] + embed.shape[1], keep.shape[2]
+    conv_rows, width = keep.shape[1:]
+    rows = conv_rows + embed.shape[1]
     plain = jax.ShapeDtypeStruct((rows, width), F32)
-    scaled = jax.ShapeDtypeStruct((rows + 8, width), F32)
-    own, *coded = local_kernel(scale_kernel, (plain,) + (scaled,) * (fsdp - 1), "scale", keep, other, embed)
+    own, *coded = local_kernel(scale_kernel, (plain,) + (plain,) * (fsdp - 1), "scale", keep, other, embed)
     received = [
         exchange(to_half(part)[1], dp, fsdp, 0, 0, place + 1).astype(F32) for place, part in enumerate(coded)
     ]
-    (coded,) = local_kernel(first_sum_kernel, (scaled,), "sum_z", own, *received)
+    (coded,) = local_kernel(functools.partial(first_sum_kernel, conv_rows), (plain,), "sum_z", own, *received)
     flip = 1
     while flip < dp // 2:
         mine, sent = to_half(coded)
         other = exchange(sent, dp, fsdp, flip, 0, 0).astype(F32)
         flip *= 2
-        outs = (plain, scaled) if flip < dp // 2 else (plain,)
-        total, *rest = local_kernel(next_sum_kernel, outs, "sum_x", mine, other)
+        outs = (plain,) * (2 if flip < dp // 2 else 1)
+        total, *rest = local_kernel(functools.partial(next_sum_kernel, conv_rows), outs, "sum_x", mine, other)
         coded = rest[0] if rest else None
     return total, exchange(total, dp, fsdp, 0, 1, 0)
 

time: 44.1 us -> 43.3 us (0.982)
  waiting for transfers between devices: 11.2 us -> 10.6 us
    ppermute x6, waiting for transfers between devices: 11.2 us -> 10.6 us  [exchange(): return lax.ppermute(block, GROUP, pairs)]
  transfers between devices with their start and end apart: 6 -> 6, of which waited for: 4 -> 4; matrix products, arithmetic and copies ran while one was open for 0% -> 0% of each run, Pallas kernels for 7% -> 6%
where the time goes in v11:
time: 43.3 us; the launch traced here: 43.1 us
  blocking collectives  14.8 us (34%)
  Pallas kernels  10.6 us (24%)
  waiting for transfers between devices  10.6 us (24%)
  starting transfers between devices  5.85 us (14%)
  between operations  0.76 us (2%)
    all_to_all x1, blocking collectives, gather_blocks(): return lax.all_to_all(copies, GROUP, 0, 0, tiled=True)  14.8 us
    ppermute x6, waiting for transfers between devices, exchange(): return lax.ppermute(block, GROUP, pairs)  10.6 us
    ppermute x6, starting transfers between devices, exchange(): return lax.ppermute(block, GROUP, pairs)  5.85 us
    pallas_call x1, Pallas kernels, forward(): pl.pallas_call(forward_kernel, out_shape=(pltpu.VMEM((samples, 2 * latent...  4.93 us
    pallas_call x1, Pallas kernels, embed_gradient(): pl.pallas_call(embed_kernel, out_shape=pltpu.VMEM((fsdp, (96 // fsdp + 7)...  2.55 us
    pallas_call x1, Pallas kernels, backward(): pl.pallas_call(lambda *refs: backward_kernel(sizes, *refs), out_shape=(pa...  1.98 us
  transfers between devices with their start and end apart: 6, of which 4 were waited for; matrix products, arithmetic and copies ran while one was open for 0% of the time, Pallas kernels for 6%

profile of v11, /device:TPU:0, one launch (start us, length us, event | category | flops | bytes accessed | tf_op | source)
XLA Modules:
  0.0 43.1 jit_solution(8574157722479026849)
XLA Ops:
  0.6 4.9 %forward.1 = (bf16[4,1280]{1,0:T(4,128)(2,1)S(1)}, bf16[8,256,1024]{2,1,0:T(8,128)(2,1)S(1)}, f32[4,256,1024]{2,1,0:T(8,128)S(1)}, bf16[4,4,256,256]{3,2,1,0:T(8...) custom-call(s32[256,2048]{1,0:T(8,128)} %bitcast.1, ...), custom_call_target="tpu_custom_call" | custom-call | tf_op jit(solution)/shard_map/forward/pallas_call | solution.py:307
  5.6 14.8 %all_to_all.5.refs_0_ = bf16[16,4,1280]{2,1,0:T(4,128)(2,1)S(1)} all-to-all(bf16[16,4,1280]{2,1,0:T(4,128)(2,1)S(1)} %broadcast_in_dim.2), channel_id=1, replica_groups=mesh['groups'=2,'dp'=4,'fsdp'=4] {'dp','fsdp'}, dimensions={0} | all-to-all | bytes 327680 | tf_op jit(solution)/shard_map/all_to_all | solution.py:372
  20.4 2.0 %backward.1 = (f32[4,128,256]{2,1,0:T(8,128)S(1)}, f32[4,128,256]{2,1,0:T(8,128)S(1)}, bf16[4,256,256]{2,1,0:T(8,128)(2,1)S(1)}, f32[64,512]{1,0:T(8,128)}) custom-call(bf16[16,4,1280]{2,1,0:T(4,128)(2,1)S(1)} %all_to_all.5.refs_0_, bf16[4,4,256,256]{3,2,1,0:T(8,128)(2,1)S(1)} %get-tuple-element.21.refs_1_, f32[4,256,256]{2,1,0:T(8,128)S(1)} %get-tuple-element.22.refs_2_, ...), custom_call_target="tpu_custom_call" | custom-call | tf_op jit(solution)/shard_map/backward/pallas_call | solution.py:332
  22.4 0.3 collective-permute-start
  22.7 2.6 %embed_gradient.1.embed = f32[4,32,256]{2,1,0:T(8,128)S(1)} custom-call(bf16[4,256,256]{2,1,0:T(8,128)(2,1)S(1)} %get-tuple-element.26.grads, bf16[1024,256]{1,0:T(8,128)(2,1)S(1)} %get-tuple-element.27.w_conv, f32[4,256,1024]{2,1,0:T(8,128)S(1)} %get-tuple-element.28.pre_embed, bf16[8,256,1024]{2,1,0:T(8,128)(2,1)S(1)} %get-tuple-element.29.one_hot), custom_call_target="tpu_custom_call" | custom-call | flops 1600000000 | bytes 10485760 | tf_op jit(solution)/shard_map/embed_gradient/pallas_call | solution.py:346
  25.3 0.0 collective-permute-done.other
  25.3 0.2 scale.1
  25.5 0.1 reduce-precision_convert_fusion.1
  25.6 0.1 reduce-precision_convert_fusion
  25.7 1.0 %collective-permute-start.3 = (f16[160,256]{1,0:T(8,128)(2,1)S(1)}, f16[160,256]{1,0:T(8,128)(2,1)S(1)}, u32[]{:S(2)}, u32[]{:S(2)}) collective-permute-start(f16[160,256]{1,0:T(8,128)(2,1)S(1)} %reduce-precision_convert_fusion), channel_id=1, source_target_pairs={{0,3},{1,2},{2,1},{3,0},{4,7},{5,6},{6,5},{7,4},{8,11},{9,10},{10,... | collective-permute-start | bytes 245768 | tf_op jit(solution)/shard_map/ppermute | solution.py:367
  26.7 1.2 %collective-permute-start.2 = (f16[160,256]{1,0:T(8,128)(2,1)S(1)}, f16[160,256]{1,0:T(8,128)(2,1)S(1)}, u32[]{:S(2)}, u32[]{:S(2)}) collective-permute-start(f16[160,256]{1,0:T(8,128)(2,1)S(1)} %reduce-precision_convert_fusion.1), channel_id=1, source_target_pairs={{0,2},{1,3},{2,0},{3,1},{4,6},{5,7},{6,4},{7,5},{8,10},{9,11},{10,... | collective-permute-start | bytes 245768 | tf_op jit(solution)/shard_map/ppermute | solution.py:367
  27.9 0.1 reduce-precision_convert_fusion.2
  28.0 2.3 %collective-permute-start.1 = (f16[160,256]{1,0:T(8,128)(2,1)S(1)}, f16[160,256]{1,0:T(8,128)(2,1)S(1)}, u32[]{:S(2)}, u32[]{:S(2)}) collective-permute-start(f16[160,256]{1,0:T(8,128)(2,1)S(1)} %reduce-precision_convert_fusion.2), channel_id=1, source_target_pairs={{0,1},{1,0},{2,3},{3,2},{4,5},{5,4},{6,7},{7,6},{8,9},{9,8},{10,11... | collective-permute-start | bytes 245768 | tf_op jit(solution)/shard_map/ppermute | solution.py:367
  30.3 2.6 %collective-permute-done.3 = f16[160,256]{1,0:T(8,128)(2,1)S(1)} collective-permute-done((f16[160,256]{1,0:T(8,128)(2,1)S(1)}, f16[160,256]{1,0:T(8,128)(2,1)S(1)}, u32[]{:S(2)}, u32[]{:S(2)}) %collective-permute-start.3) | collective-permute-done | bytes 81952 | tf_op jit(solution)/shard_map/ppermute | solution.py:367
  32.9 3.1 %collective-permute-done.2 = f16[160,256]{1,0:T(8,128)(2,1)S(1)} collective-permute-done((f16[160,256]{1,0:T(8,128)(2,1)S(1)}, f16[160,256]{1,0:T(8,128)(2,1)S(1)}, u32[]{:S(2)}, u32[]{:S(2)}) %collective-permute-start.2) | collective-permute-done | bytes 81952 | tf_op jit(solution)/shard_map/ppermute | solution.py:367
  36.0 0.0 collective-permute-done.1
  36.0 0.2 sum_z.1
  36.2 0.1 reduce-precision_convert_fusion.3
  36.3 1.0 %collective-permute-start.4 = (f16[160,256]{1,0:T(8,128)(2,1)S(1)}, f16[160,256]{1,0:T(8,128)(2,1)S(1)}, u32[]{:S(2)}, u32[]{:S(2)}) collective-permute-start(f16[160,256]{1,0:T(8,128)(2,1)S(1)} %get-tuple-element.37), channel_id=1, source_target_pairs={{0,8},{1,9},{2,10},{3,11},{4,12},{5,13},{6,14},{7,15},{8,0},{9,1},... | collective-permute-start | bytes 245768 | tf_op jit(solution)/shard_map/ppermute | solution.py:367
  37.2 3.6 %collective-permute-done.4 = f16[160,256]{1,0:T(8,128)(2,1)S(1)} collective-permute-done((f16[160,256]{1,0:T(8,128)(2,1)S(1)}, f16[160,256]{1,0:T(8,128)(2,1)S(1)}, u32[]{:S(2)}, u32[]{:S(2)}) %collective-permute-start.4) | collective-permute-done | bytes 81952 | tf_op jit(solution)/shard_map/ppermute | solution.py:367
  40.8 0.1 collective-permute-start.5
  40.9 1.4 %collective-permute-done.5.other = f32[160,256]{1,0:T(8,128)S(1)} collective-permute-done((f32[160,256]{1,0:T(8,128)S(1)}, f32[160,256]{1,0:T(8,128)S(1)}, u32[]{:S(2)}, u32[]{:S(2)}) %collective-permute-start.5) | collective-permute-done | bytes 163872 | tf_op jit(solution)/shard_map/ppermute | solution.py:367
  42.3 0.8 %outputs.1 = (f32[64,128]{1,0:T(8,128)}, f32[256,256]{1,0:T(8,128)}) custom-call(f32[160,256]{1,0:T(8,128)S(1)} %sum_x.1.own, f32[160,256]{1,0:T(8,128)S(1)} %collective-permute-done.5.other), custom_call_target="tpu_custom_call" | custom-call | tf_op jit(solution)/shard_map/outputs/pallas_call | solution.py:421
  (6 shorter events, 0.1 us)
Async XLA Ops:
  22.4 2.9 %collective-permute-start = (f32[4,128,256]{2,1,0:T(8,128)S(1)}, f32[4,128,256]{2,1,0:T(8,128)S(1)}, u32[]{:S(2)}, u32[]{:S(2)}) collective-permute-start(f32[4,128,256]{2,1,0:T(8,128)S(1)} %get-tuple-element.25), channel_id=1, source_target_pairs={{0,4},{1,5},{2,6},{3,7},{4,0},{5,1},{6,2},{7,3},{8,12},{9,13},{10,... | collective-permute-start | bytes 1572872 | tf_op jit(solution)/shard_map/ppermute | solution.py:367
  25.7 7.2 %collective-permute-start.3 = (f16[160,256]{1,0:T(8,128)(2,1)S(1)}, f16[160,256]{1,0:T(8,128)(2,1)S(1)}, u32[]{:S(2)}, u32[]{:S(2)}) collective-permute-start(f16[160,256]{1,0:T(8,128)(2,1)S(1)} %reduce-precision_convert_fusion), channel_id=1, source_target_pairs={{0,3},{1,2},{2,1},{3,0},{4,7},{5,6},{6,5},{7,4},{8,11},{9,10},{10,... | collective-permute-start | bytes 245768 | tf_op jit(solution)/shard_map/ppermute | solution.py:367
  26.7 9.3 %collective-permute-start.2 = (f16[160,256]{1,0:T(8,128)(2,1)S(1)}, f16[160,256]{1,0:T(8,128)(2,1)S(1)}, u32[]{:S(2)}, u32[]{:S(2)}) collective-permute-start(f16[160,256]{1,0:T(8,128)(2,1)S(1)} %reduce-precision_convert_fusion.1), channel_id=1, source_target_pairs={{0,2},{1,3},{2,0},{3,1},{4,6},{5,7},{6,4},{7,5},{8,10},{9,11},{10,... | collective-permute-start | bytes 245768 | tf_op jit(solution)/shard_map/ppermute | solution.py:367
  28.0 8.0 %collective-permute-start.1 = (f16[160,256]{1,0:T(8,128)(2,1)S(1)}, f16[160,256]{1,0:T(8,128)(2,1)S(1)}, u32[]{:S(2)}, u32[]{:S(2)}) collective-permute-start(f16[160,256]{1,0:T(8,128)(2,1)S(1)} %reduce-precision_convert_fusion.2), channel_id=1, source_target_pairs={{0,1},{1,0},{2,3},{3,2},{4,5},{5,4},{6,7},{7,6},{8,9},{9,8},{10,11... | collective-permute-start | bytes 245768 | tf_op jit(solution)/shard_map/ppermute | solution.py:367
  36.3 4.5 %collective-permute-start.4 = (f16[160,256]{1,0:T(8,128)(2,1)S(1)}, f16[160,256]{1,0:T(8,128)(2,1)S(1)}, u32[]{:S(2)}, u32[]{:S(2)}) collective-permute-start(f16[160,256]{1,0:T(8,128)(2,1)S(1)} %get-tuple-element.37), channel_id=1, source_target_pairs={{0,8},{1,9},{2,10},{3,11},{4,12},{5,13},{6,14},{7,15},{8,0},{9,1},... | collective-permute-start | bytes 245768 | tf_op jit(solution)/shard_map/ppermute | solution.py:367
  40.8 1.5 %collective-permute-start.5 = (f32[160,256]{1,0:T(8,128)S(1)}, f32[160,256]{1,0:T(8,128)S(1)}, u32[]{:S(2)}, u32[]{:S(2)}) collective-permute-start(f32[160,256]{1,0:T(8,128)S(1)} %sum_x.1.own), channel_id=1, source_target_pairs={{0,4},{1,5},{2,6},{3,7},{4,0},{5,1},{6,2},{7,3},{8,12},{9,13},{10,... | collective-permute-start | bytes 491528 | tf_op jit(solution)/shard_map/ppermute | solution.py:367

commit v12 on v11

--- a/solution.py
+++ b/solution.py
@@ -131,16 +131,18 @@
 
 
 def backward_kernel(
-    sizes, gathered, hidden, pre_conv, w_head,
+    sizes, gathered, gathered_other, hidden, pre_conv, w_head,
     keep, send, grads, grad_head,
     ordered, head_full
 ):
     dp, fsdp = sizes
     devices = dp * fsdp
     dp_here, fsdp_here = lax.axis_index("dp"), lax.axis_index("fsdp")
-    here = dp_here * fsdp + fsdp_here
-    for owner in range(devices):
-        ordered[owner] = gathered[owner].astype(F32)
+    here = (lax.rem(dp_here, 2) * (dp // 2) + dp_here // 2) * fsdp + fsdp_here
+    core = lax.rem(dp_here, 2)
+    for place in range(devices // 2):
+        ordered[core * (devices // 2) + place] = gathered[place].astype(F32)
+        ordered[(1 - core) * (devices // 2) + place] = gathered_other[place].astype(F32)
     samples = ordered.shape[1]
     count = devices * samples
     full = ordered[...].reshape(count, ordered.shape[2])
@@ -265,7 +267,8 @@
         store_coded(coded[0], summed, conv_rows)
 
 
-def output_kernel(own, other, grad_embed, grad_conv):
+def output_kernel(own, other, head, grad_embed, grad_conv, grad_head):
+    grad_head[...] = head[...]
     conv_rows, count = grad_conv.shape[0] // 2, grad_embed.shape[0]
     core_zero = lax.rem(lax.axis_index("dp"), 2) == 0
     grad_conv[pl.ds(0, conv_rows), :] = jnp.where(core_zero, own[pl.ds(0, conv_rows), :], other[pl.ds(0, conv_rows), :])
@@ -327,19 +330,20 @@
 
 def backward(sizes, gathered, hidden, pre_conv, w_head):
     dp, fsdp = sizes
-    devices, samples, width = gathered.shape
+    _, samples, width = gathered[0].shape
+    devices = dp * fsdp
     payload = pltpu.VMEM((fsdp, 1024 // fsdp // 2, 256), F32)
     return pl.pallas_call(
         lambda *refs: backward_kernel(sizes, *refs),
         out_shape=(
-            payload, payload, pltpu.VMEM((4, 256, 256), BF16), jax.ShapeDtypeStruct((256 // fsdp, 512), F32)
+            payload, payload, pltpu.VMEM((4, 256, 256), BF16), pltpu.VMEM((256 // fsdp, 512), F32)
         ),
-        in_specs=[VMEM] * 4,
+        in_specs=[VMEM] * 5,
         out_specs=(VMEM,) * 4,
         scratch_shapes=[pltpu.VMEM((devices, samples, width), F32), pltpu.VMEM((256, 512), F32)],
         compiler_params=pltpu.CompilerParams(vmem_limit_bytes=24 * 2**20),
         name="backward",
-    )(gathered, hidden, pre_conv, w_head)
+    )(*gathered, hidden, pre_conv, w_head)
 
 
 def embed_gradient(fsdp, grads, w_conv, pre_embed, one_hot):
@@ -367,9 +371,12 @@
     return lax.ppermute(block, GROUP, pairs)
 
 
-def gather_blocks(block, devices):
-    copies = jnp.broadcast_to(block[None], (devices,) + block.shape)
-    return lax.all_to_all(copies, GROUP, 0, 0, tiled=True)
+def gather_blocks(block, dp, fsdp):
+    peers = dp // 2 * fsdp
+    groups = [[place_of(x, core, z, fsdp) for x in range(dp // 2) for z in range(fsdp)] for core in range(2)]
+    copies = jnp.broadcast_to(block[None], (peers,) + block.shape)
+    own = lax.all_to_all(copies, GROUP, 0, 0, axis_index_groups=groups, tiled=True)
+    return own, exchange(own, dp, fsdp, 0, 1, 0)
 
 
 def local_kernel(kernel, outs, name, *operands):
@@ -413,23 +420,17 @@
     block, one_hot, pre_embed, hidden, pre_conv, w_conv, w_head = forward(
         facies, prior_draws, recon_grad, w_embed, w_conv, w_head
     )
-    gathered = gather_blocks(block, dp * fsdp)
+    gathered = gather_blocks(block, dp, fsdp)
     keep, send, grads, grad_head = backward((dp, fsdp), gathered, hidden, pre_conv, w_head)
     received = exchange(send, dp, fsdp, 0, 1, 0)
     embed = embed_gradient(fsdp, grads, w_conv, pre_embed, one_hot)
     own, other = reduce_to_owner(keep, received, embed, dp, fsdp)
-    grad_embed, grad_conv = pl.pallas_call(
-        output_kernel,
-        out_shape=(
-            jax.ShapeDtypeStruct((256 // fsdp, 128), F32),
-            jax.ShapeDtypeStruct((1024 // fsdp, 256), F32),
-        ),
-        in_specs=[VMEM] * 2,
-        out_specs=(VMEM,) * 2,
-        compiler_params=pltpu.CompilerParams(vmem_limit_bytes=16 * 2**20),
-        name="outputs",
-    )(own, other)
-    return (grad_embed, grad_conv, grad_head)
+    outs = (
+        jax.ShapeDtypeStruct((256 // fsdp, 128), F32),
+        jax.ShapeDtypeStruct((1024 // fsdp, 256), F32),
+        jax.ShapeDtypeStruct(grad_head.shape, F32),
+    )
+    return local_kernel(output_kernel, outs, "outputs", own, other, grad_head)
 
 
 def solution(mesh):

time: 43.3 us -> 43.3 us (level)
  waiting for transfers between devices: 10.6 us -> 11.7 us
  blocking collectives: 14.8 us -> 14.2 us
    ppermute x6 -> x7, waiting for transfers between devices: 10.6 us -> 11.7 us  [exchange(): return lax.ppermute(block, GROUP, pairs)]
    pallas_call x3 -> x4, Pallas kernels: 0.37 us -> 1.17 us  [local_kernel(): pl.pallas_call(kernel, out_shape=outs, in_specs=[VMEM] * len(operands), o...]
    pallas_call x1 -> x0, Pallas kernels: 0.76 us -> none  [shards(): pl.pallas_call(output_kernel, out_shape=(jax.ShapeDtypeStruct((256 // fsd...]
    all_to_all x1, blocking collectives: 14.8 us -> 14.2 us  [gather_blocks(): lax.all_to_all(copies, GROUP, 0, 0, axis_index_groups=groups, tiled=True)]
    ppermute x6 -> x7, starting transfers between devices: 5.85 us -> 5.44 us  [exchange(): return lax.ppermute(block, GROUP, pairs)]
  transfers between devices with their start and end apart: 6 -> 7, of which waited for: 4 -> 5; matrix products, arithmetic and copies ran while one was open for 0% -> 0% of each run, Pallas kernels for 6% -> 6%
where the time goes in v12:
time: 43.3 us; the launch traced here: 43.1 us
  blocking collectives  14.2 us (33%)
  waiting for transfers between devices  11.7 us (27%)
  Pallas kernels  10.6 us (24%)
  starting transfers between devices  5.44 us (13%)
  between operations  0.76 us (2%)
    all_to_all x1, blocking collectives, gather_blocks(): lax.all_to_all(copies, GROUP, 0, 0, axis_index_groups=groups, tiled=True)  14.2 us
    ppermute x7, waiting for transfers between devices, exchange(): return lax.ppermute(block, GROUP, pairs)  11.7 us
    ppermute x7, starting transfers between devices, exchange(): return lax.ppermute(block, GROUP, pairs)  5.44 us
    pallas_call x1, Pallas kernels, forward(): pl.pallas_call(forward_kernel, out_shape=(pltpu.VMEM((samples, 2 * latent...  4.93 us
    pallas_call x1, Pallas kernels, embed_gradient(): pl.pallas_call(embed_kernel, out_shape=pltpu.VMEM((fsdp, (96 // fsdp + 7)...  2.55 us
    pallas_call x1, Pallas kernels, backward(): pl.pallas_call(lambda *refs: backward_kernel(sizes, *refs), out_shape=(pa...  1.96 us
    pallas_call x4, Pallas kernels, local_kernel(): pl.pallas_call(kernel, out_shape=outs, in_specs=[VMEM] * len(operands), o...  1.17 us
  transfers between devices with their start and end apart: 7, of which 5 were waited for; matrix products, arithmetic and copies ran while one was open for 0% of the time, Pallas kernels for 6%

profile of v12, /device:TPU:0, one launch (start us, length us, event | category | flops | bytes accessed | tf_op | source)
XLA Modules:
  0.0 43.1 jit_solution(16632385064447465597)
XLA Ops:
  0.6 4.9 %forward.1 = (bf16[4,1280]{1,0:T(4,128)(2,1)S(1)}, bf16[8,256,1024]{2,1,0:T(8,128)(2,1)S(1)}, f32[4,256,1024]{2,1,0:T(8,128)S(1)}, bf16[4,4,256,256]{3,2,1,0:T(8...) custom-call(s32[256,2048]{1,0:T(8,128)} %bitcast.1, ...), custom_call_target="tpu_custom_call" | custom-call | tf_op jit(solution)/shard_map/forward/pallas_call | solution.py:310
  5.6 14.2 %all_to_all.5.refs_0_ = bf16[8,4,1280]{2,1,0:T(4,128)(2,1)S(1)} all-to-all(bf16[8,4,1280]{2,1,0:T(4,128)(2,1)S(1)} %broadcast_in_dim.2), channel_id=1, replica_groups={{0,1,2,3,8,9,10,11},{4,5,6,7,12,13,14,15},{16,17,18,19,24,25,26,27},{20..., dimensions={0} | all-to-all | bytes 163840 | tf_op jit(solution)/shard_map/all_to_all | solution.py:378
  19.8 0.0 collective-permute-start
  19.8 1.3 %collective-permute-done.refs_1_ = bf16[8,4,1280]{2,1,0:T(4,128)(2,1)S(1)} collective-permute-done((bf16[8,4,1280]{2,1,0:T(4,128)(2,1)S(1)}, bf16[8,4,1280]{2,1,0:T(4,128)(2,1)S(1)}, u32[]{:S(2)}, u32[]{:S(2)}) %collective-permute-start) | collective-permute-done | bytes 81952 | tf_op jit(solution)/shard_map/ppermute | solution.py:371
  21.1 2.0 %backward.1 = (f32[4,128,256]{2,1,0:T(8,128)S(1)}, f32[4,128,256]{2,1,0:T(8,128)S(1)}, bf16[4,256,256]{2,1,0:T(8,128)(2,1)S(1)}, f32[64,512]{1,0:T(8,128)S(1)}) custom-call(bf16[8,4,1280]{2,1,0:T(4,128)(2,1)S(1)} %all_to_all.5.refs_0_, bf16[8,4,1280]{2,1,0:T(4,128)(2,1)S(1)} %collective-permute-done.refs_1_, ...), custom_call_target="tpu_custom_call" | custom-call | tf_op jit(solution)/shard_map/backward/pallas_call | solution.py:336
  23.0 0.2 collective-permute-start.1
  23.3 2.6 %embed_gradient.1.embed = f32[4,32,256]{2,1,0:T(8,128)S(1)} custom-call(bf16[4,256,256]{2,1,0:T(8,128)(2,1)S(1)} %get-tuple-element.24.grads, bf16[1024,256]{1,0:T(8,128)(2,1)S(1)} %get-tuple-element.25.w_conv, f32[4,256,1024]{2,1,0:T(8,128)S(1)} %get-tuple-element.26.pre_embed, bf16[8,256,1024]{2,1,0:T(8,128)(2,1)S(1)} %get-tuple-element.27.one_hot), custom_call_target="tpu_custom_call" | custom-call | flops 1600000000 | bytes 10485760 | tf_op jit(solution)/shard_map/embed_gradient/pallas_call | solution.py:350
  25.8 0.0 collective-permute-done.1.other
  25.8 0.2 scale.1
  26.0 0.1 reduce-precision_convert_fusion.1
  26.1 0.1 reduce-precision_convert_fusion
  26.2 0.5 %collective-permute-start.4 = (f16[160,256]{1,0:T(8,128)(2,1)S(1)}, f16[160,256]{1,0:T(8,128)(2,1)S(1)}, u32[]{:S(2)}, u32[]{:S(2)}) collective-permute-start(f16[160,256]{1,0:T(8,128)(2,1)S(1)} %reduce-precision_convert_fusion), channel_id=1, source_target_pairs={{0,3},{1,2},{2,1},{3,0},{4,7},{5,6},{6,5},{7,4},{8,11},{9,10},{10,... | collective-permute-start | bytes 245768 | tf_op jit(solution)/shard_map/ppermute | solution.py:371
  26.7 1.3 %collective-permute-start.3 = (f16[160,256]{1,0:T(8,128)(2,1)S(1)}, f16[160,256]{1,0:T(8,128)(2,1)S(1)}, u32[]{:S(2)}, u32[]{:S(2)}) collective-permute-start(f16[160,256]{1,0:T(8,128)(2,1)S(1)} %reduce-precision_convert_fusion.1), channel_id=1, source_target_pairs={{0,2},{1,3},{2,0},{3,1},{4,6},{5,7},{6,4},{7,5},{8,10},{9,11},{10,... | collective-permute-start | bytes 245768 | tf_op jit(solution)/shard_map/ppermute | solution.py:371
  28.1 0.1 reduce-precision_convert_fusion.2
  28.2 2.7 %collective-permute-start.2 = (f16[160,256]{1,0:T(8,128)(2,1)S(1)}, f16[160,256]{1,0:T(8,128)(2,1)S(1)}, u32[]{:S(2)}, u32[]{:S(2)}) collective-permute-start(f16[160,256]{1,0:T(8,128)(2,1)S(1)} %reduce-precision_convert_fusion.2), channel_id=1, source_target_pairs={{0,1},{1,0},{2,3},{3,2},{4,5},{5,4},{6,7},{7,6},{8,9},{9,8},{10,11... | collective-permute-start | bytes 245768 | tf_op jit(solution)/shard_map/ppermute | solution.py:371
  30.8 2.6 %collective-permute-done.4 = f16[160,256]{1,0:T(8,128)(2,1)S(1)} collective-permute-done((f16[160,256]{1,0:T(8,128)(2,1)S(1)}, f16[160,256]{1,0:T(8,128)(2,1)S(1)}, u32[]{:S(2)}, u32[]{:S(2)}) %collective-permute-start.4) | collective-permute-done | bytes 81952 | tf_op jit(solution)/shard_map/ppermute | solution.py:371
  33.4 2.6 %collective-permute-done.3 = f16[160,256]{1,0:T(8,128)(2,1)S(1)} collective-permute-done((f16[160,256]{1,0:T(8,128)(2,1)S(1)}, f16[160,256]{1,0:T(8,128)(2,1)S(1)}, u32[]{:S(2)}, u32[]{:S(2)}) %collective-permute-start.3) | collective-permute-done | bytes 81952 | tf_op jit(solution)/shard_map/ppermute | solution.py:371
  36.0 0.0 collective-permute-done.2
  36.1 0.2 sum_z.1
  36.2 0.1 reduce-precision_convert_fusion.3
  36.3 0.6 %collective-permute-start.5 = (f16[160,256]{1,0:T(8,128)(2,1)S(1)}, f16[160,256]{1,0:T(8,128)(2,1)S(1)}, u32[]{:S(2)}, u32[]{:S(2)}) collective-permute-start(f16[160,256]{1,0:T(8,128)(2,1)S(1)} %get-tuple-element.33), channel_id=1, source_target_pairs={{0,8},{1,9},{2,10},{3,11},{4,12},{5,13},{6,14},{7,15},{8,0},{9,1},... | collective-permute-start | bytes 245768 | tf_op jit(solution)/shard_map/ppermute | solution.py:371
  36.9 3.9 %collective-permute-done.5 = f16[160,256]{1,0:T(8,128)(2,1)S(1)} collective-permute-done((f16[160,256]{1,0:T(8,128)(2,1)S(1)}, f16[160,256]{1,0:T(8,128)(2,1)S(1)}, u32[]{:S(2)}, u32[]{:S(2)}) %collective-permute-start.5) | collective-permute-done | bytes 81952 | tf_op jit(solution)/shard_map/ppermute | solution.py:371
  40.9 0.1 collective-permute-start.6
  41.0 1.4 %collective-permute-done.6.other = f32[160,256]{1,0:T(8,128)S(1)} collective-permute-done((f32[160,256]{1,0:T(8,128)S(1)}, f32[160,256]{1,0:T(8,128)S(1)}, u32[]{:S(2)}, u32[]{:S(2)}) %collective-permute-start.6) | collective-permute-done | bytes 163872 | tf_op jit(solution)/shard_map/ppermute | solution.py:371
  42.3 0.8 %outputs.1 = (f32[64,128]{1,0:T(8,128)}, f32[256,256]{1,0:T(8,128)}, f32[64,512]{1,0:T(8,128)}) custom-call(f32[160,256]{1,0:T(8,128)S(1)} %sum_x.1.own, f32[160,256]{1,0:T(8,128)S(1)} %collective-permute-done.6.other, f32[64,512]{1,0:T(8,128)S(1)} %get-tuple-element.32.head), custom_call_target="tpu_custom_call" | custom-call | tf_op jit(solution)/shard_map/outputs/pallas_call | solution.py:383
  (6 shorter events, 0.1 us)
Async XLA Ops:
  19.8 1.3 %collective-permute-start = (bf16[8,4,1280]{2,1,0:T(4,128)(2,1)S(1)}, bf16[8,4,1280]{2,1,0:T(4,128)(2,1)S(1)}, u32[]{:S(2)}, u32[]{:S(2)}) collective-permute-start(bf16[8,4,1280]{2,1,0:T(4,128)(2,1)S(1)} %all_to_all.5.refs_0_), channel_id=1, source_target_pairs={{0,4},{1,5},{2,6},{3,7},{4,0},{5,1},{6,2},{7,3},{8,12},{9,13},{10,... | collective-permute-start | bytes 245768 | tf_op jit(solution)/shard_map/ppermute | solution.py:371
  23.0 2.8 %collective-permute-start.1 = (f32[4,128,256]{2,1,0:T(8,128)S(1)}, f32[4,128,256]{2,1,0:T(8,128)S(1)}, u32[]{:S(2)}, u32[]{:S(2)}) collective-permute-start(f32[4,128,256]{2,1,0:T(8,128)S(1)} %get-tuple-element.23), channel_id=1, source_target_pairs={{0,4},{1,5},{2,6},{3,7},{4,0},{5,1},{6,2},{7,3},{8,12},{9,13},{10,... | collective-permute-start | bytes 1572872 | tf_op jit(solution)/shard_map/ppermute | solution.py:371
  26.2 7.2 %collective-permute-start.4 = (f16[160,256]{1,0:T(8,128)(2,1)S(1)}, f16[160,256]{1,0:T(8,128)(2,1)S(1)}, u32[]{:S(2)}, u32[]{:S(2)}) collective-permute-start(f16[160,256]{1,0:T(8,128)(2,1)S(1)} %reduce-precision_convert_fusion), channel_id=1, source_target_pairs={{0,3},{1,2},{2,1},{3,0},{4,7},{5,6},{6,5},{7,4},{8,11},{9,10},{10,... | collective-permute-start | bytes 245768 | tf_op jit(solution)/shard_map/ppermute | solution.py:371
  26.7 9.3 %collective-permute-start.3 = (f16[160,256]{1,0:T(8,128)(2,1)S(1)}, f16[160,256]{1,0:T(8,128)(2,1)S(1)}, u32[]{:S(2)}, u32[]{:S(2)}) collective-permute-start(f16[160,256]{1,0:T(8,128)(2,1)S(1)} %reduce-precision_convert_fusion.1), channel_id=1, source_target_pairs={{0,2},{1,3},{2,0},{3,1},{4,6},{5,7},{6,4},{7,5},{8,10},{9,11},{10,... | collective-permute-start | bytes 245768 | tf_op jit(solution)/shard_map/ppermute | solution.py:371
  28.2 7.9 %collective-permute-start.2 = (f16[160,256]{1,0:T(8,128)(2,1)S(1)}, f16[160,256]{1,0:T(8,128)(2,1)S(1)}, u32[]{:S(2)}, u32[]{:S(2)}) collective-permute-start(f16[160,256]{1,0:T(8,128)(2,1)S(1)} %reduce-precision_convert_fusion.2), channel_id=1, source_target_pairs={{0,1},{1,0},{2,3},{3,2},{4,5},{5,4},{6,7},{7,6},{8,9},{9,8},{10,11... | collective-permute-start | bytes 245768 | tf_op jit(solution)/shard_map/ppermute | solution.py:371
  36.3 4.5 %collective-permute-start.5 = (f16[160,256]{1,0:T(8,128)(2,1)S(1)}, f16[160,256]{1,0:T(8,128)(2,1)S(1)}, u32[]{:S(2)}, u32[]{:S(2)}) collective-permute-start(f16[160,256]{1,0:T(8,128)(2,1)S(1)} %get-tuple-element.33), channel_id=1, source_target_pairs={{0,8},{1,9},{2,10},{3,11},{4,12},{5,13},{6,14},{7,15},{8,0},{9,1},... | collective-permute-start | bytes 245768 | tf_op jit(solution)/shard_map/ppermute | solution.py:371
  40.9 1.5 %collective-permute-start.6 = (f32[160,256]{1,0:T(8,128)S(1)}, f32[160,256]{1,0:T(8,128)S(1)}, u32[]{:S(2)}, u32[]{:S(2)}) collective-permute-start(f32[160,256]{1,0:T(8,128)S(1)} %sum_x.1.own), channel_id=1, source_target_pairs={{0,4},{1,5},{2,6},{3,7},{4,0},{5,1},{6,2},{7,3},{8,12},{9,13},{10,... | collective-permute-start | bytes 491528 | tf_op jit(solution)/shard_map/ppermute | solution.py:371

commit v13 on v12

--- a/solution.py
+++ b/solution.py
@@ -249,7 +249,7 @@
 
     own[...] = share(here)
     for place, target in enumerate(coded):
-        store_scaled(target, share(here ^ (place + 1)), steps, keep.shape[1])
+        store_scaled(target, share(lax.rem(here + (len(coded) - place), keep.shape[0])), steps, keep.shape[1])
 
 
 def first_sum_kernel(conv_rows, own, *refs):
@@ -362,12 +362,13 @@
     return (2 * x + core) * fsdp + z
 
 
-def exchange(block, dp, fsdp, flip_x, flip_core, flip_z):
+def exchange(block, dp, fsdp, flip_x, flip_core, step_z):
     pairs = []
     for x in range(dp // 2):
         for core in range(2):
             for z in range(fsdp):
-                pairs.append((place_of(x, core, z, fsdp), place_of(x ^ flip_x, core ^ flip_core, z ^ flip_z, fsdp)))
+                to = place_of(x ^ flip_x, core ^ flip_core, (z + step_z) % fsdp, fsdp)
+                pairs.append((place_of(x, core, z, fsdp), to))
     return lax.ppermute(block, GROUP, pairs)
 
 
@@ -401,7 +402,7 @@
     plain = jax.ShapeDtypeStruct((rows, width), F32)
     own, *coded = local_kernel(scale_kernel, (plain,) + (plain,) * (fsdp - 1), "scale", keep, other, embed)
     received = [
-        exchange(to_half(part)[1], dp, fsdp, 0, 0, place + 1).astype(F32) for place, part in enumerate(coded)
+        exchange(to_half(part)[1], dp, fsdp, 0, 0, fsdp - 1 - place).astype(F32) for place, part in enumerate(coded)
     ]
     (coded,) = local_kernel(functools.partial(first_sum_kernel, conv_rows), (plain,), "sum_z", own, *received)
     flip = 1

time: 43.3 us -> 43.6 us (level)
  waiting for transfers between devices: 11.7 us -> 12.6 us
  starting transfers between devices: 5.44 us -> 4.86 us
    ppermute x7, waiting for transfers between devices: 11.7 us -> 12.6 us  [exchange(): return lax.ppermute(block, GROUP, pairs)]
    ppermute x7, starting transfers between devices: 5.44 us -> 4.86 us  [exchange(): return lax.ppermute(block, GROUP, pairs)]
where the time goes in v13:
time: 43.6 us; the launch traced here: 43.4 us
  blocking collectives  14.2 us (33%)
  waiting for transfers between devices  12.6 us (29%)
  Pallas kernels  10.6 us (24%)
  starting transfers between devices  4.86 us (11%)
  between operations  0.76 us (2%)
    all_to_all x1, blocking collectives, gather_blocks(): lax.all_to_all(copies, GROUP, 0, 0, axis_index_groups=groups, tiled=True)  14.2 us
    ppermute x7, waiting for transfers between devices, exchange(): return lax.ppermute(block, GROUP, pairs)  12.6 us
    pallas_call x1, Pallas kernels, forward(): pl.pallas_call(forward_kernel, out_shape=(pltpu.VMEM((samples, 2 * latent...  4.93 us
    ppermute x7, starting transfers between devices, exchange(): return lax.ppermute(block, GROUP, pairs)  4.86 us
    pallas_call x1, Pallas kernels, embed_gradient(): pl.pallas_call(embed_kernel, out_shape=pltpu.VMEM((fsdp, (96 // fsdp + 7)...  2.55 us
    pallas_call x1, Pallas kernels, backward(): pl.pallas_call(lambda *refs: backward_kernel(sizes, *refs), out_shape=(pa...  1.96 us
    pallas_call x4, Pallas kernels, local_kernel(): pl.pallas_call(kernel, out_shape=outs, in_specs=[VMEM] * len(operands), o...  1.17 us
  transfers between devices with their start and end apart: 7, of which 5 were waited for; matrix products, arithmetic and copies ran while one was open for 0% of the time, Pallas kernels for 6%

profile of v13, /device:TPU:0, one launch (start us, length us, event | category | flops | bytes accessed | tf_op | source)
XLA Modules:
  0.0 43.4 jit_solution(2086750042348565202)
XLA Ops:
  0.6 4.9 %forward.1 = (bf16[4,1280]{1,0:T(4,128)(2,1)S(1)}, bf16[8,256,1024]{2,1,0:T(8,128)(2,1)S(1)}, f32[4,256,1024]{2,1,0:T(8,128)S(1)}, bf16[4,4,256,256]{3,2,1,0:T(8...) custom-call(s32[256,2048]{1,0:T(8,128)} %bitcast.1, ...), custom_call_target="tpu_custom_call" | custom-call | tf_op jit(solution)/shard_map/forward/pallas_call | solution.py:310
  5.6 14.2 %all_to_all.5.refs_0_ = bf16[8,4,1280]{2,1,0:T(4,128)(2,1)S(1)} all-to-all(bf16[8,4,1280]{2,1,0:T(4,128)(2,1)S(1)} %broadcast_in_dim.2), channel_id=1, replica_groups={{0,1,2,3,8,9,10,11},{4,5,6,7,12,13,14,15},{16,17,18,19,24,25,26,27},{20..., dimensions={0} | all-to-all | bytes 163840 | tf_op jit(solution)/shard_map/all_to_all | solution.py:379
  19.8 0.0 collective-permute-start
  19.8 1.3 %collective-permute-done.refs_1_ = bf16[8,4,1280]{2,1,0:T(4,128)(2,1)S(1)} collective-permute-done((bf16[8,4,1280]{2,1,0:T(4,128)(2,1)S(1)}, bf16[8,4,1280]{2,1,0:T(4,128)(2,1)S(1)}, u32[]{:S(2)}, u32[]{:S(2)}) %collective-permute-start) | collective-permute-done | bytes 81952 | tf_op jit(solution)/shard_map/ppermute | solution.py:372
  21.1 2.0 %backward.1 = (f32[4,128,256]{2,1,0:T(8,128)S(1)}, f32[4,128,256]{2,1,0:T(8,128)S(1)}, bf16[4,256,256]{2,1,0:T(8,128)(2,1)S(1)}, f32[64,512]{1,0:T(8,128)S(1)}) custom-call(bf16[8,4,1280]{2,1,0:T(4,128)(2,1)S(1)} %all_to_all.5.refs_0_, bf16[8,4,1280]{2,1,0:T(4,128)(2,1)S(1)} %collective-permute-done.refs_1_, ...), custom_call_target="tpu_custom_call" | custom-call | tf_op jit(solution)/shard_map/backward/pallas_call | solution.py:336
  23.0 0.2 collective-permute-start.1
  23.3 2.6 %embed_gradient.1.embed = f32[4,32,256]{2,1,0:T(8,128)S(1)} custom-call(bf16[4,256,256]{2,1,0:T(8,128)(2,1)S(1)} %get-tuple-element.24.grads, bf16[1024,256]{1,0:T(8,128)(2,1)S(1)} %get-tuple-element.25.w_conv, f32[4,256,1024]{2,1,0:T(8,128)S(1)} %get-tuple-element.26.pre_embed, bf16[8,256,1024]{2,1,0:T(8,128)(2,1)S(1)} %get-tuple-element.27.one_hot), custom_call_target="tpu_custom_call" | custom-call | flops 1600000000 | bytes 10485760 | tf_op jit(solution)/shard_map/embed_gradient/pallas_call | solution.py:350
  25.8 0.0 collective-permute-done.1.other
  25.8 0.2 scale.1
  26.0 0.1 reduce-precision_convert_fusion.1
  26.1 0.1 reduce-precision_convert_fusion
  26.2 0.4 collective-permute-start.4
  26.6 0.7 %collective-permute-start.3 = (f16[160,256]{1,0:T(8,128)(2,1)S(1)}, f16[160,256]{1,0:T(8,128)(2,1)S(1)}, u32[]{:S(2)}, u32[]{:S(2)}) collective-permute-start(f16[160,256]{1,0:T(8,128)(2,1)S(1)} %reduce-precision_convert_fusion.1), channel_id=1, source_target_pairs={{0,2},{1,3},{2,0},{3,1},{4,6},{5,7},{6,4},{7,5},{8,10},{9,11},{10,... | collective-permute-start | bytes 245768 | tf_op jit(solution)/shard_map/ppermute | solution.py:372
  27.3 0.1 reduce-precision_convert_fusion.2
  27.4 2.9 %collective-permute-start.2 = (f16[160,256]{1,0:T(8,128)(2,1)S(1)}, f16[160,256]{1,0:T(8,128)(2,1)S(1)}, u32[]{:S(2)}, u32[]{:S(2)}) collective-permute-start(f16[160,256]{1,0:T(8,128)(2,1)S(1)} %reduce-precision_convert_fusion.2), channel_id=1, source_target_pairs={{0,3},{1,0},{2,1},{3,2},{4,7},{5,4},{6,5},{7,6},{8,11},{9,8},{10,9... | collective-permute-start | bytes 245768 | tf_op jit(solution)/shard_map/ppermute | solution.py:372
  30.2 3.2 %collective-permute-done.4 = f16[160,256]{1,0:T(8,128)(2,1)S(1)} collective-permute-done((f16[160,256]{1,0:T(8,128)(2,1)S(1)}, f16[160,256]{1,0:T(8,128)(2,1)S(1)}, u32[]{:S(2)}, u32[]{:S(2)}) %collective-permute-start.4) | collective-permute-done | bytes 81952 | tf_op jit(solution)/shard_map/ppermute | solution.py:372
  33.4 2.8 %collective-permute-done.3 = f16[160,256]{1,0:T(8,128)(2,1)S(1)} collective-permute-done((f16[160,256]{1,0:T(8,128)(2,1)S(1)}, f16[160,256]{1,0:T(8,128)(2,1)S(1)}, u32[]{:S(2)}, u32[]{:S(2)}) %collective-permute-start.3) | collective-permute-done | bytes 81952 | tf_op jit(solution)/shard_map/ppermute | solution.py:372
  36.3 0.0 collective-permute-done.2
  36.3 0.2 sum_z.1
  36.5 0.1 reduce-precision_convert_fusion.3
  36.6 0.6 %collective-permute-start.5 = (f16[160,256]{1,0:T(8,128)(2,1)S(1)}, f16[160,256]{1,0:T(8,128)(2,1)S(1)}, u32[]{:S(2)}, u32[]{:S(2)}) collective-permute-start(f16[160,256]{1,0:T(8,128)(2,1)S(1)} %get-tuple-element.33), channel_id=1, source_target_pairs={{0,8},{1,9},{2,10},{3,11},{4,12},{5,13},{6,14},{7,15},{8,0},{9,1},... | collective-permute-start | bytes 245768 | tf_op jit(solution)/shard_map/ppermute | solution.py:372
  37.2 3.9 %collective-permute-done.5 = f16[160,256]{1,0:T(8,128)(2,1)S(1)} collective-permute-done((f16[160,256]{1,0:T(8,128)(2,1)S(1)}, f16[160,256]{1,0:T(8,128)(2,1)S(1)}, u32[]{:S(2)}, u32[]{:S(2)}) %collective-permute-start.5) | collective-permute-done | bytes 81952 | tf_op jit(solution)/shard_map/ppermute | solution.py:372
  41.2 0.1 collective-permute-start.6
  41.2 1.4 %collective-permute-done.6.other = f32[160,256]{1,0:T(8,128)S(1)} collective-permute-done((f32[160,256]{1,0:T(8,128)S(1)}, f32[160,256]{1,0:T(8,128)S(1)}, u32[]{:S(2)}, u32[]{:S(2)}) %collective-permute-start.6) | collective-permute-done | bytes 163872 | tf_op jit(solution)/shard_map/ppermute | solution.py:372
  42.6 0.8 %outputs.1 = (f32[64,128]{1,0:T(8,128)}, f32[256,256]{1,0:T(8,128)}, f32[64,512]{1,0:T(8,128)}) custom-call(f32[160,256]{1,0:T(8,128)S(1)} %sum_x.1.own, f32[160,256]{1,0:T(8,128)S(1)} %collective-permute-done.6.other, f32[64,512]{1,0:T(8,128)S(1)} %get-tuple-element.32.head), custom_call_target="tpu_custom_call" | custom-call | tf_op jit(solution)/shard_map/outputs/pallas_call | solution.py:384
  (6 shorter events, 0.1 us)
Async XLA Ops:
  19.8 1.3 %collective-permute-start = (bf16[8,4,1280]{2,1,0:T(4,128)(2,1)S(1)}, bf16[8,4,1280]{2,1,0:T(4,128)(2,1)S(1)}, u32[]{:S(2)}, u32[]{:S(2)}) collective-permute-start(bf16[8,4,1280]{2,1,0:T(4,128)(2,1)S(1)} %all_to_all.5.refs_0_), channel_id=1, source_target_pairs={{0,4},{1,5},{2,6},{3,7},{4,0},{5,1},{6,2},{7,3},{8,12},{9,13},{10,... | collective-permute-start | bytes 245768 | tf_op jit(solution)/shard_map/ppermute | solution.py:372
  23.0 2.8 %collective-permute-start.1 = (f32[4,128,256]{2,1,0:T(8,128)S(1)}, f32[4,128,256]{2,1,0:T(8,128)S(1)}, u32[]{:S(2)}, u32[]{:S(2)}) collective-permute-start(f32[4,128,256]{2,1,0:T(8,128)S(1)} %get-tuple-element.23), channel_id=1, source_target_pairs={{0,4},{1,5},{2,6},{3,7},{4,0},{5,1},{6,2},{7,3},{8,12},{9,13},{10,... | collective-permute-start | bytes 1572872 | tf_op jit(solution)/shard_map/ppermute | solution.py:372
  26.2 7.2 %collective-permute-start.4 = (f16[160,256]{1,0:T(8,128)(2,1)S(1)}, f16[160,256]{1,0:T(8,128)(2,1)S(1)}, u32[]{:S(2)}, u32[]{:S(2)}) collective-permute-start(f16[160,256]{1,0:T(8,128)(2,1)S(1)} %reduce-precision_convert_fusion), channel_id=1, source_target_pairs={{0,1},{1,2},{2,3},{3,0},{4,5},{5,6},{6,7},{7,4},{8,9},{9,10},{10,1... | collective-permute-start | bytes 245768 | tf_op jit(solution)/shard_map/ppermute | solution.py:372
  26.6 9.7 %collective-permute-start.3 = (f16[160,256]{1,0:T(8,128)(2,1)S(1)}, f16[160,256]{1,0:T(8,128)(2,1)S(1)}, u32[]{:S(2)}, u32[]{:S(2)}) collective-permute-start(f16[160,256]{1,0:T(8,128)(2,1)S(1)} %reduce-precision_convert_fusion.1), channel_id=1, source_target_pairs={{0,2},{1,3},{2,0},{3,1},{4,6},{5,7},{6,4},{7,5},{8,10},{9,11},{10,... | collective-permute-start | bytes 245768 | tf_op jit(solution)/shard_map/ppermute | solution.py:372
  27.4 8.9 %collective-permute-start.2 = (f16[160,256]{1,0:T(8,128)(2,1)S(1)}, f16[160,256]{1,0:T(8,128)(2,1)S(1)}, u32[]{:S(2)}, u32[]{:S(2)}) collective-permute-start(f16[160,256]{1,0:T(8,128)(2,1)S(1)} %reduce-precision_convert_fusion.2), channel_id=1, source_target_pairs={{0,3},{1,0},{2,1},{3,2},{4,7},{5,4},{6,5},{7,6},{8,11},{9,8},{10,9... | collective-permute-start | bytes 245768 | tf_op jit(solution)/shard_map/ppermute | solution.py:372
  36.6 4.5 %collective-permute-start.5 = (f16[160,256]{1,0:T(8,128)(2,1)S(1)}, f16[160,256]{1,0:T(8,128)(2,1)S(1)}, u32[]{:S(2)}, u32[]{:S(2)}) collective-permute-start(f16[160,256]{1,0:T(8,128)(2,1)S(1)} %get-tuple-element.33), channel_id=1, source_target_pairs={{0,8},{1,9},{2,10},{3,11},{4,12},{5,13},{6,14},{7,15},{8,0},{9,1},... | collective-permute-start | bytes 245768 | tf_op jit(solution)/shard_map/ppermute | solution.py:372
  41.2 1.5 %collective-permute-start.6 = (f32[160,256]{1,0:T(8,128)S(1)}, f32[160,256]{1,0:T(8,128)S(1)}, u32[]{:S(2)}, u32[]{:S(2)}) collective-permute-start(f32[160,256]{1,0:T(8,128)S(1)} %sum_x.1.own), channel_id=1, source_target_pairs={{0,4},{1,5},{2,6},{3,7},{4,0},{5,1},{6,2},{7,3},{8,12},{9,13},{10,... | collective-permute-start | bytes 491528 | tf_op jit(solution)/shard_map/ppermute | solution.py:372

commit v14 on v11

--- a/solution.py
+++ b/solution.py
@@ -48,7 +48,7 @@
 
 def forward_kernel(
     facies_hbm, prior_hbm, recon_hbm, w_embed_hbm, w_conv_hbm, w_head_hbm,
-    block, one_hot, pre_embed, hidden, pre_conv, w_conv, w_head,
+    block, pooled_lanes, recon_lanes, one_hot, pre_embed, hidden, pre_conv, w_conv, w_head,
     facies, prior, recon, w_embed, packed, conv_turned, sem
 ):
     blocks = facies.shape[0]
@@ -111,13 +111,23 @@
         pre_conv[cp] = pre
         act = pre * sigmoid(pre)
         sums = sums + act[:, :128] + act[:, 128:]
-    pick = jnp.where(iota((8, 128), 1) // 8 % 4 == iota((8, 128), 0), 1.0, 0.0)
-    total = lax.dot_general(pick, sums, NT, precision=lax.Precision.HIGHEST, preferred_element_type=F32)
+    for rows, every in ((8, 1), (128, 8)):
+        pick = iota((rows, 128), 1) // 8 % 4 == iota((rows, 128), 0) // every % 4
+        total = lax.dot_general(
+            jnp.where(pick, 1.0, 0.0), sums, NT, precision=lax.Precision.HIGHEST, preferred_element_type=F32
+        )
+        mean = (total / 256.0).astype(BF16)
+        if rows == 8:
+            block[:, pl.ds(1024, 256)] = mean[:4]
+        else:
+            pooled_lanes[...] = mean
     for load in others[2:]:
         load.wait()
     block[:, pl.ds(0, 512)] = prior[...]
     block[:, pl.ds(512, 512)] = recon[...]
-    block[:, pl.ds(1024, 256)] = (total[:4] / 256.0).astype(BF16)
+    recon_float = recon[...].astype(F32)
+    for place in range(16):
+        recon_lanes[pl.ds(place * 8, 8), :] = jnp.broadcast_to(recon_float[place % 4 : place % 4 + 1], (8, recon.shape[1]))
 
 
 def pair_kernel(queries, query_square, keys):
@@ -130,47 +140,50 @@
     return jnp.sum(kern, axis=1, keepdims=True), mm(kern.astype(BF16), keys)
 
 
-def backward_kernel(
-    sizes, gathered, hidden, pre_conv, w_head,
-    keep, send, grads, grad_head,
-    ordered, head_full
-):
-    dp, fsdp = sizes
-    devices = dp * fsdp
-    dp_here, fsdp_here = lax.axis_index("dp"), lax.axis_index("fsdp")
-    here = dp_here * fsdp + fsdp_here
-    for owner in range(devices):
+def group_rows(gathered, ordered):
+    for owner in range(gathered.shape[0]):
         ordered[owner] = gathered[owner].astype(F32)
-    samples = ordered.shape[1]
-    count = devices * samples
-    full = ordered[...].reshape(count, ordered.shape[2])
-    prior = full[:, :512].astype(BF16)
-    recon = full[:, 512:1024]
-    pooled = full[:, 1024:].astype(BF16)
-    latent = mm(pooled, w_head[...]).astype(BF16)
-    latent_float = latent.astype(F32)
-    square = jnp.sum(latent_float * latent_float, axis=1, keepdims=True)
-    self_sum, self_mix = pair_kernel(latent, square, latent)
-    cross_sum, cross_mix = pair_kernel(latent, square, prior)
-    pull = -32.0 / count * ((self_sum - cross_sum) * latent_float - self_mix + cross_mix)
-    cotangent = (recon + pull).astype(BF16)
-    turned = jnp.transpose(full[:, 1024:]).astype(BF16)
-    head_full[...] = mm(turned, cotangent)
+    return ordered[...].reshape(gathered.shape[0] * gathered.shape[1], gathered.shape[2])
+
+
+def latent_rows(pooled, w_head):
+    return mm(pooled, w_head[...]).astype(BF16)
+
+
+def cotangent_rows(queries, keys, prior, recon):
+    query_float = queries.astype(F32)
+    square = jnp.sum(query_float * query_float, axis=1, keepdims=True)
+    self_sum, self_mix = pair_kernel(queries, square, keys)
+    cross_sum, cross_mix = pair_kernel(queries, square, prior)
+    pull = -32.0 / keys.shape[0] * ((self_sum - cross_sum) * query_float - self_mix + cross_mix)
+    return (recon + pull).astype(BF16)
+
+
+def head_kernel(gathered, w_head, after, grad_head, token, ordered, head_full):
+    token[...] = jnp.zeros(token.shape, F32)
+    full = group_rows(gathered, ordered)
+    latent = latent_rows(full[:, 1024:].astype(BF16), w_head)
+    cotangent = cotangent_rows(latent, latent, full[:, :512].astype(BF16), full[:, 512:1024])
+    head_full[...] = mm(jnp.transpose(full[:, 1024:]).astype(BF16), cotangent)
     share = grad_head.shape[0]
-    start = pl.multiple_of(fsdp_here * share, share)
+    start = pl.multiple_of(lax.axis_index("fsdp") * share, share)
     grad_head[...] = head_full[pl.ds(start, share), :]
 
-    lane_sample = iota((128, count), 0) // 8 % 4 + samples * here
-    pick = jnp.where(lane_sample == iota((128, count), 1), 1.0, 0.0).astype(BF16)
-    lanes = mm(pick, cotangent).astype(BF16)
-    back_pool = mm_nt(w_head[...], lanes) / 256.0
+
+def backward_kernel(gathered, pooled_lanes, recon_lanes, hidden, pre_conv, w_head, keep, send, grads, ordered):
+    full = group_rows(gathered, ordered)
+    queries = latent_rows(pooled_lanes[...], w_head)
+    keys = latent_rows(full[:, 1024:].astype(BF16), w_head)
+    cotangent = cotangent_rows(queries, keys, full[:, :512].astype(BF16), recon_lanes[...])
+    back_pool = mm_nt(w_head[...], cotangent) / 256.0
     back_pool = jnp.concatenate([back_pool, back_pool], axis=1)
+    fsdp = keep.shape[0]
     conv_total = None
     for cp in range(4):
         grads[cp] = (back_pool * silu_slope(pre_conv[cp])).astype(BF16)
         term = mm_nt(hidden[cp].reshape(1024, 256), grads[cp])
         conv_total = term if cp == 0 else conv_total + term
-    core_zero = lax.rem(dp_here, 2) == 0
+    core_zero = lax.rem(lax.axis_index("dp"), 2) == 0
     rows = keep.shape[1]
     for f in range(fsdp):
         at = 2 * f * rows
@@ -307,10 +320,11 @@
     return pl.pallas_call(
         forward_kernel,
         out_shape=(pltpu.VMEM((samples, 2 * latent_width + 256), BF16),)
+        + (pltpu.VMEM((128, 256), BF16), pltpu.VMEM((128, latent_width), F32))
         + tuple(pltpu.VMEM(shape, kind) for shape, kind in SAVED)
         + (pltpu.VMEM(w_conv.shape, BF16), pltpu.VMEM(w_head.shape, BF16)),
         in_specs=[HBM] * 6,
-        out_specs=(VMEM,) * 7,
+        out_specs=(VMEM,) * 9,
         scratch_shapes=[
             pltpu.VMEM((lanes // 128, rows, 128), jnp.int32),
             pltpu.VMEM(prior_draws.shape, BF16),
@@ -325,21 +339,32 @@
     )(*(pltpu.with_memory_space_constraint(operand, pltpu.HBM) for operand in operands))
 
 
-def backward(sizes, gathered, hidden, pre_conv, w_head):
-    dp, fsdp = sizes
+def backward(fsdp, gathered, *operands):
     devices, samples, width = gathered.shape
     payload = pltpu.VMEM((fsdp, 1024 // fsdp // 2, 256), F32)
     return pl.pallas_call(
-        lambda *refs: backward_kernel(sizes, *refs),
-        out_shape=(
-            payload, payload, pltpu.VMEM((4, 256, 256), BF16), jax.ShapeDtypeStruct((256 // fsdp, 512), F32)
-        ),
-        in_specs=[VMEM] * 4,
-        out_specs=(VMEM,) * 4,
-        scratch_shapes=[pltpu.VMEM((devices, samples, width), F32), pltpu.VMEM((256, 512), F32)],
+        backward_kernel,
+        out_shape=(payload, payload, pltpu.VMEM((4, 256, 256), BF16)),
+        in_specs=[VMEM] * 6,
+        out_specs=(VMEM,) * 3,
+        scratch_shapes=[pltpu.VMEM((devices, samples, width), F32)],
         compiler_params=pltpu.CompilerParams(vmem_limit_bytes=24 * 2**20),
         name="backward",
-    )(gathered, hidden, pre_conv, w_head)
+    )(gathered, *operands)
+
+
+def head_gradient(fsdp, gathered, w_head, after):
+    devices, samples, width = gathered.shape
+    return pl.pallas_call(
+        head_kernel,
+        out_shape=(jax.ShapeDtypeStruct((256 // fsdp, 512), F32), pltpu.VMEM((8, 128), F32)),
+        in_specs=[VMEM] * 2 + [HBM],
+        out_specs=(VMEM,) * 2,
+        scratch_shapes=[pltpu.VMEM((devices, samples, width), F32), pltpu.VMEM((256, 512), F32)],
+        compiler_params=pltpu.CompilerParams(vmem_limit_bytes=16 * 2**20),
+        cost_estimate=pl.CostEstimate(flops=2 * 10**9, bytes_accessed=2 * 2**20, transcendentals=10000),
+        name="head_gradient",
+    )(gathered, w_head, after)
 
 
 def embed_gradient(fsdp, grads, w_conv, pre_embed, one_hot):
@@ -372,15 +397,15 @@
     return lax.all_to_all(copies, GROUP, 0, 0, tiled=True)
 
 
-def local_kernel(kernel, outs, name, *operands):
+def local_kernel(kernel, outs, name, *operands, unread=()):
     return pl.pallas_call(
-        kernel,
+        lambda *refs: kernel(*refs[: len(operands)], *refs[len(operands) + len(unread) :]),
         out_shape=outs,
-        in_specs=[VMEM] * len(operands),
+        in_specs=[VMEM] * (len(operands) + len(unread)),
         out_specs=(VMEM,) * len(outs),
         compiler_params=pltpu.CompilerParams(vmem_limit_bytes=16 * 2**20),
         name=name,
-    )(*operands)
+    )(*operands, *unread)
 
 
 def to_half(coded):
@@ -388,7 +413,7 @@
     return rounded, rounded.astype(jnp.float16)
 
 
-def reduce_to_owner(keep, other, embed, dp, fsdp):
+def reduce_to_owner(keep, other, embed, gathered, w_head, dp, fsdp):
     conv_rows, width = keep.shape[1:]
     rows = conv_rows + embed.shape[1]
     plain = jax.ShapeDtypeStruct((rows, width), F32)
@@ -396,7 +421,10 @@
     received = [
         exchange(to_half(part)[1], dp, fsdp, 0, 0, place + 1).astype(F32) for place, part in enumerate(coded)
     ]
-    (coded,) = local_kernel(functools.partial(first_sum_kernel, conv_rows), (plain,), "sum_z", own, *received)
+    grad_head, token = head_gradient(fsdp, gathered, w_head, own)
+    (coded,) = local_kernel(
+        functools.partial(first_sum_kernel, conv_rows), (plain,), "sum_z", own, *received, unread=(token,)
+    )
     flip = 1
     while flip < dp // 2:
         mine, sent = to_half(coded)
@@ -405,19 +433,19 @@
         outs = (plain,) * (2 if flip < dp // 2 else 1)
         total, *rest = local_kernel(functools.partial(next_sum_kernel, conv_rows), outs, "sum_x", mine, other)
         coded = rest[0] if rest else None
-    return total, exchange(total, dp, fsdp, 0, 1, 0)
+    return total, exchange(total, dp, fsdp, 0, 1, 0), grad_head
 
 
 def shards(facies, prior_draws, recon_grad, w_embed, w_conv, w_head):
     dp, fsdp = lax.axis_size("dp"), lax.axis_size("fsdp")
-    block, one_hot, pre_embed, hidden, pre_conv, w_conv, w_head = forward(
+    block, pooled_lanes, recon_lanes, one_hot, pre_embed, hidden, pre_conv, w_conv, w_head = forward(
         facies, prior_draws, recon_grad, w_embed, w_conv, w_head
     )
     gathered = gather_blocks(block, dp * fsdp)
-    keep, send, grads, grad_head = backward((dp, fsdp), gathered, hidden, pre_conv, w_head)
+    keep, send, grads = backward(fsdp, gathered, pooled_lanes, recon_lanes, hidden, pre_conv, w_head)
     received = exchange(send, dp, fsdp, 0, 1, 0)
     embed = embed_gradient(fsdp, grads, w_conv, pre_embed, one_hot)
-    own, other = reduce_to_owner(keep, received, embed, dp, fsdp)
+    own, other, grad_head = reduce_to_owner(keep, received, embed, gathered, w_head, dp, fsdp)
     grad_embed, grad_conv = pl.pallas_call(
         output_kernel,
         out_shape=(

time: 43.3 us -> 43.5 us (level)
  Pallas kernels: 10.6 us -> 12.2 us
  waiting for transfers between devices: 10.6 us -> 9.44 us
    pallas_call x4 -> x5, Pallas kernels: 2.36 us -> 3.59 us  [the longest x1 1.83 us: backward(): pl.pallas_call(backward_kernel, out_shape=(payload, payload, pltpu.VMEM((...]
    ppermute x6, waiting for transfers between devices: 10.6 us -> 9.44 us  [exchange(): return lax.ppermute(block, GROUP, pairs)]
  transfers between devices with their start and end apart: 6 -> 6, of which waited for: 4 -> 4; matrix products, arithmetic and copies ran while one was open for 0% -> 0% of each run, Pallas kernels for 6% -> 9%
where the time goes in v14:
time: 43.5 us; the launch traced here: 43.3 us
  blocking collectives  14.8 us (34%)
  Pallas kernels  12.2 us (28%)
  waiting for transfers between devices  9.44 us (22%)
  starting transfers between devices  5.76 us (13%)
  between operations  0.77 us (2%)
    all_to_all x1, blocking collectives, gather_blocks(): return lax.all_to_all(copies, GROUP, 0, 0, tiled=True)  14.8 us
    ppermute x6, waiting for transfers between devices, exchange(): return lax.ppermute(block, GROUP, pairs)  9.44 us
    ppermute x6, starting transfers between devices, exchange(): return lax.ppermute(block, GROUP, pairs)  5.76 us
    pallas_call x1, Pallas kernels, forward(): pl.pallas_call(forward_kernel, out_shape=(pltpu.VMEM((samples, 2 * latent...  5.24 us
    pallas_call x1, Pallas kernels, embed_gradient(): pl.pallas_call(embed_kernel, out_shape=pltpu.VMEM((fsdp, (96 // fsdp + 7)...  2.56 us
    pallas_call x1, Pallas kernels, backward(): pl.pallas_call(backward_kernel, out_shape=(payload, payload, pltpu.VMEM((...  1.83 us
    pallas_call x1, Pallas kernels, head_gradient(): pl.pallas_call(head_kernel, out_shape=(jax.ShapeDtypeStruct((256 // fsdp,...  1.38 us
  transfers between devices with their start and end apart: 6, of which 4 were waited for; matrix products, arithmetic and copies ran while one was open for 0% of the time, Pallas kernels for 9%

profile of v14, /device:TPU:0, one launch (start us, length us, event | category | flops | bytes accessed | tf_op | source)
XLA Modules:
  0.0 43.3 jit_solution(5856661158134683463)
XLA Ops:
  0.6 5.2 %forward.1 = (bf16[4,1280]{1,0:T(4,128)(2,1)S(1)}, bf16[128,256]{1,0:T(8,128)(2,1)S(1)}, f32[128,512]{1,0:T(8,128)S(1)}, bf16[8,256,1024]{2,1,0:T(8,128)(2,1)S(1...) custom-call(s32[256,2048]{1,0:T(8,128)} %bitcast.1, ...), custom_call_target="tpu_custom_call" | custom-call | tf_op jit(solution)/shard_map/forward/pallas_call | solution.py:320
  5.9 14.8 %all_to_all.5.gathered = bf16[16,4,1280]{2,1,0:T(4,128)(2,1)S(1)} all-to-all(bf16[16,4,1280]{2,1,0:T(4,128)(2,1)S(1)} %broadcast_in_dim.2), channel_id=1, replica_groups=mesh['groups'=2,'dp'=4,'fsdp'=4] {'dp','fsdp'}, dimensions={0} | all-to-all | bytes 327680 | tf_op jit(solution)/shard_map/all_to_all | solution.py:397
  20.7 1.8 %backward.1 = (f32[4,128,256]{2,1,0:T(8,128)S(1)}, f32[4,128,256]{2,1,0:T(8,128)S(1)}, bf16[4,256,256]{2,1,0:T(8,128)(2,1)S(1)}) custom-call(bf16[16,4,1280]{2,1,0:T(4,128)(2,1)S(1)} %all_to_all.5.gathered, bf16[128,256]{1,0:T(8,128)(2,1)S(1)} %get-tuple-element.24.pooled_lanes, f32[128,512]{1,0:T(8,128)S(1)} %get-tuple-element.25.recon_lanes, ...), custom_call_target="tpu_custom_call" | custom-call | tf_op jit(solution)/shard_map/backward/pallas_call | solution.py:345
  22.6 0.3 collective-permute-start
  22.9 2.6 %embed_gradient.1.refs_2_ = f32[4,32,256]{2,1,0:T(8,128)S(1)} custom-call(bf16[4,256,256]{2,1,0:T(8,128)(2,1)S(1)} %get-tuple-element.31.grads, bf16[1024,256]{1,0:T(8,128)(2,1)S(1)} %get-tuple-element.32.w_conv, f32[4,256,1024]{2,1,0:T(8,128)S(1)} %get-tuple-element.33.pre_embed, bf16[8,256,1024]{2,1,0:T(8,128)(2,1)S(1)} %get-tuple-element.34.one_hot), custom_call_target="tpu_custom_call" | custom-call | flops 1600000000 | bytes 10485760 | tf_op jit(solution)/shard_map/embed_gradient/pallas_call | solution.py:371
  25.4 0.0 collective-permute-done.refs_1_
  25.4 0.2 scale.1
  25.6 0.1 reduce-precision_convert_fusion.2
  25.7 0.1 reduce-precision_convert_fusion.1
  25.8 0.1 reduce-precision_convert_fusion
  25.9 1.0 %collective-permute-start.3 = (f16[160,256]{1,0:T(8,128)(2,1)S(1)}, f16[160,256]{1,0:T(8,128)(2,1)S(1)}, u32[]{:S(2)}, u32[]{:S(2)}) collective-permute-start(f16[160,256]{1,0:T(8,128)(2,1)S(1)} %reduce-precision_convert_fusion), channel_id=1, source_target_pairs={{0,3},{1,2},{2,1},{3,0},{4,7},{5,6},{6,5},{7,4},{8,11},{9,10},{10,... | collective-permute-start | bytes 245768 | tf_op jit(solution)/shard_map/ppermute | solution.py:392
  26.9 1.2 %collective-permute-start.2 = (f16[160,256]{1,0:T(8,128)(2,1)S(1)}, f16[160,256]{1,0:T(8,128)(2,1)S(1)}, u32[]{:S(2)}, u32[]{:S(2)}) collective-permute-start(f16[160,256]{1,0:T(8,128)(2,1)S(1)} %reduce-precision_convert_fusion.1), channel_id=1, source_target_pairs={{0,2},{1,3},{2,0},{3,1},{4,6},{5,7},{6,4},{7,5},{8,10},{9,11},{10,... | collective-permute-start | bytes 245768 | tf_op jit(solution)/shard_map/ppermute | solution.py:392
  28.2 2.2 %collective-permute-start.1 = (f16[160,256]{1,0:T(8,128)(2,1)S(1)}, f16[160,256]{1,0:T(8,128)(2,1)S(1)}, u32[]{:S(2)}, u32[]{:S(2)}) collective-permute-start(f16[160,256]{1,0:T(8,128)(2,1)S(1)} %reduce-precision_convert_fusion.2), channel_id=1, source_target_pairs={{0,1},{1,0},{2,3},{3,2},{4,5},{5,4},{6,7},{7,6},{8,9},{9,8},{10,11... | collective-permute-start | bytes 245768 | tf_op jit(solution)/shard_map/ppermute | solution.py:392
  30.4 1.4 %head_gradient.1 = (f32[64,512]{1,0:T(8,128)}, f32[8,128]{1,0:T(8,128)S(1)}) custom-call(bf16[16,4,1280]{2,1,0:T(4,128)(2,1)S(1)} %all_to_all.5.gathered, bf16[256,512]{1,0:T(8,128)(2,1)S(1)} %get-tuple-element.28.w_head, f32[160,256]{1,0:T(8,128)S(1)} %get-tuple-element.35.after.refs_0_), custom_call_target="tpu_custom_call" | custom-call | flops 2000000000 | bytes 2097152 | tf_op jit(solution)/shard_map/head_gradient/pallas_call | solution.py:358
  31.8 1.4 %collective-permute-done.3 = f16[160,256]{1,0:T(8,128)(2,1)S(1)} collective-permute-done((f16[160,256]{1,0:T(8,128)(2,1)S(1)}, f16[160,256]{1,0:T(8,128)(2,1)S(1)}, u32[]{:S(2)}, u32[]{:S(2)}) %collective-permute-start.3) | collective-permute-done | bytes 81952 | tf_op jit(solution)/shard_map/ppermute | solution.py:392
  33.2 3.1 %collective-permute-done.2 = f16[160,256]{1,0:T(8,128)(2,1)S(1)} collective-permute-done((f16[160,256]{1,0:T(8,128)(2,1)S(1)}, f16[160,256]{1,0:T(8,128)(2,1)S(1)}, u32[]{:S(2)}, u32[]{:S(2)}) %collective-permute-start.2) | collective-permute-done | bytes 81952 | tf_op jit(solution)/shard_map/ppermute | solution.py:392
  36.3 0.0 collective-permute-done.1
  36.3 0.2 sum_z.1
  36.5 0.1 reduce-precision_convert_fusion.3
  36.6 0.9 %collective-permute-start.4 = (f16[160,256]{1,0:T(8,128)(2,1)S(1)}, f16[160,256]{1,0:T(8,128)(2,1)S(1)}, u32[]{:S(2)}, u32[]{:S(2)}) collective-permute-start(f16[160,256]{1,0:T(8,128)(2,1)S(1)} %get-tuple-element.43), channel_id=1, source_target_pairs={{0,8},{1,9},{2,10},{3,11},{4,12},{5,13},{6,14},{7,15},{8,0},{9,1},... | collective-permute-start | bytes 245768 | tf_op jit(solution)/shard_map/ppermute | solution.py:392
  37.5 3.6 %collective-permute-done.4 = f16[160,256]{1,0:T(8,128)(2,1)S(1)} collective-permute-done((f16[160,256]{1,0:T(8,128)(2,1)S(1)}, f16[160,256]{1,0:T(8,128)(2,1)S(1)}, u32[]{:S(2)}, u32[]{:S(2)}) %collective-permute-start.4) | collective-permute-done | bytes 81952 | tf_op jit(solution)/shard_map/ppermute | solution.py:392
  41.1 0.1 collective-permute-start.5
  41.2 1.4 %collective-permute-done.5.other = f32[160,256]{1,0:T(8,128)S(1)} collective-permute-done((f32[160,256]{1,0:T(8,128)S(1)}, f32[160,256]{1,0:T(8,128)S(1)}, u32[]{:S(2)}, u32[]{:S(2)}) %collective-permute-start.5) | collective-permute-done | bytes 163872 | tf_op jit(solution)/shard_map/ppermute | solution.py:392
  42.6 0.8 %outputs.1 = (f32[64,128]{1,0:T(8,128)}, f32[256,256]{1,0:T(8,128)}) custom-call(f32[160,256]{1,0:T(8,128)S(1)} %sum_x.1.own, f32[160,256]{1,0:T(8,128)S(1)} %collective-permute-done.5.other), custom_call_target="tpu_custom_call" | custom-call | tf_op jit(solution)/shard_map/outputs/pallas_call | solution.py:449
  (6 shorter events, 0.1 us)
Async XLA Ops:
  22.6 2.9 %collective-permute-start = (f32[4,128,256]{2,1,0:T(8,128)S(1)}, f32[4,128,256]{2,1,0:T(8,128)S(1)}, u32[]{:S(2)}, u32[]{:S(2)}) collective-permute-start(f32[4,128,256]{2,1,0:T(8,128)S(1)} %get-tuple-element.30), channel_id=1, source_target_pairs={{0,4},{1,5},{2,6},{3,7},{4,0},{5,1},{6,2},{7,3},{8,12},{9,13},{10,... | collective-permute-start | bytes 1572872 | tf_op jit(solution)/shard_map/ppermute | solution.py:392
  25.9 7.2 %collective-permute-start.3 = (f16[160,256]{1,0:T(8,128)(2,1)S(1)}, f16[160,256]{1,0:T(8,128)(2,1)S(1)}, u32[]{:S(2)}, u32[]{:S(2)}) collective-permute-start(f16[160,256]{1,0:T(8,128)(2,1)S(1)} %reduce-precision_convert_fusion), channel_id=1, source_target_pairs={{0,3},{1,2},{2,1},{3,0},{4,7},{5,6},{6,5},{7,4},{8,11},{9,10},{10,... | collective-permute-start | bytes 245768 | tf_op jit(solution)/shard_map/ppermute | solution.py:392
  26.9 9.3 %collective-permute-start.2 = (f16[160,256]{1,0:T(8,128)(2,1)S(1)}, f16[160,256]{1,0:T(8,128)(2,1)S(1)}, u32[]{:S(2)}, u32[]{:S(2)}) collective-permute-start(f16[160,256]{1,0:T(8,128)(2,1)S(1)} %reduce-precision_convert_fusion.1), channel_id=1, source_target_pairs={{0,2},{1,3},{2,0},{3,1},{4,6},{5,7},{6,4},{7,5},{8,10},{9,11},{10,... | collective-permute-start | bytes 245768 | tf_op jit(solution)/shard_map/ppermute | solution.py:392
  28.2 8.1 %collective-permute-start.1 = (f16[160,256]{1,0:T(8,128)(2,1)S(1)}, f16[160,256]{1,0:T(8,128)(2,1)S(1)}, u32[]{:S(2)}, u32[]{:S(2)}) collective-permute-start(f16[160,256]{1,0:T(8,128)(2,1)S(1)} %reduce-precision_convert_fusion.2), channel_id=1, source_target_pairs={{0,1},{1,0},{2,3},{3,2},{4,5},{5,4},{6,7},{7,6},{8,9},{9,8},{10,11... | collective-permute-start | bytes 245768 | tf_op jit(solution)/shard_map/ppermute | solution.py:392
  36.6 4.5 %collective-permute-start.4 = (f16[160,256]{1,0:T(8,128)(2,1)S(1)}, f16[160,256]{1,0:T(8,128)(2,1)S(1)}, u32[]{:S(2)}, u32[]{:S(2)}) collective-permute-start(f16[160,256]{1,0:T(8,128)(2,1)S(1)} %get-tuple-element.43), channel_id=1, source_target_pairs={{0,8},{1,9},{2,10},{3,11},{4,12},{5,13},{6,14},{7,15},{8,0},{9,1},... | collective-permute-start | bytes 245768 | tf_op jit(solution)/shard_map/ppermute | solution.py:392
  41.1 1.5 %collective-permute-start.5 = (f32[160,256]{1,0:T(8,128)S(1)}, f32[160,256]{1,0:T(8,128)S(1)}, u32[]{:S(2)}, u32[]{:S(2)}) collective-permute-start(f32[160,256]{1,0:T(8,128)S(1)} %sum_x.1.own), channel_id=1, source_target_pairs={{0,4},{1,5},{2,6},{3,7},{4,0},{5,1},{6,2},{7,3},{8,12},{9,13},{10,... | collective-permute-start | bytes 491528 | tf_op jit(solution)/shard_map/ppermute | solution.py:392

commit v15 on v11

--- a/solution.py
+++ b/solution.py
@@ -247,7 +247,7 @@
 
     own[...] = share(here)
     for place, target in enumerate(coded):
-        store_scaled(target, share(here ^ (place + 1)), steps, keep.shape[1])
+        store_scaled(target, share(here ^ (place % (keep.shape[0] - 1) + 1)), steps, keep.shape[1])
 
 
 def first_sum_kernel(conv_rows, own, *refs):
@@ -358,12 +358,14 @@
     return (2 * x + core) * fsdp + z
 
 
-def exchange(block, dp, fsdp, flip_x, flip_core, flip_z):
+def exchange(block, dp, fsdp, flip_x, flip_core, flip_z, among=None):
     pairs = []
     for x in range(dp // 2):
         for core in range(2):
             for z in range(fsdp):
-                pairs.append((place_of(x, core, z, fsdp), place_of(x ^ flip_x, core ^ flip_core, z ^ flip_z, fsdp)))
+                to = place_of(x ^ flip_x, core ^ flip_core, z ^ flip_z, fsdp)
+                if among is None or z in among:
+                    pairs.append((place_of(x, core, z, fsdp), to))
     return lax.ppermute(block, GROUP, pairs)
 
 
@@ -392,10 +394,13 @@
     conv_rows, width = keep.shape[1:]
     rows = conv_rows + embed.shape[1]
     plain = jax.ShapeDtypeStruct((rows, width), F32)
-    own, *coded = local_kernel(scale_kernel, (plain,) + (plain,) * (fsdp - 1), "scale", keep, other, embed)
-    received = [
-        exchange(to_half(part)[1], dp, fsdp, 0, 0, place + 1).astype(F32) for place, part in enumerate(coded)
-    ]
+    own, *coded = local_kernel(scale_kernel, (plain,) + (plain,) * (2 * fsdp - 2), "scale", keep, other, embed)
+    received = []
+    for place, part in enumerate(coded):
+        flip = place % (fsdp - 1) + 1
+        late = [0, flip]
+        among = late if place < fsdp - 1 else [z for z in range(fsdp) if z not in late]
+        received.append(exchange(part.astype(jnp.float16), dp, fsdp, 0, 0, flip, among).astype(F32))
     (coded,) = local_kernel(functools.partial(first_sum_kernel, conv_rows), (plain,), "sum_z", own, *received)
     flip = 1
     while flip < dp // 2:

time: 43.3 us -> 53.2 us (1.23)
  starting transfers between devices: 5.85 us -> 16.5 us
  waiting for transfers between devices: 10.6 us -> 9.74 us
    ppermute x6 -> x9, starting transfers between devices: 5.85 us -> 16.5 us  [exchange(): return lax.ppermute(block, GROUP, pairs)]
    ppermute x6 -> x9, waiting for transfers between devices: 10.6 us -> 9.74 us  [exchange(): return lax.ppermute(block, GROUP, pairs)]
  transfers between devices with their start and end apart: 6 -> 9, of which waited for: 4 -> 4; matrix products, arithmetic and copies ran while one was open for 0% -> 0% of each run, Pallas kernels for 6% -> 5%
where the time goes in v15:
time: 53.2 us; the launch traced here: 52.9 us
  starting transfers between devices  16.5 us (31%)
  blocking collectives  14.8 us (28%)
  Pallas kernels  10.7 us (20%)
  waiting for transfers between devices  9.74 us (18%)
  between operations  0.88 us (2%)
    ppermute x9, starting transfers between devices, exchange(): return lax.ppermute(block, GROUP, pairs)  16.5 us
    all_to_all x1, blocking collectives, gather_blocks(): return lax.all_to_all(copies, GROUP, 0, 0, tiled=True)  14.8 us
    ppermute x9, waiting for transfers between devices, exchange(): return lax.ppermute(block, GROUP, pairs)  9.74 us
    pallas_call x1, Pallas kernels, forward(): pl.pallas_call(forward_kernel, out_shape=(pltpu.VMEM((samples, 2 * latent...  4.93 us
    pallas_call x1, Pallas kernels, embed_gradient(): pl.pallas_call(embed_kernel, out_shape=pltpu.VMEM((fsdp, (96 // fsdp + 7)...  2.55 us
    pallas_call x1, Pallas kernels, backward(): pl.pallas_call(lambda *refs: backward_kernel(sizes, *refs), out_shape=(pa...  1.98 us
  transfers between devices with their start and end apart: 9, of which 4 were waited for; matrix products, arithmetic and copies ran while one was open for 0% of the time, Pallas kernels for 5%

profile of v15, /device:TPU:0, one launch (start us, length us, event | category | flops | bytes accessed | tf_op | source)
XLA Modules:
  0.0 52.9 jit_solution(16980240320035292794)
XLA Ops:
  0.6 4.9 %forward.1 = (bf16[4,1280]{1,0:T(4,128)(2,1)S(1)}, bf16[8,256,1024]{2,1,0:T(8,128)(2,1)S(1)}, f32[4,256,1024]{2,1,0:T(8,128)S(1)}, bf16[4,4,256,256]{3,2,1,0:T(8...) custom-call(s32[256,2048]{1,0:T(8,128)} %bitcast.1, ...), custom_call_target="tpu_custom_call" | custom-call | tf_op jit(solution)/shard_map/forward/pallas_call | solution.py:307
  5.6 14.8 %all_to_all.5.refs_0_ = bf16[16,4,1280]{2,1,0:T(4,128)(2,1)S(1)} all-to-all(bf16[16,4,1280]{2,1,0:T(4,128)(2,1)S(1)} %broadcast_in_dim.2), channel_id=1, replica_groups=mesh['groups'=2,'dp'=4,'fsdp'=4] {'dp','fsdp'}, dimensions={0} | all-to-all | bytes 327680 | tf_op jit(solution)/shard_map/all_to_all | solution.py:374
  20.4 2.0 %backward.1 = (f32[4,128,256]{2,1,0:T(8,128)S(1)}, f32[4,128,256]{2,1,0:T(8,128)S(1)}, bf16[4,256,256]{2,1,0:T(8,128)(2,1)S(1)}, f32[64,512]{1,0:T(8,128)}) custom-call(bf16[16,4,1280]{2,1,0:T(4,128)(2,1)S(1)} %all_to_all.5.refs_0_, bf16[4,4,256,256]{3,2,1,0:T(8,128)(2,1)S(1)} %get-tuple-element.24.refs_1_, f32[4,256,256]{2,1,0:T(8,128)S(1)} %get-tuple-element.25.refs_2_, ...), custom_call_target="tpu_custom_call" | custom-call | tf_op jit(solution)/shard_map/backward/pallas_call | solution.py:332
  22.4 0.3 collective-permute-start
  22.7 2.6 %embed_gradient.1.embed = f32[4,32,256]{2,1,0:T(8,128)S(1)} custom-call(bf16[4,256,256]{2,1,0:T(8,128)(2,1)S(1)} %get-tuple-element.29.grads, bf16[1024,256]{1,0:T(8,128)(2,1)S(1)} %get-tuple-element.30.w_conv, f32[4,256,1024]{2,1,0:T(8,128)S(1)} %get-tuple-element.31.pre_embed, bf16[8,256,1024]{2,1,0:T(8,128)(2,1)S(1)} %get-tuple-element.32.one_hot), custom_call_target="tpu_custom_call" | custom-call | flops 1600000000 | bytes 10485760 | tf_op jit(solution)/shard_map/embed_gradient/pallas_call | solution.py:346
  25.3 0.0 collective-permute-done.other
  25.3 0.2 scale.1
  25.5 0.7 %collective-permute-start.6 = (f16[160,256]{1,0:T(8,128)(2,1)S(1)}, f16[160,256]{1,0:T(8,128)(2,1)S(1)}, u32[]{:S(2)}, u32[]{:S(2)}) collective-permute-start(f16[160,256]{1,0:T(8,128)(2,1)S(1)} %convert_element_type.52), channel_id=1, source_target_pairs={{1,2},{2,1},{5,6},{6,5},{9,10},{10,9},{13,14},{14,13},{17,18},{18,... | collective-permute-start | bytes 245768 | tf_op jit(solution)/shard_map/ppermute | solution.py:369
  26.2 0.7 %collective-permute-start.5 = (f16[160,256]{1,0:T(8,128)(2,1)S(1)}, f16[160,256]{1,0:T(8,128)(2,1)S(1)}, u32[]{:S(2)}, u32[]{:S(2)}) collective-permute-start(f16[160,256]{1,0:T(8,128)(2,1)S(1)} %convert_element_type.50), channel_id=1, source_target_pairs={{1,3},{3,1},{5,7},{7,5},{9,11},{11,9},{13,15},{15,13},{17,19},{19,... | collective-permute-start | bytes 245768 | tf_op jit(solution)/shard_map/ppermute | solution.py:369
  26.9 0.7 %collective-permute-start.4 = (f16[160,256]{1,0:T(8,128)(2,1)S(1)}, f16[160,256]{1,0:T(8,128)(2,1)S(1)}, u32[]{:S(2)}, u32[]{:S(2)}) collective-permute-start(f16[160,256]{1,0:T(8,128)(2,1)S(1)} %convert_element_type.48), channel_id=1, source_target_pairs={{2,3},{3,2},{6,7},{7,6},{10,11},{11,10},{14,15},{15,14},{18,19},{1... | collective-permute-start | bytes 245768 | tf_op jit(solution)/shard_map/ppermute | solution.py:369
  27.6 9.5 %collective-permute-start.3 = (f16[160,256]{1,0:T(8,128)(2,1)S(1)}, f16[160,256]{1,0:T(8,128)(2,1)S(1)}, u32[]{:S(2)}, u32[]{:S(2)}) collective-permute-start(f16[160,256]{1,0:T(8,128)(2,1)S(1)} %convert_element_type.46), channel_id=1, source_target_pairs={{0,3},{3,0},{4,7},{7,4},{8,11},{11,8},{12,15},{15,12},{16,19},{19,... | collective-permute-start | bytes 245768 | tf_op jit(solution)/shard_map/ppermute | solution.py:369
  37.1 1.9 %collective-permute-start.2 = (f16[160,256]{1,0:T(8,128)(2,1)S(1)}, f16[160,256]{1,0:T(8,128)(2,1)S(1)}, u32[]{:S(2)}, u32[]{:S(2)}) collective-permute-start(f16[160,256]{1,0:T(8,128)(2,1)S(1)} %convert_element_type.44), channel_id=1, source_target_pairs={{0,2},{2,0},{4,6},{6,4},{8,10},{10,8},{12,14},{14,12},{16,18},{18,... | collective-permute-start | bytes 245768 | tf_op jit(solution)/shard_map/ppermute | solution.py:369
  39.1 0.0 collective-permute-done.6
  39.1 1.9 %collective-permute-start.1 = (f16[160,256]{1,0:T(8,128)(2,1)S(1)}, f16[160,256]{1,0:T(8,128)(2,1)S(1)}, u32[]{:S(2)}, u32[]{:S(2)}) collective-permute-start(f16[160,256]{1,0:T(8,128)(2,1)S(1)} %convert_element_type.42), channel_id=1, source_target_pairs={{0,1},{1,0},{4,5},{5,4},{8,9},{9,8},{12,13},{13,12},{16,17},{17,16... | collective-permute-start | bytes 245768 | tf_op jit(solution)/shard_map/ppermute | solution.py:369
  41.0 0.0 collective-permute-done.5
  41.1 0.0 collective-permute-done.4
  41.1 0.0 collective-permute-done.3
  41.1 3.4 %collective-permute-done.2 = f16[160,256]{1,0:T(8,128)(2,1)S(1)} collective-permute-done((f16[160,256]{1,0:T(8,128)(2,1)S(1)}, f16[160,256]{1,0:T(8,128)(2,1)S(1)}, u32[]{:S(2)}, u32[]{:S(2)}) %collective-permute-start.2) | collective-permute-done | bytes 81952 | tf_op jit(solution)/shard_map/ppermute | solution.py:369
  44.5 1.3 %collective-permute-done.1 = f16[160,256]{1,0:T(8,128)(2,1)S(1)} collective-permute-done((f16[160,256]{1,0:T(8,128)(2,1)S(1)}, f16[160,256]{1,0:T(8,128)(2,1)S(1)}, u32[]{:S(2)}, u32[]{:S(2)}) %collective-permute-start.1) | collective-permute-done | bytes 81952 | tf_op jit(solution)/shard_map/ppermute | solution.py:369
  45.8 0.2 sum_z.1
  46.0 0.1 reduce-precision_convert_fusion
  46.1 0.8 %collective-permute-start.7 = (f16[160,256]{1,0:T(8,128)(2,1)S(1)}, f16[160,256]{1,0:T(8,128)(2,1)S(1)}, u32[]{:S(2)}, u32[]{:S(2)}) collective-permute-start(f16[160,256]{1,0:T(8,128)(2,1)S(1)} %get-tuple-element.43), channel_id=1, source_target_pairs={{0,8},{1,9},{2,10},{3,11},{4,12},{5,13},{6,14},{7,15},{8,0},{9,1},... | collective-permute-start | bytes 245768 | tf_op jit(solution)/shard_map/ppermute | solution.py:369
  46.9 3.7 %collective-permute-done.7 = f16[160,256]{1,0:T(8,128)(2,1)S(1)} collective-permute-done((f16[160,256]{1,0:T(8,128)(2,1)S(1)}, f16[160,256]{1,0:T(8,128)(2,1)S(1)}, u32[]{:S(2)}, u32[]{:S(2)}) %collective-permute-start.7) | collective-permute-done | bytes 81952 | tf_op jit(solution)/shard_map/ppermute | solution.py:369
  50.7 0.1 collective-permute-start.8
  50.8 1.4 %collective-permute-done.8.other = f32[160,256]{1,0:T(8,128)S(1)} collective-permute-done((f32[160,256]{1,0:T(8,128)S(1)}, f32[160,256]{1,0:T(8,128)S(1)}, u32[]{:S(2)}, u32[]{:S(2)}) %collective-permute-start.8) | collective-permute-done | bytes 163872 | tf_op jit(solution)/shard_map/ppermute | solution.py:369
  52.1 0.8 %outputs.1 = (f32[64,128]{1,0:T(8,128)}, f32[256,256]{1,0:T(8,128)}) custom-call(f32[160,256]{1,0:T(8,128)S(1)} %sum_x.1.own, f32[160,256]{1,0:T(8,128)S(1)} %collective-permute-done.8.other), custom_call_target="tpu_custom_call" | custom-call | tf_op jit(solution)/shard_map/outputs/pallas_call | solution.py:426
  (15 shorter events, 0.2 us)
Async XLA Ops:
  22.4 2.9 %collective-permute-start = (f32[4,128,256]{2,1,0:T(8,128)S(1)}, f32[4,128,256]{2,1,0:T(8,128)S(1)}, u32[]{:S(2)}, u32[]{:S(2)}) collective-permute-start(f32[4,128,256]{2,1,0:T(8,128)S(1)} %get-tuple-element.28), channel_id=1, source_target_pairs={{0,4},{1,5},{2,6},{3,7},{4,0},{5,1},{6,2},{7,3},{8,12},{9,13},{10,... | collective-permute-start | bytes 1572872 | tf_op jit(solution)/shard_map/ppermute | solution.py:369
  25.5 13.6 %collective-permute-start.6 = (f16[160,256]{1,0:T(8,128)(2,1)S(1)}, f16[160,256]{1,0:T(8,128)(2,1)S(1)}, u32[]{:S(2)}, u32[]{:S(2)}) collective-permute-start(f16[160,256]{1,0:T(8,128)(2,1)S(1)} %convert_element_type.52), channel_id=1, source_target_pairs={{1,2},{2,1},{5,6},{6,5},{9,10},{10,9},{13,14},{14,13},{17,18},{18,... | collective-permute-start | bytes 245768 | tf_op jit(solution)/shard_map/ppermute | solution.py:369
  26.2 14.8 %collective-permute-start.5 = (f16[160,256]{1,0:T(8,128)(2,1)S(1)}, f16[160,256]{1,0:T(8,128)(2,1)S(1)}, u32[]{:S(2)}, u32[]{:S(2)}) collective-permute-start(f16[160,256]{1,0:T(8,128)(2,1)S(1)} %convert_element_type.50), channel_id=1, source_target_pairs={{1,3},{3,1},{5,7},{7,5},{9,11},{11,9},{13,15},{15,13},{17,19},{19,... | collective-permute-start | bytes 245768 | tf_op jit(solution)/shard_map/ppermute | solution.py:369
  26.9 14.1 %collective-permute-start.4 = (f16[160,256]{1,0:T(8,128)(2,1)S(1)}, f16[160,256]{1,0:T(8,128)(2,1)S(1)}, u32[]{:S(2)}, u32[]{:S(2)}) collective-permute-start(f16[160,256]{1,0:T(8,128)(2,1)S(1)} %convert_element_type.48), channel_id=1, source_target_pairs={{2,3},{3,2},{6,7},{7,6},{10,11},{11,10},{14,15},{15,14},{18,19},{1... | collective-permute-start | bytes 245768 | tf_op jit(solution)/shard_map/ppermute | solution.py:369
  27.6 13.5 %collective-permute-start.3 = (f16[160,256]{1,0:T(8,128)(2,1)S(1)}, f16[160,256]{1,0:T(8,128)(2,1)S(1)}, u32[]{:S(2)}, u32[]{:S(2)}) collective-permute-start(f16[160,256]{1,0:T(8,128)(2,1)S(1)} %convert_element_type.46), channel_id=1, source_target_pairs={{0,3},{3,0},{4,7},{7,4},{8,11},{11,8},{12,15},{15,12},{16,19},{19,... | collective-permute-start | bytes 245768 | tf_op jit(solution)/shard_map/ppermute | solution.py:369
  37.1 7.3 %collective-permute-start.2 = (f16[160,256]{1,0:T(8,128)(2,1)S(1)}, f16[160,256]{1,0:T(8,128)(2,1)S(1)}, u32[]{:S(2)}, u32[]{:S(2)}) collective-permute-start(f16[160,256]{1,0:T(8,128)(2,1)S(1)} %convert_element_type.44), channel_id=1, source_target_pairs={{0,2},{2,0},{4,6},{6,4},{8,10},{10,8},{12,14},{14,12},{16,18},{18,... | collective-permute-start | bytes 245768 | tf_op jit(solution)/shard_map/ppermute | solution.py:369
  39.1 6.7 %collective-permute-start.1 = (f16[160,256]{1,0:T(8,128)(2,1)S(1)}, f16[160,256]{1,0:T(8,128)(2,1)S(1)}, u32[]{:S(2)}, u32[]{:S(2)}) collective-permute-start(f16[160,256]{1,0:T(8,128)(2,1)S(1)} %convert_element_type.42), channel_id=1, source_target_pairs={{0,1},{1,0},{4,5},{5,4},{8,9},{9,8},{12,13},{13,12},{16,17},{17,16... | collective-permute-start | bytes 245768 | tf_op jit(solution)/shard_map/ppermute | solution.py:369
  46.1 4.5 %collective-permute-start.7 = (f16[160,256]{1,0:T(8,128)(2,1)S(1)}, f16[160,256]{1,0:T(8,128)(2,1)S(1)}, u32[]{:S(2)}, u32[]{:S(2)}) collective-permute-start(f16[160,256]{1,0:T(8,128)(2,1)S(1)} %get-tuple-element.43), channel_id=1, source_target_pairs={{0,8},{1,9},{2,10},{3,11},{4,12},{5,13},{6,14},{7,15},{8,0},{9,1},... | collective-permute-start | bytes 245768 | tf_op jit(solution)/shard_map/ppermute | solution.py:369
  50.7 1.5 %collective-permute-start.8 = (f32[160,256]{1,0:T(8,128)S(1)}, f32[160,256]{1,0:T(8,128)S(1)}, u32[]{:S(2)}, u32[]{:S(2)}) collective-permute-start(f32[160,256]{1,0:T(8,128)S(1)} %sum_x.1.own), channel_id=1, source_target_pairs={{0,4},{1,5},{2,6},{3,7},{4,0},{5,1},{6,2},{7,3},{8,12},{9,13},{10,... | collective-permute-start | bytes 491528 | tf_op jit(solution)/shard_map/ppermute | solution.py:369

commit v16 on v14

--- a/solution.py
+++ b/solution.py
@@ -48,8 +48,8 @@
 
 def forward_kernel(
     facies_hbm, prior_hbm, recon_hbm, w_embed_hbm, w_conv_hbm, w_head_hbm,
-    block, pooled_lanes, recon_lanes, one_hot, pre_embed, hidden, pre_conv, w_conv, w_head,
-    facies, prior, recon, w_embed, packed, conv_turned, sem
+    block, pooled_lanes, recon, one_hot, pre_embed, hidden, pre_conv, w_conv, w_head,
+    facies, prior, w_embed, packed, conv_turned, sem
 ):
     blocks = facies.shape[0]
     loads = [
@@ -67,16 +67,11 @@
     others[1].wait()
     conv_turned[...] = jnp.transpose(w_conv[...].astype(F32)).astype(BF16)
     low = iota((8, 256), 0) < 4
-    for half in range(2):
-        for load in loads[half * blocks // 2 : (half + 1) * blocks // 2]:
-            load.wait()
-        if half == 0:
-            for load in others[2:]:
-                load.start()
-        for t in range(8):
-            dx2, dx = t // 4, t % 4
+
+    def build(half, dx2):
+        for dx in range(4):
             rows = [
-                facies[2 * b2 + dy2, pl.ds(t, 32, stride=8), :]
+                facies[2 * b2 + dy2, pl.ds(4 * dx2 + dx, 32, stride=8), :]
                 for dy2 in range(2)
                 for b2 in range(4 * half, 4 * half + 4)
             ]
@@ -96,38 +91,43 @@
                         for dy2 in range(2):
                             at = (2 * dx2 + dy2) * 256 + half * 128
                             one_hot[2 * cp + dz2, pl.ds(first, 16), pl.ds(at, 128)] = hot[:, dy2 * 128 : dy2 * 128 + 128]
+
+    def embed(cp, dx2):
+        for dz2 in range(2):
+            rows, at = pl.ds(dz2 * 128, 128), pl.ds(dx2 * 512, 512)
+            pre = mm(packed[...], one_hot[2 * cp + dz2, :, at])
+            pre_embed[cp, rows, at] = pre
+            act = (pre * sigmoid(pre)).astype(BF16)
+            hidden[cp, 2 * dx2, rows, :] = act[:, :256]
+            hidden[cp, 2 * dx2 + 1, rows, :] = act[:, 256:]
+
+    for half in range(2):
+        for load in loads[half * blocks // 2 : (half + 1) * blocks // 2]:
+            load.wait()
+        if half == 0:
+            for load in others[2:]:
+                load.start()
+            build(0, 0)
+            build(0, 1)
+    build(1, 0)
+    for cp in range(4):
+        embed(cp, 0)
+    build(1, 1)
     sums = jnp.zeros((256, 128), F32)
     for cp in range(4):
-        for dz2 in range(2):
-            rows = pl.ds(dz2 * 128, 128)
-            for dx2 in range(2):
-                at = pl.ds(dx2 * 512, 512)
-                pre = mm(packed[...], one_hot[2 * cp + dz2, :, at])
-                pre_embed[cp, rows, at] = pre
-                act = (pre * sigmoid(pre)).astype(BF16)
-                hidden[cp, 2 * dx2, rows, :] = act[:, :256]
-                hidden[cp, 2 * dx2 + 1, rows, :] = act[:, 256:]
+        embed(cp, 1)
         pre = mm(conv_turned[...], hidden[cp].reshape(1024, 256))
         pre_conv[cp] = pre
         act = pre * sigmoid(pre)
         sums = sums + act[:, :128] + act[:, 128:]
-    for rows, every in ((8, 1), (128, 8)):
-        pick = iota((rows, 128), 1) // 8 % 4 == iota((rows, 128), 0) // every % 4
-        total = lax.dot_general(
-            jnp.where(pick, 1.0, 0.0), sums, NT, precision=lax.Precision.HIGHEST, preferred_element_type=F32
-        )
-        mean = (total / 256.0).astype(BF16)
-        if rows == 8:
-            block[:, pl.ds(1024, 256)] = mean[:4]
-        else:
-            pooled_lanes[...] = mean
+    pick = jnp.where(iota((128, 128), 1) // 8 % 4 == iota((128, 128), 0) // 8 % 4, 1.0, 0.0)
+    total = lax.dot_general(pick, sums, NT, precision=lax.Precision.HIGHEST, preferred_element_type=F32) / 256.0
+    pooled_lanes[...] = total.astype(BF16)
+    block[:, pl.ds(1024, 256)] = jnp.concatenate([total[8 * s : 8 * s + 1] for s in range(4)], axis=0).astype(BF16)
     for load in others[2:]:
         load.wait()
     block[:, pl.ds(0, 512)] = prior[...]
     block[:, pl.ds(512, 512)] = recon[...]
-    recon_float = recon[...].astype(F32)
-    for place in range(16):
-        recon_lanes[pl.ds(place * 8, 8), :] = jnp.broadcast_to(recon_float[place % 4 : place % 4 + 1], (8, recon.shape[1]))
 
 
 def pair_kernel(queries, query_square, keys):
@@ -170,11 +170,15 @@
     grad_head[...] = head_full[pl.ds(start, share), :]
 
 
-def backward_kernel(gathered, pooled_lanes, recon_lanes, hidden, pre_conv, w_head, keep, send, grads, ordered):
+def backward_kernel(gathered, pooled_lanes, recon, hidden, pre_conv, w_head, keep, send, grads, ordered):
     full = group_rows(gathered, ordered)
     queries = latent_rows(pooled_lanes[...], w_head)
     keys = latent_rows(full[:, 1024:].astype(BF16), w_head)
-    cotangent = cotangent_rows(queries, keys, full[:, :512].astype(BF16), recon_lanes[...])
+    recon_float = recon[...].astype(F32)
+    recon_lanes = jnp.concatenate(
+        [jnp.broadcast_to(recon_float[s : s + 1], (8, recon.shape[1])) for s in range(4)] * 4, axis=0
+    )
+    cotangent = cotangent_rows(queries, keys, full[:, :512].astype(BF16), recon_lanes)
     back_pool = mm_nt(w_head[...], cotangent) / 256.0
     back_pool = jnp.concatenate([back_pool, back_pool], axis=1)
     fsdp = keep.shape[0]
@@ -320,7 +324,7 @@
     return pl.pallas_call(
         forward_kernel,
         out_shape=(pltpu.VMEM((samples, 2 * latent_width + 256), BF16),)
-        + (pltpu.VMEM((128, 256), BF16), pltpu.VMEM((128, latent_width), F32))
+        + (pltpu.VMEM((128, 256), BF16), pltpu.VMEM(recon_grad.shape, BF16))
         + tuple(pltpu.VMEM(shape, kind) for shape, kind in SAVED)
         + (pltpu.VMEM(w_conv.shape, BF16), pltpu.VMEM(w_head.shape, BF16)),
         in_specs=[HBM] * 6,
@@ -328,7 +332,6 @@
         scratch_shapes=[
             pltpu.VMEM((lanes // 128, rows, 128), jnp.int32),
             pltpu.VMEM(prior_draws.shape, BF16),
-            pltpu.VMEM(recon_grad.shape, BF16),
             pltpu.VMEM(w_embed.shape, BF16),
             pltpu.VMEM((128, 256), BF16),
             pltpu.VMEM((256, 1024), BF16),
@@ -438,11 +441,11 @@
 
 def shards(facies, prior_draws, recon_grad, w_embed, w_conv, w_head):
     dp, fsdp = lax.axis_size("dp"), lax.axis_size("fsdp")
-    block, pooled_lanes, recon_lanes, one_hot, pre_embed, hidden, pre_conv, w_conv, w_head = forward(
+    block, pooled_lanes, recon, one_hot, pre_embed, hidden, pre_conv, w_conv, w_head = forward(
         facies, prior_draws, recon_grad, w_embed, w_conv, w_head
     )
     gathered = gather_blocks(block, dp * fsdp)
-    keep, send, grads = backward(fsdp, gathered, pooled_lanes, recon_lanes, hidden, pre_conv, w_head)
+    keep, send, grads = backward(fsdp, gathered, pooled_lanes, recon, hidden, pre_conv, w_head)
     received = exchange(send, dp, fsdp, 0, 1, 0)
     embed = embed_gradient(fsdp, grads, w_conv, pre_embed, one_hot)
     own, other, grad_head = reduce_to_owner(keep, received, embed, gathered, w_head, dp, fsdp)

time: 43.5 us -> 43.3 us (level)
  no operation moved by 1% of the time
where the time goes in v16:
time: 43.3 us; the launch traced here: 43.1 us
  blocking collectives  14.8 us (34%)
  Pallas kernels  11.9 us (27%)
  waiting for transfers between devices  9.45 us (22%)
  starting transfers between devices  5.75 us (13%)
  between operations  0.76 us (2%)
    all_to_all x1, blocking collectives, gather_blocks(): return lax.all_to_all(copies, GROUP, 0, 0, tiled=True)  14.8 us
    ppermute x6, waiting for transfers between devices, exchange(): return lax.ppermute(block, GROUP, pairs)  9.45 us
    ppermute x6, starting transfers between devices, exchange(): return lax.ppermute(block, GROUP, pairs)  5.75 us
    pallas_call x1, Pallas kernels, forward(): pl.pallas_call(forward_kernel, out_shape=(pltpu.VMEM((samples, 2 * latent...  5.09 us
    pallas_call x1, Pallas kernels, embed_gradient(): pl.pallas_call(embed_kernel, out_shape=pltpu.VMEM((fsdp, (96 // fsdp + 7)...  2.49 us
    pallas_call x1, Pallas kernels, backward(): pl.pallas_call(backward_kernel, out_shape=(payload, payload, pltpu.VMEM((...  1.83 us
    pallas_call x1, Pallas kernels, head_gradient(): pl.pallas_call(head_kernel, out_shape=(jax.ShapeDtypeStruct((256 // fsdp,...  1.39 us
  transfers between devices with their start and end apart: 6, of which 4 were waited for; matrix products, arithmetic and copies ran while one was open for 0% of the time, Pallas kernels for 9%

profile of v16, /device:TPU:0, one launch (start us, length us, event | category | flops | bytes accessed | tf_op | source)
XLA Modules:
  0.0 43.1 jit_solution(16264941370939915987)
XLA Ops:
  0.6 5.1 %forward.1 = (bf16[4,1280]{1,0:T(4,128)(2,1)S(1)}, bf16[128,256]{1,0:T(8,128)(2,1)S(1)}, bf16[4,512]{1,0:T(4,128)(2,1)S(1)}, bf16[8,256,1024]{2,1,0:T(8,128)(2,1...) custom-call(s32[256,2048]{1,0:T(8,128)} %bitcast.1, ...), custom_call_target="tpu_custom_call" | custom-call | tf_op jit(solution)/shard_map/forward/pallas_call | solution.py:324
  5.8 14.8 %all_to_all.5.gathered = bf16[16,4,1280]{2,1,0:T(4,128)(2,1)S(1)} all-to-all(bf16[16,4,1280]{2,1,0:T(4,128)(2,1)S(1)} %broadcast_in_dim.2), channel_id=1, replica_groups=mesh['groups'=2,'dp'=4,'fsdp'=4] {'dp','fsdp'}, dimensions={0} | all-to-all | bytes 327680 | tf_op jit(solution)/shard_map/all_to_all | solution.py:400
  20.6 1.8 %backward.1 = (f32[4,128,256]{2,1,0:T(8,128)S(1)}, f32[4,128,256]{2,1,0:T(8,128)S(1)}, bf16[4,256,256]{2,1,0:T(8,128)(2,1)S(1)}) custom-call(bf16[16,4,1280]{2,1,0:T(4,128)(2,1)S(1)} %all_to_all.5.gathered, bf16[128,256]{1,0:T(8,128)(2,1)S(1)} %get-tuple-element.24.pooled_lanes, bf16[4,512]{1,0:T(4,128)(2,1)S(1)} %get-tuple-element.25.recon, ...), custom_call_target="tpu_custom_call" | custom-call | tf_op jit(solution)/shard_map/backward/pallas_call | solution.py:348
  22.4 0.3 collective-permute-start
  22.7 2.5 %embed_gradient.1.refs_2_ = f32[4,32,256]{2,1,0:T(8,128)S(1)} custom-call(bf16[4,256,256]{2,1,0:T(8,128)(2,1)S(1)} %get-tuple-element.31.grads, bf16[1024,256]{1,0:T(8,128)(2,1)S(1)} %get-tuple-element.32.w_conv, f32[4,256,1024]{2,1,0:T(8,128)S(1)} %get-tuple-element.33.pre_embed, bf16[8,256,1024]{2,1,0:T(8,128)(2,1)S(1)} %get-tuple-element.34.one_hot), custom_call_target="tpu_custom_call" | custom-call | flops 1600000000 | bytes 10485760 | tf_op jit(solution)/shard_map/embed_gradient/pallas_call | solution.py:374
  25.2 0.0 collective-permute-done.refs_1_
  25.2 0.2 scale.1
  25.4 0.1 reduce-precision_convert_fusion.2
  25.5 0.1 reduce-precision_convert_fusion.1
  25.6 0.1 reduce-precision_convert_fusion
  25.7 1.0 %collective-permute-start.3 = (f16[160,256]{1,0:T(8,128)(2,1)S(1)}, f16[160,256]{1,0:T(8,128)(2,1)S(1)}, u32[]{:S(2)}, u32[]{:S(2)}) collective-permute-start(f16[160,256]{1,0:T(8,128)(2,1)S(1)} %reduce-precision_convert_fusion), channel_id=1, source_target_pairs={{0,3},{1,2},{2,1},{3,0},{4,7},{5,6},{6,5},{7,4},{8,11},{9,10},{10,... | collective-permute-start | bytes 245768 | tf_op jit(solution)/shard_map/ppermute | solution.py:395
  26.7 1.2 %collective-permute-start.2 = (f16[160,256]{1,0:T(8,128)(2,1)S(1)}, f16[160,256]{1,0:T(8,128)(2,1)S(1)}, u32[]{:S(2)}, u32[]{:S(2)}) collective-permute-start(f16[160,256]{1,0:T(8,128)(2,1)S(1)} %reduce-precision_convert_fusion.1), channel_id=1, source_target_pairs={{0,2},{1,3},{2,0},{3,1},{4,6},{5,7},{6,4},{7,5},{8,10},{9,11},{10,... | collective-permute-start | bytes 245768 | tf_op jit(solution)/shard_map/ppermute | solution.py:395
  27.9 2.2 %collective-permute-start.1 = (f16[160,256]{1,0:T(8,128)(2,1)S(1)}, f16[160,256]{1,0:T(8,128)(2,1)S(1)}, u32[]{:S(2)}, u32[]{:S(2)}) collective-permute-start(f16[160,256]{1,0:T(8,128)(2,1)S(1)} %reduce-precision_convert_fusion.2), channel_id=1, source_target_pairs={{0,1},{1,0},{2,3},{3,2},{4,5},{5,4},{6,7},{7,6},{8,9},{9,8},{10,11... | collective-permute-start | bytes 245768 | tf_op jit(solution)/shard_map/ppermute | solution.py:395
  30.2 1.4 %head_gradient.1 = (f32[64,512]{1,0:T(8,128)}, f32[8,128]{1,0:T(8,128)S(1)}) custom-call(bf16[16,4,1280]{2,1,0:T(4,128)(2,1)S(1)} %all_to_all.5.gathered, bf16[256,512]{1,0:T(8,128)(2,1)S(1)} %get-tuple-element.28.w_head, f32[160,256]{1,0:T(8,128)S(1)} %get-tuple-element.35.after.refs_0_), custom_call_target="tpu_custom_call" | custom-call | flops 2000000000 | bytes 2097152 | tf_op jit(solution)/shard_map/head_gradient/pallas_call | solution.py:361
  31.5 1.4 %collective-permute-done.3 = f16[160,256]{1,0:T(8,128)(2,1)S(1)} collective-permute-done((f16[160,256]{1,0:T(8,128)(2,1)S(1)}, f16[160,256]{1,0:T(8,128)(2,1)S(1)}, u32[]{:S(2)}, u32[]{:S(2)}) %collective-permute-start.3) | collective-permute-done | bytes 81952 | tf_op jit(solution)/shard_map/ppermute | solution.py:395
  33.0 3.1 %collective-permute-done.2 = f16[160,256]{1,0:T(8,128)(2,1)S(1)} collective-permute-done((f16[160,256]{1,0:T(8,128)(2,1)S(1)}, f16[160,256]{1,0:T(8,128)(2,1)S(1)}, u32[]{:S(2)}, u32[]{:S(2)}) %collective-permute-start.2) | collective-permute-done | bytes 81952 | tf_op jit(solution)/shard_map/ppermute | solution.py:395
  36.0 0.0 collective-permute-done.1
  36.1 0.2 sum_z.1
  36.2 0.1 reduce-precision_convert_fusion.3
  36.3 0.9 %collective-permute-start.4 = (f16[160,256]{1,0:T(8,128)(2,1)S(1)}, f16[160,256]{1,0:T(8,128)(2,1)S(1)}, u32[]{:S(2)}, u32[]{:S(2)}) collective-permute-start(f16[160,256]{1,0:T(8,128)(2,1)S(1)} %get-tuple-element.43), channel_id=1, source_target_pairs={{0,8},{1,9},{2,10},{3,11},{4,12},{5,13},{6,14},{7,15},{8,0},{9,1},... | collective-permute-start | bytes 245768 | tf_op jit(solution)/shard_map/ppermute | solution.py:395
  37.3 3.6 %collective-permute-done.4 = f16[160,256]{1,0:T(8,128)(2,1)S(1)} collective-permute-done((f16[160,256]{1,0:T(8,128)(2,1)S(1)}, f16[160,256]{1,0:T(8,128)(2,1)S(1)}, u32[]{:S(2)}, u32[]{:S(2)}) %collective-permute-start.4) | collective-permute-done | bytes 81952 | tf_op jit(solution)/shard_map/ppermute | solution.py:395
  40.9 0.1 collective-permute-start.5
  41.0 1.4 %collective-permute-done.5.other = f32[160,256]{1,0:T(8,128)S(1)} collective-permute-done((f32[160,256]{1,0:T(8,128)S(1)}, f32[160,256]{1,0:T(8,128)S(1)}, u32[]{:S(2)}, u32[]{:S(2)}) %collective-permute-start.5) | collective-permute-done | bytes 163872 | tf_op jit(solution)/shard_map/ppermute | solution.py:395
  42.4 0.8 %outputs.1 = (f32[64,128]{1,0:T(8,128)}, f32[256,256]{1,0:T(8,128)}) custom-call(f32[160,256]{1,0:T(8,128)S(1)} %sum_x.1.own, f32[160,256]{1,0:T(8,128)S(1)} %collective-permute-done.5.other), custom_call_target="tpu_custom_call" | custom-call | tf_op jit(solution)/shard_map/outputs/pallas_call | solution.py:452
  (6 shorter events, 0.1 us)
Async XLA Ops:
  22.4 2.8 %collective-permute-start = (f32[4,128,256]{2,1,0:T(8,128)S(1)}, f32[4,128,256]{2,1,0:T(8,128)S(1)}, u32[]{:S(2)}, u32[]{:S(2)}) collective-permute-start(f32[4,128,256]{2,1,0:T(8,128)S(1)} %get-tuple-element.30), channel_id=1, source_target_pairs={{0,4},{1,5},{2,6},{3,7},{4,0},{5,1},{6,2},{7,3},{8,12},{9,13},{10,... | collective-permute-start | bytes 1572872 | tf_op jit(solution)/shard_map/ppermute | solution.py:395
  25.7 7.2 %collective-permute-start.3 = (f16[160,256]{1,0:T(8,128)(2,1)S(1)}, f16[160,256]{1,0:T(8,128)(2,1)S(1)}, u32[]{:S(2)}, u32[]{:S(2)}) collective-permute-start(f16[160,256]{1,0:T(8,128)(2,1)S(1)} %reduce-precision_convert_fusion), channel_id=1, source_target_pairs={{0,3},{1,2},{2,1},{3,0},{4,7},{5,6},{6,5},{7,4},{8,11},{9,10},{10,... | collective-permute-start | bytes 245768 | tf_op jit(solution)/shard_map/ppermute | solution.py:395
  26.7 9.3 %collective-permute-start.2 = (f16[160,256]{1,0:T(8,128)(2,1)S(1)}, f16[160,256]{1,0:T(8,128)(2,1)S(1)}, u32[]{:S(2)}, u32[]{:S(2)}) collective-permute-start(f16[160,256]{1,0:T(8,128)(2,1)S(1)} %reduce-precision_convert_fusion.1), channel_id=1, source_target_pairs={{0,2},{1,3},{2,0},{3,1},{4,6},{5,7},{6,4},{7,5},{8,10},{9,11},{10,... | collective-permute-start | bytes 245768 | tf_op jit(solution)/shard_map/ppermute | solution.py:395
  27.9 8.1 %collective-permute-start.1 = (f16[160,256]{1,0:T(8,128)(2,1)S(1)}, f16[160,256]{1,0:T(8,128)(2,1)S(1)}, u32[]{:S(2)}, u32[]{:S(2)}) collective-permute-start(f16[160,256]{1,0:T(8,128)(2,1)S(1)} %reduce-precision_convert_fusion.2), channel_id=1, source_target_pairs={{0,1},{1,0},{2,3},{3,2},{4,5},{5,4},{6,7},{7,6},{8,9},{9,8},{10,11... | collective-permute-start | bytes 245768 | tf_op jit(solution)/shard_map/ppermute | solution.py:395
  36.3 4.5 %collective-permute-start.4 = (f16[160,256]{1,0:T(8,128)(2,1)S(1)}, f16[160,256]{1,0:T(8,128)(2,1)S(1)}, u32[]{:S(2)}, u32[]{:S(2)}) collective-permute-start(f16[160,256]{1,0:T(8,128)(2,1)S(1)} %get-tuple-element.43), channel_id=1, source_target_pairs={{0,8},{1,9},{2,10},{3,11},{4,12},{5,13},{6,14},{7,15},{8,0},{9,1},... | collective-permute-start | bytes 245768 | tf_op jit(solution)/shard_map/ppermute | solution.py:395
  40.9 1.5 %collective-permute-start.5 = (f32[160,256]{1,0:T(8,128)S(1)}, f32[160,256]{1,0:T(8,128)S(1)}, u32[]{:S(2)}, u32[]{:S(2)}) collective-permute-start(f32[160,256]{1,0:T(8,128)S(1)} %sum_x.1.own), channel_id=1, source_target_pairs={{0,4},{1,5},{2,6},{3,7},{4,0},{5,1},{6,2},{7,3},{8,12},{9,13},{10,... | collective-permute-start | bytes 491528 | tf_op jit(solution)/shard_map/ppermute | solution.py:395

commit v17 on v16

--- a/solution.py
+++ b/solution.py
@@ -395,9 +395,11 @@
     return lax.ppermute(block, GROUP, pairs)
 
 
-def gather_blocks(block, devices):
+def gather_blocks(block, dp, fsdp):
+    devices = dp * fsdp
+    order = [row * fsdp + z for z in reversed(range(fsdp)) for row in range(dp)]
     copies = jnp.broadcast_to(block[None], (devices,) + block.shape)
-    return lax.all_to_all(copies, GROUP, 0, 0, tiled=True)
+    return lax.all_to_all(copies, GROUP, 0, 0, axis_index_groups=[order], tiled=True)
 
 
 def local_kernel(kernel, outs, name, *operands, unread=()):
@@ -444,7 +446,7 @@
     block, pooled_lanes, recon, one_hot, pre_embed, hidden, pre_conv, w_conv, w_head = forward(
         facies, prior_draws, recon_grad, w_embed, w_conv, w_head
     )
-    gathered = gather_blocks(block, dp * fsdp)
+    gathered = gather_blocks(block, dp, fsdp)
     keep, send, grads = backward(fsdp, gathered, pooled_lanes, recon, hidden, pre_conv, w_head)
     received = exchange(send, dp, fsdp, 0, 1, 0)
     embed = embed_gradient(fsdp, grads, w_conv, pre_embed, one_hot)

time: 43.3 us -> 42 us (0.970)
  blocking collectives: 14.8 us -> 13.2 us
  waiting for transfers between devices: 9.45 us -> 10.3 us
  starting transfers between devices: 5.75 us -> 5.15 us
    all_to_all x1, blocking collectives: 14.8 us -> 13.2 us  [gather_blocks(): lax.all_to_all(copies, GROUP, 0, 0, axis_index_groups=[order], tiled=True)]
    ppermute x6, waiting for transfers between devices: 9.45 us -> 10.3 us  [exchange(): return lax.ppermute(block, GROUP, pairs)]
    ppermute x6, starting transfers between devices: 5.75 us -> 5.15 us  [exchange(): return lax.ppermute(block, GROUP, pairs)]
where the time goes in v17:
time: 42 us; the launch traced here: 41.8 us
  blocking collectives  13.2 us (31%)
  Pallas kernels  11.9 us (28%)
  waiting for transfers between devices  10.3 us (25%)
  starting transfers between devices  5.15 us (12%)
  between operations  0.76 us (2%)
    all_to_all x1, blocking collectives, gather_blocks(): lax.all_to_all(copies, GROUP, 0, 0, axis_index_groups=[order], tiled=True)  13.2 us
    ppermute x6, waiting for transfers between devices, exchange(): return lax.ppermute(block, GROUP, pairs)  10.3 us
    ppermute x6, starting transfers between devices, exchange(): return lax.ppermute(block, GROUP, pairs)  5.15 us
    pallas_call x1, Pallas kernels, forward(): pl.pallas_call(forward_kernel, out_shape=(pltpu.VMEM((samples, 2 * latent...  5.09 us
    pallas_call x1, Pallas kernels, embed_gradient(): pl.pallas_call(embed_kernel, out_shape=pltpu.VMEM((fsdp, (96 // fsdp + 7)...  2.49 us
    pallas_call x1, Pallas kernels, backward(): pl.pallas_call(backward_kernel, out_shape=(payload, payload, pltpu.VMEM((...  1.83 us
    pallas_call x1, Pallas kernels, head_gradient(): pl.pallas_call(head_kernel, out_shape=(jax.ShapeDtypeStruct((256 // fsdp,...  1.38 us
  transfers between devices with their start and end apart: 6, of which 4 were waited for; matrix products, arithmetic and copies ran while one was open for 0% of the time, Pallas kernels for 9%

profile of v17, /device:TPU:0, one launch (start us, length us, event | category | flops | bytes accessed | tf_op | source)
XLA Modules:
  0.0 41.8 jit_solution(9107542844200360963)
XLA Ops:
  0.6 5.1 %forward.1 = (bf16[4,1280]{1,0:T(4,128)(2,1)S(1)}, bf16[128,256]{1,0:T(8,128)(2,1)S(1)}, bf16[4,512]{1,0:T(4,128)(2,1)S(1)}, bf16[8,256,1024]{2,1,0:T(8,128)(2,1...) custom-call(s32[256,2048]{1,0:T(8,128)} %bitcast.1, ...), custom_call_target="tpu_custom_call" | custom-call | tf_op jit(solution)/shard_map/forward/pallas_call | solution.py:324
  5.8 13.2 %all_to_all.5.gathered = bf16[16,4,1280]{2,1,0:T(4,128)(2,1)S(1)} all-to-all(bf16[16,4,1280]{2,1,0:T(4,128)(2,1)S(1)} %broadcast_in_dim.2), channel_id=1, replica_groups={{3,7,11,15,2,6,10,14,1,5,9,13,0,4,8,12},{19,23,27,31,18,22,26,30,17,21,..., dimensions={0} | all-to-all | bytes 327680 | tf_op jit(solution)/shard_map/all_to_all | solution.py:402
  18.9 1.8 %backward.1 = (f32[4,128,256]{2,1,0:T(8,128)S(1)}, f32[4,128,256]{2,1,0:T(8,128)S(1)}, bf16[4,256,256]{2,1,0:T(8,128)(2,1)S(1)}) custom-call(bf16[16,4,1280]{2,1,0:T(4,128)(2,1)S(1)} %all_to_all.5.gathered, bf16[128,256]{1,0:T(8,128)(2,1)S(1)} %get-tuple-element.24.pooled_lanes, bf16[4,512]{1,0:T(4,128)(2,1)S(1)} %get-tuple-element.25.recon, ...), custom_call_target="tpu_custom_call" | custom-call | tf_op jit(solution)/shard_map/backward/pallas_call | solution.py:348
  20.8 0.3 collective-permute-start
  21.1 2.5 %embed_gradient.1.refs_2_ = f32[4,32,256]{2,1,0:T(8,128)S(1)} custom-call(bf16[4,256,256]{2,1,0:T(8,128)(2,1)S(1)} %get-tuple-element.31.grads, bf16[1024,256]{1,0:T(8,128)(2,1)S(1)} %get-tuple-element.32.w_conv, f32[4,256,1024]{2,1,0:T(8,128)S(1)} %get-tuple-element.33.pre_embed, bf16[8,256,1024]{2,1,0:T(8,128)(2,1)S(1)} %get-tuple-element.34.one_hot), custom_call_target="tpu_custom_call" | custom-call | flops 1600000000 | bytes 10485760 | tf_op jit(solution)/shard_map/embed_gradient/pallas_call | solution.py:374
  23.6 0.0 collective-permute-done.refs_1_
  23.6 0.2 scale.1
  23.8 0.1 reduce-precision_convert_fusion.2
  23.9 0.1 reduce-precision_convert_fusion.1
  24.0 0.1 reduce-precision_convert_fusion
  24.1 2.9 %collective-permute-start.3 = (f16[160,256]{1,0:T(8,128)(2,1)S(1)}, f16[160,256]{1,0:T(8,128)(2,1)S(1)}, u32[]{:S(2)}, u32[]{:S(2)}) collective-permute-start(f16[160,256]{1,0:T(8,128)(2,1)S(1)} %reduce-precision_convert_fusion), channel_id=1, source_target_pairs={{0,3},{1,2},{2,1},{3,0},{4,7},{5,6},{6,5},{7,4},{8,11},{9,10},{10,... | collective-permute-start | bytes 245768 | tf_op jit(solution)/shard_map/ppermute | solution.py:395
  26.9 0.0 collective-permute-start.2
  26.9 1.6 %collective-permute-start.1 = (f16[160,256]{1,0:T(8,128)(2,1)S(1)}, f16[160,256]{1,0:T(8,128)(2,1)S(1)}, u32[]{:S(2)}, u32[]{:S(2)}) collective-permute-start(f16[160,256]{1,0:T(8,128)(2,1)S(1)} %reduce-precision_convert_fusion.2), channel_id=1, source_target_pairs={{0,1},{1,0},{2,3},{3,2},{4,5},{5,4},{6,7},{7,6},{8,9},{9,8},{10,11... | collective-permute-start | bytes 245768 | tf_op jit(solution)/shard_map/ppermute | solution.py:395
  28.5 1.4 %head_gradient.1 = (f32[64,512]{1,0:T(8,128)}, f32[8,128]{1,0:T(8,128)S(1)}) custom-call(bf16[16,4,1280]{2,1,0:T(4,128)(2,1)S(1)} %all_to_all.5.gathered, bf16[256,512]{1,0:T(8,128)(2,1)S(1)} %get-tuple-element.28.w_head, f32[160,256]{1,0:T(8,128)S(1)} %get-tuple-element.35.after.refs_0_), custom_call_target="tpu_custom_call" | custom-call | flops 2000000000 | bytes 2097152 | tf_op jit(solution)/shard_map/head_gradient/pallas_call | solution.py:361
  29.9 1.4 %collective-permute-done.3 = f16[160,256]{1,0:T(8,128)(2,1)S(1)} collective-permute-done((f16[160,256]{1,0:T(8,128)(2,1)S(1)}, f16[160,256]{1,0:T(8,128)(2,1)S(1)}, u32[]{:S(2)}, u32[]{:S(2)}) %collective-permute-start.3) | collective-permute-done | bytes 81952 | tf_op jit(solution)/shard_map/ppermute | solution.py:395
  31.3 3.4 %collective-permute-done.2 = f16[160,256]{1,0:T(8,128)(2,1)S(1)} collective-permute-done((f16[160,256]{1,0:T(8,128)(2,1)S(1)}, f16[160,256]{1,0:T(8,128)(2,1)S(1)}, u32[]{:S(2)}, u32[]{:S(2)}) %collective-permute-start.2) | collective-permute-done | bytes 81952 | tf_op jit(solution)/shard_map/ppermute | solution.py:395
  34.7 0.0 collective-permute-done.1
  34.7 0.2 sum_z.1
  34.9 0.1 reduce-precision_convert_fusion.3
  35.0 0.3 collective-permute-start.4
  35.3 4.2 %collective-permute-done.4 = f16[160,256]{1,0:T(8,128)(2,1)S(1)} collective-permute-done((f16[160,256]{1,0:T(8,128)(2,1)S(1)}, f16[160,256]{1,0:T(8,128)(2,1)S(1)}, u32[]{:S(2)}, u32[]{:S(2)}) %collective-permute-start.4) | collective-permute-done | bytes 81952 | tf_op jit(solution)/shard_map/ppermute | solution.py:395
  39.5 0.1 collective-permute-start.5
  39.6 1.4 %collective-permute-done.5.other = f32[160,256]{1,0:T(8,128)S(1)} collective-permute-done((f32[160,256]{1,0:T(8,128)S(1)}, f32[160,256]{1,0:T(8,128)S(1)}, u32[]{:S(2)}, u32[]{:S(2)}) %collective-permute-start.5) | collective-permute-done | bytes 163872 | tf_op jit(solution)/shard_map/ppermute | solution.py:395
  41.0 0.8 %outputs.1 = (f32[64,128]{1,0:T(8,128)}, f32[256,256]{1,0:T(8,128)}) custom-call(f32[160,256]{1,0:T(8,128)S(1)} %sum_x.1.own, f32[160,256]{1,0:T(8,128)S(1)} %collective-permute-done.5.other), custom_call_target="tpu_custom_call" | custom-call | tf_op jit(solution)/shard_map/outputs/pallas_call | solution.py:454
  (6 shorter events, 0.1 us)
Async XLA Ops:
  20.8 2.8 %collective-permute-start = (f32[4,128,256]{2,1,0:T(8,128)S(1)}, f32[4,128,256]{2,1,0:T(8,128)S(1)}, u32[]{:S(2)}, u32[]{:S(2)}) collective-permute-start(f32[4,128,256]{2,1,0:T(8,128)S(1)} %get-tuple-element.30), channel_id=1, source_target_pairs={{0,4},{1,5},{2,6},{3,7},{4,0},{5,1},{6,2},{7,3},{8,12},{9,13},{10,... | collective-permute-start | bytes 1572872 | tf_op jit(solution)/shard_map/ppermute | solution.py:395
  24.1 7.2 %collective-permute-start.3 = (f16[160,256]{1,0:T(8,128)(2,1)S(1)}, f16[160,256]{1,0:T(8,128)(2,1)S(1)}, u32[]{:S(2)}, u32[]{:S(2)}) collective-permute-start(f16[160,256]{1,0:T(8,128)(2,1)S(1)} %reduce-precision_convert_fusion), channel_id=1, source_target_pairs={{0,3},{1,2},{2,1},{3,0},{4,7},{5,6},{6,5},{7,4},{8,11},{9,10},{10,... | collective-permute-start | bytes 245768 | tf_op jit(solution)/shard_map/ppermute | solution.py:395
  26.9 7.7 %collective-permute-start.2 = (f16[160,256]{1,0:T(8,128)(2,1)S(1)}, f16[160,256]{1,0:T(8,128)(2,1)S(1)}, u32[]{:S(2)}, u32[]{:S(2)}) collective-permute-start(f16[160,256]{1,0:T(8,128)(2,1)S(1)} %reduce-precision_convert_fusion.1), channel_id=1, source_target_pairs={{0,2},{1,3},{2,0},{3,1},{4,6},{5,7},{6,4},{7,5},{8,10},{9,11},{10,... | collective-permute-start | bytes 245768 | tf_op jit(solution)/shard_map/ppermute | solution.py:395
  26.9 7.7 %collective-permute-start.1 = (f16[160,256]{1,0:T(8,128)(2,1)S(1)}, f16[160,256]{1,0:T(8,128)(2,1)S(1)}, u32[]{:S(2)}, u32[]{:S(2)}) collective-permute-start(f16[160,256]{1,0:T(8,128)(2,1)S(1)} %reduce-precision_convert_fusion.2), channel_id=1, source_target_pairs={{0,1},{1,0},{2,3},{3,2},{4,5},{5,4},{6,7},{7,6},{8,9},{9,8},{10,11... | collective-permute-start | bytes 245768 | tf_op jit(solution)/shard_map/ppermute | solution.py:395
  35.0 4.5 %collective-permute-start.4 = (f16[160,256]{1,0:T(8,128)(2,1)S(1)}, f16[160,256]{1,0:T(8,128)(2,1)S(1)}, u32[]{:S(2)}, u32[]{:S(2)}) collective-permute-start(f16[160,256]{1,0:T(8,128)(2,1)S(1)} %get-tuple-element.43), channel_id=1, source_target_pairs={{0,8},{1,9},{2,10},{3,11},{4,12},{5,13},{6,14},{7,15},{8,0},{9,1},... | collective-permute-start | bytes 245768 | tf_op jit(solution)/shard_map/ppermute | solution.py:395
  39.5 1.5 %collective-permute-start.5 = (f32[160,256]{1,0:T(8,128)S(1)}, f32[160,256]{1,0:T(8,128)S(1)}, u32[]{:S(2)}, u32[]{:S(2)}) collective-permute-start(f32[160,256]{1,0:T(8,128)S(1)} %sum_x.1.own), channel_id=1, source_target_pairs={{0,4},{1,5},{2,6},{3,7},{4,0},{5,1},{6,2},{7,3},{8,12},{9,13},{10,... | collective-permute-start | bytes 491528 | tf_op jit(solution)/shard_map/ppermute | solution.py:395

commit v18 on v17

--- a/solution.py
+++ b/solution.py
@@ -397,7 +397,9 @@
 
 def gather_blocks(block, dp, fsdp):
     devices = dp * fsdp
-    order = [row * fsdp + z for z in reversed(range(fsdp)) for row in range(dp)]
+    order = [
+        place_of(x, core, z, fsdp) for z in reversed(range(fsdp)) for x in reversed(range(dp // 2)) for core in range(2)
+    ]
     copies = jnp.broadcast_to(block[None], (devices,) + block.shape)
     return lax.all_to_all(copies, GROUP, 0, 0, axis_index_groups=[order], tiled=True)
 

time: 42 us -> 41.6 us (level)
  waiting for transfers between devices: 10.3 us -> 8.4 us
  starting transfers between devices: 5.15 us -> 6.47 us
    ppermute x6, waiting for transfers between devices: 10.3 us -> 8.4 us  [exchange(): return lax.ppermute(block, GROUP, pairs)]
    ppermute x6, starting transfers between devices: 5.15 us -> 6.47 us  [exchange(): return lax.ppermute(block, GROUP, pairs)]
where the time goes in v18:
time: 41.6 us; the launch traced here: 41.5 us
  blocking collectives  13.5 us (32%)
  Pallas kernels  11.9 us (29%)
  waiting for transfers between devices  8.4 us (20%)
  starting transfers between devices  6.47 us (16%)
  between operations  0.76 us (2%)
    all_to_all x1, blocking collectives, gather_blocks(): lax.all_to_all(copies, GROUP, 0, 0, axis_index_groups=[order], tiled=True)  13.5 us
    ppermute x6, waiting for transfers between devices, exchange(): return lax.ppermute(block, GROUP, pairs)  8.4 us
    ppermute x6, starting transfers between devices, exchange(): return lax.ppermute(block, GROUP, pairs)  6.47 us
    pallas_call x1, Pallas kernels, forward(): pl.pallas_call(forward_kernel, out_shape=(pltpu.VMEM((samples, 2 * latent...  5.09 us
    pallas_call x1, Pallas kernels, embed_gradient(): pl.pallas_call(embed_kernel, out_shape=pltpu.VMEM((fsdp, (96 // fsdp + 7)...  2.48 us
    pallas_call x1, Pallas kernels, backward(): pl.pallas_call(backward_kernel, out_shape=(payload, payload, pltpu.VMEM((...  1.83 us
    pallas_call x1, Pallas kernels, head_gradient(): pl.pallas_call(head_kernel, out_shape=(jax.ShapeDtypeStruct((256 // fsdp,...  1.38 us
  transfers between devices with their start and end apart: 6, of which 4 were waited for; matrix products, arithmetic and copies ran while one was open for 0% of the time, Pallas kernels for 9%

profile of v18, /device:TPU:0, one launch (start us, length us, event | category | flops | bytes accessed | tf_op | source)
XLA Modules:
  0.0 41.5 jit_solution(17738382621297898641)
XLA Ops:
  0.6 5.1 %forward.1 = (bf16[4,1280]{1,0:T(4,128)(2,1)S(1)}, bf16[128,256]{1,0:T(8,128)(2,1)S(1)}, bf16[4,512]{1,0:T(4,128)(2,1)S(1)}, bf16[8,256,1024]{2,1,0:T(8,128)(2,1...) custom-call(s32[256,2048]{1,0:T(8,128)} %bitcast.1, ...), custom_call_target="tpu_custom_call" | custom-call | tf_op jit(solution)/shard_map/forward/pallas_call | solution.py:324
  5.8 13.5 %all_to_all.5.gathered = bf16[16,4,1280]{2,1,0:T(4,128)(2,1)S(1)} all-to-all(bf16[16,4,1280]{2,1,0:T(4,128)(2,1)S(1)} %broadcast_in_dim.2), channel_id=1, replica_groups={{11,15,3,7,10,14,2,6,9,13,1,5,8,12,0,4},{27,31,19,23,26,30,18,22,25,29,..., dimensions={0} | all-to-all | bytes 327680 | tf_op jit(solution)/shard_map/all_to_all | solution.py:404
  19.2 1.8 %backward.1 = (f32[4,128,256]{2,1,0:T(8,128)S(1)}, f32[4,128,256]{2,1,0:T(8,128)S(1)}, bf16[4,256,256]{2,1,0:T(8,128)(2,1)S(1)}) custom-call(bf16[16,4,1280]{2,1,0:T(4,128)(2,1)S(1)} %all_to_all.5.gathered, bf16[128,256]{1,0:T(8,128)(2,1)S(1)} %get-tuple-element.24.pooled_lanes, bf16[4,512]{1,0:T(4,128)(2,1)S(1)} %get-tuple-element.25.recon, ...), custom_call_target="tpu_custom_call" | custom-call | tf_op jit(solution)/shard_map/backward/pallas_call | solution.py:348
  21.1 0.2 collective-permute-start
  21.3 2.5 %embed_gradient.1.refs_2_ = f32[4,32,256]{2,1,0:T(8,128)S(1)} custom-call(bf16[4,256,256]{2,1,0:T(8,128)(2,1)S(1)} %get-tuple-element.31.grads, bf16[1024,256]{1,0:T(8,128)(2,1)S(1)} %get-tuple-element.32.w_conv, f32[4,256,1024]{2,1,0:T(8,128)S(1)} %get-tuple-element.33.pre_embed, bf16[8,256,1024]{2,1,0:T(8,128)(2,1)S(1)} %get-tuple-element.34.one_hot), custom_call_target="tpu_custom_call" | custom-call | flops 1600000000 | bytes 10485760 | tf_op jit(solution)/shard_map/embed_gradient/pallas_call | solution.py:374
  23.8 0.0 collective-permute-done.refs_1_
  23.8 0.2 scale.1
  24.0 0.1 reduce-precision_convert_fusion.2
  24.1 0.1 reduce-precision_convert_fusion.1
  24.2 0.1 reduce-precision_convert_fusion
  24.2 2.0 %collective-permute-start.3 = (f16[160,256]{1,0:T(8,128)(2,1)S(1)}, f16[160,256]{1,0:T(8,128)(2,1)S(1)}, u32[]{:S(2)}, u32[]{:S(2)}) collective-permute-start(f16[160,256]{1,0:T(8,128)(2,1)S(1)} %reduce-precision_convert_fusion), channel_id=1, source_target_pairs={{0,3},{1,2},{2,1},{3,0},{4,7},{5,6},{6,5},{7,4},{8,11},{9,10},{10,... | collective-permute-start | bytes 245768 | tf_op jit(solution)/shard_map/ppermute | solution.py:395
  26.2 0.1 collective-permute-start.2
  26.3 2.4 %collective-permute-start.1 = (f16[160,256]{1,0:T(8,128)(2,1)S(1)}, f16[160,256]{1,0:T(8,128)(2,1)S(1)}, u32[]{:S(2)}, u32[]{:S(2)}) collective-permute-start(f16[160,256]{1,0:T(8,128)(2,1)S(1)} %reduce-precision_convert_fusion.2), channel_id=1, source_target_pairs={{0,1},{1,0},{2,3},{3,2},{4,5},{5,4},{6,7},{7,6},{8,9},{9,8},{10,11... | collective-permute-start | bytes 245768 | tf_op jit(solution)/shard_map/ppermute | solution.py:395
  28.7 1.4 %head_gradient.1 = (f32[64,512]{1,0:T(8,128)}, f32[8,128]{1,0:T(8,128)S(1)}) custom-call(bf16[16,4,1280]{2,1,0:T(4,128)(2,1)S(1)} %all_to_all.5.gathered, bf16[256,512]{1,0:T(8,128)(2,1)S(1)} %get-tuple-element.28.w_head, f32[160,256]{1,0:T(8,128)S(1)} %get-tuple-element.35.after.refs_0_), custom_call_target="tpu_custom_call" | custom-call | flops 2000000000 | bytes 2097152 | tf_op jit(solution)/shard_map/head_gradient/pallas_call | solution.py:361
  30.1 1.4 %collective-permute-done.3 = f16[160,256]{1,0:T(8,128)(2,1)S(1)} collective-permute-done((f16[160,256]{1,0:T(8,128)(2,1)S(1)}, f16[160,256]{1,0:T(8,128)(2,1)S(1)}, u32[]{:S(2)}, u32[]{:S(2)}) %collective-permute-start.3) | collective-permute-done | bytes 81952 | tf_op jit(solution)/shard_map/ppermute | solution.py:395
  31.5 2.8 %collective-permute-done.2 = f16[160,256]{1,0:T(8,128)(2,1)S(1)} collective-permute-done((f16[160,256]{1,0:T(8,128)(2,1)S(1)}, f16[160,256]{1,0:T(8,128)(2,1)S(1)}, u32[]{:S(2)}, u32[]{:S(2)}) %collective-permute-start.2) | collective-permute-done | bytes 81952 | tf_op jit(solution)/shard_map/ppermute | solution.py:395
  34.4 0.0 collective-permute-done.1
  34.4 0.2 sum_z.1
  34.6 0.1 reduce-precision_convert_fusion.3
  34.7 1.7 %collective-permute-start.4 = (f16[160,256]{1,0:T(8,128)(2,1)S(1)}, f16[160,256]{1,0:T(8,128)(2,1)S(1)}, u32[]{:S(2)}, u32[]{:S(2)}) collective-permute-start(f16[160,256]{1,0:T(8,128)(2,1)S(1)} %get-tuple-element.43), channel_id=1, source_target_pairs={{0,8},{1,9},{2,10},{3,11},{4,12},{5,13},{6,14},{7,15},{8,0},{9,1},... | collective-permute-start | bytes 245768 | tf_op jit(solution)/shard_map/ppermute | solution.py:395
  36.4 2.8 %collective-permute-done.4 = f16[160,256]{1,0:T(8,128)(2,1)S(1)} collective-permute-done((f16[160,256]{1,0:T(8,128)(2,1)S(1)}, f16[160,256]{1,0:T(8,128)(2,1)S(1)}, u32[]{:S(2)}, u32[]{:S(2)}) %collective-permute-start.4) | collective-permute-done | bytes 81952 | tf_op jit(solution)/shard_map/ppermute | solution.py:395
  39.2 0.1 collective-permute-start.5
  39.3 1.4 %collective-permute-done.5.other = f32[160,256]{1,0:T(8,128)S(1)} collective-permute-done((f32[160,256]{1,0:T(8,128)S(1)}, f32[160,256]{1,0:T(8,128)S(1)}, u32[]{:S(2)}, u32[]{:S(2)}) %collective-permute-start.5) | collective-permute-done | bytes 163872 | tf_op jit(solution)/shard_map/ppermute | solution.py:395
  40.7 0.8 %outputs.1 = (f32[64,128]{1,0:T(8,128)}, f32[256,256]{1,0:T(8,128)}) custom-call(f32[160,256]{1,0:T(8,128)S(1)} %sum_x.1.own, f32[160,256]{1,0:T(8,128)S(1)} %collective-permute-done.5.other), custom_call_target="tpu_custom_call" | custom-call | tf_op jit(solution)/shard_map/outputs/pallas_call | solution.py:456
  (6 shorter events, 0.1 us)
Async XLA Ops:
  21.1 2.7 %collective-permute-start = (f32[4,128,256]{2,1,0:T(8,128)S(1)}, f32[4,128,256]{2,1,0:T(8,128)S(1)}, u32[]{:S(2)}, u32[]{:S(2)}) collective-permute-start(f32[4,128,256]{2,1,0:T(8,128)S(1)} %get-tuple-element.30), channel_id=1, source_target_pairs={{0,4},{1,5},{2,6},{3,7},{4,0},{5,1},{6,2},{7,3},{8,12},{9,13},{10,... | collective-permute-start | bytes 1572872 | tf_op jit(solution)/shard_map/ppermute | solution.py:395
  24.2 7.3 %collective-permute-start.3 = (f16[160,256]{1,0:T(8,128)(2,1)S(1)}, f16[160,256]{1,0:T(8,128)(2,1)S(1)}, u32[]{:S(2)}, u32[]{:S(2)}) collective-permute-start(f16[160,256]{1,0:T(8,128)(2,1)S(1)} %reduce-precision_convert_fusion), channel_id=1, source_target_pairs={{0,3},{1,2},{2,1},{3,0},{4,7},{5,6},{6,5},{7,4},{8,11},{9,10},{10,... | collective-permute-start | bytes 245768 | tf_op jit(solution)/shard_map/ppermute | solution.py:395
  26.2 8.1 %collective-permute-start.2 = (f16[160,256]{1,0:T(8,128)(2,1)S(1)}, f16[160,256]{1,0:T(8,128)(2,1)S(1)}, u32[]{:S(2)}, u32[]{:S(2)}) collective-permute-start(f16[160,256]{1,0:T(8,128)(2,1)S(1)} %reduce-precision_convert_fusion.1), channel_id=1, source_target_pairs={{0,2},{1,3},{2,0},{3,1},{4,6},{5,7},{6,4},{7,5},{8,10},{9,11},{10,... | collective-permute-start | bytes 245768 | tf_op jit(solution)/shard_map/ppermute | solution.py:395
  26.3 8.0 %collective-permute-start.1 = (f16[160,256]{1,0:T(8,128)(2,1)S(1)}, f16[160,256]{1,0:T(8,128)(2,1)S(1)}, u32[]{:S(2)}, u32[]{:S(2)}) collective-permute-start(f16[160,256]{1,0:T(8,128)(2,1)S(1)} %reduce-precision_convert_fusion.2), channel_id=1, source_target_pairs={{0,1},{1,0},{2,3},{3,2},{4,5},{5,4},{6,7},{7,6},{8,9},{9,8},{10,11... | collective-permute-start | bytes 245768 | tf_op jit(solution)/shard_map/ppermute | solution.py:395
  34.7 4.5 %collective-permute-start.4 = (f16[160,256]{1,0:T(8,128)(2,1)S(1)}, f16[160,256]{1,0:T(8,128)(2,1)S(1)}, u32[]{:S(2)}, u32[]{:S(2)}) collective-permute-start(f16[160,256]{1,0:T(8,128)(2,1)S(1)} %get-tuple-element.43), channel_id=1, source_target_pairs={{0,8},{1,9},{2,10},{3,11},{4,12},{5,13},{6,14},{7,15},{8,0},{9,1},... | collective-permute-start | bytes 245768 | tf_op jit(solution)/shard_map/ppermute | solution.py:395
  39.2 1.5 %collective-permute-start.5 = (f32[160,256]{1,0:T(8,128)S(1)}, f32[160,256]{1,0:T(8,128)S(1)}, u32[]{:S(2)}, u32[]{:S(2)}) collective-permute-start(f32[160,256]{1,0:T(8,128)S(1)} %sum_x.1.own), channel_id=1, source_target_pairs={{0,4},{1,5},{2,6},{3,7},{4,0},{5,1},{6,2},{7,3},{8,12},{9,13},{10,... | collective-permute-start | bytes 491528 | tf_op jit(solution)/shard_map/ppermute | solution.py:395

commit v19 on v18

--- a/solution.py
+++ b/solution.py
@@ -254,6 +254,10 @@
     return jnp.concatenate([coded[pl.ds(0, conv_rows), :] * jnp.exp2(coded[pl.ds(last + 1, 1), :]), embed], axis=0)
 
 
+def z_flips(fsdp):
+    return [flip for flip in range(1, fsdp) if flip != fsdp // 2] + [fsdp // 2]
+
+
 def scale_kernel(keep, other, embed, own, *coded):
     held = keep[...] + other[...]
     steps = exponent_of(held), exponent_of(embed[...])
@@ -263,8 +267,8 @@
         return jnp.concatenate([keep[z] + other[z], embed[z]], axis=0)
 
     own[...] = share(here)
-    for place, target in enumerate(coded):
-        store_scaled(target, share(here ^ (place + 1)), steps, keep.shape[1])
+    for flip, target in zip(z_flips(keep.shape[0]), coded):
+        store_scaled(target, share(here ^ flip), steps, keep.shape[1])
 
 
 def first_sum_kernel(conv_rows, own, *refs):
@@ -426,7 +430,7 @@
     plain = jax.ShapeDtypeStruct((rows, width), F32)
     own, *coded = local_kernel(scale_kernel, (plain,) + (plain,) * (fsdp - 1), "scale", keep, other, embed)
     received = [
-        exchange(to_half(part)[1], dp, fsdp, 0, 0, place + 1).astype(F32) for place, part in enumerate(coded)
+        exchange(to_half(part)[1], dp, fsdp, 0, 0, flip).astype(F32) for flip, part in zip(z_flips(fsdp), coded)
     ]
     grad_head, token = head_gradient(fsdp, gathered, w_head, own)
     (coded,) = local_kernel(

time: 41.6 us -> 41.9 us (level)
  waiting for transfers between devices: 8.4 us -> 9.97 us
  starting transfers between devices: 6.47 us -> 5.15 us
    ppermute x6, waiting for transfers between devices: 8.4 us -> 9.97 us  [exchange(): return lax.ppermute(block, GROUP, pairs)]
    ppermute x6, starting transfers between devices: 6.47 us -> 5.15 us  [exchange(): return lax.ppermute(block, GROUP, pairs)]
where the time goes in v19:
time: 41.9 us; the launch traced here: 41.7 us
  blocking collectives  13.5 us (32%)
  Pallas kernels  11.9 us (28%)
  waiting for transfers between devices  9.97 us (24%)
  starting transfers between devices  5.15 us (12%)
  between operations  0.76 us (2%)
    all_to_all x1, blocking collectives, gather_blocks(): lax.all_to_all(copies, GROUP, 0, 0, axis_index_groups=[order], tiled=True)  13.5 us
    ppermute x6, waiting for transfers between devices, exchange(): return lax.ppermute(block, GROUP, pairs)  9.97 us
    ppermute x6, starting transfers between devices, exchange(): return lax.ppermute(block, GROUP, pairs)  5.15 us
    pallas_call x1, Pallas kernels, forward(): pl.pallas_call(forward_kernel, out_shape=(pltpu.VMEM((samples, 2 * latent...  5.09 us
    pallas_call x1, Pallas kernels, embed_gradient(): pl.pallas_call(embed_kernel, out_shape=pltpu.VMEM((fsdp, (96 // fsdp + 7)...  2.48 us
    pallas_call x1, Pallas kernels, backward(): pl.pallas_call(backward_kernel, out_shape=(payload, payload, pltpu.VMEM((...  1.83 us
    pallas_call x1, Pallas kernels, head_gradient(): pl.pallas_call(head_kernel, out_shape=(jax.ShapeDtypeStruct((256 // fsdp,...  1.39 us
  transfers between devices with their start and end apart: 6, of which 4 were waited for; matrix products, arithmetic and copies ran while one was open for 0% of the time, Pallas kernels for 9%

profile of v19, /device:TPU:0, one launch (start us, length us, event | category | flops | bytes accessed | tf_op | source)
XLA Modules:
  0.0 41.7 jit_solution(18248412018593591439)
XLA Ops:
  0.6 5.1 %forward.1 = (bf16[4,1280]{1,0:T(4,128)(2,1)S(1)}, bf16[128,256]{1,0:T(8,128)(2,1)S(1)}, bf16[4,512]{1,0:T(4,128)(2,1)S(1)}, bf16[8,256,1024]{2,1,0:T(8,128)(2,1...) custom-call(s32[256,2048]{1,0:T(8,128)} %bitcast.1, ...), custom_call_target="tpu_custom_call" | custom-call | tf_op jit(solution)/shard_map/forward/pallas_call | solution.py:328
  5.8 13.5 %all_to_all.5.gathered = bf16[16,4,1280]{2,1,0:T(4,128)(2,1)S(1)} all-to-all(bf16[16,4,1280]{2,1,0:T(4,128)(2,1)S(1)} %broadcast_in_dim.2), channel_id=1, replica_groups={{11,15,3,7,10,14,2,6,9,13,1,5,8,12,0,4},{27,31,19,23,26,30,18,22,25,29,..., dimensions={0} | all-to-all | bytes 327680 | tf_op jit(solution)/shard_map/all_to_all | solution.py:408
  19.2 1.8 %backward.1 = (f32[4,128,256]{2,1,0:T(8,128)S(1)}, f32[4,128,256]{2,1,0:T(8,128)S(1)}, bf16[4,256,256]{2,1,0:T(8,128)(2,1)S(1)}) custom-call(bf16[16,4,1280]{2,1,0:T(4,128)(2,1)S(1)} %all_to_all.5.gathered, bf16[128,256]{1,0:T(8,128)(2,1)S(1)} %get-tuple-element.24.pooled_lanes, bf16[4,512]{1,0:T(4,128)(2,1)S(1)} %get-tuple-element.25.recon, ...), custom_call_target="tpu_custom_call" | custom-call | tf_op jit(solution)/shard_map/backward/pallas_call | solution.py:352
  21.1 0.2 collective-permute-start
  21.3 2.5 %embed_gradient.1.refs_2_ = f32[4,32,256]{2,1,0:T(8,128)S(1)} custom-call(bf16[4,256,256]{2,1,0:T(8,128)(2,1)S(1)} %get-tuple-element.31.grads, bf16[1024,256]{1,0:T(8,128)(2,1)S(1)} %get-tuple-element.32.w_conv, f32[4,256,1024]{2,1,0:T(8,128)S(1)} %get-tuple-element.33.pre_embed, bf16[8,256,1024]{2,1,0:T(8,128)(2,1)S(1)} %get-tuple-element.34.one_hot), custom_call_target="tpu_custom_call" | custom-call | flops 1600000000 | bytes 10485760 | tf_op jit(solution)/shard_map/embed_gradient/pallas_call | solution.py:378
  23.8 0.0 collective-permute-done.refs_1_
  23.8 0.2 scale.1
  24.0 0.1 reduce-precision_convert_fusion.2
  24.1 0.1 reduce-precision_convert_fusion.1
  24.2 0.1 reduce-precision_convert_fusion
  24.2 1.5 %collective-permute-start.3 = (f16[160,256]{1,0:T(8,128)(2,1)S(1)}, f16[160,256]{1,0:T(8,128)(2,1)S(1)}, u32[]{:S(2)}, u32[]{:S(2)}) collective-permute-start(f16[160,256]{1,0:T(8,128)(2,1)S(1)} %reduce-precision_convert_fusion), channel_id=1, source_target_pairs={{0,2},{1,3},{2,0},{3,1},{4,6},{5,7},{6,4},{7,5},{8,10},{9,11},{10,... | collective-permute-start | bytes 245768 | tf_op jit(solution)/shard_map/ppermute | solution.py:399
  25.7 1.5 %collective-permute-start.2 = (f16[160,256]{1,0:T(8,128)(2,1)S(1)}, f16[160,256]{1,0:T(8,128)(2,1)S(1)}, u32[]{:S(2)}, u32[]{:S(2)}) collective-permute-start(f16[160,256]{1,0:T(8,128)(2,1)S(1)} %reduce-precision_convert_fusion.1), channel_id=1, source_target_pairs={{0,3},{1,2},{2,1},{3,0},{4,7},{5,6},{6,5},{7,4},{8,11},{9,10},{10,... | collective-permute-start | bytes 245768 | tf_op jit(solution)/shard_map/ppermute | solution.py:399
  27.2 0.6 %collective-permute-start.1 = (f16[160,256]{1,0:T(8,128)(2,1)S(1)}, f16[160,256]{1,0:T(8,128)(2,1)S(1)}, u32[]{:S(2)}, u32[]{:S(2)}) collective-permute-start(f16[160,256]{1,0:T(8,128)(2,1)S(1)} %reduce-precision_convert_fusion.2), channel_id=1, source_target_pairs={{0,1},{1,0},{2,3},{3,2},{4,5},{5,4},{6,7},{7,6},{8,9},{9,8},{10,11... | collective-permute-start | bytes 245768 | tf_op jit(solution)/shard_map/ppermute | solution.py:399
  27.8 1.4 %head_gradient.1 = (f32[64,512]{1,0:T(8,128)}, f32[8,128]{1,0:T(8,128)S(1)}) custom-call(bf16[16,4,1280]{2,1,0:T(4,128)(2,1)S(1)} %all_to_all.5.gathered, bf16[256,512]{1,0:T(8,128)(2,1)S(1)} %get-tuple-element.28.w_head, f32[160,256]{1,0:T(8,128)S(1)} %get-tuple-element.35.after.refs_0_), custom_call_target="tpu_custom_call" | custom-call | flops 2000000000 | bytes 2097152 | tf_op jit(solution)/shard_map/head_gradient/pallas_call | solution.py:365
  29.2 4.2 %collective-permute-done.3 = f16[160,256]{1,0:T(8,128)(2,1)S(1)} collective-permute-done((f16[160,256]{1,0:T(8,128)(2,1)S(1)}, f16[160,256]{1,0:T(8,128)(2,1)S(1)}, u32[]{:S(2)}, u32[]{:S(2)}) %collective-permute-start.3) | collective-permute-done | bytes 81952 | tf_op jit(solution)/shard_map/ppermute | solution.py:399
  33.4 0.0 collective-permute-done.2
  33.5 1.2 %collective-permute-done.1 = f16[160,256]{1,0:T(8,128)(2,1)S(1)} collective-permute-done((f16[160,256]{1,0:T(8,128)(2,1)S(1)}, f16[160,256]{1,0:T(8,128)(2,1)S(1)}, u32[]{:S(2)}, u32[]{:S(2)}) %collective-permute-start.1) | collective-permute-done | bytes 81952 | tf_op jit(solution)/shard_map/ppermute | solution.py:399
  34.7 0.2 sum_z.1
  34.8 0.1 reduce-precision_convert_fusion.3
  34.9 1.3 %collective-permute-start.4 = (f16[160,256]{1,0:T(8,128)(2,1)S(1)}, f16[160,256]{1,0:T(8,128)(2,1)S(1)}, u32[]{:S(2)}, u32[]{:S(2)}) collective-permute-start(f16[160,256]{1,0:T(8,128)(2,1)S(1)} %get-tuple-element.43), channel_id=1, source_target_pairs={{0,8},{1,9},{2,10},{3,11},{4,12},{5,13},{6,14},{7,15},{8,0},{9,1},... | collective-permute-start | bytes 245768 | tf_op jit(solution)/shard_map/ppermute | solution.py:399
  36.2 3.2 %collective-permute-done.4 = f16[160,256]{1,0:T(8,128)(2,1)S(1)} collective-permute-done((f16[160,256]{1,0:T(8,128)(2,1)S(1)}, f16[160,256]{1,0:T(8,128)(2,1)S(1)}, u32[]{:S(2)}, u32[]{:S(2)}) %collective-permute-start.4) | collective-permute-done | bytes 81952 | tf_op jit(solution)/shard_map/ppermute | solution.py:399
  39.5 0.1 collective-permute-start.5
  39.6 1.4 %collective-permute-done.5.other = f32[160,256]{1,0:T(8,128)S(1)} collective-permute-done((f32[160,256]{1,0:T(8,128)S(1)}, f32[160,256]{1,0:T(8,128)S(1)}, u32[]{:S(2)}, u32[]{:S(2)}) %collective-permute-start.5) | collective-permute-done | bytes 163872 | tf_op jit(solution)/shard_map/ppermute | solution.py:399
  41.0 0.8 %outputs.1 = (f32[64,128]{1,0:T(8,128)}, f32[256,256]{1,0:T(8,128)}) custom-call(f32[160,256]{1,0:T(8,128)S(1)} %sum_x.1.own, f32[160,256]{1,0:T(8,128)S(1)} %collective-permute-done.5.other), custom_call_target="tpu_custom_call" | custom-call | tf_op jit(solution)/shard_map/outputs/pallas_call | solution.py:460
  (6 shorter events, 0.1 us)
Async XLA Ops:
  21.1 2.7 %collective-permute-start = (f32[4,128,256]{2,1,0:T(8,128)S(1)}, f32[4,128,256]{2,1,0:T(8,128)S(1)}, u32[]{:S(2)}, u32[]{:S(2)}) collective-permute-start(f32[4,128,256]{2,1,0:T(8,128)S(1)} %get-tuple-element.30), channel_id=1, source_target_pairs={{0,4},{1,5},{2,6},{3,7},{4,0},{5,1},{6,2},{7,3},{8,12},{9,13},{10,... | collective-permute-start | bytes 1572872 | tf_op jit(solution)/shard_map/ppermute | solution.py:399
  24.2 9.2 %collective-permute-start.3 = (f16[160,256]{1,0:T(8,128)(2,1)S(1)}, f16[160,256]{1,0:T(8,128)(2,1)S(1)}, u32[]{:S(2)}, u32[]{:S(2)}) collective-permute-start(f16[160,256]{1,0:T(8,128)(2,1)S(1)} %reduce-precision_convert_fusion), channel_id=1, source_target_pairs={{0,2},{1,3},{2,0},{3,1},{4,6},{5,7},{6,4},{7,5},{8,10},{9,11},{10,... | collective-permute-start | bytes 245768 | tf_op jit(solution)/shard_map/ppermute | solution.py:399
  25.7 7.7 %collective-permute-start.2 = (f16[160,256]{1,0:T(8,128)(2,1)S(1)}, f16[160,256]{1,0:T(8,128)(2,1)S(1)}, u32[]{:S(2)}, u32[]{:S(2)}) collective-permute-start(f16[160,256]{1,0:T(8,128)(2,1)S(1)} %reduce-precision_convert_fusion.1), channel_id=1, source_target_pairs={{0,3},{1,2},{2,1},{3,0},{4,7},{5,6},{6,5},{7,4},{8,11},{9,10},{10,... | collective-permute-start | bytes 245768 | tf_op jit(solution)/shard_map/ppermute | solution.py:399
  27.2 7.4 %collective-permute-start.1 = (f16[160,256]{1,0:T(8,128)(2,1)S(1)}, f16[160,256]{1,0:T(8,128)(2,1)S(1)}, u32[]{:S(2)}, u32[]{:S(2)}) collective-permute-start(f16[160,256]{1,0:T(8,128)(2,1)S(1)} %reduce-precision_convert_fusion.2), channel_id=1, source_target_pairs={{0,1},{1,0},{2,3},{3,2},{4,5},{5,4},{6,7},{7,6},{8,9},{9,8},{10,11... | collective-permute-start | bytes 245768 | tf_op jit(solution)/shard_map/ppermute | solution.py:399
  34.9 4.5 %collective-permute-start.4 = (f16[160,256]{1,0:T(8,128)(2,1)S(1)}, f16[160,256]{1,0:T(8,128)(2,1)S(1)}, u32[]{:S(2)}, u32[]{:S(2)}) collective-permute-start(f16[160,256]{1,0:T(8,128)(2,1)S(1)} %get-tuple-element.43), channel_id=1, source_target_pairs={{0,8},{1,9},{2,10},{3,11},{4,12},{5,13},{6,14},{7,15},{8,0},{9,1},... | collective-permute-start | bytes 245768 | tf_op jit(solution)/shard_map/ppermute | solution.py:399
  39.5 1.5 %collective-permute-start.5 = (f32[160,256]{1,0:T(8,128)S(1)}, f32[160,256]{1,0:T(8,128)S(1)}, u32[]{:S(2)}, u32[]{:S(2)}) collective-permute-start(f32[160,256]{1,0:T(8,128)S(1)} %sum_x.1.own), channel_id=1, source_target_pairs={{0,4},{1,5},{2,6},{3,7},{4,0},{5,1},{6,2},{7,3},{8,12},{9,13},{10,... | collective-permute-start | bytes 491528 | tf_op jit(solution)/shard_map/ppermute | solution.py:399

commit v20 on v17

--- a/solution.py
+++ b/solution.py
@@ -120,10 +120,11 @@
         pre_conv[cp] = pre
         act = pre * sigmoid(pre)
         sums = sums + act[:, :128] + act[:, 128:]
-    pick = jnp.where(iota((128, 128), 1) // 8 % 4 == iota((128, 128), 0) // 8 % 4, 1.0, 0.0)
+    pick = jnp.where(iota((8, 128), 1) // 8 % 4 == iota((8, 128), 0), 1.0, 0.0)
     total = lax.dot_general(pick, sums, NT, precision=lax.Precision.HIGHEST, preferred_element_type=F32) / 256.0
-    pooled_lanes[...] = total.astype(BF16)
-    block[:, pl.ds(1024, 256)] = jnp.concatenate([total[8 * s : 8 * s + 1] for s in range(4)], axis=0).astype(BF16)
+    block[:, pl.ds(1024, 256)] = total[:4].astype(BF16)
+    lanes = [jnp.broadcast_to(total[s : s + 1], (8, total.shape[1])) for s in range(4)] * 4
+    pooled_lanes[...] = jnp.concatenate(lanes, axis=0).astype(BF16)
     for load in others[2:]:
         load.wait()
     block[:, pl.ds(0, 512)] = prior[...]
@@ -140,10 +141,13 @@
     return jnp.sum(kern, axis=1, keepdims=True), mm(kern.astype(BF16), keys)
 
 
-def group_rows(gathered, ordered):
-    for owner in range(gathered.shape[0]):
-        ordered[owner] = gathered[owner].astype(F32)
-    return ordered[...].reshape(gathered.shape[0] * gathered.shape[1], gathered.shape[2])
+def group_rows(gathered, gathered_other, ordered):
+    peers = gathered.shape[0]
+    core = lax.rem(lax.axis_index("dp"), 2)
+    for place in range(peers):
+        ordered[core * peers + place] = gathered[place].astype(F32)
+        ordered[(1 - core) * peers + place] = gathered_other[place].astype(F32)
+    return ordered[...].reshape(2 * peers * gathered.shape[1], gathered.shape[2])
 
 
 def latent_rows(pooled, w_head):
@@ -159,9 +163,9 @@
     return (recon + pull).astype(BF16)
 
 
-def head_kernel(gathered, w_head, after, grad_head, token, ordered, head_full):
+def head_kernel(gathered, gathered_other, w_head, after, grad_head, token, ordered, head_full):
     token[...] = jnp.zeros(token.shape, F32)
-    full = group_rows(gathered, ordered)
+    full = group_rows(gathered, gathered_other, ordered)
     latent = latent_rows(full[:, 1024:].astype(BF16), w_head)
     cotangent = cotangent_rows(latent, latent, full[:, :512].astype(BF16), full[:, 512:1024])
     head_full[...] = mm(jnp.transpose(full[:, 1024:]).astype(BF16), cotangent)
@@ -170,8 +174,8 @@
     grad_head[...] = head_full[pl.ds(start, share), :]
 
 
-def backward_kernel(gathered, pooled_lanes, recon, hidden, pre_conv, w_head, keep, send, grads, ordered):
-    full = group_rows(gathered, ordered)
+def backward_kernel(gathered, gathered_other, pooled_lanes, recon, hidden, pre_conv, w_head, keep, send, grads, ordered):
+    full = group_rows(gathered, gathered_other, ordered)
     queries = latent_rows(pooled_lanes[...], w_head)
     keys = latent_rows(full[:, 1024:].astype(BF16), w_head)
     recon_float = recon[...].astype(F32)
@@ -343,31 +347,31 @@
 
 
 def backward(fsdp, gathered, *operands):
-    devices, samples, width = gathered.shape
+    peers, samples, width = gathered[0].shape
     payload = pltpu.VMEM((fsdp, 1024 // fsdp // 2, 256), F32)
     return pl.pallas_call(
         backward_kernel,
         out_shape=(payload, payload, pltpu.VMEM((4, 256, 256), BF16)),
-        in_specs=[VMEM] * 6,
+        in_specs=[VMEM] * 7,
         out_specs=(VMEM,) * 3,
-        scratch_shapes=[pltpu.VMEM((devices, samples, width), F32)],
+        scratch_shapes=[pltpu.VMEM((2 * peers, samples, width), F32)],
         compiler_params=pltpu.CompilerParams(vmem_limit_bytes=24 * 2**20),
         name="backward",
-    )(gathered, *operands)
+    )(*gathered, *operands)
 
 
 def head_gradient(fsdp, gathered, w_head, after):
-    devices, samples, width = gathered.shape
+    peers, samples, width = gathered[0].shape
     return pl.pallas_call(
         head_kernel,
         out_shape=(jax.ShapeDtypeStruct((256 // fsdp, 512), F32), pltpu.VMEM((8, 128), F32)),
-        in_specs=[VMEM] * 2 + [HBM],
+        in_specs=[VMEM] * 3 + [HBM],
         out_specs=(VMEM,) * 2,
-        scratch_shapes=[pltpu.VMEM((devices, samples, width), F32), pltpu.VMEM((256, 512), F32)],
+        scratch_shapes=[pltpu.VMEM((2 * peers, samples, width), F32), pltpu.VMEM((256, 512), F32)],
         compiler_params=pltpu.CompilerParams(vmem_limit_bytes=16 * 2**20),
         cost_estimate=pl.CostEstimate(flops=2 * 10**9, bytes_accessed=2 * 2**20, transcendentals=10000),
         name="head_gradient",
-    )(gathered, w_head, after)
+    )(*gathered, w_head, after)
 
 
 def embed_gradient(fsdp, grads, w_conv, pre_embed, one_hot):
@@ -396,10 +400,11 @@
 
 
 def gather_blocks(block, dp, fsdp):
-    devices = dp * fsdp
-    order = [row * fsdp + z for z in reversed(range(fsdp)) for row in range(dp)]
-    copies = jnp.broadcast_to(block[None], (devices,) + block.shape)
-    return lax.all_to_all(copies, GROUP, 0, 0, axis_index_groups=[order], tiled=True)
+    backward = [(x, z) for z in reversed(range(fsdp)) for x in reversed(range(dp // 2))]
+    groups = [[place_of(x, core, z, fsdp) for x, z in backward] for core in range(2)]
+    copies = jnp.broadcast_to(block[None], (len(backward),) + block.shape)
+    own = lax.all_to_all(copies, GROUP, 0, 0, axis_index_groups=groups, tiled=True)
+    return own, exchange(own, dp, fsdp, 0, 1, 0)
 
 
 def local_kernel(kernel, outs, name, *operands, unread=()):

time: 42 us -> 41.3 us (0.983)
  blocking collectives: 13.2 us -> 11.5 us
  starting transfers between devices: 5.15 us -> 6.33 us
    all_to_all x1, blocking collectives: 13.2 us -> 11.5 us  [gather_blocks(): lax.all_to_all(copies, GROUP, 0, 0, axis_index_groups=groups, tiled=True)]
    ppermute x6 -> x7, starting transfers between devices: 5.15 us -> 6.33 us  [exchange(): return lax.ppermute(block, GROUP, pairs)]
    ppermute x6 -> x7, waiting for transfers between devices: 10.3 us -> 10.2 us  [exchange(): return lax.ppermute(block, GROUP, pairs)]
  transfers between devices with their start and end apart: 6 -> 7, of which waited for: 4 -> 5; matrix products, arithmetic and copies ran while one was open for 0% -> 0% of each run, Pallas kernels for 9% -> 9%
where the time goes in v20:
time: 41.3 us; the launch traced here: 41.2 us
  Pallas kernels  11.9 us (29%)
  blocking collectives  11.5 us (28%)
  waiting for transfers between devices  10.2 us (25%)
  starting transfers between devices  6.33 us (15%)
  between operations  0.77 us (2%)
    all_to_all x1, blocking collectives, gather_blocks(): lax.all_to_all(copies, GROUP, 0, 0, axis_index_groups=groups, tiled=True)  11.5 us
    ppermute x7, waiting for transfers between devices, exchange(): return lax.ppermute(block, GROUP, pairs)  10.2 us
    ppermute x7, starting transfers between devices, exchange(): return lax.ppermute(block, GROUP, pairs)  6.33 us
    pallas_call x1, Pallas kernels, forward(): pl.pallas_call(forward_kernel, out_shape=(pltpu.VMEM((samples, 2 * latent...  5.07 us
    pallas_call x1, Pallas kernels, embed_gradient(): pl.pallas_call(embed_kernel, out_shape=pltpu.VMEM((fsdp, (96 // fsdp + 7)...  2.48 us
    pallas_call x1, Pallas kernels, backward(): pl.pallas_call(backward_kernel, out_shape=(payload, payload, pltpu.VMEM((...  1.83 us
    pallas_call x1, Pallas kernels, head_gradient(): pl.pallas_call(head_kernel, out_shape=(jax.ShapeDtypeStruct((256 // fsdp,...  1.39 us
  transfers between devices with their start and end apart: 7, of which 5 were waited for; matrix products, arithmetic and copies ran while one was open for 0% of the time, Pallas kernels for 9%

profile of v20, /device:TPU:0, one launch (start us, length us, event | category | flops | bytes accessed | tf_op | source)
XLA Modules:
  0.0 41.2 jit_solution(8859449342521720204)
XLA Ops:
  0.6 5.1 %forward.1 = (bf16[4,1280]{1,0:T(4,128)(2,1)S(1)}, bf16[128,256]{1,0:T(8,128)(2,1)S(1)}, bf16[4,512]{1,0:T(4,128)(2,1)S(1)}, bf16[8,256,1024]{2,1,0:T(8,128)(2,1...) custom-call(s32[256,2048]{1,0:T(8,128)} %bitcast.1, ...), custom_call_target="tpu_custom_call" | custom-call | tf_op jit(solution)/shard_map/forward/pallas_call | solution.py:328
  5.7 11.5 %all_to_all.5.gathered = bf16[8,4,1280]{2,1,0:T(4,128)(2,1)S(1)} all-to-all(bf16[8,4,1280]{2,1,0:T(4,128)(2,1)S(1)} %broadcast_in_dim.2), channel_id=1, replica_groups={{11,3,10,2,9,1,8,0},{15,7,14,6,13,5,12,4},{27,19,26,18,25,17,24,16},{31..., dimensions={0} | all-to-all | bytes 163840 | tf_op jit(solution)/shard_map/all_to_all | solution.py:406
  17.3 0.0 collective-permute-start
  17.3 1.3 %collective-permute-done.gathered_other = bf16[8,4,1280]{2,1,0:T(4,128)(2,1)S(1)} collective-permute-done((bf16[8,4,1280]{2,1,0:T(4,128)(2,1)S(1)}, bf16[8,4,1280]{2,1,0:T(4,128)(2,1)S(1)}, u32[]{:S(2)}, u32[]{:S(2)}) %collective-permute-start) | collective-permute-done | bytes 81952 | tf_op jit(solution)/shard_map/ppermute | solution.py:399
  18.6 1.8 %backward.1 = (f32[4,128,256]{2,1,0:T(8,128)S(1)}, f32[4,128,256]{2,1,0:T(8,128)S(1)}, bf16[4,256,256]{2,1,0:T(8,128)(2,1)S(1)}) custom-call(bf16[8,4,1280]{2,1,0:T(4,128)(2,1)S(1)} %all_to_all.5.gathered, bf16[8,4,1280]{2,1,0:T(4,128)(2,1)S(1)} %collective-permute-done.gathered_other, bf16[128,256]{1,0:T(8,128)(2,1)S(1)} %get-tuple-element.24.pooled_lanes, ...), custom_call_target="tpu_custom_call" | custom-call | tf_op jit(solution)/shard_map/backward/pallas_call | solution.py:352
  20.4 0.2 collective-permute-start.1
  20.6 2.5 %embed_gradient.1.refs_2_ = f32[4,32,256]{2,1,0:T(8,128)S(1)} custom-call(bf16[4,256,256]{2,1,0:T(8,128)(2,1)S(1)} %get-tuple-element.31.grads, bf16[1024,256]{1,0:T(8,128)(2,1)S(1)} %get-tuple-element.32.w_conv, f32[4,256,1024]{2,1,0:T(8,128)S(1)} %get-tuple-element.33.pre_embed, bf16[8,256,1024]{2,1,0:T(8,128)(2,1)S(1)} %get-tuple-element.34.one_hot), custom_call_target="tpu_custom_call" | custom-call | flops 1600000000 | bytes 10485760 | tf_op jit(solution)/shard_map/embed_gradient/pallas_call | solution.py:378
  23.1 0.0 collective-permute-done.1.refs_1_
  23.1 0.2 scale.1
  23.3 0.1 reduce-precision_convert_fusion.2
  23.4 0.1 reduce-precision_convert_fusion.1
  23.5 0.1 reduce-precision_convert_fusion
  23.6 2.8 %collective-permute-start.4 = (f16[160,256]{1,0:T(8,128)(2,1)S(1)}, f16[160,256]{1,0:T(8,128)(2,1)S(1)}, u32[]{:S(2)}, u32[]{:S(2)}) collective-permute-start(f16[160,256]{1,0:T(8,128)(2,1)S(1)} %reduce-precision_convert_fusion), channel_id=1, source_target_pairs={{0,3},{1,2},{2,1},{3,0},{4,7},{5,6},{6,5},{7,4},{8,11},{9,10},{10,... | collective-permute-start | bytes 245768 | tf_op jit(solution)/shard_map/ppermute | solution.py:399
  26.4 0.0 collective-permute-start.3
  26.4 1.7 %collective-permute-start.2 = (f16[160,256]{1,0:T(8,128)(2,1)S(1)}, f16[160,256]{1,0:T(8,128)(2,1)S(1)}, u32[]{:S(2)}, u32[]{:S(2)}) collective-permute-start(f16[160,256]{1,0:T(8,128)(2,1)S(1)} %reduce-precision_convert_fusion.2), channel_id=1, source_target_pairs={{0,1},{1,0},{2,3},{3,2},{4,5},{5,4},{6,7},{7,6},{8,9},{9,8},{10,11... | collective-permute-start | bytes 245768 | tf_op jit(solution)/shard_map/ppermute | solution.py:399
  28.1 1.4 %head_gradient.1 = (f32[64,512]{1,0:T(8,128)}, f32[8,128]{1,0:T(8,128)S(1)}) custom-call(bf16[8,4,1280]{2,1,0:T(4,128)(2,1)S(1)} %all_to_all.5.gathered, bf16[8,4,1280]{2,1,0:T(4,128)(2,1)S(1)} %collective-permute-done.gathered_other, bf16[256,512]{1,0:T(8,128)(2,1)S(1)} %get-tuple-element.28.w_head, f32[160,256]{1,0:T(8,128)S(1)} %get-tuple-element.35.after.refs_0_), custom_call_target="tpu_custom_call" | custom-call | flops 2000000000 | bytes 2097152 | tf_op jit(solution)/shard_map/head_gradient/pallas_call | solution.py:365
  29.4 1.4 %collective-permute-done.4 = f16[160,256]{1,0:T(8,128)(2,1)S(1)} collective-permute-done((f16[160,256]{1,0:T(8,128)(2,1)S(1)}, f16[160,256]{1,0:T(8,128)(2,1)S(1)}, u32[]{:S(2)}, u32[]{:S(2)}) %collective-permute-start.4) | collective-permute-done | bytes 81952 | tf_op jit(solution)/shard_map/ppermute | solution.py:399
  30.8 3.2 %collective-permute-done.3 = f16[160,256]{1,0:T(8,128)(2,1)S(1)} collective-permute-done((f16[160,256]{1,0:T(8,128)(2,1)S(1)}, f16[160,256]{1,0:T(8,128)(2,1)S(1)}, u32[]{:S(2)}, u32[]{:S(2)}) %collective-permute-start.3) | collective-permute-done | bytes 81952 | tf_op jit(solution)/shard_map/ppermute | solution.py:399
  34.1 0.0 collective-permute-done.2
  34.1 0.2 sum_z.1
  34.3 0.1 reduce-precision_convert_fusion.3
  34.4 1.6 %collective-permute-start.5 = (f16[160,256]{1,0:T(8,128)(2,1)S(1)}, f16[160,256]{1,0:T(8,128)(2,1)S(1)}, u32[]{:S(2)}, u32[]{:S(2)}) collective-permute-start(f16[160,256]{1,0:T(8,128)(2,1)S(1)} %get-tuple-element.43), channel_id=1, source_target_pairs={{0,8},{1,9},{2,10},{3,11},{4,12},{5,13},{6,14},{7,15},{8,0},{9,1},... | collective-permute-start | bytes 245768 | tf_op jit(solution)/shard_map/ppermute | solution.py:399
  36.0 2.9 %collective-permute-done.5 = f16[160,256]{1,0:T(8,128)(2,1)S(1)} collective-permute-done((f16[160,256]{1,0:T(8,128)(2,1)S(1)}, f16[160,256]{1,0:T(8,128)(2,1)S(1)}, u32[]{:S(2)}, u32[]{:S(2)}) %collective-permute-start.5) | collective-permute-done | bytes 81952 | tf_op jit(solution)/shard_map/ppermute | solution.py:399
  38.9 0.1 collective-permute-start.6
  39.0 1.4 %collective-permute-done.6.other = f32[160,256]{1,0:T(8,128)S(1)} collective-permute-done((f32[160,256]{1,0:T(8,128)S(1)}, f32[160,256]{1,0:T(8,128)S(1)}, u32[]{:S(2)}, u32[]{:S(2)}) %collective-permute-start.6) | collective-permute-done | bytes 163872 | tf_op jit(solution)/shard_map/ppermute | solution.py:399
  40.4 0.8 %outputs.1 = (f32[64,128]{1,0:T(8,128)}, f32[256,256]{1,0:T(8,128)}) custom-call(f32[160,256]{1,0:T(8,128)S(1)} %sum_x.1.own, f32[160,256]{1,0:T(8,128)S(1)} %collective-permute-done.6.other), custom_call_target="tpu_custom_call" | custom-call | tf_op jit(solution)/shard_map/outputs/pallas_call | solution.py:459
  (6 shorter events, 0.1 us)
Async XLA Ops:
  17.3 1.3 %collective-permute-start = (bf16[8,4,1280]{2,1,0:T(4,128)(2,1)S(1)}, bf16[8,4,1280]{2,1,0:T(4,128)(2,1)S(1)}, u32[]{:S(2)}, u32[]{:S(2)}) collective-permute-start(bf16[8,4,1280]{2,1,0:T(4,128)(2,1)S(1)} %all_to_all.5.gathered), channel_id=1, source_target_pairs={{0,4},{1,5},{2,6},{3,7},{4,0},{5,1},{6,2},{7,3},{8,12},{9,13},{10,... | collective-permute-start | bytes 245768 | tf_op jit(solution)/shard_map/ppermute | solution.py:399
  20.4 2.7 %collective-permute-start.1 = (f32[4,128,256]{2,1,0:T(8,128)S(1)}, f32[4,128,256]{2,1,0:T(8,128)S(1)}, u32[]{:S(2)}, u32[]{:S(2)}) collective-permute-start(f32[4,128,256]{2,1,0:T(8,128)S(1)} %get-tuple-element.30), channel_id=1, source_target_pairs={{0,4},{1,5},{2,6},{3,7},{4,0},{5,1},{6,2},{7,3},{8,12},{9,13},{10,... | collective-permute-start | bytes 1572872 | tf_op jit(solution)/shard_map/ppermute | solution.py:399
  23.6 7.2 %collective-permute-start.4 = (f16[160,256]{1,0:T(8,128)(2,1)S(1)}, f16[160,256]{1,0:T(8,128)(2,1)S(1)}, u32[]{:S(2)}, u32[]{:S(2)}) collective-permute-start(f16[160,256]{1,0:T(8,128)(2,1)S(1)} %reduce-precision_convert_fusion), channel_id=1, source_target_pairs={{0,3},{1,2},{2,1},{3,0},{4,7},{5,6},{6,5},{7,4},{8,11},{9,10},{10,... | collective-permute-start | bytes 245768 | tf_op jit(solution)/shard_map/ppermute | solution.py:399
  26.4 7.7 %collective-permute-start.3 = (f16[160,256]{1,0:T(8,128)(2,1)S(1)}, f16[160,256]{1,0:T(8,128)(2,1)S(1)}, u32[]{:S(2)}, u32[]{:S(2)}) collective-permute-start(f16[160,256]{1,0:T(8,128)(2,1)S(1)} %reduce-precision_convert_fusion.1), channel_id=1, source_target_pairs={{0,2},{1,3},{2,0},{3,1},{4,6},{5,7},{6,4},{7,5},{8,10},{9,11},{10,... | collective-permute-start | bytes 245768 | tf_op jit(solution)/shard_map/ppermute | solution.py:399
  26.4 7.7 %collective-permute-start.2 = (f16[160,256]{1,0:T(8,128)(2,1)S(1)}, f16[160,256]{1,0:T(8,128)(2,1)S(1)}, u32[]{:S(2)}, u32[]{:S(2)}) collective-permute-start(f16[160,256]{1,0:T(8,128)(2,1)S(1)} %reduce-precision_convert_fusion.2), channel_id=1, source_target_pairs={{0,1},{1,0},{2,3},{3,2},{4,5},{5,4},{6,7},{7,6},{8,9},{9,8},{10,11... | collective-permute-start | bytes 245768 | tf_op jit(solution)/shard_map/ppermute | solution.py:399
  34.4 4.5 %collective-permute-start.5 = (f16[160,256]{1,0:T(8,128)(2,1)S(1)}, f16[160,256]{1,0:T(8,128)(2,1)S(1)}, u32[]{:S(2)}, u32[]{:S(2)}) collective-permute-start(f16[160,256]{1,0:T(8,128)(2,1)S(1)} %get-tuple-element.43), channel_id=1, source_target_pairs={{0,8},{1,9},{2,10},{3,11},{4,12},{5,13},{6,14},{7,15},{8,0},{9,1},... | collective-permute-start | bytes 245768 | tf_op jit(solution)/shard_map/ppermute | solution.py:399
  38.9 1.5 %collective-permute-start.6 = (f32[160,256]{1,0:T(8,128)S(1)}, f32[160,256]{1,0:T(8,128)S(1)}, u32[]{:S(2)}, u32[]{:S(2)}) collective-permute-start(f32[160,256]{1,0:T(8,128)S(1)} %sum_x.1.own), channel_id=1, source_target_pairs={{0,4},{1,5},{2,6},{3,7},{4,0},{5,1},{6,2},{7,3},{8,12},{9,13},{10,... | collective-permute-start | bytes 491528 | tf_op jit(solution)/shard_map/ppermute | solution.py:399

commit v21 on v20

--- a/solution.py
+++ b/solution.py
@@ -110,11 +110,10 @@
             build(0, 0)
             build(0, 1)
     build(1, 0)
-    for cp in range(4):
-        embed(cp, 0)
     build(1, 1)
     sums = jnp.zeros((256, 128), F32)
     for cp in range(4):
+        embed(cp, 0)
         embed(cp, 1)
         pre = mm(conv_turned[...], hidden[cp].reshape(1024, 256))
         pre_conv[cp] = pre

time: 41.3 us -> 41.2 us (level)
  no operation moved by 1% of the time
where the time goes in v21:
time: 41.2 us; the launch traced here: 41 us
  Pallas kernels  11.8 us (29%)
  blocking collectives  11.5 us (28%)
  waiting for transfers between devices  10.2 us (25%)
  starting transfers between devices  6.34 us (15%)
  between operations  0.77 us (2%)
    all_to_all x1, blocking collectives, gather_blocks(): lax.all_to_all(copies, GROUP, 0, 0, axis_index_groups=groups, tiled=True)  11.5 us
    ppermute x7, waiting for transfers between devices, exchange(): return lax.ppermute(block, GROUP, pairs)  10.2 us
    ppermute x7, starting transfers between devices, exchange(): return lax.ppermute(block, GROUP, pairs)  6.34 us
    pallas_call x1, Pallas kernels, forward(): pl.pallas_call(forward_kernel, out_shape=(pltpu.VMEM((samples, 2 * latent...  4.96 us
    pallas_call x1, Pallas kernels, embed_gradient(): pl.pallas_call(embed_kernel, out_shape=pltpu.VMEM((fsdp, (96 // fsdp + 7)...  2.48 us
    pallas_call x1, Pallas kernels, backward(): pl.pallas_call(backward_kernel, out_shape=(payload, payload, pltpu.VMEM((...  1.83 us
    pallas_call x1, Pallas kernels, head_gradient(): pl.pallas_call(head_kernel, out_shape=(jax.ShapeDtypeStruct((256 // fsdp,...  1.39 us
  transfers between devices with their start and end apart: 7, of which 5 were waited for; matrix products, arithmetic and copies ran while one was open for 0% of the time, Pallas kernels for 9%

profile of v21, /device:TPU:0, one launch (start us, length us, event | category | flops | bytes accessed | tf_op | source)
XLA Modules:
  0.0 41.0 jit_solution(2582346412864833679)
XLA Ops:
  0.6 5.0 %forward.1 = (bf16[4,1280]{1,0:T(4,128)(2,1)S(1)}, bf16[128,256]{1,0:T(8,128)(2,1)S(1)}, bf16[4,512]{1,0:T(4,128)(2,1)S(1)}, bf16[8,256,1024]{2,1,0:T(8,128)(2,1...) custom-call(s32[256,2048]{1,0:T(8,128)} %bitcast.1, ...), custom_call_target="tpu_custom_call" | custom-call | tf_op jit(solution)/shard_map/forward/pallas_call | solution.py:327
  5.6 11.5 %all_to_all.5.gathered = bf16[8,4,1280]{2,1,0:T(4,128)(2,1)S(1)} all-to-all(bf16[8,4,1280]{2,1,0:T(4,128)(2,1)S(1)} %broadcast_in_dim.2), channel_id=1, replica_groups={{11,3,10,2,9,1,8,0},{15,7,14,6,13,5,12,4},{27,19,26,18,25,17,24,16},{31..., dimensions={0} | all-to-all | bytes 163840 | tf_op jit(solution)/shard_map/all_to_all | solution.py:405
  17.2 0.0 collective-permute-start
  17.2 1.3 %collective-permute-done.gathered_other = bf16[8,4,1280]{2,1,0:T(4,128)(2,1)S(1)} collective-permute-done((bf16[8,4,1280]{2,1,0:T(4,128)(2,1)S(1)}, bf16[8,4,1280]{2,1,0:T(4,128)(2,1)S(1)}, u32[]{:S(2)}, u32[]{:S(2)}) %collective-permute-start) | collective-permute-done | bytes 81952 | tf_op jit(solution)/shard_map/ppermute | solution.py:398
  18.4 1.8 %backward.1 = (f32[4,128,256]{2,1,0:T(8,128)S(1)}, f32[4,128,256]{2,1,0:T(8,128)S(1)}, bf16[4,256,256]{2,1,0:T(8,128)(2,1)S(1)}) custom-call(bf16[8,4,1280]{2,1,0:T(4,128)(2,1)S(1)} %all_to_all.5.gathered, bf16[8,4,1280]{2,1,0:T(4,128)(2,1)S(1)} %collective-permute-done.gathered_other, bf16[128,256]{1,0:T(8,128)(2,1)S(1)} %get-tuple-element.24.pooled_lanes, ...), custom_call_target="tpu_custom_call" | custom-call | tf_op jit(solution)/shard_map/backward/pallas_call | solution.py:351
  20.3 0.2 collective-permute-start.1
  20.5 2.5 %embed_gradient.1.refs_2_ = f32[4,32,256]{2,1,0:T(8,128)S(1)} custom-call(bf16[4,256,256]{2,1,0:T(8,128)(2,1)S(1)} %get-tuple-element.31.grads, bf16[1024,256]{1,0:T(8,128)(2,1)S(1)} %get-tuple-element.32.w_conv, f32[4,256,1024]{2,1,0:T(8,128)S(1)} %get-tuple-element.33.pre_embed, bf16[8,256,1024]{2,1,0:T(8,128)(2,1)S(1)} %get-tuple-element.34.one_hot), custom_call_target="tpu_custom_call" | custom-call | flops 1600000000 | bytes 10485760 | tf_op jit(solution)/shard_map/embed_gradient/pallas_call | solution.py:377
  23.0 0.0 collective-permute-done.1.refs_1_
  23.0 0.2 scale.1
  23.2 0.1 reduce-precision_convert_fusion.2
  23.3 0.1 reduce-precision_convert_fusion.1
  23.4 0.1 reduce-precision_convert_fusion
  23.5 2.8 %collective-permute-start.4 = (f16[160,256]{1,0:T(8,128)(2,1)S(1)}, f16[160,256]{1,0:T(8,128)(2,1)S(1)}, u32[]{:S(2)}, u32[]{:S(2)}) collective-permute-start(f16[160,256]{1,0:T(8,128)(2,1)S(1)} %reduce-precision_convert_fusion), channel_id=1, source_target_pairs={{0,3},{1,2},{2,1},{3,0},{4,7},{5,6},{6,5},{7,4},{8,11},{9,10},{10,... | collective-permute-start | bytes 245768 | tf_op jit(solution)/shard_map/ppermute | solution.py:398
  26.3 0.0 collective-permute-start.3
  26.3 1.6 %collective-permute-start.2 = (f16[160,256]{1,0:T(8,128)(2,1)S(1)}, f16[160,256]{1,0:T(8,128)(2,1)S(1)}, u32[]{:S(2)}, u32[]{:S(2)}) collective-permute-start(f16[160,256]{1,0:T(8,128)(2,1)S(1)} %reduce-precision_convert_fusion.2), channel_id=1, source_target_pairs={{0,1},{1,0},{2,3},{3,2},{4,5},{5,4},{6,7},{7,6},{8,9},{9,8},{10,11... | collective-permute-start | bytes 245768 | tf_op jit(solution)/shard_map/ppermute | solution.py:398
  28.0 1.4 %head_gradient.1 = (f32[64,512]{1,0:T(8,128)}, f32[8,128]{1,0:T(8,128)S(1)}) custom-call(bf16[8,4,1280]{2,1,0:T(4,128)(2,1)S(1)} %all_to_all.5.gathered, bf16[8,4,1280]{2,1,0:T(4,128)(2,1)S(1)} %collective-permute-done.gathered_other, bf16[256,512]{1,0:T(8,128)(2,1)S(1)} %get-tuple-element.28.w_head, f32[160,256]{1,0:T(8,128)S(1)} %get-tuple-element.35.after.refs_0_), custom_call_target="tpu_custom_call" | custom-call | flops 2000000000 | bytes 2097152 | tf_op jit(solution)/shard_map/head_gradient/pallas_call | solution.py:364
  29.3 1.4 %collective-permute-done.4 = f16[160,256]{1,0:T(8,128)(2,1)S(1)} collective-permute-done((f16[160,256]{1,0:T(8,128)(2,1)S(1)}, f16[160,256]{1,0:T(8,128)(2,1)S(1)}, u32[]{:S(2)}, u32[]{:S(2)}) %collective-permute-start.4) | collective-permute-done | bytes 81952 | tf_op jit(solution)/shard_map/ppermute | solution.py:398
  30.7 3.2 %collective-permute-done.3 = f16[160,256]{1,0:T(8,128)(2,1)S(1)} collective-permute-done((f16[160,256]{1,0:T(8,128)(2,1)S(1)}, f16[160,256]{1,0:T(8,128)(2,1)S(1)}, u32[]{:S(2)}, u32[]{:S(2)}) %collective-permute-start.3) | collective-permute-done | bytes 81952 | tf_op jit(solution)/shard_map/ppermute | solution.py:398
  34.0 0.0 collective-permute-done.2
  34.0 0.2 sum_z.1
  34.2 0.1 reduce-precision_convert_fusion.3
  34.3 1.6 %collective-permute-start.5 = (f16[160,256]{1,0:T(8,128)(2,1)S(1)}, f16[160,256]{1,0:T(8,128)(2,1)S(1)}, u32[]{:S(2)}, u32[]{:S(2)}) collective-permute-start(f16[160,256]{1,0:T(8,128)(2,1)S(1)} %get-tuple-element.43), channel_id=1, source_target_pairs={{0,8},{1,9},{2,10},{3,11},{4,12},{5,13},{6,14},{7,15},{8,0},{9,1},... | collective-permute-start | bytes 245768 | tf_op jit(solution)/shard_map/ppermute | solution.py:398
  35.8 2.9 %collective-permute-done.5 = f16[160,256]{1,0:T(8,128)(2,1)S(1)} collective-permute-done((f16[160,256]{1,0:T(8,128)(2,1)S(1)}, f16[160,256]{1,0:T(8,128)(2,1)S(1)}, u32[]{:S(2)}, u32[]{:S(2)}) %collective-permute-start.5) | collective-permute-done | bytes 81952 | tf_op jit(solution)/shard_map/ppermute | solution.py:398
  38.8 0.1 collective-permute-start.6
  38.9 1.4 %collective-permute-done.6.other = f32[160,256]{1,0:T(8,128)S(1)} collective-permute-done((f32[160,256]{1,0:T(8,128)S(1)}, f32[160,256]{1,0:T(8,128)S(1)}, u32[]{:S(2)}, u32[]{:S(2)}) %collective-permute-start.6) | collective-permute-done | bytes 163872 | tf_op jit(solution)/shard_map/ppermute | solution.py:398
  40.3 0.8 %outputs.1 = (f32[64,128]{1,0:T(8,128)}, f32[256,256]{1,0:T(8,128)}) custom-call(f32[160,256]{1,0:T(8,128)S(1)} %sum_x.1.own, f32[160,256]{1,0:T(8,128)S(1)} %collective-permute-done.6.other), custom_call_target="tpu_custom_call" | custom-call | tf_op jit(solution)/shard_map/outputs/pallas_call | solution.py:458
  (6 shorter events, 0.1 us)
Async XLA Ops:
  17.2 1.3 %collective-permute-start = (bf16[8,4,1280]{2,1,0:T(4,128)(2,1)S(1)}, bf16[8,4,1280]{2,1,0:T(4,128)(2,1)S(1)}, u32[]{:S(2)}, u32[]{:S(2)}) collective-permute-start(bf16[8,4,1280]{2,1,0:T(4,128)(2,1)S(1)} %all_to_all.5.gathered), channel_id=1, source_target_pairs={{0,4},{1,5},{2,6},{3,7},{4,0},{5,1},{6,2},{7,3},{8,12},{9,13},{10,... | collective-permute-start | bytes 245768 | tf_op jit(solution)/shard_map/ppermute | solution.py:398
  20.3 2.7 %collective-permute-start.1 = (f32[4,128,256]{2,1,0:T(8,128)S(1)}, f32[4,128,256]{2,1,0:T(8,128)S(1)}, u32[]{:S(2)}, u32[]{:S(2)}) collective-permute-start(f32[4,128,256]{2,1,0:T(8,128)S(1)} %get-tuple-element.30), channel_id=1, source_target_pairs={{0,4},{1,5},{2,6},{3,7},{4,0},{5,1},{6,2},{7,3},{8,12},{9,13},{10,... | collective-permute-start | bytes 1572872 | tf_op jit(solution)/shard_map/ppermute | solution.py:398
  23.5 7.2 %collective-permute-start.4 = (f16[160,256]{1,0:T(8,128)(2,1)S(1)}, f16[160,256]{1,0:T(8,128)(2,1)S(1)}, u32[]{:S(2)}, u32[]{:S(2)}) collective-permute-start(f16[160,256]{1,0:T(8,128)(2,1)S(1)} %reduce-precision_convert_fusion), channel_id=1, source_target_pairs={{0,3},{1,2},{2,1},{3,0},{4,7},{5,6},{6,5},{7,4},{8,11},{9,10},{10,... | collective-permute-start | bytes 245768 | tf_op jit(solution)/shard_map/ppermute | solution.py:398
  26.3 7.6 %collective-permute-start.3 = (f16[160,256]{1,0:T(8,128)(2,1)S(1)}, f16[160,256]{1,0:T(8,128)(2,1)S(1)}, u32[]{:S(2)}, u32[]{:S(2)}) collective-permute-start(f16[160,256]{1,0:T(8,128)(2,1)S(1)} %reduce-precision_convert_fusion.1), channel_id=1, source_target_pairs={{0,2},{1,3},{2,0},{3,1},{4,6},{5,7},{6,4},{7,5},{8,10},{9,11},{10,... | collective-permute-start | bytes 245768 | tf_op jit(solution)/shard_map/ppermute | solution.py:398
  26.3 7.7 %collective-permute-start.2 = (f16[160,256]{1,0:T(8,128)(2,1)S(1)}, f16[160,256]{1,0:T(8,128)(2,1)S(1)}, u32[]{:S(2)}, u32[]{:S(2)}) collective-permute-start(f16[160,256]{1,0:T(8,128)(2,1)S(1)} %reduce-precision_convert_fusion.2), channel_id=1, source_target_pairs={{0,1},{1,0},{2,3},{3,2},{4,5},{5,4},{6,7},{7,6},{8,9},{9,8},{10,11... | collective-permute-start | bytes 245768 | tf_op jit(solution)/shard_map/ppermute | solution.py:398
  34.3 4.5 %collective-permute-start.5 = (f16[160,256]{1,0:T(8,128)(2,1)S(1)}, f16[160,256]{1,0:T(8,128)(2,1)S(1)}, u32[]{:S(2)}, u32[]{:S(2)}) collective-permute-start(f16[160,256]{1,0:T(8,128)(2,1)S(1)} %get-tuple-element.43), channel_id=1, source_target_pairs={{0,8},{1,9},{2,10},{3,11},{4,12},{5,13},{6,14},{7,15},{8,0},{9,1},... | collective-permute-start | bytes 245768 | tf_op jit(solution)/shard_map/ppermute | solution.py:398
  38.8 1.5 %collective-permute-start.6 = (f32[160,256]{1,0:T(8,128)S(1)}, f32[160,256]{1,0:T(8,128)S(1)}, u32[]{:S(2)}, u32[]{:S(2)}) collective-permute-start(f32[160,256]{1,0:T(8,128)S(1)} %sum_x.1.own), channel_id=1, source_target_pairs={{0,4},{1,5},{2,6},{3,7},{4,0},{5,1},{6,2},{7,3},{8,12},{9,13},{10,... | collective-permute-start | bytes 491528 | tf_op jit(solution)/shard_map/ppermute | solution.py:398

commit v22 on v21

--- a/solution.py
+++ b/solution.py
@@ -428,7 +428,7 @@
     plain = jax.ShapeDtypeStruct((rows, width), F32)
     own, *coded = local_kernel(scale_kernel, (plain,) + (plain,) * (fsdp - 1), "scale", keep, other, embed)
     received = [
-        exchange(to_half(part)[1], dp, fsdp, 0, 0, place + 1).astype(F32) for place, part in enumerate(coded)
+        exchange(part.astype(jnp.float16), dp, fsdp, 0, 0, place + 1).astype(F32) for place, part in enumerate(coded)
     ]
     grad_head, token = head_gradient(fsdp, gathered, w_head, own)
     (coded,) = local_kernel(

time: 41.2 us -> 41 us (level)
  no operation moved by 1% of the time
where the time goes in v22:
time: 41 us; the launch traced here: 40.8 us
  Pallas kernels  11.8 us (29%)
  blocking collectives  11.5 us (28%)
  waiting for transfers between devices  10.2 us (25%)
  starting transfers between devices  6.34 us (15%)
  between operations  0.77 us (2%)
    all_to_all x1, blocking collectives, gather_blocks(): lax.all_to_all(copies, GROUP, 0, 0, axis_index_groups=groups, tiled=True)  11.5 us
    ppermute x7, waiting for transfers between devices, exchange(): return lax.ppermute(block, GROUP, pairs)  10.2 us
    ppermute x7, starting transfers between devices, exchange(): return lax.ppermute(block, GROUP, pairs)  6.34 us
    pallas_call x1, Pallas kernels, forward(): pl.pallas_call(forward_kernel, out_shape=(pltpu.VMEM((samples, 2 * latent...  4.96 us
    pallas_call x1, Pallas kernels, embed_gradient(): pl.pallas_call(embed_kernel, out_shape=pltpu.VMEM((fsdp, (96 // fsdp + 7)...  2.48 us
    pallas_call x1, Pallas kernels, backward(): pl.pallas_call(backward_kernel, out_shape=(payload, payload, pltpu.VMEM((...  1.83 us
    pallas_call x1, Pallas kernels, head_gradient(): pl.pallas_call(head_kernel, out_shape=(jax.ShapeDtypeStruct((256 // fsdp,...  1.38 us
  transfers between devices with their start and end apart: 7, of which 5 were waited for; matrix products, arithmetic and copies ran while one was open for 0% of the time, Pallas kernels for 9%

profile of v22, /device:TPU:0, one launch (start us, length us, event | category | flops | bytes accessed | tf_op | source)
XLA Modules:
  0.0 40.8 jit_solution(215340708182913096)
XLA Ops:
  0.6 5.0 %forward.1 = (bf16[4,1280]{1,0:T(4,128)(2,1)S(1)}, bf16[128,256]{1,0:T(8,128)(2,1)S(1)}, bf16[4,512]{1,0:T(4,128)(2,1)S(1)}, bf16[8,256,1024]{2,1,0:T(8,128)(2,1...) custom-call(s32[256,2048]{1,0:T(8,128)} %bitcast.1, ...), custom_call_target="tpu_custom_call" | custom-call | tf_op jit(solution)/shard_map/forward/pallas_call | solution.py:327
  5.6 11.5 %all_to_all.5.gathered = bf16[8,4,1280]{2,1,0:T(4,128)(2,1)S(1)} all-to-all(bf16[8,4,1280]{2,1,0:T(4,128)(2,1)S(1)} %broadcast_in_dim.2), channel_id=1, replica_groups={{11,3,10,2,9,1,8,0},{15,7,14,6,13,5,12,4},{27,19,26,18,25,17,24,16},{31..., dimensions={0} | all-to-all | bytes 163840 | tf_op jit(solution)/shard_map/all_to_all | solution.py:405
  17.2 0.0 collective-permute-start
  17.2 1.3 %collective-permute-done.gathered_other = bf16[8,4,1280]{2,1,0:T(4,128)(2,1)S(1)} collective-permute-done((bf16[8,4,1280]{2,1,0:T(4,128)(2,1)S(1)}, bf16[8,4,1280]{2,1,0:T(4,128)(2,1)S(1)}, u32[]{:S(2)}, u32[]{:S(2)}) %collective-permute-start) | collective-permute-done | bytes 81952 | tf_op jit(solution)/shard_map/ppermute | solution.py:398
  18.4 1.8 %backward.1 = (f32[4,128,256]{2,1,0:T(8,128)S(1)}, f32[4,128,256]{2,1,0:T(8,128)S(1)}, bf16[4,256,256]{2,1,0:T(8,128)(2,1)S(1)}) custom-call(bf16[8,4,1280]{2,1,0:T(4,128)(2,1)S(1)} %all_to_all.5.gathered, bf16[8,4,1280]{2,1,0:T(4,128)(2,1)S(1)} %collective-permute-done.gathered_other, bf16[128,256]{1,0:T(8,128)(2,1)S(1)} %get-tuple-element.24.pooled_lanes, ...), custom_call_target="tpu_custom_call" | custom-call | tf_op jit(solution)/shard_map/backward/pallas_call | solution.py:351
  20.3 0.2 collective-permute-start.1
  20.5 2.5 %embed_gradient.1.refs_2_ = f32[4,32,256]{2,1,0:T(8,128)S(1)} custom-call(bf16[4,256,256]{2,1,0:T(8,128)(2,1)S(1)} %get-tuple-element.31.grads, bf16[1024,256]{1,0:T(8,128)(2,1)S(1)} %get-tuple-element.32.w_conv, f32[4,256,1024]{2,1,0:T(8,128)S(1)} %get-tuple-element.33.pre_embed, bf16[8,256,1024]{2,1,0:T(8,128)(2,1)S(1)} %get-tuple-element.34.one_hot), custom_call_target="tpu_custom_call" | custom-call | flops 1600000000 | bytes 10485760 | tf_op jit(solution)/shard_map/embed_gradient/pallas_call | solution.py:377
  23.0 0.0 collective-permute-done.1.refs_1_
  23.0 0.2 scale.1
  23.3 2.8 %collective-permute-start.4 = (f16[160,256]{1,0:T(8,128)(2,1)S(1)}, f16[160,256]{1,0:T(8,128)(2,1)S(1)}, u32[]{:S(2)}, u32[]{:S(2)}) collective-permute-start(f16[160,256]{1,0:T(8,128)(2,1)S(1)} %convert_element_type.28), channel_id=1, source_target_pairs={{0,3},{1,2},{2,1},{3,0},{4,7},{5,6},{6,5},{7,4},{8,11},{9,10},{10,... | collective-permute-start | bytes 245768 | tf_op jit(solution)/shard_map/ppermute | solution.py:398
  26.1 0.0 collective-permute-start.3
  26.1 1.6 %collective-permute-start.2 = (f16[160,256]{1,0:T(8,128)(2,1)S(1)}, f16[160,256]{1,0:T(8,128)(2,1)S(1)}, u32[]{:S(2)}, u32[]{:S(2)}) collective-permute-start(f16[160,256]{1,0:T(8,128)(2,1)S(1)} %convert_element_type.24), channel_id=1, source_target_pairs={{0,1},{1,0},{2,3},{3,2},{4,5},{5,4},{6,7},{7,6},{8,9},{9,8},{10,11... | collective-permute-start | bytes 245768 | tf_op jit(solution)/shard_map/ppermute | solution.py:398
  27.7 1.4 %head_gradient.1 = (f32[64,512]{1,0:T(8,128)}, f32[8,128]{1,0:T(8,128)S(1)}) custom-call(bf16[8,4,1280]{2,1,0:T(4,128)(2,1)S(1)} %all_to_all.5.gathered, bf16[8,4,1280]{2,1,0:T(4,128)(2,1)S(1)} %collective-permute-done.gathered_other, bf16[256,512]{1,0:T(8,128)(2,1)S(1)} %get-tuple-element.28.w_head, f32[160,256]{1,0:T(8,128)S(1)} %get-tuple-element.35.after.refs_0_), custom_call_target="tpu_custom_call" | custom-call | flops 2000000000 | bytes 2097152 | tf_op jit(solution)/shard_map/head_gradient/pallas_call | solution.py:364
  29.1 1.4 %collective-permute-done.4 = f16[160,256]{1,0:T(8,128)(2,1)S(1)} collective-permute-done((f16[160,256]{1,0:T(8,128)(2,1)S(1)}, f16[160,256]{1,0:T(8,128)(2,1)S(1)}, u32[]{:S(2)}, u32[]{:S(2)}) %collective-permute-start.4) | collective-permute-done | bytes 81952 | tf_op jit(solution)/shard_map/ppermute | solution.py:398
  30.5 3.2 %collective-permute-done.3 = f16[160,256]{1,0:T(8,128)(2,1)S(1)} collective-permute-done((f16[160,256]{1,0:T(8,128)(2,1)S(1)}, f16[160,256]{1,0:T(8,128)(2,1)S(1)}, u32[]{:S(2)}, u32[]{:S(2)}) %collective-permute-start.3) | collective-permute-done | bytes 81952 | tf_op jit(solution)/shard_map/ppermute | solution.py:398
  33.7 0.0 collective-permute-done.2
  33.8 0.2 sum_z.1
  33.9 0.1 reduce-precision_convert_fusion
  34.0 1.6 %collective-permute-start.5 = (f16[160,256]{1,0:T(8,128)(2,1)S(1)}, f16[160,256]{1,0:T(8,128)(2,1)S(1)}, u32[]{:S(2)}, u32[]{:S(2)}) collective-permute-start(f16[160,256]{1,0:T(8,128)(2,1)S(1)} %get-tuple-element.43), channel_id=1, source_target_pairs={{0,8},{1,9},{2,10},{3,11},{4,12},{5,13},{6,14},{7,15},{8,0},{9,1},... | collective-permute-start | bytes 245768 | tf_op jit(solution)/shard_map/ppermute | solution.py:398
  35.6 2.9 %collective-permute-done.5 = f16[160,256]{1,0:T(8,128)(2,1)S(1)} collective-permute-done((f16[160,256]{1,0:T(8,128)(2,1)S(1)}, f16[160,256]{1,0:T(8,128)(2,1)S(1)}, u32[]{:S(2)}, u32[]{:S(2)}) %collective-permute-start.5) | collective-permute-done | bytes 81952 | tf_op jit(solution)/shard_map/ppermute | solution.py:398
  38.6 0.1 collective-permute-start.6
  38.7 1.4 %collective-permute-done.6.other = f32[160,256]{1,0:T(8,128)S(1)} collective-permute-done((f32[160,256]{1,0:T(8,128)S(1)}, f32[160,256]{1,0:T(8,128)S(1)}, u32[]{:S(2)}, u32[]{:S(2)}) %collective-permute-start.6) | collective-permute-done | bytes 163872 | tf_op jit(solution)/shard_map/ppermute | solution.py:398
  40.1 0.8 %outputs.1 = (f32[64,128]{1,0:T(8,128)}, f32[256,256]{1,0:T(8,128)}) custom-call(f32[160,256]{1,0:T(8,128)S(1)} %sum_x.1.own, f32[160,256]{1,0:T(8,128)S(1)} %collective-permute-done.6.other), custom_call_target="tpu_custom_call" | custom-call | tf_op jit(solution)/shard_map/outputs/pallas_call | solution.py:458
  (9 shorter events, 0.1 us)
Async XLA Ops:
  17.2 1.3 %collective-permute-start = (bf16[8,4,1280]{2,1,0:T(4,128)(2,1)S(1)}, bf16[8,4,1280]{2,1,0:T(4,128)(2,1)S(1)}, u32[]{:S(2)}, u32[]{:S(2)}) collective-permute-start(bf16[8,4,1280]{2,1,0:T(4,128)(2,1)S(1)} %all_to_all.5.gathered), channel_id=1, source_target_pairs={{0,4},{1,5},{2,6},{3,7},{4,0},{5,1},{6,2},{7,3},{8,12},{9,13},{10,... | collective-permute-start | bytes 245768 | tf_op jit(solution)/shard_map/ppermute | solution.py:398
  20.3 2.7 %collective-permute-start.1 = (f32[4,128,256]{2,1,0:T(8,128)S(1)}, f32[4,128,256]{2,1,0:T(8,128)S(1)}, u32[]{:S(2)}, u32[]{:S(2)}) collective-permute-start(f32[4,128,256]{2,1,0:T(8,128)S(1)} %get-tuple-element.30), channel_id=1, source_target_pairs={{0,4},{1,5},{2,6},{3,7},{4,0},{5,1},{6,2},{7,3},{8,12},{9,13},{10,... | collective-permute-start | bytes 1572872 | tf_op jit(solution)/shard_map/ppermute | solution.py:398
  23.3 7.2 %collective-permute-start.4 = (f16[160,256]{1,0:T(8,128)(2,1)S(1)}, f16[160,256]{1,0:T(8,128)(2,1)S(1)}, u32[]{:S(2)}, u32[]{:S(2)}) collective-permute-start(f16[160,256]{1,0:T(8,128)(2,1)S(1)} %convert_element_type.28), channel_id=1, source_target_pairs={{0,3},{1,2},{2,1},{3,0},{4,7},{5,6},{6,5},{7,4},{8,11},{9,10},{10,... | collective-permute-start | bytes 245768 | tf_op jit(solution)/shard_map/ppermute | solution.py:398
  26.1 7.6 %collective-permute-start.3 = (f16[160,256]{1,0:T(8,128)(2,1)S(1)}, f16[160,256]{1,0:T(8,128)(2,1)S(1)}, u32[]{:S(2)}, u32[]{:S(2)}) collective-permute-start(f16[160,256]{1,0:T(8,128)(2,1)S(1)} %convert_element_type.26), channel_id=1, source_target_pairs={{0,2},{1,3},{2,0},{3,1},{4,6},{5,7},{6,4},{7,5},{8,10},{9,11},{10,... | collective-permute-start | bytes 245768 | tf_op jit(solution)/shard_map/ppermute | solution.py:398
  26.1 7.7 %collective-permute-start.2 = (f16[160,256]{1,0:T(8,128)(2,1)S(1)}, f16[160,256]{1,0:T(8,128)(2,1)S(1)}, u32[]{:S(2)}, u32[]{:S(2)}) collective-permute-start(f16[160,256]{1,0:T(8,128)(2,1)S(1)} %convert_element_type.24), channel_id=1, source_target_pairs={{0,1},{1,0},{2,3},{3,2},{4,5},{5,4},{6,7},{7,6},{8,9},{9,8},{10,11... | collective-permute-start | bytes 245768 | tf_op jit(solution)/shard_map/ppermute | solution.py:398
  34.0 4.5 %collective-permute-start.5 = (f16[160,256]{1,0:T(8,128)(2,1)S(1)}, f16[160,256]{1,0:T(8,128)(2,1)S(1)}, u32[]{:S(2)}, u32[]{:S(2)}) collective-permute-start(f16[160,256]{1,0:T(8,128)(2,1)S(1)} %get-tuple-element.43), channel_id=1, source_target_pairs={{0,8},{1,9},{2,10},{3,11},{4,12},{5,13},{6,14},{7,15},{8,0},{9,1},... | collective-permute-start | bytes 245768 | tf_op jit(solution)/shard_map/ppermute | solution.py:398
  38.6 1.5 %collective-permute-start.6 = (f32[160,256]{1,0:T(8,128)S(1)}, f32[160,256]{1,0:T(8,128)S(1)}, u32[]{:S(2)}, u32[]{:S(2)}) collective-permute-start(f32[160,256]{1,0:T(8,128)S(1)} %sum_x.1.own), channel_id=1, source_target_pairs={{0,4},{1,5},{2,6},{3,7},{4,0},{5,1},{6,2},{7,3},{8,12},{9,13},{10,... | collective-permute-start | bytes 491528 | tf_op jit(solution)/shard_map/ppermute | solution.py:398
